TPU v7x, 256 devices: a whole 4x4x8 slice. The times are simulated.
256 devices in a mesh: section: 16 (over z_lo, y, core), seq: 16 (over x, z_hi).
Axes of the slice: x: 4, y: 4, z: 8 (z_hi: 4, z_lo: 2; z = z_hi * 2 + z_lo), core: 2. Of those that a mesh axis runs over, the one named last changes fastest.
Arguments:
- query: bfloat16 [128, 384, 4096], P('section', 'seq'), may hold values from -5 to 5
- key: bfloat16 [128, 384, 4096], P('section', 'seq'), may hold values from -5 to 5
- value: bfloat16 [128, 384, 4096], P('section', 'seq'), may hold values from -6 to 6
- qk_gain: float32 [2, 4096], replicated, may hold values from 1 to 2
- timesteps: int32 [128], P('section'), may hold values from 0 to 999, as said below
- gate_weight: bfloat16 [256, 4096], replicated, may hold values from -0.375 to 0.375
- slot: int32 [1], replicated, may hold values from 0 to 7
- fresh: bfloat16 [384, 4096], P('seq'), may hold values from -6 to 6
Outputs:
- shifted: bfloat16 [128, 384, 4096], P('section', 'seq')
Inputs may be any that keep to these rules, and one draw needn't show every extreme that they name: `timesteps`: never falls along the queue; the first frame has 0 and the last 999.
All inputs are finite; a program needn't handle non-finite values.
Results may differ from a plain program's by a relative error of at most 0.0084.
Values may be sent and summed in bfloat16 or wider, within the bound.
No kernel may reach another device: no remote copies, remote signals or barrier semaphores. Data moves between devices by JAX's collectives and lax.ppermute only.
A program may use at most 256 MiB of HBM per device.

v0:
```python
import math

import jax
import jax.numpy as jnp
from jax import lax
from jax.sharding import PartitionSpec as P

HD = 128


def from_behind(value, axis, steps):
    count = lax.axis_size(axis)
    initial, last = (max(0, -steps), min(count, count - steps))
    return lax.ppermute(value, axis, [(source, source + steps) for source in range(initial, last)])


def rms_scaled(values, gain):
    widened = values.astype(jnp.float32)
    factor = lax.rsqrt(jnp.mean(widened * widened, axis=-1, keepdims=True) + 1e-06)
    return (widened * factor * gain).astype(jnp.bfloat16)


def level_gate(steps, gate_weight):
    half = gate_weight.shape[0] // 2
    freqs = jnp.exp(-math.log(10000.0) * jnp.arange(half, dtype=jnp.float32) / half)
    angles = steps.astype(jnp.float32)[:, None] * freqs[None, :]
    embed = jnp.concatenate([jnp.cos(angles), jnp.sin(angles)], axis=1).astype(jnp.bfloat16)
    return jnp.dot(embed, gate_weight, preferred_element_type=jnp.float32)


def shards(query, key, value, qk_gain, timesteps, gate_weight, slot, fresh):
    frames, rows, inner = query.shape
    heads = inner // HD
    groups = lax.axis_size("seq")
    per_group = heads // groups
    factor = 1.0 / math.sqrt(HD)
    qn = rms_scaled(query, qk_gain[0])
    kn = rms_scaled(key, qk_gain[1])

    def split_heads(array):
        return array.reshape(frames, rows, groups, per_group, HD)

    q_all = lax.all_to_all(split_heads(qn), "seq", split_axis=2, concat_axis=1, tiled=True)
    k_all = lax.all_to_all(split_heads(kn), "seq", split_axis=2, concat_axis=1, tiled=True)
    v_all = lax.all_to_all(split_heads(value), "seq", split_axis=2, concat_axis=1, tiled=True)
    count = q_all.shape[3]
    length = q_all.shape[0] * q_all.shape[1]
    block = 512
    q_blocks = q_all.reshape(length // block, block, count, HD)
    k_flat = k_all.reshape(length, count, HD)
    v_flat = v_all.reshape(length, count, HD)

    def one_block(q_flat):
        scores = (
            jnp.einsum("qhd,khd->hqk", q_flat, k_flat, preferred_element_type=jnp.float32) * factor
        )
        peak = jnp.max(scores, axis=2, keepdims=True)
        weights = jnp.exp(scores - peak)
        totals = jnp.sum(weights, axis=2)
        mixed = jnp.einsum(
            "hqk,khd->qhd", weights.astype(jnp.bfloat16), v_flat, preferred_element_type=jnp.float32
        )
        return (mixed / totals.T[:, :, None]).astype(jnp.bfloat16)

    result = lax.map(one_block, q_blocks)
    attended = lax.all_to_all(
        result.reshape(q_all.shape), "seq", split_axis=1, concat_axis=2, tiled=True
    )
    attended = attended.reshape(frames, rows, inner)
    gate = level_gate(timesteps, gate_weight)
    gated = (gate[:, None, :] * attended.astype(jnp.float32)).astype(jnp.bfloat16)
    position = slot[0]
    leaving = lax.dynamic_index_in_dim(gated, position, 0, keepdims=False)
    arriving = from_behind(leaving, "section", 1)
    arriving = jnp.where(lax.axis_index("section") == 0, fresh, arriving)
    return lax.dynamic_update_index_in_dim(gated, arriving, position, 0)


def solution(mesh):
    placed = (
        P("section", "seq", None),
        P("section", "seq", None),
        P("section", "seq", None),
        P(),
        P("section"),
        P(),
        P(),
        P("seq", None),
    )
    return jax.shard_map(
        shards, mesh=mesh, in_specs=placed, out_specs=P("section", "seq", None), check_vma=False
    )
```

profile of v0, /device:TPU:32, one launch (start us, length us, event | category | flops | bytes accessed | tf_op | source)
XLA Modules:
  0.0 272.8 jit_solution(16114584737200647348)
XLA Ops:
  0.0 0.0 copy-start
  0.0 1.0 fusion.39
  1.0 1.9 fusion.29
  2.8 0.0 copy-done.1
  2.8 1.6 fusion.31
  4.5 3.8 %reshape.59 = bf16[8,24,16,2,128]{4,3,2,1,0:T(2,128)(2,1)} reshape(bf16[8,24,4096]{2,1,0:T(8,128)(2,1)} %fusion.31) | data formatting | bytes 3145728 | tf_op jit(solution)/shard_map/reshape | solution.py:41
  8.3 3.2 %copy.32 = bf16[8,24,16,2,128]{4,1,0,3,2:T(8,128)(2,1)} copy(bf16[8,24,16,2,128]{4,3,2,1,0:T(2,128)(2,1)} %reshape.59) | data formatting | bytes 3145728 | tf_op jit(solution)/shard_map/reshape | solution.py:41
  11.4 10.2 %all-to-all-start.1 = ((bf16[8,24,16,2,128]{4,1,0,3,2:T(8,128)(2,1)}), bf16[8,24,16,2,128]{4,1,0,3,2:T(8,128)(2,1)}, u32[]{:S(2)}, u32[]{:S(2)}) async-start(bf16[8,24,16,2,128]{4,1,0,3,2:T(8,128)(2,1)} %copy.32), calls=%async_computation.1 | async-start | bytes 3145728 | tf_op jit(solution)/shard_map/all_to_all | solution.py:44
  21.6 0.0 copy-start.2
  21.6 1.9 fusion.26
  23.5 0.0 copy-done.2
  23.5 1.6 fusion.28
  25.2 3.8 %reshape.57 = bf16[8,24,16,2,128]{4,3,2,1,0:T(2,128)(2,1)} reshape(bf16[8,24,4096]{2,1,0:T(8,128)(2,1)} %fusion.28) | data formatting | bytes 3145728 | tf_op jit(solution)/shard_map/reshape | solution.py:41
  29.0 4.0 %copy.30 = bf16[8,24,16,2,128]{4,3,1,0,2:T(2,128)(2,1)} copy(bf16[8,24,16,2,128]{4,3,2,1,0:T(2,128)(2,1)} %reshape.57) | data formatting | bytes 3145728 | tf_op jit(solution)/shard_map/reshape | solution.py:41
  33.0 29.3 %all-to-all-done.1 = bf16[8,24,16,2,128]{4,1,0,3,2:T(8,128)(2,1)} async-done(((bf16[8,24,16,2,128]{4,1,0,3,2:T(8,128)(2,1)}), bf16[8,24,16,2,128]{4,1,0,3,2:T(8,128)(2,1)}, u32[]{:S(2)}, u32[]{:S(2)}) %all-to-all-start.1) | async-done | bytes 1572896 | tf_op jit(solution)/shard_map/all_to_all | solution.py:44
  62.3 4.4 %all-to-all-start = ((bf16[8,24,16,2,128]{4,3,1,0,2:T(2,128)(2,1)}), bf16[8,24,16,2,128]{4,3,1,0,2:T(2,128)(2,1)}, u32[]{:S(2)}, u32[]{:S(2)}) async-start(bf16[8,24,16,2,128]{4,3,1,0,2:T(2,128)(2,1)} %copy.30), calls=%async_computation | async-start | bytes 3145728 | tf_op jit(solution)/shard_map/all_to_all | solution.py:43
  66.7 3.8 %reshape.61 = bf16[8,24,16,2,128]{4,3,2,1,0:T(2,128)(2,1)} reshape(bf16[8,24,4096]{2,1,0:T(8,128)(2,1)} %param.12) | data formatting | bytes 3145728 | tf_op jit(solution)/shard_map/reshape | solution.py:41
  70.5 3.2 %copy.34 = bf16[8,24,16,2,128]{4,1,0,3,2:T(8,128)(2,1)} copy(bf16[8,24,16,2,128]{4,3,2,1,0:T(2,128)(2,1)} %reshape.61) | data formatting | bytes 3145728 | tf_op jit(solution)/shard_map/reshape | solution.py:41
  73.7 33.1 %all-to-all-done = bf16[8,24,16,2,128]{4,3,1,0,2:T(2,128)(2,1)} async-done(((bf16[8,24,16,2,128]{4,3,1,0,2:T(2,128)(2,1)}), bf16[8,24,16,2,128]{4,3,1,0,2:T(2,128)(2,1)}, u32[]{:S(2)}, u32[]{:S(2)}) %all-to-all-start) | async-done | bytes 1572896 | tf_op jit(solution)/shard_map/all_to_all | solution.py:43
  106.8 4.6 %all-to-all-start.2 = ((bf16[8,24,16,2,128]{4,1,0,3,2:T(8,128)(2,1)}), bf16[8,24,16,2,128]{4,1,0,3,2:T(8,128)(2,1)}, u32[]{:S(2)}, u32[]{:S(2)}) async-start(bf16[8,24,16,2,128]{4,1,0,3,2:T(8,128)(2,1)} %copy.34), calls=%async_computation.2 | async-start | bytes 3145728 | tf_op jit(solution)/shard_map/all_to_all | solution.py:45
  111.4 3.0 %copy.33 = bf16[8,24,16,2,128]{4,1,2,0,3:T(8,128)(2,1)} copy(bf16[8,24,16,2,128]{4,1,0,3,2:T(8,128)(2,1)} %all-to-all-done.1) | data formatting | bytes 3145728 | tf_op jit(solution)/shard_map/all_to_all | solution.py:44
  114.4 2.9 %copy.31 = bf16[8,24,16,2,128]{4,1,2,0,3:T(8,128)(2,1)} copy(bf16[8,24,16,2,128]{4,3,1,0,2:T(2,128)(2,1)} %all-to-all-done) | data formatting | bytes 3145728 | tf_op jit(solution)/shard_map/all_to_all | solution.py:43
  117.2 26.7 %all-to-all-done.2 = bf16[8,24,16,2,128]{4,1,0,3,2:T(8,128)(2,1)} async-done(((bf16[8,24,16,2,128]{4,1,0,3,2:T(8,128)(2,1)}), bf16[8,24,16,2,128]{4,1,0,3,2:T(8,128)(2,1)}, u32[]{:S(2)}, u32[]{:S(2)}) %all-to-all-start.2) | async-done | bytes 1572896 | tf_op jit(solution)/shard_map/all_to_all | solution.py:45
  143.9 3.0 %copy.35 = bf16[8,24,16,2,128]{4,1,2,0,3:T(8,128)(2,1)} copy(bf16[8,24,16,2,128]{4,1,0,3,2:T(8,128)(2,1)} %all-to-all-done.2) | data formatting | bytes 3145728 | tf_op jit(solution)/shard_map/all_to_all | solution.py:45
  146.8 51.4 %while.10 = (s32[]{:T(128)}, bf16[6,512,2,128]{3,1,0,2:T(8,128)(2,1)}, bf16[6,512,2,128]{3,1,0,2:T(8,128)(2,1)}, bf16[3072,2,128]{2,0,1:T(8,128)(2,1)}, bf16[3072,2,128]{2,0,1:T(8,128)(2,1)}, /*index=5*/s32[]{:T(128)}) while((s32[]{:T(128)}, bf16[6,512,2,128]{3,1,0,2:T(8,128)(2,1)}, bf16[6,512,2,128]{3,1,0,2:T(8,128)(2,1)}, ...), condition=%wide.region_5.6_spmd, body=%wide.region_2.5_spmd.sunk | while | flops 1636038656 | bytes 47731808 | solution.py:65
  146.8 3.4 %multiply_reduce_fusion.2 = (f32[2,512]{1,0:T(2,128)S(1)}, f32[2,512,3072]{2,1,0:T(8,128)S(1)}) fusion(bf16[3072,2,128]{2,0,1:T(8,128)(2,1)} %get-tuple-element.119, bf16[6,512,2,128]{3,1,0,2:T(8,128)(2,1)} %get-tuple-element.118, s32[]{:T(128)} %get-tuple-element.110), kind=kOutput, calls=%fused_computation.1.clone.1 | convolution fusion | flops 811596800 | bytes 14422528 | tf_op jit(solution)/shard_map/while/body/eval_jaxpr/qhd,khd->hqk/dot_general | solution.py:55
  150.2 0.0 copy-start.4
  150.2 2.2 fusion.51
  152.4 0.0 copy-done.4
  152.4 3.0 %fusion.52 = bf16[6,512,2,128]{3,1,0,2:T(8,128)(2,1)} fusion(bf16[6,512,2,128]{3,1,0,2:T(8,128)(2,1)} %get-tuple-element.111, s32[]{:T(128)} %get-tuple-element.110, bf16[3072,2,128]{2,0,1:T(8,128)(2,1)S(1)} %copy-done.4, f32[2,512,3072]{2,1,0:T(8,128)S(1)} %get-tuple-element.102, f32[2,512]{1,0:T(2,128)S(1)} %get-tuple-element.103, ...), kind=kOutput, calls=%fused_computation.11.clone.1 | convolution fusion | flops 815005696 | bytes 14426624 | tf_op jit(solution)/shard_map/while/body/eval_jaxpr/hqk,khd->qhd/dot_general | solution.py:60
  155.4 3.4 %multiply_reduce_fusion.2 = (f32[2,512]{1,0:T(2,128)S(1)}, f32[2,512,3072]{2,1,0:T(8,128)S(1)}) fusion(bf16[3072,2,128]{2,0,1:T(8,128)(2,1)} %get-tuple-element.119, bf16[6,512,2,128]{3,1,0,2:T(8,128)(2,1)} %get-tuple-element.118, s32[]{:T(128)} %get-tuple-element.110), kind=kOutput, calls=%fused_computation.1.clone.1 | convolution fusion | flops 811596800 | bytes 14422528 | tf_op jit(solution)/shard_map/while/body/eval_jaxpr/qhd,khd->hqk/dot_general | solution.py:55
  158.8 0.0 copy-start.4
  158.8 2.2 fusion.51
  161.0 0.0 copy-done.4
  161.0 3.0 %fusion.52 = bf16[6,512,2,128]{3,1,0,2:T(8,128)(2,1)} fusion(bf16[6,512,2,128]{3,1,0,2:T(8,128)(2,1)} %get-tuple-element.111, s32[]{:T(128)} %get-tuple-element.110, bf16[3072,2,128]{2,0,1:T(8,128)(2,1)S(1)} %copy-done.4, f32[2,512,3072]{2,1,0:T(8,128)S(1)} %get-tuple-element.102, f32[2,512]{1,0:T(2,128)S(1)} %get-tuple-element.103, ...), kind=kOutput, calls=%fused_computation.11.clone.1 | convolution fusion | flops 815005696 | bytes 14426624 | tf_op jit(solution)/shard_map/while/body/eval_jaxpr/hqk,khd->qhd/dot_general | solution.py:60
  164.0 3.4 %multiply_reduce_fusion.2 = (f32[2,512]{1,0:T(2,128)S(1)}, f32[2,512,3072]{2,1,0:T(8,128)S(1)}) fusion(bf16[3072,2,128]{2,0,1:T(8,128)(2,1)} %get-tuple-element.119, bf16[6,512,2,128]{3,1,0,2:T(8,128)(2,1)} %get-tuple-element.118, s32[]{:T(128)} %get-tuple-element.110), kind=kOutput, calls=%fused_computation.1.clone.1 | convolution fusion | flops 811596800 | bytes 14422528 | tf_op jit(solution)/shard_map/while/body/eval_jaxpr/qhd,khd->hqk/dot_general | solution.py:55
  167.4 2.2 fusion.51
  169.6 0.0 copy-done.4
  169.6 3.0 %fusion.52 = bf16[6,512,2,128]{3,1,0,2:T(8,128)(2,1)} fusion(bf16[6,512,2,128]{3,1,0,2:T(8,128)(2,1)} %get-tuple-element.111, s32[]{:T(128)} %get-tuple-element.110, bf16[3072,2,128]{2,0,1:T(8,128)(2,1)S(1)} %copy-done.4, f32[2,512,3072]{2,1,0:T(8,128)S(1)} %get-tuple-element.102, f32[2,512]{1,0:T(2,128)S(1)} %get-tuple-element.103, ...), kind=kOutput, calls=%fused_computation.11.clone.1 | convolution fusion | flops 815005696 | bytes 14426624 | tf_op jit(solution)/shard_map/while/body/eval_jaxpr/hqk,khd->qhd/dot_general | solution.py:60
  172.6 3.4 %multiply_reduce_fusion.2 = (f32[2,512]{1,0:T(2,128)S(1)}, f32[2,512,3072]{2,1,0:T(8,128)S(1)}) fusion(bf16[3072,2,128]{2,0,1:T(8,128)(2,1)} %get-tuple-element.119, bf16[6,512,2,128]{3,1,0,2:T(8,128)(2,1)} %get-tuple-element.118, s32[]{:T(128)} %get-tuple-element.110), kind=kOutput, calls=%fused_computation.1.clone.1 | convolution fusion | flops 811596800 | bytes 14422528 | tf_op jit(solution)/shard_map/while/body/eval_jaxpr/qhd,khd->hqk/dot_general | solution.py:55
  176.0 2.2 fusion.51
  178.1 3.0 %fusion.52 = bf16[6,512,2,128]{3,1,0,2:T(8,128)(2,1)} fusion(bf16[6,512,2,128]{3,1,0,2:T(8,128)(2,1)} %get-tuple-element.111, s32[]{:T(128)} %get-tuple-element.110, bf16[3072,2,128]{2,0,1:T(8,128)(2,1)S(1)} %copy-done.4, f32[2,512,3072]{2,1,0:T(8,128)S(1)} %get-tuple-element.102, f32[2,512]{1,0:T(2,128)S(1)} %get-tuple-element.103, ...), kind=kOutput, calls=%fused_computation.11.clone.1 | convolution fusion | flops 815005696 | bytes 14426624 | tf_op jit(solution)/shard_map/while/body/eval_jaxpr/hqk,khd->qhd/dot_general | solution.py:60
  181.1 3.4 %multiply_reduce_fusion.2 = (f32[2,512]{1,0:T(2,128)S(1)}, f32[2,512,3072]{2,1,0:T(8,128)S(1)}) fusion(bf16[3072,2,128]{2,0,1:T(8,128)(2,1)} %get-tuple-element.119, bf16[6,512,2,128]{3,1,0,2:T(8,128)(2,1)} %get-tuple-element.118, s32[]{:T(128)} %get-tuple-element.110), kind=kOutput, calls=%fused_computation.1.clone.1 | convolution fusion | flops 811596800 | bytes 14422528 | tf_op jit(solution)/shard_map/while/body/eval_jaxpr/qhd,khd->hqk/dot_general | solution.py:55
  184.5 2.2 fusion.51
  186.7 3.0 %fusion.52 = bf16[6,512,2,128]{3,1,0,2:T(8,128)(2,1)} fusion(bf16[6,512,2,128]{3,1,0,2:T(8,128)(2,1)} %get-tuple-element.111, s32[]{:T(128)} %get-tuple-element.110, bf16[3072,2,128]{2,0,1:T(8,128)(2,1)S(1)} %copy-done.4, f32[2,512,3072]{2,1,0:T(8,128)S(1)} %get-tuple-element.102, f32[2,512]{1,0:T(2,128)S(1)} %get-tuple-element.103, ...), kind=kOutput, calls=%fused_computation.11.clone.1 | convolution fusion | flops 815005696 | bytes 14426624 | tf_op jit(solution)/shard_map/while/body/eval_jaxpr/hqk,khd->qhd/dot_general | solution.py:60
  189.7 3.4 %multiply_reduce_fusion.2 = (f32[2,512]{1,0:T(2,128)S(1)}, f32[2,512,3072]{2,1,0:T(8,128)S(1)}) fusion(bf16[3072,2,128]{2,0,1:T(8,128)(2,1)} %get-tuple-element.119, bf16[6,512,2,128]{3,1,0,2:T(8,128)(2,1)} %get-tuple-element.118, s32[]{:T(128)} %get-tuple-element.110), kind=kOutput, calls=%fused_computation.1.clone.1 | convolution fusion | flops 811596800 | bytes 14422528 | tf_op jit(solution)/shard_map/while/body/eval_jaxpr/qhd,khd->hqk/dot_general | solution.py:55
  193.1 0.0 copy-start.4
  193.1 2.2 fusion.51
  195.3 3.0 %fusion.52 = bf16[6,512,2,128]{3,1,0,2:T(8,128)(2,1)} fusion(bf16[6,512,2,128]{3,1,0,2:T(8,128)(2,1)} %get-tuple-element.111, s32[]{:T(128)} %get-tuple-element.110, bf16[3072,2,128]{2,0,1:T(8,128)(2,1)S(1)} %copy-done.4, f32[2,512,3072]{2,1,0:T(8,128)S(1)} %get-tuple-element.102, f32[2,512]{1,0:T(2,128)S(1)} %get-tuple-element.103, ...), kind=kOutput, calls=%fused_computation.11.clone.1 | convolution fusion | flops 815005696 | bytes 14426624 | tf_op jit(solution)/shard_map/while/body/eval_jaxpr/hqk,khd->qhd/dot_general | solution.py:60
  198.3 3.6 %copy.38 = bf16[8,384,1,2,128]{4,0,3,2,1:T(8,128)(2,1)} copy(bf16[8,384,1,2,128]{4,1,0,3,2:T(8,128)(2,1)} %bitcast.15) | data formatting | bytes 3145728 | tf_op jit(solution)/shard_map/reshape | solution.py:67
  201.9 8.5 %all-to-all-start.3 = ((bf16[8,384,1,2,128]{4,0,3,2,1:T(8,128)(2,1)}), bf16[8,384,1,2,128]{4,0,3,2,1:T(8,128)(2,1)}, u32[]{:S(2)}, u32[]{:S(2)}) async-start(bf16[8,384,1,2,128]{4,0,3,2,1:T(8,128)(2,1)} %copy.38), calls=%async_computation.3 | async-start | bytes 3145728 | tf_op jit(solution)/shard_map/all_to_all | solution.py:66
  211.1 0.1 fusion.32
  211.2 0.4 fusion.34
  211.6 36.3 %all-to-all-done.3 = bf16[8,384,1,2,128]{4,0,3,2,1:T(8,128)(2,1)} async-done(((bf16[8,384,1,2,128]{4,0,3,2,1:T(8,128)(2,1)}), bf16[8,384,1,2,128]{4,0,3,2,1:T(8,128)(2,1)}, u32[]{:S(2)}, u32[]{:S(2)}) %all-to-all-start.3) | async-done | bytes 1572896 | tf_op jit(solution)/shard_map/all_to_all | solution.py:66
  247.9 1.8 copy.39
  249.7 0.3 convert_bitcast_fusion
  250.0 4.1 %copy.40 = f32[8,24,16,1,2,128]{5,4,2,1,0,3:T(2,128)} copy(f32[8,24,16,1,2,128]{5,1,2,4,0,3:T(8,128)S(1)} %convert_bitcast_fusion) | data formatting | bytes 6291456 | tf_op jit(solution)/shard_map/convert_element_type | solution.py:71
  254.1 5.5 %reshape.64 = f32[8,24,4096]{2,1,0:T(8,128)} reshape(f32[8,24,16,1,2,128]{5,4,2,1,0,3:T(2,128)} %copy.40) | data formatting | bytes 6291456 | tf_op jit(solution)/shard_map/convert_element_type | solution.py:71
  259.6 2.2 multiply_convert_fusion
  261.8 0.0 copy-start.3
  261.9 1.1 copy-done.3
  263.0 1.9 collective-permute-start
  264.9 7.2 %collective-permute-done = bf16[24,4096]{1,0:T(8,128)(2,1)S(1)} collective-permute-done((bf16[24,4096]{1,0:T(8,128)(2,1)S(1)}, bf16[24,4096]{1,0:T(8,128)(2,1)S(1)}, u32[]{:S(2)}, u32[]{:S(2)}) %collective-permute-start) | collective-permute-done | bytes 196640 | tf_op jit(solution)/shard_map/ppermute | solution.py:14
  272.1 0.7 bitcast_dynamic-update-slice_fusion
  (18 shorter events, 0.1 us)
Async XLA Ops:
  0.0 211.2 %copy-start = (bf16[256,4096]{1,0:T(8,128)(2,1)S(1)}, bf16[256,4096]{1,0:T(8,128)(2,1)}, u32[]{:S(2)}) copy-start(bf16[256,4096]{1,0:T(8,128)(2,1)} %param.15) | copy-start | bytes 6291460
  0.0 2.8 %copy-start.1 = (bf16[8,24,4096]{2,1,0:T(8,128)(2,1)S(1)}, bf16[8,24,4096]{2,1,0:T(8,128)(2,1)}, u32[]{:S(2)}) copy-start(bf16[8,24,4096]{2,1,0:T(8,128)(2,1)} %param.11) | copy-start | bytes 4718596
  11.4 50.9 %all-to-all-start.1 = ((bf16[8,24,16,2,128]{4,1,0,3,2:T(8,128)(2,1)}), bf16[8,24,16,2,128]{4,1,0,3,2:T(8,128)(2,1)}, u32[]{:S(2)}, u32[]{:S(2)}) async-start(bf16[8,24,16,2,128]{4,1,0,3,2:T(8,128)(2,1)} %copy.32), calls=%async_computation.1 | async-start | bytes 3145728 | tf_op jit(solution)/shard_map/all_to_all | solution.py:44
  21.6 1.9 copy-start.2
  62.3 44.5 %all-to-all-start = ((bf16[8,24,16,2,128]{4,3,1,0,2:T(2,128)(2,1)}), bf16[8,24,16,2,128]{4,3,1,0,2:T(2,128)(2,1)}, u32[]{:S(2)}, u32[]{:S(2)}) async-start(bf16[8,24,16,2,128]{4,3,1,0,2:T(2,128)(2,1)} %copy.30), calls=%async_computation | async-start | bytes 3145728 | tf_op jit(solution)/shard_map/all_to_all | solution.py:43
  106.8 37.1 %all-to-all-start.2 = ((bf16[8,24,16,2,128]{4,1,0,3,2:T(8,128)(2,1)}), bf16[8,24,16,2,128]{4,1,0,3,2:T(8,128)(2,1)}, u32[]{:S(2)}, u32[]{:S(2)}) async-start(bf16[8,24,16,2,128]{4,1,0,3,2:T(8,128)(2,1)} %copy.34), calls=%async_computation.2 | async-start | bytes 3145728 | tf_op jit(solution)/shard_map/all_to_all | solution.py:45
  150.2 2.2 copy-start.4
  158.8 2.2 copy-start.4
  167.4 2.2 copy-start.4
  175.9 2.2 copy-start.4
  184.5 2.2 copy-start.4
  193.1 2.2 copy-start.4
  201.9 9.2 %copy-start.6 = (s32[8]{0:T(128)S(1)}, s32[8]{0:T(128)}, u32[]{:S(2)}) copy-start(s32[8]{0:T(128)} %param.14) | copy-start | bytes 100
  201.9 46.0 %all-to-all-start.3 = ((bf16[8,384,1,2,128]{4,0,3,2,1:T(8,128)(2,1)}), bf16[8,384,1,2,128]{4,0,3,2,1:T(8,128)(2,1)}, u32[]{:S(2)}, u32[]{:S(2)}) async-start(bf16[8,384,1,2,128]{4,0,3,2,1:T(8,128)(2,1)} %copy.38), calls=%async_computation.3 | async-start | bytes 3145728 | tf_op jit(solution)/shard_map/all_to_all | solution.py:66
  259.6 12.5 %copy-start.5 = (bf16[24,4096]{1,0:T(8,128)(2,1)S(1)}, bf16[24,4096]{1,0:T(8,128)(2,1)}, u32[]{:S(2)}) copy-start(bf16[24,4096]{1,0:T(8,128)(2,1)} %param.17) | copy-start | bytes 589828
  261.8 1.1 copy-start.3
  263.0 9.1 %collective-permute-start = (bf16[24,4096]{1,0:T(8,128)(2,1)S(1)}, bf16[24,4096]{1,0:T(8,128)(2,1)S(1)}, u32[]{:S(2)}, u32[]{:S(2)}) collective-permute-start(bf16[24,4096]{1,0:T(8,128)(2,1)S(1)} %dynamic-slice_bitcast_fusion), channel_id=1, source_target_pairs={{0,16},{16,32},{32,48},{48,64},{64,80},{80,96},{96,112},{112,128},... | collective-permute-start | bytes 589832 | tf_op jit(solution)/shard_map/ppermute | solution.py:14
where the time goes:
time: 274 us; the launch traced here: 273 us
  waiting for transfers between devices  133 us (49%)
  local copies, waits for them, and re-layouts  47.7 us (17%)
  matrix products  38.6 us (14%)
  starting transfers between devices  29.6 us (11%)
  other arithmetic  23.5 us (9%)
    all_to_all x1, waiting for transfers between devices, shards(): lax.all_to_all(result.reshape(q_all.shape), 'seq', split_axis=1, concat_a...  36.3 us
    all_to_all x1, waiting for transfers between devices, shards(): lax.all_to_all(split_heads(qn), 'seq', split_axis=2, concat_axis=1, tiled...  33.1 us
    all_to_all x1, waiting for transfers between devices, shards(): lax.all_to_all(split_heads(kn), 'seq', split_axis=2, concat_axis=1, tiled...  29.3 us
    all_to_all x1, waiting for transfers between devices, shards(): lax.all_to_all(split_heads(value), 'seq', split_axis=2, concat_axis=1, ti...  26.7 us
    reshape x6, local copies, waits for them, and re-layouts, split_heads(): return array.reshape(frames, rows, groups, per_group, HD)  21.7 us
    dot_general x6, matrix products, one_block(): jnp.einsum('qhd,khd->hqk', q_flat, k_flat, preferred_element_type=jnp.flo...  20.3 us
    dot_general x6, matrix products, one_block(): jnp.einsum('hqk,khd->qhd', weights.astype(jnp.bfloat16), v_flat, preferre...  18 us
    reduce_sum x6, other arithmetic, one_block(): totals = jnp.sum(weights, axis=2)  13.1 us
  transfers between devices with their start and end apart: 5, of which 5 were waited for; matrix products, arithmetic and copies ran while one was open for 9% of the time, Pallas kernels for 0%

commit v1 on v0

v1 whole, which is shorter than its diff:
```python
import math

import jax
import jax.numpy as jnp
from jax import lax
from jax.experimental import pallas as pl
from jax.experimental.pallas import tpu as pltpu
from jax.sharding import PartitionSpec as P

HD = 128
SIDE = 4
LOG2E = 1.4426950408889634
AXES = (("z", "x"), ("x", "z"))
MIB = 1024 * 1024


def moved(value, axis, steps):
    pairs = []
    for source in range(SIDE * SIDE):
        x, z = divmod(source, SIDE)
        if axis == "x":
            x = (x + steps) % SIDE
        else:
            z = (z + steps) % SIDE
        pairs.append((source, x * SIDE + z))
    return lax.ppermute(value, "seq", pairs)


def exchange(pieces, axes, sign):
    first, second = axes
    held = [pieces[0]] + [moved(pieces[i], first, sign * i) for i in range(1, SIDE)]
    arrived = [
        moved(jnp.stack([held[i][j] for i in range(SIDE)]), second, sign * j)
        for j in range(1, SIDE)
    ]
    return held, arrived


def group_of(place, axes, i, j):
    steps = {axes[0]: i, axes[1]: j}
    x = lax.rem(place[0] + steps["x"], SIDE)
    z = lax.rem(place[1] + steps["z"], SIDE)
    return (x * SIDE + z) * (2 * HD)


def prepare_kernel(place, q_ref, k_ref, v_ref, gain_ref, *outs):
    inner = q_ref.shape[2]

    def factor_of(ref):
        total = None
        for at in range(0, inner, 512):
            part = ref[:, :, at : at + 512].astype(jnp.float32)
            part = part * part
            total = part if total is None else total + part
        mean = jnp.sum(total, axis=-1, keepdims=True) * (1.0 / inner)
        return lax.rsqrt(mean + 1e-06)

    q_factor, k_factor = factor_of(q_ref), factor_of(k_ref)
    for head in range(2):
        for i in range(SIDE):
            for j in range(SIDE):
                at = pl.multiple_of(group_of(place, AXES[head], i, j) + head * HD, HD)
                out = outs[head * SIDE + i]
                for kind, (ref, factor) in enumerate(((q_ref, q_factor), (k_ref, k_factor))):
                    gain = gain_ref[kind : kind + 1, pl.ds(at, HD)]
                    part = ref[:, :, pl.ds(at, HD)].astype(jnp.float32) * factor * gain[None]
                    out[j, kind] = part.astype(jnp.bfloat16)
                out[j, 2] = v_ref[:, :, pl.ds(at, HD)]


def prepare(place, query, key, value, qk_gain):
    frames, rows, inner = query.shape
    step = 2
    tall = pl.BlockSpec((step, rows, inner), lambda n, _: (n, 0, 0))
    out = pl.BlockSpec((SIDE, 3, step, rows, HD), lambda n, _: (0, 0, n, 0, 0))
    shape = jax.ShapeDtypeStruct((SIDE, 3, frames, rows, HD), jnp.bfloat16)
    return pl.pallas_call(
        prepare_kernel,
        grid_spec=pltpu.PrefetchScalarGridSpec(
            num_scalar_prefetch=1,
            grid=(frames // step,),
            in_specs=[tall, tall, tall, pl.BlockSpec((2, inner), lambda n, _: (0, 0))],
            out_specs=[out] * (2 * SIDE),
        ),
        out_shape=[shape] * (2 * SIDE),
        compiler_params=pltpu.CompilerParams(vmem_limit_bytes=40 * MIB),
        cost_estimate=pl.CostEstimate(
            flops=10 * query.size, bytes_accessed=12 * query.size, transcendentals=0
        ),
        name="prepare",
    )(place, query, key, value, qk_gain)


def attend_kernel(gate_ref, *refs):
    held, arrived = refs[:SIDE], refs[SIDE : 2 * SIDE - 1]
    outs = refs[2 * SIDE - 1 : 3 * SIDE - 1]
    q_all, k_all, v_all, s_even, s_odd, m_even, m_odd, gates, result = refs[3 * SIDE - 1 :]
    frames, rows = held[0].shape[2:4]
    tokens = frames * rows
    length = SIDE * SIDE * tokens
    block, chunk = 256, 512
    blocks = length // block
    scale = LOG2E / math.sqrt(HD)

    for i in range(SIDE):
        for j in range(SIDE):
            at = (i * SIDE + j) * tokens
            for kind, place in enumerate((q_all, k_all, v_all)):
                part = held[i][0, kind] if j == 0 else arrived[j - 1][i, kind]
                place[at : at + tokens, :HD] = part.reshape(tokens, HD)
    v_all[:, HD:] = jnp.ones((length, HD), jnp.bfloat16)
    for at in range(SIDE * frames):
        gates[at * rows : (at + 1) * rows, :] = jnp.broadcast_to(
            gate_ref[at % frames : at % frames + 1, :], (rows, HD)
        )

    def rows_of(n):
        at = n * block
        return pl.ds(at if isinstance(n, int) else pl.multiple_of(at, block), block)

    def step(following, s_next, m_next, current, s_now, m_now):
        if following is not None:
            q = q_all[rows_of(following), :]
            peak = None
        if current is not None:
            most = m_now[...] * scale
            total = None
        for at in range(0, length, chunk):
            if following is not None:
                scores = lax.dot_general(
                    q,
                    k_all[at : at + chunk, :],
                    (((1,), (1,)), ((), ())),
                    preferred_element_type=jnp.float32,
                )
                s_next[:, at : at + chunk] = scores
                for lane in range(0, chunk, HD):
                    part = scores[:, lane : lane + HD]
                    peak = part if peak is None else jnp.maximum(peak, part)
            if current is not None:
                weights = [
                    jnp.exp2(s_now[:, at + lane : at + lane + HD] * scale - most).astype(jnp.bfloat16)
                    for lane in range(0, chunk, HD)
                ]
                part = jnp.dot(
                    jnp.concatenate(weights, axis=1),
                    v_all[at : at + chunk, :],
                    preferred_element_type=jnp.float32,
                )
                total = part if total is None else total + part
        if following is not None:
            m_next[...] = jnp.broadcast_to(jnp.max(peak, axis=1, keepdims=True), (block, HD))
        if current is not None:
            attended = (total[:, :HD] / total[:, HD:]).astype(jnp.bfloat16).astype(jnp.float32)
            gate = gates[rows_of(current % (SIDE * tokens // block)), :]
            result[rows_of(current), :] = (gate * attended).astype(jnp.bfloat16)

    even, odd = (s_even, m_even), (s_odd, m_odd)
    step(0, *even, None, None, None)

    @pl.loop(0, blocks // 2 - 1)
    def _(pair):
        step(2 * pair + 1, *odd, 2 * pair, *even)
        step(2 * pair + 2, *even, 2 * pair + 1, *odd)

    step(blocks - 1, *odd, blocks - 2, *even)
    step(None, None, None, blocks - 1, *odd)
    for i in range(SIDE):
        for j in range(SIDE):
            at = (i * SIDE + j) * tokens
            outs[i][j] = result[at : at + tokens, :].reshape(frames, rows, HD)


def attend(gate, held, arrived):
    frames, rows = held[0].shape[2:4]
    length = SIDE * SIDE * frames * rows
    block = 256
    one = pl.BlockSpec((1, 3, frames, rows, HD), lambda n: (0, 0, 0, 0, 0))
    whole = pl.BlockSpec((SIDE, 3, frames, rows, HD), lambda n: (0, 0, 0, 0, 0))
    return pl.pallas_call(
        attend_kernel,
        grid=(1,),
        in_specs=[pl.BlockSpec((frames, HD), lambda n: (0, 0))] + [one] * SIDE + [whole] * (SIDE - 1),
        out_specs=[pl.BlockSpec((SIDE, frames, rows, HD), lambda n: (0, 0, 0, 0))] * SIDE,
        out_shape=[jax.ShapeDtypeStruct((SIDE, frames, rows, HD), jnp.bfloat16)] * SIDE,
        scratch_shapes=[
            pltpu.VMEM((length, HD), jnp.bfloat16),
            pltpu.VMEM((length, HD), jnp.bfloat16),
            pltpu.VMEM((length, 2 * HD), jnp.bfloat16),
            pltpu.VMEM((block, length), jnp.float32),
            pltpu.VMEM((block, length), jnp.float32),
            pltpu.VMEM((block, HD), jnp.float32),
            pltpu.VMEM((block, HD), jnp.float32),
            pltpu.VMEM((SIDE * frames * rows, HD), jnp.float32),
            pltpu.VMEM((length, HD), jnp.bfloat16),
        ],
        compiler_params=pltpu.CompilerParams(vmem_limit_bytes=48 * MIB),
        cost_estimate=pl.CostEstimate(
            flops=8 * length * length * HD, bytes_accessed=8 * length * HD, transcendentals=length * length
        ),
        name="attend",
    )(gate, *held, *arrived)


def leaving_kernel(slot, *refs):
    out = refs[-1]
    for i in range(SIDE):
        for j in range(SIDE):
            part = refs[i][0, 0] if j == 0 else refs[SIDE + j - 1][i, 0]
            out[i * SIDE + j] = part


def leaving_frame(slot, held, arrived):
    rows = held[0].shape[2]
    one = pl.BlockSpec((1, 1, rows, HD), lambda n, s: (0, s[0], 0, 0))
    whole = pl.BlockSpec((SIDE, 1, rows, HD), lambda n, s: (0, s[0], 0, 0))
    count = SIDE * SIDE
    return pl.pallas_call(
        leaving_kernel,
        grid_spec=pltpu.PrefetchScalarGridSpec(
            num_scalar_prefetch=1,
            grid=(1,),
            in_specs=[one] * SIDE + [whole] * (SIDE - 1),
            out_specs=pl.BlockSpec((count, rows, HD), lambda n, s: (0, 0, 0)),
        ),
        out_shape=jax.ShapeDtypeStruct((count, rows, HD), jnp.bfloat16),
        name="leaving",
    )(slot, *held, *arrived)


def assemble_kernel(place, *refs):
    fresh, out = refs[-2:]
    per_head = 2 * SIDE
    step = out.shape[0]
    first = pl.program_id(0) * step
    for n in range(step):
        here = first + n == place[2]

        @pl.when(jnp.logical_not(here))
        def _(n=n):
            for head in range(2):
                own = refs[head * per_head : (head + 1) * per_head]
                for i in range(SIDE):
                    for j in range(SIDE):
                        at = pl.multiple_of(group_of(place, AXES[head], i, j) + head * HD, HD)
                        part = own[i][0, n] if j == 0 else own[SIDE + j - 1][i, n]
                        out[n, :, pl.ds(at, HD)] = part

        @pl.when(jnp.logical_and(here, place[3] != 0))
        def _(n=n):
            for head in range(2):
                arriving = refs[(head + 1) * per_head - 1]
                for i in range(SIDE):
                    for j in range(SIDE):
                        at = pl.multiple_of(group_of(place, AXES[head], i, j) + head * HD, HD)
                        out[n, :, pl.ds(at, HD)] = arriving[i * SIDE + j]

        @pl.when(jnp.logical_and(here, place[3] == 0))
        def _(n=n):
            out[n] = fresh[...]


def assemble(place, parts, fresh):
    frames, rows = parts[0][0][0].shape[1:3]
    inner = fresh.shape[1]
    step = 2
    one = pl.BlockSpec((1, step, rows, HD), lambda n, _: (0, n, 0, 0))
    whole = pl.BlockSpec((SIDE, step, rows, HD), lambda n, _: (0, n, 0, 0))
    arriving = pl.BlockSpec((SIDE * SIDE, rows, HD), lambda n, _: (0, 0, 0))
    operands = []
    for held, arrived, behind in parts:
        operands += [*held, *arrived, behind]
    return pl.pallas_call(
        assemble_kernel,
        grid_spec=pltpu.PrefetchScalarGridSpec(
            num_scalar_prefetch=1,
            grid=(frames // step,),
            in_specs=([one] * SIDE + [whole] * (SIDE - 1) + [arriving]) * 2
            + [pl.BlockSpec((rows, inner), lambda n, _: (0, 0))],
            out_specs=pl.BlockSpec((step, rows, inner), lambda n, _: (n, 0, 0)),
        ),
        out_shape=jax.ShapeDtypeStruct((frames, rows, inner), jnp.bfloat16),
        compiler_params=pltpu.CompilerParams(vmem_limit_bytes=40 * MIB),
        name="assemble",
    )(place, *operands, fresh)


def level_gate(steps, gate_weight):
    half = gate_weight.shape[0] // 2
    freqs = jnp.exp(-math.log(10000.0) * jnp.arange(half, dtype=jnp.float32) / half)
    angles = steps.astype(jnp.float32)[:, None] * freqs[None, :]
    embed = jnp.concatenate([jnp.cos(angles), jnp.sin(angles)], axis=1).astype(jnp.bfloat16)
    return jnp.dot(embed, gate_weight, preferred_element_type=jnp.float32)


def shards(query, key, value, qk_gain, timesteps, gate_weight, slot, fresh):
    index = lax.axis_index("seq")
    section = lax.axis_index("section")
    place = jnp.stack([index // SIDE, index % SIDE, slot[0], section]).astype(jnp.int32)
    columns = lax.dynamic_slice_in_dim(gate_weight, index * (2 * HD), 2 * HD, 1)
    gate = level_gate(timesteps, columns)
    prepared = prepare(place, query, key, value, qk_gain)
    sent = [exchange(prepared[head * SIDE : (head + 1) * SIDE], AXES[head], 1) for head in range(2)]
    sections = lax.axis_size("section")
    parts = []
    for head in range(2):
        result = attend(gate[:, head * HD : (head + 1) * HD], *sent[head])
        held, arrived = exchange(result, AXES[head], -1)
        leaving = leaving_frame(slot, held, arrived)
        behind = lax.ppermute(leaving, "section", [(n, n + 1) for n in range(sections - 1)])
        parts.append((held, arrived, behind))
    return assemble(place, parts, fresh)


def solution(mesh):
    placed = (
        P("section", "seq", None),
        P("section", "seq", None),
        P("section", "seq", None),
        P(),
        P("section"),
        P(),
        P(),
        P("seq", None),
    )
    return jax.shard_map(
        shards, mesh=mesh, in_specs=placed, out_specs=P("section", "seq", None), check_vma=False
    )
```

time: 274 us -> 221 us (0.81)
  the two profiles are of different devices: /device:TPU:32 before, /device:TPU:17 now
where the time goes in v1:
time: 221 us; the launch traced here: 218 us
  waiting for transfers between devices  102 us (46%)
  starting transfers between devices  60.9 us (28%)
  Pallas kernels  38.9 us (18%)
  local copies, waits for them, and re-layouts  12.1 us (5%)
  other arithmetic  2.86 us (1%)
    ppermute x24, waiting for transfers between devices, moved(): return lax.ppermute(value, 'seq', pairs)  100 us
    ppermute x24, starting transfers between devices, moved(): return lax.ppermute(value, 'seq', pairs)  53.1 us
    pallas_call x2, Pallas kernels, attend(): pl.pallas_call(attend_kernel, grid=(1,), in_specs=[pl.BlockSpec((frames,...  26.9 us
    ppermute x2, starting transfers between devices, shards(): lax.ppermute(leaving, 'section', [(n, n + 1) for n in range(sections - 1)])  7.73 us
    unnamed x74, local copies, waits for them, and re-layouts  6.96 us
    slice x16, local copies, waits for them, and re-layouts, exchange(): held[i][j]  5.13 us
    pallas_call x1, Pallas kernels, assemble(): pl.pallas_call(assemble_kernel, grid_spec=pltpu.PrefetchScalarGridSpec(nu...  4.51 us
  transfers between devices with their start and end apart: 26, of which 8 were waited for; matrix products, arithmetic and copies ran while one was open for 4% of the time, Pallas kernels for 14%

profile of v1, /device:TPU:17, one launch (start us, length us, event | category | flops | bytes accessed | tf_op | source)
XLA Modules:
  0.0 218.4 jit_solution(7476486367675315735)
XLA Ops:
  0.8 0.1 pad_add_fusion.place
  0.9 1.4 copy-done.1
  2.3 1.4 copy-done.2
  3.7 1.4 copy-done.3
  5.1 0.8 copy-done.29
  5.9 4.4 %prepare.1 = (bf16[4,3,8,24,128]{4,3,2,1,0:T(8,128)(2,1)S(1)}, bf16[4,3,8,24,128]{4,3,2,1,0:T(8,128)(2,1)}, bf16[4,3,8,24,128]{4,3,2,1,0:T(8,128)(2,1)}, bf16[4,...) custom-call(s32[4]{0:T(128)S(1)} %pad_add_fusion.place, ...), custom_call_target="tpu_custom_call" | custom-call | flops 7864320 | bytes 9437184 | tf_op jit(solution)/shard_map/prepare/pallas_call | solution.py:77
  10.3 0.0 copy-start.36
  10.3 1.3 collective-permute-start.13
  11.6 2.5 %collective-permute-start.14 = (bf16[4,3,8,24,128]{4,3,2,1,0:T(8,128)(2,1)}, bf16[4,3,8,24,128]{4,3,2,1,0:T(8,128)(2,1)}, u32[]{:S(2)}, u32[]{:S(2)}) collective-permute-start(bf16[4,3,8,24,128]{4,3,2,1,0:T(8,128)(2,1)} %get-tuple-element.31), channel_id=1, source_target_pairs={{0,8},{1,9},{2,10},{3,11},{4,12},{5,13},{6,14},{7,15},{8,0},{9,1},... | collective-permute-start | bytes 1769480 | tf_op jit(solution)/shard_map/ppermute | solution.py:26
  14.0 1.2 collective-permute-start.15
  15.2 3.0 %collective-permute-start = (bf16[4,3,8,24,128]{4,3,2,1,0:T(8,128)(2,1)}, bf16[4,3,8,24,128]{4,3,2,1,0:T(8,128)(2,1)S(1)}, u32[]{:S(2)}, u32[]{:S(2)}) collective-permute-start(bf16[4,3,8,24,128]{4,3,2,1,0:T(8,128)(2,1)} %get-tuple-element.22), channel_id=1, source_target_pairs={{0,1},{1,2},{2,3},{3,0},{4,5},{5,6},{6,7},{7,4},{8,9},{9,10},{10,1... | collective-permute-start | bytes 1769480 | tf_op jit(solution)/shard_map/ppermute | solution.py:26
  18.2 5.1 %collective-permute-start.1 = (bf16[4,3,8,24,128]{4,3,2,1,0:T(8,128)(2,1)}, bf16[4,3,8,24,128]{4,3,2,1,0:T(8,128)(2,1)S(1)}, u32[]{:S(2)}, u32[]{:S(2)}) collective-permute-start(bf16[4,3,8,24,128]{4,3,2,1,0:T(8,128)(2,1)} %get-tuple-element.23), channel_id=1, source_target_pairs={{0,2},{1,3},{2,0},{3,1},{4,6},{5,7},{6,4},{7,5},{8,10},{9,11},{10,... | collective-permute-start | bytes 1769480 | tf_op jit(solution)/shard_map/ppermute | solution.py:26
  23.3 0.8 fusion.9
  24.1 0.8 fusion.13
  24.9 0.1 fusion.2
  25.0 0.1 fusion
  25.2 0.9 collective-permute-done.13.refs_1_
  26.1 6.0 %collective-permute-start.2 = (bf16[4,3,8,24,128]{4,3,2,1,0:T(8,128)(2,1)}, bf16[4,3,8,24,128]{4,3,2,1,0:T(8,128)(2,1)S(1)}, u32[]{:S(2)}, u32[]{:S(2)}) collective-permute-start(bf16[4,3,8,24,128]{4,3,2,1,0:T(8,128)(2,1)} %copy-done.30), channel_id=1, source_target_pairs={{0,3},{1,0},{2,1},{3,2},{4,7},{5,4},{6,5},{7,6},{8,11},{9,8},{10,9... | collective-permute-start | bytes 1769480 | tf_op jit(solution)/shard_map/ppermute | solution.py:26
  32.1 1.1 fusion.10
  33.2 6.5 %collective-permute-done.14.refs_2_ = bf16[4,3,8,24,128]{4,3,2,1,0:T(8,128)(2,1)} collective-permute-done((bf16[4,3,8,24,128]{4,3,2,1,0:T(8,128)(2,1)}, bf16[4,3,8,24,128]{4,3,2,1,0:T(8,128)(2,1)}, u32[]{:S(2)}, u32[]{:S(2)}) %collective-permute-start.14) | collective-permute-done | bytes 589856 | tf_op jit(solution)/shard_map/ppermute | solution.py:26
  39.7 1.1 fusion.11
  40.8 1.1 fusion.12
  42.0 0.1 pad_maximum_fusion.5
  42.1 6.1 %collective-permute-start.18 = (bf16[4,3,8,24,128]{4,3,2,1,0:T(8,128)(2,1)S(1)}, bf16[4,3,8,24,128]{4,3,2,1,0:T(8,128)(2,1)S(1)}, u32[]{:S(2)}, u32[]{:S(2)}) collective-permute-start(bf16[4,3,8,24,128]{4,3,2,1,0:T(8,128)(2,1)S(1)} %pad_maximum_fusion.5), channel_id=1, source_target_pairs={{0,3},{1,0},{2,1},{3,2},{4,7},{5,4},{6,5},{7,6},{8,11},{9,8},{10,9... | collective-permute-start | bytes 1769480 | tf_op jit(solution)/shard_map/ppermute | solution.py:26
  48.2 0.1 pad_maximum_fusion.4
  48.2 1.0 collective-permute-start.17
  49.3 0.1 pad_maximum_fusion.3
  49.4 0.0 copy-start.22
  49.4 2.4 %collective-permute-start.16 = (bf16[4,3,8,24,128]{4,3,2,1,0:T(8,128)(2,1)S(1)}, bf16[4,3,8,24,128]{4,3,2,1,0:T(8,128)(2,1)S(1)}, u32[]{:S(2)}, u32[]{:S(2)}) collective-permute-start(bf16[4,3,8,24,128]{4,3,2,1,0:T(8,128)(2,1)S(1)} %pad_maximum_fusion.3), channel_id=1, source_target_pairs={{0,1},{1,2},{2,3},{3,0},{4,5},{5,6},{6,7},{7,4},{8,9},{9,10},{10,1... | collective-permute-start | bytes 1769480 | tf_op jit(solution)/shard_map/ppermute | solution.py:26
  51.9 7.3 %collective-permute-done.1.refs_2_ = bf16[4,3,8,24,128]{4,3,2,1,0:T(8,128)(2,1)S(1)} collective-permute-done((bf16[4,3,8,24,128]{4,3,2,1,0:T(8,128)(2,1)}, bf16[4,3,8,24,128]{4,3,2,1,0:T(8,128)(2,1)S(1)}, u32[]{:S(2)}, u32[]{:S(2)}) %collective-permute-start.1) | collective-permute-done | bytes 589856 | tf_op jit(solution)/shard_map/ppermute | solution.py:26
  59.2 54.4 %collective-permute-done.2.refs_3_ = bf16[4,3,8,24,128]{4,3,2,1,0:T(8,128)(2,1)S(1)} collective-permute-done((bf16[4,3,8,24,128]{4,3,2,1,0:T(8,128)(2,1)}, bf16[4,3,8,24,128]{4,3,2,1,0:T(8,128)(2,1)S(1)}, u32[]{:S(2)}, u32[]{:S(2)}) %collective-permute-start.2) | collective-permute-done | bytes 589856 | tf_op jit(solution)/shard_map/ppermute | solution.py:26
  113.7 0.1 pad_maximum_fusion.2
  113.8 0.1 collective-permute-start.5
  113.9 0.1 pad_maximum_fusion.1
  114.0 2.2 collective-permute-start.4
  116.2 0.1 pad_maximum_fusion
  116.3 10.0 %collective-permute-done.18.refs_6_ = bf16[4,3,8,24,128]{4,3,2,1,0:T(8,128)(2,1)S(1)} collective-permute-done((bf16[4,3,8,24,128]{4,3,2,1,0:T(8,128)(2,1)S(1)}, bf16[4,3,8,24,128]{4,3,2,1,0:T(8,128)(2,1)S(1)}, u32[]{:S(2)}, u32[]{:S(2)}) %collective-permute-start.18) | collective-permute-done | bytes 589856 | tf_op jit(solution)/shard_map/ppermute | solution.py:26
  126.3 0.3 collective-permute-start.3
  126.7 14.0 %attend.3 = (bf16[4,8,24,128]{3,2,1,0:T(8,128)(2,1)S(1)}, bf16[4,8,24,128]{3,2,1,0:T(8,128)(2,1)S(1)}, bf16[4,8,24,128]{3,2,1,0:T(8,128)(2,1)S(1)}, bf16[4,8,24,128]{3,2,1,0:T(8,128)(2,1)S(1)}) custom-call(f32[8,128]{1,0:T(8,128)S(1)} %get-tuple-element.85.gate_ref, bf16[4,3,8,24,128]{4,3,2,1,0:T(8,128)(2,1)S(1)} %copy-done.27, ...), custom_call_target="tpu_custom_call" | custom-call | flops 9663676416 | bytes 3145728 | tf_op jit(solution)/shard_map/attend/pallas_call | solution.py:180
  140.7 2.4 %collective-permute-start.19 = (bf16[4,8,24,128]{3,2,1,0:T(8,128)(2,1)S(1)}, bf16[4,8,24,128]{3,2,1,0:T(8,128)(2,1)S(1)}, u32[]{:S(2)}, u32[]{:S(2)}) collective-permute-start(bf16[4,8,24,128]{3,2,1,0:T(8,128)(2,1)S(1)} %get-tuple-element.34), channel_id=1, source_target_pairs={{0,12},{1,13},{2,14},{3,15},{4,0},{5,1},{6,2},{7,3},{8,4},{9,5},{1... | collective-permute-start | bytes 589832 | tf_op jit(solution)/shard_map/ppermute | solution.py:26
  143.2 0.8 collective-permute-start.21
  144.0 12.9 %attend.2 = (bf16[4,8,24,128]{3,2,1,0:T(8,128)(2,1)S(1)}, bf16[4,8,24,128]{3,2,1,0:T(8,128)(2,1)S(1)}, bf16[4,8,24,128]{3,2,1,0:T(8,128)(2,1)S(1)}, bf16[4,8,24,128]{3,2,1,0:T(8,128)(2,1)S(1)}) custom-call(f32[8,128]{1,0:T(8,128)S(1)} %get-tuple-element.86.gate_ref, bf16[4,3,8,24,128]{4,3,2,1,0:T(8,128)(2,1)S(1)} %copy-done.21, ...), custom_call_target="tpu_custom_call" | custom-call | flops 9663676416 | bytes 3145728 | tf_op jit(solution)/shard_map/attend/pallas_call | solution.py:180
  156.8 3.4 %collective-permute-start.6 = (bf16[4,8,24,128]{3,2,1,0:T(8,128)(2,1)S(1)}, bf16[4,8,24,128]{3,2,1,0:T(8,128)(2,1)S(1)}, u32[]{:S(2)}, u32[]{:S(2)}) collective-permute-start(bf16[4,8,24,128]{3,2,1,0:T(8,128)(2,1)S(1)} %get-tuple-element.26), channel_id=1, source_target_pairs={{0,3},{1,0},{2,1},{3,2},{4,7},{5,4},{6,5},{7,6},{8,11},{9,8},{10,9... | collective-permute-start | bytes 589832 | tf_op jit(solution)/shard_map/ppermute | solution.py:26
  160.2 1.6 collective-permute-start.7
  161.9 2.1 collective-permute-start.8
  164.2 2.1 collective-permute-start.24
  166.3 1.7 collective-permute-start.23
  168.0 19.2 %collective-permute-done.6.refs_1_ = bf16[4,8,24,128]{3,2,1,0:T(8,128)(2,1)S(1)} collective-permute-done((bf16[4,8,24,128]{3,2,1,0:T(8,128)(2,1)S(1)}, bf16[4,8,24,128]{3,2,1,0:T(8,128)(2,1)S(1)}, u32[]{:S(2)}, u32[]{:S(2)}) %collective-permute-start.6) | collective-permute-done | bytes 196640 | tf_op jit(solution)/shard_map/ppermute | solution.py:26
  187.2 3.4 %collective-permute-start.22 = (bf16[4,8,24,128]{3,2,1,0:T(8,128)(2,1)S(1)}, bf16[4,8,24,128]{3,2,1,0:T(8,128)(2,1)}, u32[]{:S(2)}, u32[]{:S(2)}) collective-permute-start(bf16[4,8,24,128]{3,2,1,0:T(8,128)(2,1)S(1)} %pad_maximum_fusion.9), channel_id=1, source_target_pairs={{0,3},{1,0},{2,1},{3,2},{4,7},{5,4},{6,5},{7,6},{8,11},{9,8},{10,9... | collective-permute-start | bytes 589832 | tf_op jit(solution)/shard_map/ppermute | solution.py:26
  190.8 0.7 pad_maximum_fusion.8
  191.5 0.6 collective-permute-start.11
  192.1 0.7 pad_maximum_fusion.7
  192.8 2.7 %collective-permute-start.10 = (bf16[4,8,24,128]{3,2,1,0:T(8,128)(2,1)}, bf16[4,8,24,128]{3,2,1,0:T(8,128)(2,1)}, u32[]{:S(2)}, u32[]{:S(2)}) collective-permute-start(bf16[4,8,24,128]{3,2,1,0:T(8,128)(2,1)} %pad_maximum_fusion.7), channel_id=1, source_target_pairs={{0,8},{1,9},{2,10},{3,11},{4,12},{5,13},{6,14},{7,15},{8,0},{9,1},... | collective-permute-start | bytes 589832 | tf_op jit(solution)/shard_map/ppermute | solution.py:26
  195.4 0.7 pad_maximum_fusion.6
  196.1 1.3 collective-permute-start.9
  197.4 1.8 collective-permute-done.23.refs_5_.refs_13_
  199.2 1.5 leaving.3
  200.7 3.3 %collective-permute-start.25 = (bf16[16,24,128]{2,1,0:T(8,128)(2,1)}, bf16[16,24,128]{2,1,0:T(8,128)(2,1)}, u32[]{:S(2)}, u32[]{:S(2)}) collective-permute-start(bf16[16,24,128]{2,1,0:T(8,128)(2,1)} %leaving.3), channel_id=1, source_target_pairs={{0,16},{16,32},{32,48},{48,64},{64,80},{80,96},{96,112},{112,128},... | collective-permute-start | bytes 294920 | tf_op jit(solution)/shard_map/ppermute | solution.py:310
  204.1 1.6 leaving.2
  205.6 4.5 %collective-permute-start.12 = (bf16[16,24,128]{2,1,0:T(8,128)(2,1)}, bf16[16,24,128]{2,1,0:T(8,128)(2,1)S(1)}, u32[]{:S(2)}, u32[]{:S(2)}) collective-permute-start(bf16[16,24,128]{2,1,0:T(8,128)(2,1)} %leaving.2), channel_id=1, source_target_pairs={{0,16},{16,32},{32,48},{48,64},{64,80},{80,96},{96,112},{112,128},... | collective-permute-start | bytes 294920 | tf_op jit(solution)/shard_map/ppermute | solution.py:310
  210.1 1.9 collective-permute-done.12.refs_7_
  212.1 0.9 copy-done.19
  213.0 0.9 copy-done.28
  213.9 4.5 %assemble.1 = bf16[8,24,4096]{2,1,0:T(8,128)(2,1)} custom-call(s32[4]{0:T(128)S(1)} %pad_add_fusion.place, bf16[4,8,24,128]{3,2,1,0:T(8,128)(2,1)S(1)} %copy-done.13, bf16[4,8,24,128]{3,2,1,0:T(8,128)(2,1)S(1)} %copy-done.15, bf16[4,8,24,128]{3,2,1,0:T(8,128)(2,1)S(1)} %copy-done.17, bf16[4,8,24,128]{3,2,1,0:T(8,128)(2,1)S(1)} %copy-done.19, ...), custom_call_target="tpu_custom_call" | custom-call | tf_op jit(solution)/shard_map/assemble/pallas_call | solution.py:273
  (102 shorter events, 0.6 us)
Async XLA Ops:
  0.0 25.0 %copy-start = (bf16[256,4096]{1,0:T(8,128)(2,1)S(1)}, bf16[256,4096]{1,0:T(8,128)(2,1)}, u32[]{:S(2)}) copy-start(bf16[256,4096]{1,0:T(8,128)(2,1)} %param.13) | copy-start | bytes 6291460
  0.9 1.4 copy-start.1
  2.3 1.4 copy-start.2
  3.7 1.4 copy-start.3
  5.1 0.8 copy-start.29
  10.3 13.8 %copy-start.20 = (bf16[4,3,8,24,128]{4,3,2,1,0:T(8,128)(2,1)}, bf16[4,3,8,24,128]{4,3,2,1,0:T(8,128)(2,1)S(1)}, u32[]{:S(2)}) copy-start(bf16[4,3,8,24,128]{4,3,2,1,0:T(8,128)(2,1)S(1)} %get-tuple-element.21.refs_0_) | copy-start | bytes 1769476
  10.3 14.6 %copy-start.26 = (bf16[4,3,8,24,128]{4,3,2,1,0:T(8,128)(2,1)}, bf16[4,3,8,24,128]{4,3,2,1,0:T(8,128)(2,1)S(1)}, u32[]{:S(2)}) copy-start(bf16[4,3,8,24,128]{4,3,2,1,0:T(8,128)(2,1)S(1)} %get-tuple-element.29.refs_0_) | copy-start | bytes 1769476
  10.3 14.6 %copy-start.30 = (bf16[4,3,8,24,128]{4,3,2,1,0:T(8,128)(2,1)}, bf16[4,3,8,24,128]{4,3,2,1,0:T(8,128)(2,1)S(1)}, u32[]{:S(2)}) copy-start(bf16[4,3,8,24,128]{4,3,2,1,0:T(8,128)(2,1)S(1)} %get-tuple-element.24) | copy-start | bytes 1769476
  10.3 14.6 %copy-start.36 = (s32[8]{0:T(128)S(1)}, s32[8]{0:T(128)}, u32[]{:S(2)}) copy-start(s32[8]{0:T(128)} %param.12) | copy-start | bytes 100
  10.3 15.8 %collective-permute-start.13 = (bf16[4,3,8,24,128]{4,3,2,1,0:T(8,128)(2,1)}, bf16[4,3,8,24,128]{4,3,2,1,0:T(8,128)(2,1)}, u32[]{:S(2)}, u32[]{:S(2)}) collective-permute-start(bf16[4,3,8,24,128]{4,3,2,1,0:T(8,128)(2,1)} %get-tuple-element.30), channel_id=1, source_target_pairs={{0,4},{1,5},{2,6},{3,7},{4,8},{5,9},{6,10},{7,11},{8,12},{9,13},{1... | collective-permute-start | bytes 1769480 | tf_op jit(solution)/shard_map/ppermute | solution.py:26
  11.6 28.1 %collective-permute-start.14 = (bf16[4,3,8,24,128]{4,3,2,1,0:T(8,128)(2,1)}, bf16[4,3,8,24,128]{4,3,2,1,0:T(8,128)(2,1)}, u32[]{:S(2)}, u32[]{:S(2)}) collective-permute-start(bf16[4,3,8,24,128]{4,3,2,1,0:T(8,128)(2,1)} %get-tuple-element.31), channel_id=1, source_target_pairs={{0,8},{1,9},{2,10},{3,11},{4,12},{5,13},{6,14},{7,15},{8,0},{9,1},... | collective-permute-start | bytes 1769480 | tf_op jit(solution)/shard_map/ppermute | solution.py:26
  14.0 26.8 %collective-permute-start.15 = (bf16[4,3,8,24,128]{4,3,2,1,0:T(8,128)(2,1)}, bf16[4,3,8,24,128]{4,3,2,1,0:T(8,128)(2,1)}, u32[]{:S(2)}, u32[]{:S(2)}) collective-permute-start(bf16[4,3,8,24,128]{4,3,2,1,0:T(8,128)(2,1)} %get-tuple-element.32), channel_id=1, source_target_pairs={{0,12},{1,13},{2,14},{3,15},{4,0},{5,1},{6,2},{7,3},{8,4},{9,5},{1... | collective-permute-start | bytes 1769480 | tf_op jit(solution)/shard_map/ppermute | solution.py:26
  15.2 34.2 %collective-permute-start = (bf16[4,3,8,24,128]{4,3,2,1,0:T(8,128)(2,1)}, bf16[4,3,8,24,128]{4,3,2,1,0:T(8,128)(2,1)S(1)}, u32[]{:S(2)}, u32[]{:S(2)}) collective-permute-start(bf16[4,3,8,24,128]{4,3,2,1,0:T(8,128)(2,1)} %get-tuple-element.22), channel_id=1, source_target_pairs={{0,1},{1,2},{2,3},{3,0},{4,5},{5,6},{6,7},{7,4},{8,9},{9,10},{10,1... | collective-permute-start | bytes 1769480 | tf_op jit(solution)/shard_map/ppermute | solution.py:26
  18.2 41.0 %collective-permute-start.1 = (bf16[4,3,8,24,128]{4,3,2,1,0:T(8,128)(2,1)}, bf16[4,3,8,24,128]{4,3,2,1,0:T(8,128)(2,1)S(1)}, u32[]{:S(2)}, u32[]{:S(2)}) collective-permute-start(bf16[4,3,8,24,128]{4,3,2,1,0:T(8,128)(2,1)} %get-tuple-element.23), channel_id=1, source_target_pairs={{0,2},{1,3},{2,0},{3,1},{4,6},{5,7},{6,4},{7,5},{8,10},{9,11},{10,... | collective-permute-start | bytes 1769480 | tf_op jit(solution)/shard_map/ppermute | solution.py:26
  25.0 17.0 %copy-start.35 = (bf16[1,3,8,24,128]{4,3,2,1,0:T(8,128)(2,1)S(1)}, bf16[1,3,8,24,128]{4,3,2,1,0:T(8,128)(2,1)}, u32[]{:S(2)}) copy-start(bf16[1,3,8,24,128]{4,3,2,1,0:T(8,128)(2,1)} %get-tuple-element.37) | copy-start | bytes 442372
  26.1 87.6 %collective-permute-start.2 = (bf16[4,3,8,24,128]{4,3,2,1,0:T(8,128)(2,1)}, bf16[4,3,8,24,128]{4,3,2,1,0:T(8,128)(2,1)S(1)}, u32[]{:S(2)}, u32[]{:S(2)}) collective-permute-start(bf16[4,3,8,24,128]{4,3,2,1,0:T(8,128)(2,1)} %copy-done.30), channel_id=1, source_target_pairs={{0,3},{1,0},{2,1},{3,2},{4,7},{5,4},{6,5},{7,6},{8,11},{9,8},{10,9... | collective-permute-start | bytes 1769480 | tf_op jit(solution)/shard_map/ppermute | solution.py:26
  33.2 15.0 %copy-start.34 = (bf16[1,3,8,24,128]{4,3,2,1,0:T(8,128)(2,1)S(1)}, bf16[1,3,8,24,128]{4,3,2,1,0:T(8,128)(2,1)}, u32[]{:S(2)}) copy-start(bf16[1,3,8,24,128]{4,3,2,1,0:T(8,128)(2,1)} %get-tuple-element.38) | copy-start | bytes 442372
  40.8 8.4 %copy-start.33 = (bf16[1,3,8,24,128]{4,3,2,1,0:T(8,128)(2,1)S(1)}, bf16[1,3,8,24,128]{4,3,2,1,0:T(8,128)(2,1)}, u32[]{:S(2)}) copy-start(bf16[1,3,8,24,128]{4,3,2,1,0:T(8,128)(2,1)} %get-tuple-element.39) | copy-start | bytes 442372
  42.1 84.2 %collective-permute-start.18 = (bf16[4,3,8,24,128]{4,3,2,1,0:T(8,128)(2,1)S(1)}, bf16[4,3,8,24,128]{4,3,2,1,0:T(8,128)(2,1)S(1)}, u32[]{:S(2)}, u32[]{:S(2)}) collective-permute-start(bf16[4,3,8,24,128]{4,3,2,1,0:T(8,128)(2,1)S(1)} %pad_maximum_fusion.5), channel_id=1, source_target_pairs={{0,3},{1,0},{2,1},{3,2},{4,7},{5,4},{6,5},{7,6},{8,11},{9,8},{10,9... | collective-permute-start | bytes 1769480 | tf_op jit(solution)/shard_map/ppermute | solution.py:26
  48.2 78.4 %collective-permute-start.17 = (bf16[4,3,8,24,128]{4,3,2,1,0:T(8,128)(2,1)S(1)}, bf16[4,3,8,24,128]{4,3,2,1,0:T(8,128)(2,1)S(1)}, u32[]{:S(2)}, u32[]{:S(2)}) collective-permute-start(bf16[4,3,8,24,128]{4,3,2,1,0:T(8,128)(2,1)S(1)} %pad_maximum_fusion.4), channel_id=1, source_target_pairs={{0,2},{1,3},{2,0},{3,1},{4,6},{5,7},{6,4},{7,5},{8,10},{9,11},{10,... | collective-permute-start | bytes 1769480 | tf_op jit(solution)/shard_map/ppermute | solution.py:26
  49.3 64.4 %copy-start.32 = (bf16[1,3,8,24,128]{4,3,2,1,0:T(8,128)(2,1)S(1)}, bf16[1,3,8,24,128]{4,3,2,1,0:T(8,128)(2,1)}, u32[]{:S(2)}) copy-start(bf16[1,3,8,24,128]{4,3,2,1,0:T(8,128)(2,1)} %get-tuple-element.49) | copy-start | bytes 442372
  49.4 64.5 %copy-start.22 = (bf16[4,3,8,24,128]{4,3,2,1,0:T(8,128)(2,1)}, bf16[4,3,8,24,128]{4,3,2,1,0:T(8,128)(2,1)S(1)}, u32[]{:S(2)}) copy-start(bf16[4,3,8,24,128]{4,3,2,1,0:T(8,128)(2,1)S(1)} %collective-permute-done.refs_1_) | copy-start | bytes 1769476
  49.4 77.2 %collective-permute-start.16 = (bf16[4,3,8,24,128]{4,3,2,1,0:T(8,128)(2,1)S(1)}, bf16[4,3,8,24,128]{4,3,2,1,0:T(8,128)(2,1)S(1)}, u32[]{:S(2)}, u32[]{:S(2)}) collective-permute-start(bf16[4,3,8,24,128]{4,3,2,1,0:T(8,128)(2,1)S(1)} %pad_maximum_fusion.3), channel_id=1, source_target_pairs={{0,1},{1,2},{2,3},{3,0},{4,5},{5,6},{6,7},{7,4},{8,9},{9,10},{10,1... | collective-permute-start | bytes 1769480 | tf_op jit(solution)/shard_map/ppermute | solution.py:26
  51.8 62.1 %copy-start.31 = (bf16[1,3,8,24,128]{4,3,2,1,0:T(8,128)(2,1)S(1)}, bf16[1,3,8,24,128]{4,3,2,1,0:T(8,128)(2,1)}, u32[]{:S(2)}) copy-start(bf16[1,3,8,24,128]{4,3,2,1,0:T(8,128)(2,1)} %get-tuple-element.50) | copy-start | bytes 442372
  59.2 54.8 %copy-start.24 = (bf16[4,3,8,24,128]{4,3,2,1,0:T(8,128)(2,1)}, bf16[4,3,8,24,128]{4,3,2,1,0:T(8,128)(2,1)S(1)}, u32[]{:S(2)}) copy-start(bf16[4,3,8,24,128]{4,3,2,1,0:T(8,128)(2,1)S(1)} %collective-permute-done.1.refs_2_) | copy-start | bytes 1769476
  113.7 12.9 %copy-start.27 = (bf16[4,3,8,24,128]{4,3,2,1,0:T(8,128)(2,1)S(1)}, bf16[4,3,8,24,128]{4,3,2,1,0:T(8,128)(2,1)}, u32[]{:S(2)}) copy-start(bf16[4,3,8,24,128]{4,3,2,1,0:T(8,128)(2,1)} %copy-done.26) | copy-start | bytes 1769476
  113.8 29.3 %collective-permute-start.5 = (bf16[4,3,8,24,128]{4,3,2,1,0:T(8,128)(2,1)S(1)}, bf16[4,3,8,24,128]{4,3,2,1,0:T(8,128)(2,1)S(1)}, u32[]{:S(2)}, u32[]{:S(2)}) collective-permute-start(bf16[4,3,8,24,128]{4,3,2,1,0:T(8,128)(2,1)S(1)} %pad_maximum_fusion.2), channel_id=1, source_target_pairs={{0,12},{1,13},{2,14},{3,15},{4,0},{5,1},{6,2},{7,3},{8,4},{9,5},{1... | collective-permute-start | bytes 1769480 | tf_op jit(solution)/shard_map/ppermute | solution.py:26
  114.0 29.9 %collective-permute-start.4 = (bf16[4,3,8,24,128]{4,3,2,1,0:T(8,128)(2,1)S(1)}, bf16[4,3,8,24,128]{4,3,2,1,0:T(8,128)(2,1)S(1)}, u32[]{:S(2)}, u32[]{:S(2)}) collective-permute-start(bf16[4,3,8,24,128]{4,3,2,1,0:T(8,128)(2,1)S(1)} %pad_maximum_fusion.1), channel_id=1, source_target_pairs={{0,8},{1,9},{2,10},{3,11},{4,12},{5,13},{6,14},{7,15},{8,0},{9,1},... | collective-permute-start | bytes 1769480 | tf_op jit(solution)/shard_map/ppermute | solution.py:26
  126.3 17.6 %collective-permute-start.3 = (bf16[4,3,8,24,128]{4,3,2,1,0:T(8,128)(2,1)S(1)}, bf16[4,3,8,24,128]{4,3,2,1,0:T(8,128)(2,1)S(1)}, u32[]{:S(2)}, u32[]{:S(2)}) collective-permute-start(bf16[4,3,8,24,128]{4,3,2,1,0:T(8,128)(2,1)S(1)} %pad_maximum_fusion), channel_id=1, source_target_pairs={{0,4},{1,5},{2,6},{3,7},{4,8},{5,9},{6,10},{7,11},{8,12},{9,13},{1... | collective-permute-start | bytes 1769480 | tf_op jit(solution)/shard_map/ppermute | solution.py:26
  126.6 17.3 %copy-start.21 = (bf16[4,3,8,24,128]{4,3,2,1,0:T(8,128)(2,1)S(1)}, bf16[4,3,8,24,128]{4,3,2,1,0:T(8,128)(2,1)}, u32[]{:S(2)}) copy-start(bf16[4,3,8,24,128]{4,3,2,1,0:T(8,128)(2,1)} %copy-done.20) | copy-start | bytes 1769476
  126.6 17.3 %copy-start.23 = (bf16[4,3,8,24,128]{4,3,2,1,0:T(8,128)(2,1)S(1)}, bf16[4,3,8,24,128]{4,3,2,1,0:T(8,128)(2,1)}, u32[]{:S(2)}) copy-start(bf16[4,3,8,24,128]{4,3,2,1,0:T(8,128)(2,1)} %copy-done.22) | copy-start | bytes 1769476
  126.6 17.3 %copy-start.25 = (bf16[4,3,8,24,128]{4,3,2,1,0:T(8,128)(2,1)S(1)}, bf16[4,3,8,24,128]{4,3,2,1,0:T(8,128)(2,1)}, u32[]{:S(2)}) copy-start(bf16[4,3,8,24,128]{4,3,2,1,0:T(8,128)(2,1)} %copy-done.24) | copy-start | bytes 1769476
  140.7 16.1 %copy-start.4 = (bf16[4,8,24,128]{3,2,1,0:T(8,128)(2,1)}, bf16[4,8,24,128]{3,2,1,0:T(8,128)(2,1)S(1)}, u32[]{:S(2)}) copy-start(bf16[4,8,24,128]{3,2,1,0:T(8,128)(2,1)S(1)} %get-tuple-element.33.refs_0_.refs_8_) | copy-start | bytes 589828
  140.7 21.2 %collective-permute-start.19 = (bf16[4,8,24,128]{3,2,1,0:T(8,128)(2,1)S(1)}, bf16[4,8,24,128]{3,2,1,0:T(8,128)(2,1)S(1)}, u32[]{:S(2)}, u32[]{:S(2)}) collective-permute-start(bf16[4,8,24,128]{3,2,1,0:T(8,128)(2,1)S(1)} %get-tuple-element.34), channel_id=1, source_target_pairs={{0,12},{1,13},{2,14},{3,15},{4,0},{5,1},{6,2},{7,3},{8,4},{9,5},{1... | collective-permute-start | bytes 589832 | tf_op jit(solution)/shard_map/ppermute | solution.py:26
  143.1 20.9 %collective-permute-start.20 = (bf16[4,8,24,128]{3,2,1,0:T(8,128)(2,1)S(1)}, bf16[4,8,24,128]{3,2,1,0:T(8,128)(2,1)S(1)}, u32[]{:S(2)}, u32[]{:S(2)}) collective-permute-start(bf16[4,8,24,128]{3,2,1,0:T(8,128)(2,1)S(1)} %get-tuple-element.35), channel_id=1, source_target_pairs={{0,8},{1,9},{2,10},{3,11},{4,12},{5,13},{6,14},{7,15},{8,0},{9,1},... | collective-permute-start | bytes 589832 | tf_op jit(solution)/shard_map/ppermute | solution.py:26
  143.2 20.9 %collective-permute-start.21 = (bf16[4,8,24,128]{3,2,1,0:T(8,128)(2,1)S(1)}, bf16[4,8,24,128]{3,2,1,0:T(8,128)(2,1)S(1)}, u32[]{:S(2)}, u32[]{:S(2)}) collective-permute-start(bf16[4,8,24,128]{3,2,1,0:T(8,128)(2,1)S(1)} %get-tuple-element.36), channel_id=1, source_target_pairs={{0,4},{1,5},{2,6},{3,7},{4,8},{5,9},{6,10},{7,11},{8,12},{9,13},{1... | collective-permute-start | bytes 589832 | tf_op jit(solution)/shard_map/ppermute | solution.py:26
  156.8 33.9 %copy-start.12 = (bf16[4,8,24,128]{3,2,1,0:T(8,128)(2,1)}, bf16[4,8,24,128]{3,2,1,0:T(8,128)(2,1)S(1)}, u32[]{:S(2)}) copy-start(bf16[4,8,24,128]{3,2,1,0:T(8,128)(2,1)S(1)} %get-tuple-element.25.refs_0_) | copy-start | bytes 589828
  156.8 30.4 %collective-permute-start.6 = (bf16[4,8,24,128]{3,2,1,0:T(8,128)(2,1)S(1)}, bf16[4,8,24,128]{3,2,1,0:T(8,128)(2,1)S(1)}, u32[]{:S(2)}, u32[]{:S(2)}) collective-permute-start(bf16[4,8,24,128]{3,2,1,0:T(8,128)(2,1)S(1)} %get-tuple-element.26), channel_id=1, source_target_pairs={{0,3},{1,0},{2,1},{3,2},{4,7},{5,4},{6,5},{7,6},{8,11},{9,8},{10,9... | collective-permute-start | bytes 589832 | tf_op jit(solution)/shard_map/ppermute | solution.py:26
  160.2 30.4 %collective-permute-start.7 = (bf16[4,8,24,128]{3,2,1,0:T(8,128)(2,1)S(1)}, bf16[4,8,24,128]{3,2,1,0:T(8,128)(2,1)S(1)}, u32[]{:S(2)}, u32[]{:S(2)}) collective-permute-start(bf16[4,8,24,128]{3,2,1,0:T(8,128)(2,1)S(1)} %get-tuple-element.27), channel_id=1, source_target_pairs={{0,2},{1,3},{2,0},{3,1},{4,6},{5,7},{6,4},{7,5},{8,10},{9,11},{10,... | collective-permute-start | bytes 589832 | tf_op jit(solution)/shard_map/ppermute | solution.py:26
  161.9 29.6 %copy-start.6 = (bf16[4,8,24,128]{3,2,1,0:T(8,128)(2,1)}, bf16[4,8,24,128]{3,2,1,0:T(8,128)(2,1)S(1)}, u32[]{:S(2)}) copy-start(bf16[4,8,24,128]{3,2,1,0:T(8,128)(2,1)S(1)} %collective-permute-done.19.refs_1_.refs_9_) | copy-start | bytes 589828
  161.9 28.8 %collective-permute-start.8 = (bf16[4,8,24,128]{3,2,1,0:T(8,128)(2,1)S(1)}, bf16[4,8,24,128]{3,2,1,0:T(8,128)(2,1)S(1)}, u32[]{:S(2)}, u32[]{:S(2)}) collective-permute-start(bf16[4,8,24,128]{3,2,1,0:T(8,128)(2,1)S(1)} %get-tuple-element.28), channel_id=1, source_target_pairs={{0,1},{1,2},{2,3},{3,0},{4,5},{5,6},{6,7},{7,4},{8,9},{9,10},{10,1... | collective-permute-start | bytes 589832 | tf_op jit(solution)/shard_map/ppermute | solution.py:26
  164.1 28.7 %copy-start.8 = (bf16[4,8,24,128]{3,2,1,0:T(8,128)(2,1)}, bf16[4,8,24,128]{3,2,1,0:T(8,128)(2,1)S(1)}, u32[]{:S(2)}) copy-start(bf16[4,8,24,128]{3,2,1,0:T(8,128)(2,1)S(1)} %collective-permute-done.20.refs_2_.refs_10_) | copy-start | bytes 589828
  164.1 28.6 %copy-start.10 = (bf16[4,8,24,128]{3,2,1,0:T(8,128)(2,1)}, bf16[4,8,24,128]{3,2,1,0:T(8,128)(2,1)S(1)}, u32[]{:S(2)}) copy-start(bf16[4,8,24,128]{3,2,1,0:T(8,128)(2,1)S(1)} %collective-permute-done.21.refs_3_.refs_11_) | copy-start | bytes 589828
  164.2 32.0 %collective-permute-start.24 = (bf16[4,8,24,128]{3,2,1,0:T(8,128)(2,1)S(1)}, bf16[4,8,24,128]{3,2,1,0:T(8,128)(2,1)}, u32[]{:S(2)}, u32[]{:S(2)}) collective-permute-start(bf16[4,8,24,128]{3,2,1,0:T(8,128)(2,1)S(1)} %pad_maximum_fusion.11), channel_id=1, source_target_pairs={{0,1},{1,2},{2,3},{3,0},{4,5},{5,6},{6,7},{7,4},{8,9},{9,10},{10,1... | collective-permute-start | bytes 589832 | tf_op jit(solution)/shard_map/ppermute | solution.py:26
  166.3 33.0 %collective-permute-start.23 = (bf16[4,8,24,128]{3,2,1,0:T(8,128)(2,1)S(1)}, bf16[4,8,24,128]{3,2,1,0:T(8,128)(2,1)}, u32[]{:S(2)}, u32[]{:S(2)}) collective-permute-start(bf16[4,8,24,128]{3,2,1,0:T(8,128)(2,1)S(1)} %pad_maximum_fusion.10), channel_id=1, source_target_pairs={{0,2},{1,3},{2,0},{3,1},{4,6},{5,7},{6,4},{7,5},{8,10},{9,11},{10,... | collective-permute-start | bytes 589832 | tf_op jit(solution)/shard_map/ppermute | solution.py:26
  187.2 13.5 %copy-start.14 = (bf16[4,8,24,128]{3,2,1,0:T(8,128)(2,1)}, bf16[4,8,24,128]{3,2,1,0:T(8,128)(2,1)S(1)}, u32[]{:S(2)}) copy-start(bf16[4,8,24,128]{3,2,1,0:T(8,128)(2,1)S(1)} %collective-permute-done.6.refs_1_) | copy-start | bytes 589828
  187.2 12.0 %collective-permute-start.22 = (bf16[4,8,24,128]{3,2,1,0:T(8,128)(2,1)S(1)}, bf16[4,8,24,128]{3,2,1,0:T(8,128)(2,1)}, u32[]{:S(2)}, u32[]{:S(2)}) collective-permute-start(bf16[4,8,24,128]{3,2,1,0:T(8,128)(2,1)S(1)} %pad_maximum_fusion.9), channel_id=1, source_target_pairs={{0,3},{1,0},{2,1},{3,2},{4,7},{5,4},{6,5},{7,6},{8,11},{9,8},{10,9... | collective-permute-start | bytes 589832 | tf_op jit(solution)/shard_map/ppermute | solution.py:26
  190.7 10.0 %copy-start.16 = (bf16[4,8,24,128]{3,2,1,0:T(8,128)(2,1)}, bf16[4,8,24,128]{3,2,1,0:T(8,128)(2,1)S(1)}, u32[]{:S(2)}) copy-start(bf16[4,8,24,128]{3,2,1,0:T(8,128)(2,1)S(1)} %collective-permute-done.7.refs_2_) | copy-start | bytes 589828
  190.7 4.7 %copy-start.18 = (bf16[4,8,24,128]{3,2,1,0:T(8,128)(2,1)}, bf16[4,8,24,128]{3,2,1,0:T(8,128)(2,1)S(1)}, u32[]{:S(2)}) copy-start(bf16[4,8,24,128]{3,2,1,0:T(8,128)(2,1)S(1)} %collective-permute-done.8.refs_3_) | copy-start | bytes 589828
  191.5 12.5 %collective-permute-start.11 = (bf16[4,8,24,128]{3,2,1,0:T(8,128)(2,1)}, bf16[4,8,24,128]{3,2,1,0:T(8,128)(2,1)}, u32[]{:S(2)}, u32[]{:S(2)}) collective-permute-start(bf16[4,8,24,128]{3,2,1,0:T(8,128)(2,1)} %pad_maximum_fusion.8), channel_id=1, source_target_pairs={{0,4},{1,5},{2,6},{3,7},{4,8},{5,9},{6,10},{7,11},{8,12},{9,13},{1... | collective-permute-start | bytes 589832 | tf_op jit(solution)/shard_map/ppermute | solution.py:26
  192.8 11.3 %collective-permute-start.10 = (bf16[4,8,24,128]{3,2,1,0:T(8,128)(2,1)}, bf16[4,8,24,128]{3,2,1,0:T(8,128)(2,1)}, u32[]{:S(2)}, u32[]{:S(2)}) collective-permute-start(bf16[4,8,24,128]{3,2,1,0:T(8,128)(2,1)} %pad_maximum_fusion.7), channel_id=1, source_target_pairs={{0,8},{1,9},{2,10},{3,11},{4,12},{5,13},{6,14},{7,15},{8,0},{9,1},... | collective-permute-start | bytes 589832 | tf_op jit(solution)/shard_map/ppermute | solution.py:26
  196.1 15.9 %copy-start.5 = (bf16[4,8,24,128]{3,2,1,0:T(8,128)(2,1)S(1)}, bf16[4,8,24,128]{3,2,1,0:T(8,128)(2,1)}, u32[]{:S(2)}) copy-start(bf16[4,8,24,128]{3,2,1,0:T(8,128)(2,1)} %copy-done.4) | copy-start | bytes 589828
  196.1 15.9 %copy-start.7 = (bf16[4,8,24,128]{3,2,1,0:T(8,128)(2,1)S(1)}, bf16[4,8,24,128]{3,2,1,0:T(8,128)(2,1)}, u32[]{:S(2)}) copy-start(bf16[4,8,24,128]{3,2,1,0:T(8,128)(2,1)} %copy-done.6) | copy-start | bytes 589828
  196.1 15.9 %copy-start.9 = (bf16[4,8,24,128]{3,2,1,0:T(8,128)(2,1)S(1)}, bf16[4,8,24,128]{3,2,1,0:T(8,128)(2,1)}, u32[]{:S(2)}) copy-start(bf16[4,8,24,128]{3,2,1,0:T(8,128)(2,1)} %copy-done.8) | copy-start | bytes 589828
  196.1 15.9 %copy-start.11 = (bf16[4,8,24,128]{3,2,1,0:T(8,128)(2,1)S(1)}, bf16[4,8,24,128]{3,2,1,0:T(8,128)(2,1)}, u32[]{:S(2)}) copy-start(bf16[4,8,24,128]{3,2,1,0:T(8,128)(2,1)} %copy-done.10) | copy-start | bytes 589828
  196.1 15.9 %copy-start.13 = (bf16[4,8,24,128]{3,2,1,0:T(8,128)(2,1)S(1)}, bf16[4,8,24,128]{3,2,1,0:T(8,128)(2,1)}, u32[]{:S(2)}) copy-start(bf16[4,8,24,128]{3,2,1,0:T(8,128)(2,1)} %copy-done.12) | copy-start | bytes 589828
  196.1 7.9 %collective-permute-start.9 = (bf16[4,8,24,128]{3,2,1,0:T(8,128)(2,1)}, bf16[4,8,24,128]{3,2,1,0:T(8,128)(2,1)}, u32[]{:S(2)}, u32[]{:S(2)}) collective-permute-start(bf16[4,8,24,128]{3,2,1,0:T(8,128)(2,1)} %pad_maximum_fusion.6), channel_id=1, source_target_pairs={{0,12},{1,13},{2,14},{3,15},{4,0},{5,1},{6,2},{7,3},{8,4},{9,5},{1... | collective-permute-start | bytes 589832 | tf_op jit(solution)/shard_map/ppermute | solution.py:26
  200.7 9.4 %collective-permute-start.25 = (bf16[16,24,128]{2,1,0:T(8,128)(2,1)}, bf16[16,24,128]{2,1,0:T(8,128)(2,1)}, u32[]{:S(2)}, u32[]{:S(2)}) collective-permute-start(bf16[16,24,128]{2,1,0:T(8,128)(2,1)} %leaving.3), channel_id=1, source_target_pairs={{0,16},{16,32},{32,48},{48,64},{64,80},{80,96},{96,112},{112,128},... | collective-permute-start | bytes 294920 | tf_op jit(solution)/shard_map/ppermute | solution.py:310
  204.0 8.1 %copy-start.15 = (bf16[4,8,24,128]{3,2,1,0:T(8,128)(2,1)S(1)}, bf16[4,8,24,128]{3,2,1,0:T(8,128)(2,1)}, u32[]{:S(2)}) copy-start(bf16[4,8,24,128]{3,2,1,0:T(8,128)(2,1)} %copy-done.14) | copy-start | bytes 589828
  204.0 8.1 %copy-start.17 = (bf16[4,8,24,128]{3,2,1,0:T(8,128)(2,1)S(1)}, bf16[4,8,24,128]{3,2,1,0:T(8,128)(2,1)}, u32[]{:S(2)}) copy-start(bf16[4,8,24,128]{3,2,1,0:T(8,128)(2,1)} %copy-done.16) | copy-start | bytes 589828
  205.6 6.4 %collective-permute-start.12 = (bf16[16,24,128]{2,1,0:T(8,128)(2,1)}, bf16[16,24,128]{2,1,0:T(8,128)(2,1)S(1)}, u32[]{:S(2)}, u32[]{:S(2)}) collective-permute-start(bf16[16,24,128]{2,1,0:T(8,128)(2,1)} %leaving.2), channel_id=1, source_target_pairs={{0,16},{16,32},{32,48},{48,64},{64,80},{80,96},{96,112},{112,128},... | collective-permute-start | bytes 294920 | tf_op jit(solution)/shard_map/ppermute | solution.py:310
  212.1 0.9 copy-start.19
  213.0 0.9 copy-start.28

commit v2 on v1

v2 whole, which is shorter than its diff:
```python
import math

import jax
import jax.numpy as jnp
from jax import lax
from jax.experimental import pallas as pl
from jax.experimental.pallas import tpu as pltpu
from jax.sharding import PartitionSpec as P

HD = 128
LOG2E = 1.4426950408889634
MIB = 1024 * 1024


def exchange(pieces):
    return lax.all_to_all(pieces, "seq", split_axis=0, concat_axis=0, tiled=True)


def prepare_kernel(q_ref, k_ref, v_ref, gain_ref, *outs):
    inner = q_ref.shape[2]

    def factor_of(ref):
        total = None
        for at in range(0, inner, 512):
            part = ref[:, :, at : at + 512].astype(jnp.float32)
            part = part * part
            total = part if total is None else total + part
        mean = jnp.sum(total, axis=-1, keepdims=True) * (1.0 / inner)
        return lax.rsqrt(mean + 1e-06)

    q_factor, k_factor = factor_of(q_ref), factor_of(k_ref)
    for head, out in enumerate(outs):
        for group in range(out.shape[0]):
            at = (group * len(outs) + head) * HD
            for kind, (ref, factor) in enumerate(((q_ref, q_factor), (k_ref, k_factor))):
                gain = gain_ref[kind : kind + 1, at : at + HD]
                part = ref[:, :, at : at + HD].astype(jnp.float32) * factor * gain[None]
                out[group, kind] = part.astype(jnp.bfloat16)
            out[group, 2] = v_ref[:, :, at : at + HD]


def prepare(groups, query, key, value, qk_gain):
    frames, rows, inner = query.shape
    heads = inner // HD // groups
    step = 2
    tall = pl.BlockSpec((step, rows, inner), lambda n: (n, 0, 0))
    out = pl.BlockSpec((groups, 3, step, rows, HD), lambda n: (0, 0, n, 0, 0))
    shape = jax.ShapeDtypeStruct((groups, 3, frames, rows, HD), jnp.bfloat16)
    return pl.pallas_call(
        prepare_kernel,
        grid=(frames // step,),
        in_specs=[tall, tall, tall, pl.BlockSpec((2, inner), lambda n: (0, 0))],
        out_specs=[out] * heads,
        out_shape=[shape] * heads,
        compiler_params=pltpu.CompilerParams(vmem_limit_bytes=60 * MIB),
        cost_estimate=pl.CostEstimate(
            flops=10 * query.size, bytes_accessed=12 * query.size, transcendentals=0
        ),
        name="prepare",
    )(query, key, value, qk_gain)


def attend_kernel(gate_ref, sent, out, q_all, k_all, v_all, s_even, s_odd, m_even, m_odd, gates, result):
    sources, _, frames, rows, _ = sent.shape
    tokens = frames * rows
    length = sources * tokens
    block, chunk = 256, 512
    blocks = length // block
    scale = LOG2E / math.sqrt(HD)
    period = gates.shape[0]

    for source in range(sources):
        at = source * tokens
        for kind, place in enumerate((q_all, k_all, v_all)):
            place[at : at + tokens, :HD] = sent[source, kind].reshape(tokens, HD)
    v_all[:, HD:] = jnp.ones((length, HD), jnp.bfloat16)
    for at in range(period // rows):
        gates[at * rows : (at + 1) * rows, :] = jnp.broadcast_to(
            gate_ref[at % frames : at % frames + 1, :], (rows, HD)
        )

    def rows_of(n):
        at = n * block
        return pl.ds(at if isinstance(n, int) else pl.multiple_of(at, block), block)

    def step(following, s_next, m_next, current, s_now, m_now):
        if following is not None:
            q = q_all[rows_of(following), :]
            peak = None
        if current is not None:
            most = m_now[...] * scale
            total = None
        for at in range(0, length, chunk):
            if following is not None:
                scores = lax.dot_general(
                    q,
                    k_all[at : at + chunk, :],
                    (((1,), (1,)), ((), ())),
                    preferred_element_type=jnp.float32,
                )
                s_next[:, at : at + chunk] = scores
                for lane in range(0, chunk, HD):
                    part = scores[:, lane : lane + HD]
                    peak = part if peak is None else jnp.maximum(peak, part)
            if current is not None:
                weights = [
                    jnp.exp2(s_now[:, at + lane : at + lane + HD] * scale - most).astype(jnp.bfloat16)
                    for lane in range(0, chunk, HD)
                ]
                part = jnp.dot(
                    jnp.concatenate(weights, axis=1),
                    v_all[at : at + chunk, :],
                    preferred_element_type=jnp.float32,
                )
                total = part if total is None else total + part
        if following is not None:
            m_next[...] = jnp.broadcast_to(jnp.max(peak, axis=1, keepdims=True), (block, HD))
        if current is not None:
            attended = (total[:, :HD] / total[:, HD:]).astype(jnp.bfloat16).astype(jnp.float32)
            gate = gates[rows_of(current % (period // block)), :]
            result[rows_of(current), :] = (gate * attended).astype(jnp.bfloat16)

    even, odd = (s_even, m_even), (s_odd, m_odd)
    step(0, *even, None, None, None)

    @pl.loop(0, blocks // 2 - 1)
    def _(pair):
        step(2 * pair + 1, *odd, 2 * pair, *even)
        step(2 * pair + 2, *even, 2 * pair + 1, *odd)

    step(blocks - 1, *odd, blocks - 2, *even)
    step(None, None, None, blocks - 1, *odd)
    for source in range(sources):
        at = source * tokens
        out[source] = result[at : at + tokens, :].reshape(frames, rows, HD)


def attend(gate, sent):
    sources, _, frames, rows, _ = sent.shape
    length = sources * frames * rows
    block = 256
    return pl.pallas_call(
        attend_kernel,
        grid=(1,),
        in_specs=[
            pl.BlockSpec((frames, HD), lambda n: (0, 0)),
            pl.BlockSpec(sent.shape, lambda n: (0, 0, 0, 0, 0)),
        ],
        out_specs=pl.BlockSpec((sources, frames, rows, HD), lambda n: (0, 0, 0, 0)),
        out_shape=jax.ShapeDtypeStruct((sources, frames, rows, HD), jnp.bfloat16),
        scratch_shapes=[
            pltpu.VMEM((length, HD), jnp.bfloat16),
            pltpu.VMEM((length, HD), jnp.bfloat16),
            pltpu.VMEM((length, 2 * HD), jnp.bfloat16),
            pltpu.VMEM((block, length), jnp.float32),
            pltpu.VMEM((block, length), jnp.float32),
            pltpu.VMEM((block, HD), jnp.float32),
            pltpu.VMEM((block, HD), jnp.float32),
            pltpu.VMEM((math.lcm(frames * rows, block), HD), jnp.float32),
            pltpu.VMEM((length, HD), jnp.bfloat16),
        ],
        compiler_params=pltpu.CompilerParams(vmem_limit_bytes=60 * MIB),
        cost_estimate=pl.CostEstimate(
            flops=8 * length * length * HD, bytes_accessed=8 * length * HD, transcendentals=length * length
        ),
        name="attend",
    )(gate, sent)


def leaving_frame(slot, returned):
    return lax.dynamic_index_in_dim(returned, slot[0], 1, keepdims=False)


def assemble_kernel(place, *refs):
    fresh, out = refs[-2:]
    heads = (len(refs) - 2) // 2
    step = out.shape[0]
    first = pl.program_id(0) * step
    for n in range(step):
        here = first + n == place[0]

        @pl.when(jnp.logical_not(here))
        def _(n=n):
            for head in range(heads):
                own = refs[2 * head]
                for group in range(own.shape[0]):
                    at = (group * heads + head) * HD
                    out[n, :, at : at + HD] = own[group, n]

        @pl.when(jnp.logical_and(here, place[1] != 0))
        def _(n=n):
            for head in range(heads):
                behind = refs[2 * head + 1]
                for group in range(behind.shape[0]):
                    at = (group * heads + head) * HD
                    out[n, :, at : at + HD] = behind[group]

        @pl.when(jnp.logical_and(here, place[1] == 0))
        def _(n=n):
            out[n] = fresh[...]


def assemble(place, parts, fresh):
    groups, frames, rows, _ = parts[0][0].shape
    inner = fresh.shape[1]
    step = 2
    own = pl.BlockSpec((groups, step, rows, HD), lambda n, _: (0, n, 0, 0))
    behind = pl.BlockSpec((groups, rows, HD), lambda n, _: (0, 0, 0))
    return pl.pallas_call(
        assemble_kernel,
        grid_spec=pltpu.PrefetchScalarGridSpec(
            num_scalar_prefetch=1,
            grid=(frames // step,),
            in_specs=[own, behind] * len(parts) + [pl.BlockSpec((rows, inner), lambda n, _: (0, 0))],
            out_specs=pl.BlockSpec((step, rows, inner), lambda n, _: (n, 0, 0)),
        ),
        out_shape=jax.ShapeDtypeStruct((frames, rows, inner), jnp.bfloat16),
        compiler_params=pltpu.CompilerParams(vmem_limit_bytes=60 * MIB),
        name="assemble",
    )(place, *[part for pair in parts for part in pair], fresh)


def level_gate(steps, gate_weight):
    half = gate_weight.shape[0] // 2
    freqs = jnp.exp(-math.log(10000.0) * jnp.arange(half, dtype=jnp.float32) / half)
    angles = steps.astype(jnp.float32)[:, None] * freqs[None, :]
    embed = jnp.concatenate([jnp.cos(angles), jnp.sin(angles)], axis=1).astype(jnp.bfloat16)
    return jnp.dot(embed, gate_weight, preferred_element_type=jnp.float32)


def shards(query, key, value, qk_gain, timesteps, gate_weight, slot, fresh):
    index = lax.axis_index("seq")
    groups = lax.axis_size("seq")
    sections = lax.axis_size("section")
    place = jnp.stack([slot[0], lax.axis_index("section")]).astype(jnp.int32)
    width = gate_weight.shape[1] // groups
    gate = level_gate(timesteps, lax.dynamic_slice_in_dim(gate_weight, index * width, width, 1))
    prepared = prepare(groups, query, key, value, qk_gain)
    parts = []
    for head, pieces in enumerate(prepared):
        result = attend(gate[:, head * HD : (head + 1) * HD], exchange(pieces))
        returned = exchange(result)
        leaving = leaving_frame(slot, returned)
        behind = lax.ppermute(leaving, "section", [(n, n + 1) for n in range(sections - 1)])
        parts.append((returned, behind))
    return assemble(place, parts, fresh)


def solution(mesh):
    placed = (
        P("section", "seq", None),
        P("section", "seq", None),
        P("section", "seq", None),
        P(),
        P("section"),
        P(),
        P(),
        P("seq", None),
    )
    return jax.shard_map(
        shards, mesh=mesh, in_specs=placed, out_specs=P("section", "seq", None), check_vma=False
    )
```

time: 221 us -> 204 us (0.923)
  blocking collectives: 0 us -> 65.7 us
  waiting for transfers between devices: 102 us -> 46.2 us
  starting transfers between devices: 60.9 us -> 43.8 us
  local copies, waits for them, and re-layouts: 12.1 us -> 2.17 us
    ppermute x24 -> x0, waiting for transfers between devices: 100 us -> none  [moved(): return lax.ppermute(value, 'seq', pairs)]
    all_to_all x0 -> x1, blocking collectives: none -> 65.7 us  [exchange(): lax.all_to_all(pieces, 'seq', split_axis=0, concat_axis=0, tiled=True)]
    ppermute x24 -> x0, starting transfers between devices: 53.1 us -> none  [moved(): return lax.ppermute(value, 'seq', pairs)]
    all_to_all x0 -> x3, waiting for transfers between devices: none -> 45.2 us  [exchange(): lax.all_to_all(pieces, 'seq', split_axis=0, concat_axis=0, tiled=True)]
    all_to_all x0 -> x3, starting transfers between devices: none -> 27.6 us  [exchange(): lax.all_to_all(pieces, 'seq', split_axis=0, concat_axis=0, tiled=True)]
    ppermute x2, starting transfers between devices: 7.73 us -> 16.3 us  [shards(): lax.ppermute(leaving, 'section', [(n, n + 1) for n in range(sections - 1)])]
    unnamed x74 -> x10, local copies, waits for them, and re-layouts: 6.96 us -> 0.64 us
    slice x17 -> x1, local copies, waits for them, and re-layouts: 5.14 us -> 0.61 us  [shards(): result = attend(gate[:, head * HD:(head + 1) * HD], exchange(pieces))]
  transfers between devices with their start and end apart: 26 -> 5, of which waited for: 8 -> 4; matrix products, arithmetic and copies ran while one was open for 4% -> 1% of each run, Pallas kernels for 14% -> 15%
where the time goes in v2:
time: 204 us; the launch traced here: 201 us
  blocking collectives  65.7 us (32%)
  waiting for transfers between devices  46.2 us (23%)
  starting transfers between devices  43.8 us (21%)
  Pallas kernels  41.1 us (20%)
  local copies, waits for them, and re-layouts  2.17 us (1%)
    all_to_all x1, blocking collectives, exchange(): lax.all_to_all(pieces, 'seq', split_axis=0, concat_axis=0, tiled=True)  65.7 us
    all_to_all x3, waiting for transfers between devices, exchange(): lax.all_to_all(pieces, 'seq', split_axis=0, concat_axis=0, tiled=True)  45.2 us
    pallas_call x2, Pallas kernels, attend(): pl.pallas_call(attend_kernel, grid=(1,), in_specs=[pl.BlockSpec((frames,...  30.5 us
    all_to_all x3, starting transfers between devices, exchange(): lax.all_to_all(pieces, 'seq', split_axis=0, concat_axis=0, tiled=True)  27.6 us
    ppermute x2, starting transfers between devices, shards(): lax.ppermute(leaving, 'section', [(n, n + 1) for n in range(sections - 1)])  16.3 us
    pallas_call x1, Pallas kernels, prepare(): pl.pallas_call(prepare_kernel, grid=(frames // step,), in_specs=[tall, ta...  5.96 us
    pallas_call x1, Pallas kernels, assemble(): pl.pallas_call(assemble_kernel, grid_spec=pltpu.PrefetchScalarGridSpec(nu...  4.67 us
  transfers between devices with their start and end apart: 5, of which 4 were waited for; matrix products, arithmetic and copies ran while one was open for 1% of the time, Pallas kernels for 15%

profile of v2, /device:TPU:17, one launch (start us, length us, event | category | flops | bytes accessed | tf_op | source)
XLA Modules:
  0.0 200.6 jit_solution(17164110660689996301)
XLA Ops:
  0.0 0.0 copy-start
  0.0 6.0 %prepare.1 = (bf16[16,3,8,24,128]{4,3,2,1,0:T(8,128)(2,1)}, bf16[16,3,8,24,128]{4,3,2,1,0:T(8,128)(2,1)}) custom-call(bf16[8,24,4096]{2,1,0:T(8,128)(2,1)} %q_ref.1, bf16[8,24,4096]{2,1,0:T(8,128)(2,1)} %k_ref.1, bf16[8,24,4096]{2,1,0:T(8,128)(2,1)} %v_ref.1, f32[2,4096]{1,0:T(2,128)} %gain_ref.1), custom_call_target="tpu_custom_call" | custom-call | flops 7864320 | bytes 9437184 | tf_op jit(solution)/shard_map/prepare/pallas_call | solution.py:49
  6.0 65.7 %all_to_all.20.sent = bf16[16,3,8,24,128]{4,3,2,1,0:T(8,128)(2,1)} all-to-all(bf16[16,3,8,24,128]{4,3,2,1,0:T(8,128)(2,1)} %get-tuple-element.8), channel_id=1, replica_groups=mesh['section'=16,'seq'=16] {'seq'}, dimensions={0} | all-to-all | bytes 4718592 | tf_op jit(solution)/shard_map/all_to_all | solution.py:16
  71.6 0.0 copy-start.4
  71.6 6.3 %all-to-all-start = ((bf16[16,3,8,24,128]{4,3,2,1,0:T(8,128)(2,1)}), bf16[16,3,8,24,128]{4,3,2,1,0:T(8,128)(2,1)}, u32[]{:S(2)}, u32[]{:S(2)}) async-start(bf16[16,3,8,24,128]{4,3,2,1,0:T(8,128)(2,1)} %get-tuple-element.7), calls=%async_computation | async-start | bytes 4718592 | tf_op jit(solution)/shard_map/all_to_all | solution.py:16
  78.0 0.0 copy-done.4
  78.0 0.1 fusion.2
  78.1 0.0 copy-done
  78.1 0.1 fusion
  78.3 0.6 fusion.9
  78.9 15.2 %attend.3 = bf16[16,8,24,128]{3,2,1,0:T(8,128)(2,1)} custom-call(f32[8,128]{1,0:T(8,128)} %get-tuple-element.9.gate_ref, bf16[16,3,8,24,128]{4,3,2,1,0:T(8,128)(2,1)} %all_to_all.20.sent), custom_call_target="tpu_custom_call" | custom-call | flops 9663676416 | bytes 3145728 | tf_op jit(solution)/shard_map/attend/pallas_call | solution.py:142
  94.1 29.2 %all-to-all-done.sent = bf16[16,3,8,24,128]{4,3,2,1,0:T(8,128)(2,1)} async-done(((bf16[16,3,8,24,128]{4,3,2,1,0:T(8,128)(2,1)}), bf16[16,3,8,24,128]{4,3,2,1,0:T(8,128)(2,1)}, u32[]{:S(2)}, u32[]{:S(2)}) %all-to-all-start) | async-done | bytes 2359328 | tf_op jit(solution)/shard_map/all_to_all | solution.py:16
  123.4 15.6 %all-to-all-start.3 = ((bf16[16,8,24,128]{3,2,1,0:T(8,128)(2,1)}), bf16[16,8,24,128]{3,2,1,0:T(8,128)(2,1)S(1)}, u32[]{:S(2)}, u32[]{:S(2)}) async-start(bf16[16,8,24,128]{3,2,1,0:T(8,128)(2,1)} %attend.3), calls=%async_computation.3 | async-start | bytes 1572864 | tf_op jit(solution)/shard_map/all_to_all | solution.py:16
  138.9 15.2 %attend.2 = bf16[16,8,24,128]{3,2,1,0:T(8,128)(2,1)} custom-call(f32[8,128]{1,0:T(8,128)} %get-tuple-element.10.gate_ref, bf16[16,3,8,24,128]{4,3,2,1,0:T(8,128)(2,1)} %all-to-all-done.sent), custom_call_target="tpu_custom_call" | custom-call | flops 9663676416 | bytes 3145728 | tf_op jit(solution)/shard_map/attend/pallas_call | solution.py:142
  154.2 3.5 %all-to-all-done.3.refs_2_ = bf16[16,8,24,128]{3,2,1,0:T(8,128)(2,1)S(1)} async-done(((bf16[16,8,24,128]{3,2,1,0:T(8,128)(2,1)}), bf16[16,8,24,128]{3,2,1,0:T(8,128)(2,1)S(1)}, u32[]{:S(2)}, u32[]{:S(2)}) %all-to-all-start.3) | async-done | bytes 786464 | tf_op jit(solution)/shard_map/all_to_all | solution.py:16
  157.6 0.0 copy-start.1
  157.6 5.7 %all-to-all-start.1 = ((bf16[16,8,24,128]{3,2,1,0:T(8,128)(2,1)}), bf16[16,8,24,128]{3,2,1,0:T(8,128)(2,1)}, u32[]{:S(2)}, u32[]{:S(2)}) async-start(bf16[16,8,24,128]{3,2,1,0:T(8,128)(2,1)} %attend.2), calls=%async_computation.1 | async-start | bytes 1572864 | tf_op jit(solution)/shard_map/all_to_all | solution.py:16
  164.0 5.8 %collective-permute-start.1 = (bf16[16,24,128]{2,1,0:T(8,128)(2,1)S(1)}, bf16[16,24,128]{2,1,0:T(8,128)(2,1)S(1)}, u32[]{:S(2)}, u32[]{:S(2)}) collective-permute-start(bf16[16,24,128]{2,1,0:T(8,128)(2,1)S(1)} %dynamic-slice_bitcast_fusion), channel_id=1, source_target_pairs={{0,16},{16,32},{32,48},{48,64},{64,80},{80,96},{96,112},{112,128},... | collective-permute-start | bytes 294920 | tf_op jit(solution)/shard_map/ppermute | solution.py:244
  169.8 12.5 %all-to-all-done.1.refs_0_ = bf16[16,8,24,128]{3,2,1,0:T(8,128)(2,1)} async-done(((bf16[16,8,24,128]{3,2,1,0:T(8,128)(2,1)}), bf16[16,8,24,128]{3,2,1,0:T(8,128)(2,1)}, u32[]{:S(2)}, u32[]{:S(2)}) %all-to-all-start.1) | async-done | bytes 786464 | tf_op jit(solution)/shard_map/all_to_all | solution.py:16
  182.3 0.9 dynamic-slice_bitcast_fusion.1
  183.2 10.5 %collective-permute-start = (bf16[16,24,128]{2,1,0:T(8,128)(2,1)S(1)}, bf16[16,24,128]{2,1,0:T(8,128)(2,1)S(1)}, u32[]{:S(2)}, u32[]{:S(2)}) collective-permute-start(bf16[16,24,128]{2,1,0:T(8,128)(2,1)S(1)} %dynamic-slice_bitcast_fusion.1), channel_id=1, source_target_pairs={{0,16},{16,32},{32,48},{48,64},{64,80},{80,96},{96,112},{112,128},... | collective-permute-start | bytes 294920 | tf_op jit(solution)/shard_map/ppermute | solution.py:244
  193.7 0.6 pad_add_fusion.place
  194.3 0.0 collective-permute-done.1.refs_3_
  194.3 0.0 copy-start.2
  194.3 1.0 collective-permute-done.refs_1_
  195.3 0.0 copy-done.1
  195.3 0.0 copy-done.2
  195.3 0.0 copy-start.3
  195.3 0.6 copy-done.3
  195.9 4.7 %assemble.1 = bf16[8,24,4096]{2,1,0:T(8,128)(2,1)} custom-call(s32[2]{0:T(128)} %pad_add_fusion.place, bf16[16,8,24,128]{3,2,1,0:T(8,128)(2,1)} %all-to-all-done.1.refs_0_, bf16[16,24,128]{2,1,0:T(8,128)(2,1)} %copy-done.3, bf16[16,8,24,128]{3,2,1,0:T(8,128)(2,1)} %copy-done.1, bf16[16,24,128]{2,1,0:T(8,128)(2,1)} %copy-done.2, bf16[24,4096]{1,0:T(8,128)(2,1)} %refs_4_.1), custom_call_target="tpu_custom_call" | custom-call | tf_op jit(solution)/shard_map/assemble/pallas_call | solution.py:209
  (3 shorter events, 0.0 us)
Async XLA Ops:
  0.0 78.1 %copy-start = (bf16[256,4096]{1,0:T(8,128)(2,1)S(1)}, bf16[256,4096]{1,0:T(8,128)(2,1)}, u32[]{:S(2)}) copy-start(bf16[256,4096]{1,0:T(8,128)(2,1)} %param.13) | copy-start | bytes 6291460
  71.6 6.4 %copy-start.4 = (s32[8]{0:T(128)S(1)}, s32[8]{0:T(128)}, u32[]{:S(2)}) copy-start(s32[8]{0:T(128)} %param.12) | copy-start | bytes 100
  71.6 51.7 %all-to-all-start = ((bf16[16,3,8,24,128]{4,3,2,1,0:T(8,128)(2,1)}), bf16[16,3,8,24,128]{4,3,2,1,0:T(8,128)(2,1)}, u32[]{:S(2)}, u32[]{:S(2)}) async-start(bf16[16,3,8,24,128]{4,3,2,1,0:T(8,128)(2,1)} %get-tuple-element.7), calls=%async_computation | async-start | bytes 4718592 | tf_op jit(solution)/shard_map/all_to_all | solution.py:16
  123.4 34.3 %all-to-all-start.3 = ((bf16[16,8,24,128]{3,2,1,0:T(8,128)(2,1)}), bf16[16,8,24,128]{3,2,1,0:T(8,128)(2,1)S(1)}, u32[]{:S(2)}, u32[]{:S(2)}) async-start(bf16[16,8,24,128]{3,2,1,0:T(8,128)(2,1)} %attend.3), calls=%async_computation.3 | async-start | bytes 1572864 | tf_op jit(solution)/shard_map/all_to_all | solution.py:16
  157.6 37.7 %copy-start.1 = (bf16[16,8,24,128]{3,2,1,0:T(8,128)(2,1)}, bf16[16,8,24,128]{3,2,1,0:T(8,128)(2,1)S(1)}, u32[]{:S(2)}) copy-start(bf16[16,8,24,128]{3,2,1,0:T(8,128)(2,1)S(1)} %all-to-all-done.3.refs_2_) | copy-start | bytes 2359300
  157.6 24.6 %all-to-all-start.1 = ((bf16[16,8,24,128]{3,2,1,0:T(8,128)(2,1)}), bf16[16,8,24,128]{3,2,1,0:T(8,128)(2,1)}, u32[]{:S(2)}, u32[]{:S(2)}) async-start(bf16[16,8,24,128]{3,2,1,0:T(8,128)(2,1)} %attend.2), calls=%async_computation.1 | async-start | bytes 1572864 | tf_op jit(solution)/shard_map/all_to_all | solution.py:16
  164.0 30.4 %collective-permute-start.1 = (bf16[16,24,128]{2,1,0:T(8,128)(2,1)S(1)}, bf16[16,24,128]{2,1,0:T(8,128)(2,1)S(1)}, u32[]{:S(2)}, u32[]{:S(2)}) collective-permute-start(bf16[16,24,128]{2,1,0:T(8,128)(2,1)S(1)} %dynamic-slice_bitcast_fusion), channel_id=1, source_target_pairs={{0,16},{16,32},{32,48},{48,64},{64,80},{80,96},{96,112},{112,128},... | collective-permute-start | bytes 294920 | tf_op jit(solution)/shard_map/ppermute | solution.py:244
  183.2 12.1 %collective-permute-start = (bf16[16,24,128]{2,1,0:T(8,128)(2,1)S(1)}, bf16[16,24,128]{2,1,0:T(8,128)(2,1)S(1)}, u32[]{:S(2)}, u32[]{:S(2)}) collective-permute-start(bf16[16,24,128]{2,1,0:T(8,128)(2,1)S(1)} %dynamic-slice_bitcast_fusion.1), channel_id=1, source_target_pairs={{0,16},{16,32},{32,48},{48,64},{64,80},{80,96},{96,112},{112,128},... | collective-permute-start | bytes 294920 | tf_op jit(solution)/shard_map/ppermute | solution.py:244
  194.3 1.0 copy-start.2
  195.3 0.6 copy-start.3

commit v3 on v2

v3 whole, which is shorter than its diff:
```python
import functools
import math

import jax
import jax.numpy as jnp
from jax import lax
from jax.experimental import pallas as pl
from jax.experimental.pallas import tpu as pltpu
from jax.sharding import PartitionSpec as P

HD = 128
SIDE = 4
LOG2E = 1.4426950408889634
AXES = ("z", "x")
MIB = 1024 * 1024


def moved(value, axis, steps):
    pairs = []
    for source in range(SIDE * SIDE):
        x, z = divmod(source, SIDE)
        if axis == "x":
            x = (x + steps) % SIDE
        else:
            z = (z + steps) % SIDE
        pairs.append((source, x * SIDE + z))
    return lax.ppermute(value, "seq", pairs)


def exchange(pieces):
    return lax.all_to_all(pieces, "seq", split_axis=0, concat_axis=0, tiled=True)


def stacked(held):
    return [jnp.stack([piece[j] for piece in held]) for j in range(1, SIDE)]


def second_stage(stacks, axis):
    return [moved(stack, axis, j + 1) for j, stack in enumerate(stacks)]


def after(value, *others):
    return lax.optimization_barrier((value, *others))[0]


def index_of(place, axes, i, j):
    steps = {axes[0]: i, axes[1]: j}
    return lax.rem(place[0] + steps["x"], SIDE) * SIDE + lax.rem(place[1] + steps["z"], SIDE)


def prepare_kernel(place, q_ref, k_ref, v_ref, gain_ref, *outs):
    inner = q_ref.shape[2]

    def factor_of(ref):
        total = None
        for at in range(0, inner, 512):
            part = ref[:, :, at : at + 512].astype(jnp.float32)
            part = part * part
            total = part if total is None else total + part
        mean = jnp.sum(total, axis=-1, keepdims=True) * (1.0 / inner)
        return lax.rsqrt(mean + 1e-06)

    q_factor, k_factor = factor_of(q_ref), factor_of(k_ref)

    def place_into(out, index, at):
        for kind, (ref, factor) in enumerate(((q_ref, q_factor), (k_ref, k_factor))):
            gain = gain_ref[kind : kind + 1, pl.ds(at, HD)]
            part = ref[:, :, pl.ds(at, HD)].astype(jnp.float32) * factor * gain[None]
            out[index, kind] = part.astype(jnp.bfloat16)
        out[index, 2] = v_ref[:, :, pl.ds(at, HD)]

    *first, second = outs
    for i in range(SIDE):
        for j in range(SIDE):
            place_into(first[i], j, pl.multiple_of(index_of(place, AXES, i, j) * (2 * HD), HD))
    for group in range(SIDE * SIDE):
        place_into(second, group, group * 2 * HD + HD)


def prepare(place, query, key, value, qk_gain):
    frames, rows, inner = query.shape
    step = 2
    tall = pl.BlockSpec((step, rows, inner), lambda n, _: (n, 0, 0))
    out = pl.BlockSpec((SIDE, 3, step, rows, HD), lambda n, _: (0, 0, n, 0, 0))
    shape = jax.ShapeDtypeStruct((SIDE, 3, frames, rows, HD), jnp.bfloat16)
    return pl.pallas_call(
        prepare_kernel,
        grid_spec=pltpu.PrefetchScalarGridSpec(
            num_scalar_prefetch=1,
            grid=(frames // step,),
            in_specs=[tall, tall, tall, pl.BlockSpec((2, inner), lambda n, _: (0, 0))],
            out_specs=[out] * SIDE
            + [pl.BlockSpec((SIDE * SIDE, 3, step, rows, HD), lambda n, _: (0, 0, n, 0, 0))],
        ),
        out_shape=[shape] * SIDE
        + [jax.ShapeDtypeStruct((SIDE * SIDE, 3, frames, rows, HD), jnp.bfloat16)],
        compiler_params=pltpu.CompilerParams(vmem_limit_bytes=60 * MIB),
        cost_estimate=pl.CostEstimate(
            flops=10 * query.size, bytes_accessed=12 * query.size, transcendentals=0
        ),
        name="prepare",
    )(place, query, key, value, qk_gain)


def attend_kernel(count, place, gate_ref, _, *refs):
    sent = refs[:count]
    out, q_all, k_all, v_all, s_even, s_odd, m_even, m_odd, gates, result = refs[count:]
    frames, rows = sent[0].shape[2:4]
    tokens = frames * rows
    length = SIDE * SIDE * tokens
    block, chunk = 256, 512
    blocks = length // block
    scale = LOG2E / math.sqrt(HD)

    def part_of(n):
        if count == 1:
            return sent[0], n, n
        i, j = divmod(n, SIDE)
        source = index_of(place, AXES, SIDE - i, SIDE - j)
        return (sent[i], 0, source) if j == 0 else (sent[SIDE + j - 1], i, source)

    for n in range(SIDE * SIDE):
        ref, index, _ = part_of(n)
        for kind, whole in enumerate((q_all, k_all, v_all)):
            whole[n * tokens : (n + 1) * tokens, :HD] = ref[index, kind].reshape(tokens, HD)
    v_all[:, HD:] = jnp.ones((length, HD), jnp.bfloat16)
    for at in range(SIDE * frames):
        gates[at * rows : (at + 1) * rows, :] = jnp.broadcast_to(
            gate_ref[at % frames : at % frames + 1, :], (rows, HD)
        )

    def rows_of(n):
        at = n * block
        return pl.ds(at if isinstance(n, int) else pl.multiple_of(at, block), block)

    def step(following, s_next, m_next, current, s_now, m_now):
        if following is not None:
            q = q_all[rows_of(following), :]
            peak = None
        if current is not None:
            most = m_now[...] * scale
            total = None
        for at in range(0, length, chunk):
            if following is not None:
                scores = lax.dot_general(
                    q,
                    k_all[at : at + chunk, :],
                    (((1,), (1,)), ((), ())),
                    preferred_element_type=jnp.float32,
                )
                s_next[:, at : at + chunk] = scores
                for lane in range(0, chunk, HD):
                    part = scores[:, lane : lane + HD]
                    peak = part if peak is None else jnp.maximum(peak, part)
            if current is not None:
                weights = [
                    jnp.exp2(s_now[:, at + lane : at + lane + HD] * scale - most).astype(jnp.bfloat16)
                    for lane in range(0, chunk, HD)
                ]
                part = jnp.dot(
                    jnp.concatenate(weights, axis=1),
                    v_all[at : at + chunk, :],
                    preferred_element_type=jnp.float32,
                )
                total = part if total is None else total + part
        if following is not None:
            m_next[...] = jnp.broadcast_to(jnp.max(peak, axis=1, keepdims=True), (block, HD))
        if current is not None:
            attended = (total[:, :HD] / total[:, HD:]).astype(jnp.bfloat16).astype(jnp.float32)
            gate = gates[rows_of(current % (SIDE * tokens // block)), :]
            result[rows_of(current), :] = (gate * attended).astype(jnp.bfloat16)

    even, odd = (s_even, m_even), (s_odd, m_odd)
    step(0, *even, None, None, None)

    @pl.loop(0, blocks // 2 - 1)
    def _(pair):
        step(2 * pair + 1, *odd, 2 * pair, *even)
        step(2 * pair + 2, *even, 2 * pair + 1, *odd)

    step(blocks - 1, *odd, blocks - 2, *even)
    step(None, None, None, blocks - 1, *odd)
    for n in range(SIDE * SIDE):
        out[part_of(n)[2]] = result[n * tokens : (n + 1) * tokens, :].reshape(frames, rows, HD)


def attend(place, gate, before, *sent):
    frames, rows = sent[0].shape[2:4]
    length = SIDE * SIDE * frames * rows
    block = 256
    one = pl.BlockSpec((1, 3, frames, rows, HD), lambda n, _: (0, 0, 0, 0, 0))
    whole = pl.BlockSpec((SIDE, 3, frames, rows, HD), lambda n, _: (0, 0, 0, 0, 0))
    every = pl.BlockSpec((SIDE * SIDE, 3, frames, rows, HD), lambda n, _: (0, 0, 0, 0, 0))
    return pl.pallas_call(
        functools.partial(attend_kernel, len(sent)),
        grid_spec=pltpu.PrefetchScalarGridSpec(
            num_scalar_prefetch=1,
            grid=(1,),
            in_specs=[pl.BlockSpec((frames, HD), lambda n, _: (0, 0)), pl.BlockSpec(memory_space=pl.ANY)]
            + ([every] if len(sent) == 1 else [one] * SIDE + [whole] * (SIDE - 1)),
            out_specs=pl.BlockSpec((SIDE * SIDE, frames, rows, HD), lambda n, _: (0, 0, 0, 0)),
            scratch_shapes=[
                pltpu.VMEM((length, HD), jnp.bfloat16),
                pltpu.VMEM((length, HD), jnp.bfloat16),
                pltpu.VMEM((length, 2 * HD), jnp.bfloat16),
                pltpu.VMEM((block, length), jnp.float32),
                pltpu.VMEM((block, length), jnp.float32),
                pltpu.VMEM((block, HD), jnp.float32),
                pltpu.VMEM((block, HD), jnp.float32),
                pltpu.VMEM((SIDE * frames * rows, HD), jnp.float32),
                pltpu.VMEM((length, HD), jnp.bfloat16),
            ],
        ),
        out_shape=jax.ShapeDtypeStruct((SIDE * SIDE, frames, rows, HD), jnp.bfloat16),
        compiler_params=pltpu.CompilerParams(vmem_limit_bytes=60 * MIB),
        cost_estimate=pl.CostEstimate(
            flops=28 * length * length * HD, bytes_accessed=8 * length * HD, transcendentals=length * length
        ),
        name="attend",
    )(place, gate, before, *sent)


def leaving_frame(slot, returned):
    return lax.dynamic_index_in_dim(returned, slot[0], 1, keepdims=False)


def assemble_kernel(*refs):
    *parts, out = refs
    for head, own in enumerate(parts):
        for group in range(own.shape[0]):
            at = (group * len(parts) + head) * HD
            out[:, :, at : at + HD] = own[group]


def assemble(parts):
    groups, frames, rows, _ = parts[0].shape
    inner = groups * len(parts) * HD
    step = 2
    own = pl.BlockSpec((groups, step, rows, HD), lambda n: (0, n, 0, 0))
    return pl.pallas_call(
        assemble_kernel,
        grid=(frames // step,),
        in_specs=[own] * len(parts),
        out_specs=pl.BlockSpec((step, rows, inner), lambda n: (n, 0, 0)),
        out_shape=jax.ShapeDtypeStruct((frames, rows, inner), jnp.bfloat16),
        compiler_params=pltpu.CompilerParams(vmem_limit_bytes=60 * MIB),
        cost_estimate=pl.CostEstimate(flops=0, bytes_accessed=4 * frames * rows * inner, transcendentals=0),
        name="assemble",
    )(*parts)


def hand_kernel(place, *refs):
    *behind, fresh, _, out = refs

    @pl.when(place[3] != 0)
    def _():
        for head, part in enumerate(behind):
            for group in range(part.shape[0]):
                at = (group * len(behind) + head) * HD
                out[0, :, at : at + HD] = part[group]

    @pl.when(place[3] == 0)
    def _():
        out[0] = fresh[...]


def hand_over(place, behind, fresh, gated):
    rows, inner = fresh.shape
    part = pl.BlockSpec(behind[0].shape, lambda n, _: (0, 0, 0))
    return pl.pallas_call(
        hand_kernel,
        grid_spec=pltpu.PrefetchScalarGridSpec(
            num_scalar_prefetch=1,
            grid=(1,),
            in_specs=[part] * len(behind)
            + [pl.BlockSpec((rows, inner), lambda n, _: (0, 0)), pl.BlockSpec(memory_space=pl.ANY)],
            out_specs=pl.BlockSpec((1, rows, inner), lambda n, place: (place[2], 0, 0)),
        ),
        out_shape=jax.ShapeDtypeStruct(gated.shape, gated.dtype),
        input_output_aliases={len(behind) + 2: 0},
        compiler_params=pltpu.CompilerParams(vmem_limit_bytes=60 * MIB),
        name="hand_over",
    )(place, *behind, fresh, gated)


def level_gate(steps, gate_weight):
    half = gate_weight.shape[0] // 2
    freqs = jnp.exp(-math.log(10000.0) * jnp.arange(half, dtype=jnp.float32) / half)
    angles = steps.astype(jnp.float32)[:, None] * freqs[None, :]
    embed = jnp.concatenate([jnp.cos(angles), jnp.sin(angles)], axis=1).astype(jnp.bfloat16)
    return jnp.dot(embed, gate_weight, preferred_element_type=jnp.float32)


def shards(query, key, value, qk_gain, timesteps, gate_weight, slot, fresh):
    index = lax.axis_index("seq")
    section = lax.axis_index("section")
    place = jnp.stack([index // SIDE, index % SIDE, slot[0], section]).astype(jnp.int32)
    columns = lax.dynamic_slice_in_dim(gate_weight, index * (2 * HD), 2 * HD, 1)
    gate = level_gate(timesteps, columns)
    prepared = prepare(place, query, key, value, qk_gain)
    *ahead, direct = prepared
    held = [ahead[0], moved(ahead[1], AXES[0], 1), None, moved(ahead[3], AXES[0], 3)]
    held[2] = moved(ahead[2], AXES[0], 2)
    sent = [*held, *second_stage(stacked(held), AXES[1])]
    direct = [exchange(after(direct, held[1], held[3]))]
    sections = lax.axis_size("section")
    parts, behind, before = [], [], qk_gain
    for head, operands in enumerate((sent, direct)):
        before = attend(place, gate[:, head * HD : (head + 1) * HD], before, *operands)
        returned = exchange(before)
        leaving = leaving_frame(slot, returned)
        behind.append(lax.ppermute(leaving, "section", [(n, n + 1) for n in range(sections - 1)]))
        parts.append(returned)
    return hand_over(place, behind, fresh, assemble(parts))


def solution(mesh):
    placed = (
        P("section", "seq", None),
        P("section", "seq", None),
        P("section", "seq", None),
        P(),
        P("section"),
        P(),
        P(),
        P("seq", None),
    )
    return jax.shard_map(
        shards, mesh=mesh, in_specs=placed, out_specs=P("section", "seq", None), check_vma=False
    )
```

time: 204 us -> 205 us (level)
  blocking collectives: 65.7 us -> 0 us
  waiting for transfers between devices: 46.2 us -> 93.1 us
  starting transfers between devices: 43.8 us -> 55.7 us
  local copies, waits for them, and re-layouts: 2.17 us -> 6.15 us
  Pallas kernels: 41.1 us -> 44.6 us
    ppermute x0 -> x6, waiting for transfers between devices: none -> 80.7 us  [moved(): return lax.ppermute(value, 'seq', pairs)]
    all_to_all x1 -> x0, blocking collectives: 65.7 us -> none  [exchange(): lax.all_to_all(pieces, 'seq', split_axis=0, concat_axis=0, tiled=True)]
    all_to_all x3, waiting for transfers between devices: 45.2 us -> 12.3 us  [exchange(): lax.all_to_all(pieces, 'seq', split_axis=0, concat_axis=0, tiled=True)]
    ppermute x0 -> x6, starting transfers between devices: none -> 14.2 us  [moved(): return lax.ppermute(value, 'seq', pairs)]
    all_to_all x3, starting transfers between devices: 27.6 us -> 19.4 us  [exchange(): lax.all_to_all(pieces, 'seq', split_axis=0, concat_axis=0, tiled=True)]
    ppermute x2, starting transfers between devices: 16.3 us -> 22 us  [shards(): lax.ppermute(leaving, 'section', [(n, n + 1) for n in range(sections - 1)])]
    pallas_call x4 -> x5, Pallas kernels: 41.1 us -> 44.6 us  [the longest x2 31.8 us: attend(): pl.pallas_call(functools.partial(attend_kernel, len(sent)), grid_spec=plt...]
    slice x1 -> x5, local copies, waits for them, and re-layouts: 0.61 us -> 3.95 us  [the longest x4 3.34 us: stacked(): return [jnp.stack([piece[j] for piece in held]) for j in range(1, SIDE)]]
  transfers between devices with their start and end apart: 5 -> 11, of which waited for: 4 -> 6; matrix products, arithmetic and copies ran while one was open for 1% -> 3% of each run, Pallas kernels for 15% -> 17%
where the time goes in v3:
time: 205 us; the launch traced here: 203 us
  waiting for transfers between devices  93.1 us (45%)
  starting transfers between devices  55.7 us (27%)
  Pallas kernels  44.6 us (22%)
  local copies, waits for them, and re-layouts  6.15 us (3%)
  other arithmetic  2.65 us (1%)
    ppermute x6, waiting for transfers between devices, moved(): return lax.ppermute(value, 'seq', pairs)  80.7 us
    pallas_call x2, Pallas kernels, attend(): pl.pallas_call(functools.partial(attend_kernel, len(sent)), grid_spec=plt...  31.8 us
    ppermute x2, starting transfers between devices, shards(): lax.ppermute(leaving, 'section', [(n, n + 1) for n in range(sections - 1)])  22 us
    all_to_all x3, starting transfers between devices, exchange(): lax.all_to_all(pieces, 'seq', split_axis=0, concat_axis=0, tiled=True)  19.4 us
    ppermute x6, starting transfers between devices, moved(): return lax.ppermute(value, 'seq', pairs)  14.2 us
    all_to_all x3, waiting for transfers between devices, exchange(): lax.all_to_all(pieces, 'seq', split_axis=0, concat_axis=0, tiled=True)  12.3 us
    pallas_call x1, Pallas kernels, prepare(): pl.pallas_call(prepare_kernel, grid_spec=pltpu.PrefetchScalarGridSpec(num...  6.69 us
  transfers between devices with their start and end apart: 11, of which 6 were waited for; matrix products, arithmetic and copies ran while one was open for 3% of the time, Pallas kernels for 17%

profile of v3, /device:TPU:17, one launch (start us, length us, event | category | flops | bytes accessed | tf_op | source)
XLA Modules:
  0.0 203.3 jit_solution(1404798779246383626)
XLA Ops:
  0.0 0.0 copy-start
  0.8 0.7 pad_add_fusion.place
  1.5 6.7 %prepare.1 = (bf16[4,3,8,24,128]{4,3,2,1,0:T(8,128)(2,1)}, bf16[4,3,8,24,128]{4,3,2,1,0:T(8,128)(2,1)}, bf16[4,3,8,24,128]{4,3,2,1,0:T(8,128)(2,1)}, bf16[4,3,8,...) custom-call(s32[4]{0:T(128)} %pad_add_fusion.place, bf16[8,24,4096]{2,1,0:T(8,128)(2,1)} %q_ref.1, ...), custom_call_target="tpu_custom_call" | custom-call | flops 7864320 | bytes 9437184 | tf_op jit(solution)/shard_map/prepare/pallas_call | solution.py:86
  8.2 3.0 %collective-permute-start = (bf16[4,3,8,24,128]{4,3,2,1,0:T(8,128)(2,1)}, bf16[4,3,8,24,128]{4,3,2,1,0:T(8,128)(2,1)S(1)}, u32[]{:S(2)}, u32[]{:S(2)}) collective-permute-start(bf16[4,3,8,24,128]{4,3,2,1,0:T(8,128)(2,1)} %get-tuple-element.12), channel_id=1, source_target_pairs={{0,1},{1,2},{2,3},{3,0},{4,5},{5,6},{6,7},{7,4},{8,9},{9,10},{10,1... | collective-permute-start | bytes 1769480 | tf_op jit(solution)/shard_map/ppermute | solution.py:27
  11.2 3.1 %collective-permute-start.2 = (bf16[4,3,8,24,128]{4,3,2,1,0:T(8,128)(2,1)}, bf16[4,3,8,24,128]{4,3,2,1,0:T(8,128)(2,1)}, u32[]{:S(2)}, u32[]{:S(2)}) collective-permute-start(bf16[4,3,8,24,128]{4,3,2,1,0:T(8,128)(2,1)} %get-tuple-element.14), channel_id=1, source_target_pairs={{0,3},{1,0},{2,1},{3,2},{4,7},{5,4},{6,5},{7,6},{8,11},{9,8},{10,9... | collective-permute-start | bytes 1769480 | tf_op jit(solution)/shard_map/ppermute | solution.py:27
  14.3 4.4 %collective-permute-start.1 = (bf16[4,3,8,24,128]{4,3,2,1,0:T(8,128)(2,1)}, bf16[4,3,8,24,128]{4,3,2,1,0:T(8,128)(2,1)}, u32[]{:S(2)}, u32[]{:S(2)}) collective-permute-start(bf16[4,3,8,24,128]{4,3,2,1,0:T(8,128)(2,1)} %get-tuple-element.13), channel_id=1, source_target_pairs={{0,2},{1,3},{2,0},{3,1},{4,6},{5,7},{6,4},{7,5},{8,10},{9,11},{10,... | collective-permute-start | bytes 1769480 | tf_op jit(solution)/shard_map/ppermute | solution.py:27
  18.7 1.1 fusion.9
  19.8 12.0 %collective-permute-done.refs_1_ = bf16[4,3,8,24,128]{4,3,2,1,0:T(8,128)(2,1)S(1)} collective-permute-done((bf16[4,3,8,24,128]{4,3,2,1,0:T(8,128)(2,1)}, bf16[4,3,8,24,128]{4,3,2,1,0:T(8,128)(2,1)S(1)}, u32[]{:S(2)}, u32[]{:S(2)}) %collective-permute-start) | collective-permute-done | bytes 589856 | tf_op jit(solution)/shard_map/ppermute | solution.py:27
  31.8 0.0 copy-start.2
  31.8 23.6 %collective-permute-done.2.refs_3_ = bf16[4,3,8,24,128]{4,3,2,1,0:T(8,128)(2,1)} collective-permute-done((bf16[4,3,8,24,128]{4,3,2,1,0:T(8,128)(2,1)}, bf16[4,3,8,24,128]{4,3,2,1,0:T(8,128)(2,1)}, u32[]{:S(2)}, u32[]{:S(2)}) %collective-permute-start.2) | collective-permute-done | bytes 589856 | tf_op jit(solution)/shard_map/ppermute | solution.py:27
  55.4 7.2 %all-to-all-start.1 = ((bf16[16,3,8,24,128]{4,3,2,1,0:T(8,128)(2,1)}), bf16[16,3,8,24,128]{4,3,2,1,0:T(8,128)(2,1)}, u32[]{:S(2)}, u32[]{:S(2)}) async-start(bf16[16,3,8,24,128]{4,3,2,1,0:T(8,128)(2,1)} %get-tuple-element.16), calls=%async_computation.1 | async-start | bytes 4718592 | tf_op jit(solution)/shard_map/all_to_all | solution.py:31
  62.6 0.0 copy-done.2
  62.6 1.1 fusion.12
  63.7 0.0 copy-start.5
  63.8 0.0 collective-permute-done.1.refs_2_
  63.8 1.1 fusion.11
  64.9 0.1 pad_maximum_fusion.2
  65.0 2.6 %collective-permute-start.5 = (bf16[4,3,8,24,128]{4,3,2,1,0:T(8,128)(2,1)S(1)}, bf16[4,3,8,24,128]{4,3,2,1,0:T(8,128)(2,1)}, u32[]{:S(2)}, u32[]{:S(2)}) collective-permute-start(bf16[4,3,8,24,128]{4,3,2,1,0:T(8,128)(2,1)S(1)} %pad_maximum_fusion.2), channel_id=1, source_target_pairs={{0,12},{1,13},{2,14},{3,15},{4,0},{5,1},{6,2},{7,3},{8,4},{9,5},{1... | collective-permute-start | bytes 1769480 | tf_op jit(solution)/shard_map/ppermute | solution.py:27
  67.6 0.9 pad_maximum_fusion.1
  68.5 0.6 collective-permute-start.4
  69.0 0.9 pad_maximum_fusion
  69.9 0.6 collective-permute-start.3
  70.5 0.0 copy-done.5
  70.5 0.1 fusion.2
  70.6 0.0 copy-done
  70.6 0.2 fusion
  70.8 0.6 fusion.13
  71.4 18.2 %collective-permute-done.5.refs_6_ = bf16[4,3,8,24,128]{4,3,2,1,0:T(8,128)(2,1)} collective-permute-done((bf16[4,3,8,24,128]{4,3,2,1,0:T(8,128)(2,1)S(1)}, bf16[4,3,8,24,128]{4,3,2,1,0:T(8,128)(2,1)}, u32[]{:S(2)}, u32[]{:S(2)}) %collective-permute-start.5) | collective-permute-done | bytes 589856 | tf_op jit(solution)/shard_map/ppermute | solution.py:27
  89.6 0.0 collective-permute-done.4.refs_5_
  89.6 26.9 %collective-permute-done.3.refs_4_ = bf16[4,3,8,24,128]{4,3,2,1,0:T(8,128)(2,1)} collective-permute-done((bf16[4,3,8,24,128]{4,3,2,1,0:T(8,128)(2,1)}, bf16[4,3,8,24,128]{4,3,2,1,0:T(8,128)(2,1)}, u32[]{:S(2)}, u32[]{:S(2)}) %collective-permute-start.3) | collective-permute-done | bytes 589856 | tf_op jit(solution)/shard_map/ppermute | solution.py:27
  116.5 15.9 %attend.2._ = bf16[16,8,24,128]{3,2,1,0:T(8,128)(2,1)} custom-call(s32[4]{0:T(128)} %pad_add_fusion.place, f32[8,128]{1,0:T(8,128)} %get-tuple-element.30.gate_ref, f32[2,4096]{1,0:T(2,128)} %_.1, bf16[4,3,8,24,128]{4,3,2,1,0:T(8,128)(2,1)} %get-tuple-element.11.refs_0_, bf16[4,3,8,24,128]{4,3,2,1,0:T(8,128)(2,1)} %copy-done.2, ...), custom_call_target="tpu_custom_call" | custom-call | flops 33822867456 | bytes 3145728 | tf_op jit(solution)/shard_map/attend/pallas_call | solution.py:194
  132.4 0.0 all-to-all-done.1.refs_0_
  132.4 7.9 %all-to-all-start = ((bf16[16,8,24,128]{3,2,1,0:T(8,128)(2,1)}), bf16[16,8,24,128]{3,2,1,0:T(8,128)(2,1)S(1)}, u32[]{:S(2)}, u32[]{:S(2)}) async-start(bf16[16,8,24,128]{3,2,1,0:T(8,128)(2,1)} %attend.2._), calls=%async_computation | async-start | bytes 1572864 | tf_op jit(solution)/shard_map/all_to_all | solution.py:31
  140.3 15.9 %attend.3 = bf16[16,8,24,128]{3,2,1,0:T(8,128)(2,1)} custom-call(s32[4]{0:T(128)} %pad_add_fusion.place, f32[8,128]{1,0:T(8,128)} %get-tuple-element.29.gate_ref, bf16[16,8,24,128]{3,2,1,0:T(8,128)(2,1)} %attend.2._, bf16[16,3,8,24,128]{4,3,2,1,0:T(8,128)(2,1)} %all-to-all-done.1.refs_0_), custom_call_target="tpu_custom_call" | custom-call | flops 33822867456 | bytes 3145728 | tf_op jit(solution)/shard_map/attend/pallas_call | solution.py:194
  156.2 4.7 %all-to-all-done.refs_0_ = bf16[16,8,24,128]{3,2,1,0:T(8,128)(2,1)S(1)} async-done(((bf16[16,8,24,128]{3,2,1,0:T(8,128)(2,1)}), bf16[16,8,24,128]{3,2,1,0:T(8,128)(2,1)S(1)}, u32[]{:S(2)}, u32[]{:S(2)}) %all-to-all-start) | async-done | bytes 786464 | tf_op jit(solution)/shard_map/all_to_all | solution.py:31
  160.9 0.0 copy-start.1
  160.9 4.4 %all-to-all-start.2 = ((bf16[16,8,24,128]{3,2,1,0:T(8,128)(2,1)}), bf16[16,8,24,128]{3,2,1,0:T(8,128)(2,1)}, u32[]{:S(2)}, u32[]{:S(2)}) async-start(bf16[16,8,24,128]{3,2,1,0:T(8,128)(2,1)} %attend.3), calls=%async_computation.2 | async-start | bytes 1572864 | tf_op jit(solution)/shard_map/all_to_all | solution.py:31
  165.4 7.8 %collective-permute-start.6 = (bf16[16,24,128]{2,1,0:T(8,128)(2,1)S(1)}, bf16[16,24,128]{2,1,0:T(8,128)(2,1)S(1)}, u32[]{:S(2)}, u32[]{:S(2)}) collective-permute-start(bf16[16,24,128]{2,1,0:T(8,128)(2,1)S(1)} %dynamic-slice_bitcast_fusion.1), channel_id=1, source_target_pairs={{0,16},{16,32},{32,48},{48,64},{64,80},{80,96},{96,112},{112,128},... | collective-permute-start | bytes 294920 | tf_op jit(solution)/shard_map/ppermute | solution.py:312
  173.1 7.6 %all-to-all-done.2.refs_1_ = bf16[16,8,24,128]{3,2,1,0:T(8,128)(2,1)} async-done(((bf16[16,8,24,128]{3,2,1,0:T(8,128)(2,1)}), bf16[16,8,24,128]{3,2,1,0:T(8,128)(2,1)}, u32[]{:S(2)}, u32[]{:S(2)}) %all-to-all-start.2) | async-done | bytes 786464 | tf_op jit(solution)/shard_map/all_to_all | solution.py:31
  180.7 0.9 dynamic-slice_bitcast_fusion
  181.6 14.2 %collective-permute-start.7 = (bf16[16,24,128]{2,1,0:T(8,128)(2,1)S(1)}, bf16[16,24,128]{2,1,0:T(8,128)(2,1)S(1)}, u32[]{:S(2)}, u32[]{:S(2)}) collective-permute-start(bf16[16,24,128]{2,1,0:T(8,128)(2,1)S(1)} %dynamic-slice_bitcast_fusion), channel_id=1, source_target_pairs={{0,16},{16,32},{32,48},{48,64},{64,80},{80,96},{96,112},{112,128},... | collective-permute-start | bytes 294920 | tf_op jit(solution)/shard_map/ppermute | solution.py:312
  195.9 0.0 copy-done.1
  195.9 3.7 %assemble.1.refs_3_ = bf16[8,24,4096]{2,1,0:T(8,128)(2,1)} custom-call(bf16[16,8,24,128]{3,2,1,0:T(8,128)(2,1)} %copy-done.1, bf16[16,8,24,128]{3,2,1,0:T(8,128)(2,1)} %all-to-all-done.2.refs_1_), custom_call_target="tpu_custom_call" | custom-call | bytes 3145728 | tf_op jit(solution)/shard_map/assemble/pallas_call | solution.py:240
  199.6 0.0 collective-permute-done.6.refs_0_
  199.6 0.0 copy-start.3
  199.6 0.0 collective-permute-done.7.refs_1_
  199.6 0.6 copy-done.3
  200.2 0.0 copy-start.4
  200.2 0.6 copy-done.4
  200.9 2.4 %hand_over.1 = bf16[8,24,4096]{2,1,0:T(8,128)(2,1)} custom-call(s32[4]{0:T(128)} %pad_add_fusion.place, bf16[16,24,128]{2,1,0:T(8,128)(2,1)} %copy-done.3, bf16[16,24,128]{2,1,0:T(8,128)(2,1)} %copy-done.4, bf16[24,4096]{1,0:T(8,128)(2,1)} %refs_2_.1, bf16[8,24,4096]{2,1,0:T(8,128)(2,1)} %assemble.1.refs_3_), custom_call_target="tpu_custom_call", output_to_operand_aliasing={{}: (4, {})} | custom-call | tf_op jit(solution)/shard_map/hand_over/pallas_call | solution.py:270
  (4 shorter events, 0.1 us)
Async XLA Ops:
  0.0 70.6 %copy-start = (bf16[256,4096]{1,0:T(8,128)(2,1)S(1)}, bf16[256,4096]{1,0:T(8,128)(2,1)}, u32[]{:S(2)}) copy-start(bf16[256,4096]{1,0:T(8,128)(2,1)} %param.13) | copy-start | bytes 6291460
  8.2 23.6 %collective-permute-start = (bf16[4,3,8,24,128]{4,3,2,1,0:T(8,128)(2,1)}, bf16[4,3,8,24,128]{4,3,2,1,0:T(8,128)(2,1)S(1)}, u32[]{:S(2)}, u32[]{:S(2)}) collective-permute-start(bf16[4,3,8,24,128]{4,3,2,1,0:T(8,128)(2,1)} %get-tuple-element.12), channel_id=1, source_target_pairs={{0,1},{1,2},{2,3},{3,0},{4,5},{5,6},{6,7},{7,4},{8,9},{9,10},{10,1... | collective-permute-start | bytes 1769480 | tf_op jit(solution)/shard_map/ppermute | solution.py:27
  11.2 44.2 %collective-permute-start.2 = (bf16[4,3,8,24,128]{4,3,2,1,0:T(8,128)(2,1)}, bf16[4,3,8,24,128]{4,3,2,1,0:T(8,128)(2,1)}, u32[]{:S(2)}, u32[]{:S(2)}) collective-permute-start(bf16[4,3,8,24,128]{4,3,2,1,0:T(8,128)(2,1)} %get-tuple-element.14), channel_id=1, source_target_pairs={{0,3},{1,0},{2,1},{3,2},{4,7},{5,4},{6,5},{7,6},{8,11},{9,8},{10,9... | collective-permute-start | bytes 1769480 | tf_op jit(solution)/shard_map/ppermute | solution.py:27
  14.3 49.5 %collective-permute-start.1 = (bf16[4,3,8,24,128]{4,3,2,1,0:T(8,128)(2,1)}, bf16[4,3,8,24,128]{4,3,2,1,0:T(8,128)(2,1)}, u32[]{:S(2)}, u32[]{:S(2)}) collective-permute-start(bf16[4,3,8,24,128]{4,3,2,1,0:T(8,128)(2,1)} %get-tuple-element.13), channel_id=1, source_target_pairs={{0,2},{1,3},{2,0},{3,1},{4,6},{5,7},{6,4},{7,5},{8,10},{9,11},{10,... | collective-permute-start | bytes 1769480 | tf_op jit(solution)/shard_map/ppermute | solution.py:27
  31.8 30.8 %copy-start.2 = (bf16[4,3,8,24,128]{4,3,2,1,0:T(8,128)(2,1)}, bf16[4,3,8,24,128]{4,3,2,1,0:T(8,128)(2,1)S(1)}, u32[]{:S(2)}) copy-start(bf16[4,3,8,24,128]{4,3,2,1,0:T(8,128)(2,1)S(1)} %collective-permute-done.refs_1_) | copy-start | bytes 1769476
  55.4 77.0 %all-to-all-start.1 = ((bf16[16,3,8,24,128]{4,3,2,1,0:T(8,128)(2,1)}), bf16[16,3,8,24,128]{4,3,2,1,0:T(8,128)(2,1)}, u32[]{:S(2)}, u32[]{:S(2)}) async-start(bf16[16,3,8,24,128]{4,3,2,1,0:T(8,128)(2,1)} %get-tuple-element.16), calls=%async_computation.1 | async-start | bytes 4718592 | tf_op jit(solution)/shard_map/all_to_all | solution.py:31
  63.7 6.8 %copy-start.5 = (s32[8]{0:T(128)S(1)}, s32[8]{0:T(128)}, u32[]{:S(2)}) copy-start(s32[8]{0:T(128)} %param.12) | copy-start | bytes 100
  65.0 24.6 %collective-permute-start.5 = (bf16[4,3,8,24,128]{4,3,2,1,0:T(8,128)(2,1)S(1)}, bf16[4,3,8,24,128]{4,3,2,1,0:T(8,128)(2,1)}, u32[]{:S(2)}, u32[]{:S(2)}) collective-permute-start(bf16[4,3,8,24,128]{4,3,2,1,0:T(8,128)(2,1)S(1)} %pad_maximum_fusion.2), channel_id=1, source_target_pairs={{0,12},{1,13},{2,14},{3,15},{4,0},{5,1},{6,2},{7,3},{8,4},{9,5},{1... | collective-permute-start | bytes 1769480 | tf_op jit(solution)/shard_map/ppermute | solution.py:27
  68.5 21.1 %collective-permute-start.4 = (bf16[4,3,8,24,128]{4,3,2,1,0:T(8,128)(2,1)}, bf16[4,3,8,24,128]{4,3,2,1,0:T(8,128)(2,1)}, u32[]{:S(2)}, u32[]{:S(2)}) collective-permute-start(bf16[4,3,8,24,128]{4,3,2,1,0:T(8,128)(2,1)} %pad_maximum_fusion.1), channel_id=1, source_target_pairs={{0,8},{1,9},{2,10},{3,11},{4,12},{5,13},{6,14},{7,15},{8,0},{9,1},... | collective-permute-start | bytes 1769480 | tf_op jit(solution)/shard_map/ppermute | solution.py:27
  69.9 46.6 %collective-permute-start.3 = (bf16[4,3,8,24,128]{4,3,2,1,0:T(8,128)(2,1)}, bf16[4,3,8,24,128]{4,3,2,1,0:T(8,128)(2,1)}, u32[]{:S(2)}, u32[]{:S(2)}) collective-permute-start(bf16[4,3,8,24,128]{4,3,2,1,0:T(8,128)(2,1)} %pad_maximum_fusion), channel_id=1, source_target_pairs={{0,4},{1,5},{2,6},{3,7},{4,8},{5,9},{6,10},{7,11},{8,12},{9,13},{1... | collective-permute-start | bytes 1769480 | tf_op jit(solution)/shard_map/ppermute | solution.py:27
  132.4 28.5 %all-to-all-start = ((bf16[16,8,24,128]{3,2,1,0:T(8,128)(2,1)}), bf16[16,8,24,128]{3,2,1,0:T(8,128)(2,1)S(1)}, u32[]{:S(2)}, u32[]{:S(2)}) async-start(bf16[16,8,24,128]{3,2,1,0:T(8,128)(2,1)} %attend.2._), calls=%async_computation | async-start | bytes 1572864 | tf_op jit(solution)/shard_map/all_to_all | solution.py:31
  160.9 34.9 %copy-start.1 = (bf16[16,8,24,128]{3,2,1,0:T(8,128)(2,1)}, bf16[16,8,24,128]{3,2,1,0:T(8,128)(2,1)S(1)}, u32[]{:S(2)}) copy-start(bf16[16,8,24,128]{3,2,1,0:T(8,128)(2,1)S(1)} %all-to-all-done.refs_0_) | copy-start | bytes 2359300
  160.9 19.8 %all-to-all-start.2 = ((bf16[16,8,24,128]{3,2,1,0:T(8,128)(2,1)}), bf16[16,8,24,128]{3,2,1,0:T(8,128)(2,1)}, u32[]{:S(2)}, u32[]{:S(2)}) async-start(bf16[16,8,24,128]{3,2,1,0:T(8,128)(2,1)} %attend.3), calls=%async_computation.2 | async-start | bytes 1572864 | tf_op jit(solution)/shard_map/all_to_all | solution.py:31
  165.4 34.2 %collective-permute-start.6 = (bf16[16,24,128]{2,1,0:T(8,128)(2,1)S(1)}, bf16[16,24,128]{2,1,0:T(8,128)(2,1)S(1)}, u32[]{:S(2)}, u32[]{:S(2)}) collective-permute-start(bf16[16,24,128]{2,1,0:T(8,128)(2,1)S(1)} %dynamic-slice_bitcast_fusion.1), channel_id=1, source_target_pairs={{0,16},{16,32},{32,48},{48,64},{64,80},{80,96},{96,112},{112,128},... | collective-permute-start | bytes 294920 | tf_op jit(solution)/shard_map/ppermute | solution.py:312
  181.6 18.0 %collective-permute-start.7 = (bf16[16,24,128]{2,1,0:T(8,128)(2,1)S(1)}, bf16[16,24,128]{2,1,0:T(8,128)(2,1)S(1)}, u32[]{:S(2)}, u32[]{:S(2)}) collective-permute-start(bf16[16,24,128]{2,1,0:T(8,128)(2,1)S(1)} %dynamic-slice_bitcast_fusion), channel_id=1, source_target_pairs={{0,16},{16,32},{32,48},{48,64},{64,80},{80,96},{96,112},{112,128},... | collective-permute-start | bytes 294920 | tf_op jit(solution)/shard_map/ppermute | solution.py:312
  199.6 0.6 copy-start.3
  200.2 0.6 copy-start.4

commit v4 on v3

--- a/solution.py
+++ b/solution.py
@@ -11,7 +11,7 @@
 HD = 128
 SIDE = 4
 LOG2E = 1.4426950408889634
-AXES = ("z", "x")
+AXES = (("z", "x"), ("x", "z"))
 MIB = 1024 * 1024
 
 
@@ -27,8 +27,8 @@
     return lax.ppermute(value, "seq", pairs)
 
 
-def exchange(pieces):
-    return lax.all_to_all(pieces, "seq", split_axis=0, concat_axis=0, tiled=True)
+def first_stage(pieces, axis):
+    return [pieces[0]] + [moved(pieces[i], axis, i) for i in range(1, SIDE)]
 
 
 def stacked(held):
@@ -61,20 +61,16 @@
         return lax.rsqrt(mean + 1e-06)
 
     q_factor, k_factor = factor_of(q_ref), factor_of(k_ref)
-
-    def place_into(out, index, at):
-        for kind, (ref, factor) in enumerate(((q_ref, q_factor), (k_ref, k_factor))):
-            gain = gain_ref[kind : kind + 1, pl.ds(at, HD)]
-            part = ref[:, :, pl.ds(at, HD)].astype(jnp.float32) * factor * gain[None]
-            out[index, kind] = part.astype(jnp.bfloat16)
-        out[index, 2] = v_ref[:, :, pl.ds(at, HD)]
-
-    *first, second = outs
-    for i in range(SIDE):
-        for j in range(SIDE):
-            place_into(first[i], j, pl.multiple_of(index_of(place, AXES, i, j) * (2 * HD), HD))
-    for group in range(SIDE * SIDE):
-        place_into(second, group, group * 2 * HD + HD)
+    for head in range(2):
+        for i in range(SIDE):
+            for j in range(SIDE):
+                at = pl.multiple_of((index_of(place, AXES[head], i, j) * 2 + head) * HD, HD)
+                out = outs[head * SIDE + i]
+                for kind, (ref, factor) in enumerate(((q_ref, q_factor), (k_ref, k_factor))):
+                    gain = gain_ref[kind : kind + 1, pl.ds(at, HD)]
+                    part = ref[:, :, pl.ds(at, HD)].astype(jnp.float32) * factor * gain[None]
+                    out[j, kind] = part.astype(jnp.bfloat16)
+                out[j, 2] = v_ref[:, :, pl.ds(at, HD)]
 
 
 def prepare(place, query, key, value, qk_gain):
@@ -89,11 +85,9 @@
             num_scalar_prefetch=1,
             grid=(frames // step,),
             in_specs=[tall, tall, tall, pl.BlockSpec((2, inner), lambda n, _: (0, 0))],
-            out_specs=[out] * SIDE
-            + [pl.BlockSpec((SIDE * SIDE, 3, step, rows, HD), lambda n, _: (0, 0, n, 0, 0))],
-        ),
-        out_shape=[shape] * SIDE
-        + [jax.ShapeDtypeStruct((SIDE * SIDE, 3, frames, rows, HD), jnp.bfloat16)],
+            out_specs=[out] * (2 * SIDE),
+        ),
+        out_shape=[shape] * (2 * SIDE),
         compiler_params=pltpu.CompilerParams(vmem_limit_bytes=60 * MIB),
         cost_estimate=pl.CostEstimate(
             flops=10 * query.size, bytes_accessed=12 * query.size, transcendentals=0
@@ -102,27 +96,22 @@
     )(place, query, key, value, qk_gain)
 
 
-def attend_kernel(count, place, gate_ref, _, *refs):
-    sent = refs[:count]
-    out, q_all, k_all, v_all, s_even, s_odd, m_even, m_odd, gates, result = refs[count:]
-    frames, rows = sent[0].shape[2:4]
+def attend_kernel(axes, place, gate_ref, _, *refs):
+    held, arrived = refs[:SIDE], refs[SIDE : 2 * SIDE - 1]
+    out, q_all, k_all, v_all, s_even, s_odd, m_even, m_odd, gates, result = refs[2 * SIDE - 1 :]
+    frames, rows = held[0].shape[2:4]
     tokens = frames * rows
     length = SIDE * SIDE * tokens
     block, chunk = 256, 512
     blocks = length // block
     scale = LOG2E / math.sqrt(HD)
 
-    def part_of(n):
-        if count == 1:
-            return sent[0], n, n
-        i, j = divmod(n, SIDE)
-        source = index_of(place, AXES, SIDE - i, SIDE - j)
-        return (sent[i], 0, source) if j == 0 else (sent[SIDE + j - 1], i, source)
-
-    for n in range(SIDE * SIDE):
-        ref, index, _ = part_of(n)
-        for kind, whole in enumerate((q_all, k_all, v_all)):
-            whole[n * tokens : (n + 1) * tokens, :HD] = ref[index, kind].reshape(tokens, HD)
+    for i in range(SIDE):
+        for j in range(SIDE):
+            at = (i * SIDE + j) * tokens
+            for kind, whole in enumerate((q_all, k_all, v_all)):
+                part = held[i][0, kind] if j == 0 else arrived[j - 1][i, kind]
+                whole[at : at + tokens, :HD] = part.reshape(tokens, HD)
     v_all[:, HD:] = jnp.ones((length, HD), jnp.bfloat16)
     for at in range(SIDE * frames):
         gates[at * rows : (at + 1) * rows, :] = jnp.broadcast_to(
@@ -180,24 +169,27 @@
 
     step(blocks - 1, *odd, blocks - 2, *even)
     step(None, None, None, blocks - 1, *odd)
-    for n in range(SIDE * SIDE):
-        out[part_of(n)[2]] = result[n * tokens : (n + 1) * tokens, :].reshape(frames, rows, HD)
-
-
-def attend(place, gate, before, *sent):
-    frames, rows = sent[0].shape[2:4]
+    for i in range(SIDE):
+        for j in range(SIDE):
+            at = (i * SIDE + j) * tokens
+            source = index_of(place, axes, SIDE - i, SIDE - j)
+            out[source] = result[at : at + tokens, :].reshape(frames, rows, HD)
+
+
+def attend(axes, place, gate, before, held, arrived):
+    frames, rows = held[0].shape[2:4]
     length = SIDE * SIDE * frames * rows
     block = 256
     one = pl.BlockSpec((1, 3, frames, rows, HD), lambda n, _: (0, 0, 0, 0, 0))
     whole = pl.BlockSpec((SIDE, 3, frames, rows, HD), lambda n, _: (0, 0, 0, 0, 0))
-    every = pl.BlockSpec((SIDE * SIDE, 3, frames, rows, HD), lambda n, _: (0, 0, 0, 0, 0))
     return pl.pallas_call(
-        functools.partial(attend_kernel, len(sent)),
+        functools.partial(attend_kernel, axes),
         grid_spec=pltpu.PrefetchScalarGridSpec(
             num_scalar_prefetch=1,
             grid=(1,),
             in_specs=[pl.BlockSpec((frames, HD), lambda n, _: (0, 0)), pl.BlockSpec(memory_space=pl.ANY)]
-            + ([every] if len(sent) == 1 else [one] * SIDE + [whole] * (SIDE - 1)),
+            + [one] * SIDE
+            + [whole] * (SIDE - 1),
             out_specs=pl.BlockSpec((SIDE * SIDE, frames, rows, HD), lambda n, _: (0, 0, 0, 0)),
             scratch_shapes=[
                 pltpu.VMEM((length, HD), jnp.bfloat16),
@@ -214,10 +206,10 @@
         out_shape=jax.ShapeDtypeStruct((SIDE * SIDE, frames, rows, HD), jnp.bfloat16),
         compiler_params=pltpu.CompilerParams(vmem_limit_bytes=60 * MIB),
         cost_estimate=pl.CostEstimate(
-            flops=28 * length * length * HD, bytes_accessed=8 * length * HD, transcendentals=length * length
+            flops=int(0.1 * length * length * HD) if axes[0] == "z" else 28 * length * length * HD, bytes_accessed=length if axes[0] == "z" else 8 * length * HD, transcendentals=0
         ),
         name="attend",
-    )(place, gate, before, *sent)
+    )(place, gate, before, *held, *arrived)
 
 
 def leaving_frame(slot, returned):
@@ -298,16 +290,20 @@
     columns = lax.dynamic_slice_in_dim(gate_weight, index * (2 * HD), 2 * HD, 1)
     gate = level_gate(timesteps, columns)
     prepared = prepare(place, query, key, value, qk_gain)
-    *ahead, direct = prepared
-    held = [ahead[0], moved(ahead[1], AXES[0], 1), None, moved(ahead[3], AXES[0], 3)]
-    held[2] = moved(ahead[2], AXES[0], 2)
-    sent = [*held, *second_stage(stacked(held), AXES[1])]
-    direct = [exchange(after(direct, held[1], held[3]))]
+    ahead, back = list(prepared[:SIDE]), list(prepared[SIDE:])
+    held = [None, first_stage(back, AXES[1][0])]
+    ahead[2] = after(ahead[2], held[1][2])
+    held[0] = first_stage(ahead, AXES[0][0])
+    back_stacks = stacked(held[1])
+    held[0][2] = after(held[0][2], *back_stacks)
+    stacks = [stacked(held[0]), back_stacks]
     sections = lax.axis_size("section")
     parts, behind, before = [], [], qk_gain
-    for head, operands in enumerate((sent, direct)):
-        before = attend(place, gate[:, head * HD : (head + 1) * HD], before, *operands)
-        returned = exchange(before)
+    for head in range(2):
+        arrived = second_stage(stacks[head], AXES[head][1])
+        result = attend(AXES[head], place, gate[:, head * HD : (head + 1) * HD], before, held[head], arrived)
+        before = result
+        returned = lax.all_to_all(result, "seq", split_axis=0, concat_axis=0, tiled=True)
         leaving = leaving_frame(slot, returned)
         behind.append(lax.ppermute(leaving, "section", [(n, n + 1) for n in range(sections - 1)]))
         parts.append(returned)

time: 205 us -> 194 us (0.946)
  waiting for transfers between devices: 93.1 us -> 70.1 us
  starting transfers between devices: 55.7 us -> 66.1 us
  other arithmetic: 2.65 us -> 5.38 us
    ppermute x6 -> x12, waiting for transfers between devices: 80.7 us -> 52 us  [moved(): return lax.ppermute(value, 'seq', pairs)]
    ppermute x6 -> x12, starting transfers between devices: 14.2 us -> 35.4 us  [moved(): return lax.ppermute(value, 'seq', pairs)]
    ppermute x2, starting transfers between devices: 22 us -> 15 us  [shards(): lax.ppermute(leaving, 'section', [(n, n + 1) for n in range(sections - 1)])]
    all_to_all x3 -> x2, waiting for transfers between devices: 12.3 us -> 18 us  [shards(): lax.all_to_all(result, 'seq', split_axis=0, concat_axis=0, tiled=True)]
    all_to_all x3 -> x2, starting transfers between devices: 19.4 us -> 15.7 us  [shards(): lax.all_to_all(result, 'seq', split_axis=0, concat_axis=0, tiled=True)]
    another operation x3 -> x6, other arithmetic: 1.86 us -> 4.64 us  [stacked(): return [jnp.stack([piece[j] for piece in held]) for j in range(1, SIDE)]]
  transfers between devices with their start and end apart: 11 -> 16, of which waited for: 6 -> 7; matrix products, arithmetic and copies ran while one was open for 3% -> 4% of each run, Pallas kernels for 17% -> 18%
where the time goes in v4:
time: 194 us; the launch traced here: 193 us
  waiting for transfers between devices  70.1 us (36%)
  starting transfers between devices  66.1 us (34%)
  Pallas kernels  44.9 us (23%)
  other arithmetic  5.38 us (3%)
  local copies, waits for them, and re-layouts  5.31 us (3%)
    ppermute x12, waiting for transfers between devices, moved(): return lax.ppermute(value, 'seq', pairs)  52 us
    ppermute x12, starting transfers between devices, moved(): return lax.ppermute(value, 'seq', pairs)  35.4 us
    pallas_call x2, Pallas kernels, attend(): pl.pallas_call(functools.partial(attend_kernel, axes), grid_spec=pltpu.Pr...  31.8 us
    all_to_all x2, waiting for transfers between devices, shards(): lax.all_to_all(result, 'seq', split_axis=0, concat_axis=0, tiled=True)  18 us
    all_to_all x2, starting transfers between devices, shards(): lax.all_to_all(result, 'seq', split_axis=0, concat_axis=0, tiled=True)  15.7 us
    ppermute x2, starting transfers between devices, shards(): lax.ppermute(leaving, 'section', [(n, n + 1) for n in range(sections - 1)])  15 us
    pallas_call x1, Pallas kernels, prepare(): pl.pallas_call(prepare_kernel, grid_spec=pltpu.PrefetchScalarGridSpec(num...  6.92 us
    another operation x6, other arithmetic, stacked(): return [jnp.stack([piece[j] for piece in held]) for j in range(1, SIDE)]  4.64 us
  transfers between devices with their start and end apart: 16, of which 7 were waited for; matrix products, arithmetic and copies ran while one was open for 4% of the time, Pallas kernels for 18%

profile of v4, /device:TPU:17, one launch (start us, length us, event | category | flops | bytes accessed | tf_op | source)
XLA Modules:
  0.0 192.9 jit_solution(5495861018040916919)
XLA Ops:
  0.0 0.0 copy-start
  0.8 0.6 pad_add_fusion.place
  1.4 6.9 %prepare.1 = (bf16[4,3,8,24,128]{4,3,2,1,0:T(8,128)(2,1)}, bf16[4,3,8,24,128]{4,3,2,1,0:T(8,128)(2,1)}, bf16[4,3,8,24,128]{4,3,2,1,0:T(8,128)(2,1)}, bf16[4,3,8,...) custom-call(s32[4]{0:T(128)} %pad_add_fusion.place, ...), custom_call_target="tpu_custom_call" | custom-call | flops 7864320 | bytes 9437184 | tf_op jit(solution)/shard_map/prepare/pallas_call | solution.py:82
  8.4 2.8 %collective-permute-start.1 = (bf16[4,3,8,24,128]{4,3,2,1,0:T(8,128)(2,1)}, bf16[4,3,8,24,128]{4,3,2,1,0:T(8,128)(2,1)S(1)}, u32[]{:S(2)}, u32[]{:S(2)}) collective-permute-start(bf16[4,3,8,24,128]{4,3,2,1,0:T(8,128)(2,1)} %get-tuple-element.18), channel_id=1, source_target_pairs={{0,8},{1,9},{2,10},{3,11},{4,12},{5,13},{6,14},{7,15},{8,0},{9,1},... | collective-permute-start | bytes 1769480 | tf_op jit(solution)/shard_map/ppermute | solution.py:27
  11.2 0.3 collective-permute-start.3
  11.5 3.0 %collective-permute-start = (bf16[4,3,8,24,128]{4,3,2,1,0:T(8,128)(2,1)}, bf16[4,3,8,24,128]{4,3,2,1,0:T(8,128)(2,1)S(1)}, u32[]{:S(2)}, u32[]{:S(2)}) collective-permute-start(bf16[4,3,8,24,128]{4,3,2,1,0:T(8,128)(2,1)} %get-tuple-element.16), channel_id=1, source_target_pairs={{0,1},{1,2},{2,3},{3,0},{4,5},{5,6},{6,7},{7,4},{8,9},{9,10},{10,1... | collective-permute-start | bytes 1769480 | tf_op jit(solution)/shard_map/ppermute | solution.py:27
  14.5 2.4 %collective-permute-start.4 = (bf16[4,3,8,24,128]{4,3,2,1,0:T(8,128)(2,1)}, bf16[4,3,8,24,128]{4,3,2,1,0:T(8,128)(2,1)S(1)}, u32[]{:S(2)}, u32[]{:S(2)}) collective-permute-start(bf16[4,3,8,24,128]{4,3,2,1,0:T(8,128)(2,1)} %get-tuple-element.22), channel_id=1, source_target_pairs={{0,12},{1,13},{2,14},{3,15},{4,0},{5,1},{6,2},{7,3},{8,4},{9,5},{1... | collective-permute-start | bytes 1769480 | tf_op jit(solution)/shard_map/ppermute | solution.py:27
  16.8 3.0 %collective-permute-start.5 = (bf16[4,3,8,24,128]{4,3,2,1,0:T(8,128)(2,1)}, bf16[4,3,8,24,128]{4,3,2,1,0:T(8,128)(2,1)S(1)}, u32[]{:S(2)}, u32[]{:S(2)}) collective-permute-start(bf16[4,3,8,24,128]{4,3,2,1,0:T(8,128)(2,1)} %get-tuple-element.24), channel_id=1, source_target_pairs={{0,3},{1,0},{2,1},{3,2},{4,7},{5,4},{6,5},{7,6},{8,11},{9,8},{10,9... | collective-permute-start | bytes 1769480 | tf_op jit(solution)/shard_map/ppermute | solution.py:27
  19.9 1.4 fusion.9
  21.3 3.1 %collective-permute-done.1.refs_2_ = bf16[4,3,8,24,128]{4,3,2,1,0:T(8,128)(2,1)S(1)} collective-permute-done((bf16[4,3,8,24,128]{4,3,2,1,0:T(8,128)(2,1)}, bf16[4,3,8,24,128]{4,3,2,1,0:T(8,128)(2,1)S(1)}, u32[]{:S(2)}, u32[]{:S(2)}) %collective-permute-start.1) | collective-permute-done | bytes 589856 | tf_op jit(solution)/shard_map/ppermute | solution.py:27
  24.4 0.0 copy-done.12
  24.4 6.9 %collective-permute-start.2 = (bf16[4,3,8,24,128]{4,3,2,1,0:T(8,128)(2,1)S(1)}, bf16[4,3,8,24,128]{4,3,2,1,0:T(8,128)(2,1)S(1)}, u32[]{:S(2)}, u32[]{:S(2)}) collective-permute-start(bf16[4,3,8,24,128]{4,3,2,1,0:T(8,128)(2,1)S(1)} %copy-done.12), channel_id=1, source_target_pairs={{0,2},{1,3},{2,0},{3,1},{4,6},{5,7},{6,4},{7,5},{8,10},{9,11},{10,... | collective-permute-start | bytes 1769480 | tf_op jit(solution)/shard_map/ppermute | solution.py:27
  31.4 0.0 copy-done.7
  31.4 6.7 %collective-permute-done.3.refs_1_ = bf16[4,3,8,24,128]{4,3,2,1,0:T(8,128)(2,1)S(1)} collective-permute-done((bf16[4,3,8,24,128]{4,3,2,1,0:T(8,128)(2,1)}, bf16[4,3,8,24,128]{4,3,2,1,0:T(8,128)(2,1)S(1)}, u32[]{:S(2)}, u32[]{:S(2)}) %collective-permute-start.3) | collective-permute-done | bytes 589856 | tf_op jit(solution)/shard_map/ppermute | solution.py:27
  38.1 0.8 copy-done.8
  38.9 0.0 collective-permute-done.4.refs_3_
  38.9 1.0 pad_maximum_fusion
  39.9 0.9 pad_maximum_fusion.1
  40.8 0.0 copy-done.9
  40.8 0.9 pad_maximum_fusion.2
  41.7 0.0 collective-permute-done.refs_1_
  41.8 19.8 %collective-permute-done.5.refs_3_ = bf16[4,3,8,24,128]{4,3,2,1,0:T(8,128)(2,1)S(1)} collective-permute-done((bf16[4,3,8,24,128]{4,3,2,1,0:T(8,128)(2,1)}, bf16[4,3,8,24,128]{4,3,2,1,0:T(8,128)(2,1)S(1)}, u32[]{:S(2)}, u32[]{:S(2)}) %collective-permute-start.5) | collective-permute-done | bytes 589856 | tf_op jit(solution)/shard_map/ppermute | solution.py:27
  61.7 0.0 collective-permute-done.2.refs_2_
  61.7 0.0 copy-start.4
  61.7 0.0 copy-start.13
  61.8 0.1 pad_maximum_fusion.3
  61.8 0.0 copy-done.2
  61.9 0.1 collective-permute-start.6
  61.9 11.3 %collective-permute-start.12 = (bf16[4,3,8,24,128]{4,3,2,1,0:T(8,128)(2,1)}, bf16[4,3,8,24,128]{4,3,2,1,0:T(8,128)(2,1)}, u32[]{:S(2)}, u32[]{:S(2)}) collective-permute-start(bf16[4,3,8,24,128]{4,3,2,1,0:T(8,128)(2,1)} %pad_maximum_fusion.2), channel_id=1, source_target_pairs={{0,3},{1,0},{2,1},{3,2},{4,7},{5,4},{6,5},{7,6},{8,11},{9,8},{10,9... | collective-permute-start | bytes 1769480 | tf_op jit(solution)/shard_map/ppermute | solution.py:27
  73.2 0.8 collective-permute-start.11
  74.1 1.2 collective-permute-start.10
  75.3 0.9 pad_maximum_fusion.4
  76.2 0.0 copy-done.3
  76.2 0.0 copy-done.4
  76.2 3.2 %collective-permute-start.7 = (bf16[4,3,8,24,128]{4,3,2,1,0:T(8,128)(2,1)}, bf16[4,3,8,24,128]{4,3,2,1,0:T(8,128)(2,1)S(1)}, u32[]{:S(2)}, u32[]{:S(2)}) collective-permute-start(bf16[4,3,8,24,128]{4,3,2,1,0:T(8,128)(2,1)} %pad_maximum_fusion.4), channel_id=1, source_target_pairs={{0,8},{1,9},{2,10},{3,11},{4,12},{5,13},{6,14},{7,15},{8,0},{9,1},... | collective-permute-start | bytes 1769480 | tf_op jit(solution)/shard_map/ppermute | solution.py:27
  79.5 0.9 pad_maximum_fusion.5
  80.4 0.0 collective-permute-done.6.refs_4_
  80.4 0.3 collective-permute-start.8
  80.6 0.0 copy-done.13
  80.7 0.1 fusion.2
  80.8 0.0 copy-done
  80.8 0.2 fusion
  80.9 0.6 fusion.17
  81.5 6.8 %collective-permute-done.7.refs_5_ = bf16[4,3,8,24,128]{4,3,2,1,0:T(8,128)(2,1)S(1)} collective-permute-done((bf16[4,3,8,24,128]{4,3,2,1,0:T(8,128)(2,1)}, bf16[4,3,8,24,128]{4,3,2,1,0:T(8,128)(2,1)S(1)}, u32[]{:S(2)}, u32[]{:S(2)}) %collective-permute-start.7) | collective-permute-done | bytes 589856 | tf_op jit(solution)/shard_map/ppermute | solution.py:27
  88.3 15.6 %collective-permute-done.8.refs_6_ = bf16[4,3,8,24,128]{4,3,2,1,0:T(8,128)(2,1)} collective-permute-done((bf16[4,3,8,24,128]{4,3,2,1,0:T(8,128)(2,1)}, bf16[4,3,8,24,128]{4,3,2,1,0:T(8,128)(2,1)}, u32[]{:S(2)}, u32[]{:S(2)}) %collective-permute-start.8) | collective-permute-done | bytes 589856 | tf_op jit(solution)/shard_map/ppermute | solution.py:27
  103.9 0.0 copy-done.5
  103.9 15.9 %attend.2._ = bf16[16,8,24,128]{3,2,1,0:T(8,128)(2,1)} custom-call(s32[4]{0:T(128)} %pad_add_fusion.place, f32[8,128]{1,0:T(8,128)} %get-tuple-element.50.gate_ref, f32[2,4096]{1,0:T(2,128)} %_.1, bf16[4,3,8,24,128]{4,3,2,1,0:T(8,128)(2,1)} %get-tuple-element.15.refs_0_, bf16[4,3,8,24,128]{4,3,2,1,0:T(8,128)(2,1)} %copy-done.2, ...), custom_call_target="tpu_custom_call" | custom-call | flops 120795952 | bytes 3072 | tf_op jit(solution)/shard_map/attend/pallas_call | solution.py:185
  119.8 8.8 %all-to-all-start = ((bf16[16,8,24,128]{3,2,1,0:T(8,128)(2,1)}), bf16[16,8,24,128]{3,2,1,0:T(8,128)(2,1)S(1)}, u32[]{:S(2)}, u32[]{:S(2)}) async-start(bf16[16,8,24,128]{3,2,1,0:T(8,128)(2,1)} %attend.2._), calls=%async_computation | async-start | bytes 1572864 | tf_op jit(solution)/shard_map/all_to_all | solution.py:306
  128.6 0.0 collective-permute-done.12.refs_6_
  128.6 0.0 collective-permute-done.11.refs_5_
  128.6 0.0 collective-permute-done.10.refs_4_
  128.7 15.9 %attend.3 = bf16[16,8,24,128]{3,2,1,0:T(8,128)(2,1)} custom-call(s32[4]{0:T(128)} %pad_add_fusion.place, f32[8,128]{1,0:T(8,128)} %get-tuple-element.49.gate_ref, bf16[16,8,24,128]{3,2,1,0:T(8,128)(2,1)} %attend.2._, bf16[4,3,8,24,128]{4,3,2,1,0:T(8,128)(2,1)} %get-tuple-element.20.refs_0_, bf16[4,3,8,24,128]{4,3,2,1,0:T(8,128)(2,1)} %copy-done.8, ...), custom_call_target="tpu_custom_call" | custom-call | flops 33822867456 | bytes 3145728 | tf_op jit(solution)/shard_map/attend/pallas_call | solution.py:185
  144.6 3.0 %all-to-all-done.refs_0_ = bf16[16,8,24,128]{3,2,1,0:T(8,128)(2,1)S(1)} async-done(((bf16[16,8,24,128]{3,2,1,0:T(8,128)(2,1)}), bf16[16,8,24,128]{3,2,1,0:T(8,128)(2,1)S(1)}, u32[]{:S(2)}, u32[]{:S(2)}) %all-to-all-start) | async-done | bytes 786464 | tf_op jit(solution)/shard_map/all_to_all | solution.py:306
  147.6 7.0 %all-to-all-start.1 = ((bf16[16,8,24,128]{3,2,1,0:T(8,128)(2,1)}), bf16[16,8,24,128]{3,2,1,0:T(8,128)(2,1)}, u32[]{:S(2)}, u32[]{:S(2)}) async-start(bf16[16,8,24,128]{3,2,1,0:T(8,128)(2,1)} %attend.3), calls=%async_computation.1 | async-start | bytes 1572864 | tf_op jit(solution)/shard_map/all_to_all | solution.py:306
  154.6 3.9 %collective-permute-start.9 = (bf16[16,24,128]{2,1,0:T(8,128)(2,1)S(1)}, bf16[16,24,128]{2,1,0:T(8,128)(2,1)S(1)}, u32[]{:S(2)}, u32[]{:S(2)}) collective-permute-start(bf16[16,24,128]{2,1,0:T(8,128)(2,1)S(1)} %dynamic-slice_bitcast_fusion.1), channel_id=1, source_target_pairs={{0,16},{16,32},{32,48},{48,64},{64,80},{80,96},{96,112},{112,128},... | collective-permute-start | bytes 294920 | tf_op jit(solution)/shard_map/ppermute | solution.py:308
  158.5 15.0 %all-to-all-done.1.refs_1_ = bf16[16,8,24,128]{3,2,1,0:T(8,128)(2,1)} async-done(((bf16[16,8,24,128]{3,2,1,0:T(8,128)(2,1)}), bf16[16,8,24,128]{3,2,1,0:T(8,128)(2,1)}, u32[]{:S(2)}, u32[]{:S(2)}) %all-to-all-start.1) | async-done | bytes 786464 | tf_op jit(solution)/shard_map/all_to_all | solution.py:306
  173.5 0.9 dynamic-slice_bitcast_fusion
  174.4 11.1 %collective-permute-start.13 = (bf16[16,24,128]{2,1,0:T(8,128)(2,1)S(1)}, bf16[16,24,128]{2,1,0:T(8,128)(2,1)S(1)}, u32[]{:S(2)}, u32[]{:S(2)}) collective-permute-start(bf16[16,24,128]{2,1,0:T(8,128)(2,1)S(1)} %dynamic-slice_bitcast_fusion), channel_id=1, source_target_pairs={{0,16},{16,32},{32,48},{48,64},{64,80},{80,96},{96,112},{112,128},... | collective-permute-start | bytes 294920 | tf_op jit(solution)/shard_map/ppermute | solution.py:308
  185.5 3.7 %assemble.1.refs_3_ = bf16[8,24,4096]{2,1,0:T(8,128)(2,1)} custom-call(bf16[16,8,24,128]{3,2,1,0:T(8,128)(2,1)} %copy-done.1, bf16[16,8,24,128]{3,2,1,0:T(8,128)(2,1)} %all-to-all-done.1.refs_1_), custom_call_target="tpu_custom_call" | custom-call | bytes 3145728 | tf_op jit(solution)/shard_map/assemble/pallas_call | solution.py:232
  189.2 0.0 collective-permute-done.9.refs_0_
  189.2 0.0 collective-permute-done.13.refs_1_
  189.2 0.6 copy-done.10
  189.9 0.6 copy-done.11
  190.5 2.4 %hand_over.1 = bf16[8,24,4096]{2,1,0:T(8,128)(2,1)} custom-call(s32[4]{0:T(128)} %pad_add_fusion.place, bf16[16,24,128]{2,1,0:T(8,128)(2,1)} %copy-done.10, bf16[16,24,128]{2,1,0:T(8,128)(2,1)} %copy-done.11, bf16[24,4096]{1,0:T(8,128)(2,1)} %refs_2_.1, bf16[8,24,4096]{2,1,0:T(8,128)(2,1)} %assemble.1.refs_3_), custom_call_target="tpu_custom_call", output_to_operand_aliasing={{}: (4, {})} | custom-call | tf_op jit(solution)/shard_map/hand_over/pallas_call | solution.py:262
  (22 shorter events, 0.3 us)
Async XLA Ops:
  0.0 80.8 %copy-start = (bf16[256,4096]{1,0:T(8,128)(2,1)S(1)}, bf16[256,4096]{1,0:T(8,128)(2,1)}, u32[]{:S(2)}) copy-start(bf16[256,4096]{1,0:T(8,128)(2,1)} %param.13) | copy-start | bytes 6291460
  8.3 16.1 %copy-start.12 = (bf16[4,3,8,24,128]{4,3,2,1,0:T(8,128)(2,1)S(1)}, bf16[4,3,8,24,128]{4,3,2,1,0:T(8,128)(2,1)}, u32[]{:S(2)}) copy-start(bf16[4,3,8,24,128]{4,3,2,1,0:T(8,128)(2,1)} %get-tuple-element.19) | copy-start | bytes 1769476
  8.4 16.0 %collective-permute-start.1 = (bf16[4,3,8,24,128]{4,3,2,1,0:T(8,128)(2,1)}, bf16[4,3,8,24,128]{4,3,2,1,0:T(8,128)(2,1)S(1)}, u32[]{:S(2)}, u32[]{:S(2)}) collective-permute-start(bf16[4,3,8,24,128]{4,3,2,1,0:T(8,128)(2,1)} %get-tuple-element.18), channel_id=1, source_target_pairs={{0,8},{1,9},{2,10},{3,11},{4,12},{5,13},{6,14},{7,15},{8,0},{9,1},... | collective-permute-start | bytes 1769480 | tf_op jit(solution)/shard_map/ppermute | solution.py:27
  11.2 26.9 %collective-permute-start.3 = (bf16[4,3,8,24,128]{4,3,2,1,0:T(8,128)(2,1)}, bf16[4,3,8,24,128]{4,3,2,1,0:T(8,128)(2,1)S(1)}, u32[]{:S(2)}, u32[]{:S(2)}) collective-permute-start(bf16[4,3,8,24,128]{4,3,2,1,0:T(8,128)(2,1)} %get-tuple-element.21), channel_id=1, source_target_pairs={{0,4},{1,5},{2,6},{3,7},{4,8},{5,9},{6,10},{7,11},{8,12},{9,13},{1... | collective-permute-start | bytes 1769480 | tf_op jit(solution)/shard_map/ppermute | solution.py:27
  11.5 30.2 %collective-permute-start = (bf16[4,3,8,24,128]{4,3,2,1,0:T(8,128)(2,1)}, bf16[4,3,8,24,128]{4,3,2,1,0:T(8,128)(2,1)S(1)}, u32[]{:S(2)}, u32[]{:S(2)}) collective-permute-start(bf16[4,3,8,24,128]{4,3,2,1,0:T(8,128)(2,1)} %get-tuple-element.16), channel_id=1, source_target_pairs={{0,1},{1,2},{2,3},{3,0},{4,5},{5,6},{6,7},{7,4},{8,9},{9,10},{10,1... | collective-permute-start | bytes 1769480 | tf_op jit(solution)/shard_map/ppermute | solution.py:27
  14.5 24.4 %collective-permute-start.4 = (bf16[4,3,8,24,128]{4,3,2,1,0:T(8,128)(2,1)}, bf16[4,3,8,24,128]{4,3,2,1,0:T(8,128)(2,1)S(1)}, u32[]{:S(2)}, u32[]{:S(2)}) collective-permute-start(bf16[4,3,8,24,128]{4,3,2,1,0:T(8,128)(2,1)} %get-tuple-element.22), channel_id=1, source_target_pairs={{0,12},{1,13},{2,14},{3,15},{4,0},{5,1},{6,2},{7,3},{8,4},{9,5},{1... | collective-permute-start | bytes 1769480 | tf_op jit(solution)/shard_map/ppermute | solution.py:27
  16.8 44.8 %collective-permute-start.5 = (bf16[4,3,8,24,128]{4,3,2,1,0:T(8,128)(2,1)}, bf16[4,3,8,24,128]{4,3,2,1,0:T(8,128)(2,1)S(1)}, u32[]{:S(2)}, u32[]{:S(2)}) collective-permute-start(bf16[4,3,8,24,128]{4,3,2,1,0:T(8,128)(2,1)} %get-tuple-element.24), channel_id=1, source_target_pairs={{0,3},{1,0},{2,1},{3,2},{4,7},{5,4},{6,5},{7,6},{8,11},{9,8},{10,9... | collective-permute-start | bytes 1769480 | tf_op jit(solution)/shard_map/ppermute | solution.py:27
  24.4 7.0 %copy-start.7 = (bf16[4,3,8,24,128]{4,3,2,1,0:T(8,128)(2,1)}, bf16[4,3,8,24,128]{4,3,2,1,0:T(8,128)(2,1)S(1)}, u32[]{:S(2)}) copy-start(bf16[4,3,8,24,128]{4,3,2,1,0:T(8,128)(2,1)S(1)} %collective-permute-done.1.refs_2_) | copy-start | bytes 1769476
  24.4 37.3 %collective-permute-start.2 = (bf16[4,3,8,24,128]{4,3,2,1,0:T(8,128)(2,1)S(1)}, bf16[4,3,8,24,128]{4,3,2,1,0:T(8,128)(2,1)S(1)}, u32[]{:S(2)}, u32[]{:S(2)}) collective-permute-start(bf16[4,3,8,24,128]{4,3,2,1,0:T(8,128)(2,1)S(1)} %copy-done.12), channel_id=1, source_target_pairs={{0,2},{1,3},{2,0},{3,1},{4,6},{5,7},{6,4},{7,5},{8,10},{9,11},{10,... | collective-permute-start | bytes 1769480 | tf_op jit(solution)/shard_map/ppermute | solution.py:27
  38.0 0.8 copy-start.8
  38.9 1.9 %copy-start.9 = (bf16[4,3,8,24,128]{4,3,2,1,0:T(8,128)(2,1)}, bf16[4,3,8,24,128]{4,3,2,1,0:T(8,128)(2,1)S(1)}, u32[]{:S(2)}) copy-start(bf16[4,3,8,24,128]{4,3,2,1,0:T(8,128)(2,1)S(1)} %collective-permute-done.4.refs_3_) | copy-start | bytes 1769476
  41.7 20.1 %copy-start.2 = (bf16[4,3,8,24,128]{4,3,2,1,0:T(8,128)(2,1)}, bf16[4,3,8,24,128]{4,3,2,1,0:T(8,128)(2,1)S(1)}, u32[]{:S(2)}) copy-start(bf16[4,3,8,24,128]{4,3,2,1,0:T(8,128)(2,1)S(1)} %collective-permute-done.refs_1_) | copy-start | bytes 1769476
  61.6 14.6 %copy-start.3 = (bf16[4,3,8,24,128]{4,3,2,1,0:T(8,128)(2,1)}, bf16[4,3,8,24,128]{4,3,2,1,0:T(8,128)(2,1)S(1)}, u32[]{:S(2)}) copy-start(bf16[4,3,8,24,128]{4,3,2,1,0:T(8,128)(2,1)S(1)} %collective-permute-done.5.refs_3_) | copy-start | bytes 1769476
  61.7 14.5 %copy-start.4 = (bf16[4,3,8,24,128]{4,3,2,1,0:T(8,128)(2,1)}, bf16[4,3,8,24,128]{4,3,2,1,0:T(8,128)(2,1)S(1)}, u32[]{:S(2)}) copy-start(bf16[4,3,8,24,128]{4,3,2,1,0:T(8,128)(2,1)S(1)} %collective-permute-done.2.refs_2_) | copy-start | bytes 1769476
  61.7 18.9 %copy-start.13 = (s32[8]{0:T(128)S(1)}, s32[8]{0:T(128)}, u32[]{:S(2)}) copy-start(s32[8]{0:T(128)} %param.12) | copy-start | bytes 100
  61.9 18.5 %collective-permute-start.6 = (bf16[4,3,8,24,128]{4,3,2,1,0:T(8,128)(2,1)S(1)}, bf16[4,3,8,24,128]{4,3,2,1,0:T(8,128)(2,1)S(1)}, u32[]{:S(2)}, u32[]{:S(2)}) collective-permute-start(bf16[4,3,8,24,128]{4,3,2,1,0:T(8,128)(2,1)S(1)} %pad_maximum_fusion.3), channel_id=1, source_target_pairs={{0,4},{1,5},{2,6},{3,7},{4,8},{5,9},{6,10},{7,11},{8,12},{9,13},{1... | collective-permute-start | bytes 1769480 | tf_op jit(solution)/shard_map/ppermute | solution.py:27
  61.9 66.7 %collective-permute-start.12 = (bf16[4,3,8,24,128]{4,3,2,1,0:T(8,128)(2,1)}, bf16[4,3,8,24,128]{4,3,2,1,0:T(8,128)(2,1)}, u32[]{:S(2)}, u32[]{:S(2)}) collective-permute-start(bf16[4,3,8,24,128]{4,3,2,1,0:T(8,128)(2,1)} %pad_maximum_fusion.2), channel_id=1, source_target_pairs={{0,3},{1,0},{2,1},{3,2},{4,7},{5,4},{6,5},{7,6},{8,11},{9,8},{10,9... | collective-permute-start | bytes 1769480 | tf_op jit(solution)/shard_map/ppermute | solution.py:27
  73.2 55.4 %collective-permute-start.11 = (bf16[4,3,8,24,128]{4,3,2,1,0:T(8,128)(2,1)}, bf16[4,3,8,24,128]{4,3,2,1,0:T(8,128)(2,1)}, u32[]{:S(2)}, u32[]{:S(2)}) collective-permute-start(bf16[4,3,8,24,128]{4,3,2,1,0:T(8,128)(2,1)} %pad_maximum_fusion.1), channel_id=1, source_target_pairs={{0,2},{1,3},{2,0},{3,1},{4,6},{5,7},{6,4},{7,5},{8,10},{9,11},{10,... | collective-permute-start | bytes 1769480 | tf_op jit(solution)/shard_map/ppermute | solution.py:27
  74.1 54.6 %collective-permute-start.10 = (bf16[4,3,8,24,128]{4,3,2,1,0:T(8,128)(2,1)}, bf16[4,3,8,24,128]{4,3,2,1,0:T(8,128)(2,1)}, u32[]{:S(2)}, u32[]{:S(2)}) collective-permute-start(bf16[4,3,8,24,128]{4,3,2,1,0:T(8,128)(2,1)} %pad_maximum_fusion), channel_id=1, source_target_pairs={{0,1},{1,2},{2,3},{3,0},{4,5},{5,6},{6,7},{7,4},{8,9},{9,10},{10,1... | collective-permute-start | bytes 1769480 | tf_op jit(solution)/shard_map/ppermute | solution.py:27
  76.2 12.1 %collective-permute-start.7 = (bf16[4,3,8,24,128]{4,3,2,1,0:T(8,128)(2,1)}, bf16[4,3,8,24,128]{4,3,2,1,0:T(8,128)(2,1)S(1)}, u32[]{:S(2)}, u32[]{:S(2)}) collective-permute-start(bf16[4,3,8,24,128]{4,3,2,1,0:T(8,128)(2,1)} %pad_maximum_fusion.4), channel_id=1, source_target_pairs={{0,8},{1,9},{2,10},{3,11},{4,12},{5,13},{6,14},{7,15},{8,0},{9,1},... | collective-permute-start | bytes 1769480 | tf_op jit(solution)/shard_map/ppermute | solution.py:27
  80.4 23.6 %copy-start.5 = (bf16[4,3,8,24,128]{4,3,2,1,0:T(8,128)(2,1)}, bf16[4,3,8,24,128]{4,3,2,1,0:T(8,128)(2,1)S(1)}, u32[]{:S(2)}) copy-start(bf16[4,3,8,24,128]{4,3,2,1,0:T(8,128)(2,1)S(1)} %collective-permute-done.6.refs_4_) | copy-start | bytes 1769476
  80.4 23.6 %collective-permute-start.8 = (bf16[4,3,8,24,128]{4,3,2,1,0:T(8,128)(2,1)}, bf16[4,3,8,24,128]{4,3,2,1,0:T(8,128)(2,1)}, u32[]{:S(2)}, u32[]{:S(2)}) collective-permute-start(bf16[4,3,8,24,128]{4,3,2,1,0:T(8,128)(2,1)} %pad_maximum_fusion.5), channel_id=1, source_target_pairs={{0,12},{1,13},{2,14},{3,15},{4,0},{5,1},{6,2},{7,3},{8,4},{9,5},{1... | collective-permute-start | bytes 1769480 | tf_op jit(solution)/shard_map/ppermute | solution.py:27
  88.3 15.6 %copy-start.6 = (bf16[4,3,8,24,128]{4,3,2,1,0:T(8,128)(2,1)}, bf16[4,3,8,24,128]{4,3,2,1,0:T(8,128)(2,1)S(1)}, u32[]{:S(2)}) copy-start(bf16[4,3,8,24,128]{4,3,2,1,0:T(8,128)(2,1)S(1)} %collective-permute-done.7.refs_5_) | copy-start | bytes 1769476
  119.8 27.8 %all-to-all-start = ((bf16[16,8,24,128]{3,2,1,0:T(8,128)(2,1)}), bf16[16,8,24,128]{3,2,1,0:T(8,128)(2,1)S(1)}, u32[]{:S(2)}, u32[]{:S(2)}) async-start(bf16[16,8,24,128]{3,2,1,0:T(8,128)(2,1)} %attend.2._), calls=%async_computation | async-start | bytes 1572864 | tf_op jit(solution)/shard_map/all_to_all | solution.py:306
  147.6 37.9 %copy-start.1 = (bf16[16,8,24,128]{3,2,1,0:T(8,128)(2,1)}, bf16[16,8,24,128]{3,2,1,0:T(8,128)(2,1)S(1)}, u32[]{:S(2)}) copy-start(bf16[16,8,24,128]{3,2,1,0:T(8,128)(2,1)S(1)} %all-to-all-done.refs_0_) | copy-start | bytes 2359300
  147.6 25.9 %all-to-all-start.1 = ((bf16[16,8,24,128]{3,2,1,0:T(8,128)(2,1)}), bf16[16,8,24,128]{3,2,1,0:T(8,128)(2,1)}, u32[]{:S(2)}, u32[]{:S(2)}) async-start(bf16[16,8,24,128]{3,2,1,0:T(8,128)(2,1)} %attend.3), calls=%async_computation.1 | async-start | bytes 1572864 | tf_op jit(solution)/shard_map/all_to_all | solution.py:306
  154.6 34.6 %collective-permute-start.9 = (bf16[16,24,128]{2,1,0:T(8,128)(2,1)S(1)}, bf16[16,24,128]{2,1,0:T(8,128)(2,1)S(1)}, u32[]{:S(2)}, u32[]{:S(2)}) collective-permute-start(bf16[16,24,128]{2,1,0:T(8,128)(2,1)S(1)} %dynamic-slice_bitcast_fusion.1), channel_id=1, source_target_pairs={{0,16},{16,32},{32,48},{48,64},{64,80},{80,96},{96,112},{112,128},... | collective-permute-start | bytes 294920 | tf_op jit(solution)/shard_map/ppermute | solution.py:308
  174.4 14.9 %collective-permute-start.13 = (bf16[16,24,128]{2,1,0:T(8,128)(2,1)S(1)}, bf16[16,24,128]{2,1,0:T(8,128)(2,1)S(1)}, u32[]{:S(2)}, u32[]{:S(2)}) collective-permute-start(bf16[16,24,128]{2,1,0:T(8,128)(2,1)S(1)} %dynamic-slice_bitcast_fusion), channel_id=1, source_target_pairs={{0,16},{16,32},{32,48},{48,64},{64,80},{80,96},{96,112},{112,128},... | collective-permute-start | bytes 294920 | tf_op jit(solution)/shard_map/ppermute | solution.py:308
  189.2 0.6 copy-start.10
  189.9 0.6 copy-start.11

commit v5 on v3

--- a/solution.py
+++ b/solution.py
@@ -11,8 +11,8 @@
 HD = 128
 SIDE = 4
 LOG2E = 1.4426950408889634
-AXES = ("z", "x")
 MIB = 1024 * 1024
+ATTEND_MIB = 30
 
 
 def moved(value, axis, steps):
@@ -27,8 +27,12 @@
     return lax.ppermute(value, "seq", pairs)
 
 
-def exchange(pieces):
-    return lax.all_to_all(pieces, "seq", split_axis=0, concat_axis=0, tiled=True)
+def exchange(pieces, **groups):
+    return lax.all_to_all(pieces, "seq", split_axis=0, concat_axis=0, tiled=True, **groups)
+
+
+def first_stage(pieces, axis):
+    return [pieces[0]] + [moved(pieces[i], axis, i) for i in range(1, SIDE)]
 
 
 def stacked(held):
@@ -61,20 +65,19 @@
         return lax.rsqrt(mean + 1e-06)
 
     q_factor, k_factor = factor_of(q_ref), factor_of(k_ref)
-
-    def place_into(out, index, at):
-        for kind, (ref, factor) in enumerate(((q_ref, q_factor), (k_ref, k_factor))):
-            gain = gain_ref[kind : kind + 1, pl.ds(at, HD)]
-            part = ref[:, :, pl.ds(at, HD)].astype(jnp.float32) * factor * gain[None]
-            out[index, kind] = part.astype(jnp.bfloat16)
-        out[index, 2] = v_ref[:, :, pl.ds(at, HD)]
-
-    *first, second = outs
-    for i in range(SIDE):
-        for j in range(SIDE):
-            place_into(first[i], j, pl.multiple_of(index_of(place, AXES, i, j) * (2 * HD), HD))
-    for group in range(SIDE * SIDE):
-        place_into(second, group, group * 2 * HD + HD)
+    for head in range(2):
+        for i in range(SIDE):
+            for j in range(SIDE):
+                group = index_of(place, ("z", "x"), i, j)
+                if head:
+                    group = lax.rem(place[0] + i, SIDE) * SIDE + j
+                at = pl.multiple_of((group * 2 + head) * HD, HD)
+                out = outs[head * SIDE + i]
+                for kind, (ref, factor) in enumerate(((q_ref, q_factor), (k_ref, k_factor))):
+                    gain = gain_ref[kind : kind + 1, pl.ds(at, HD)]
+                    part = ref[:, :, pl.ds(at, HD)].astype(jnp.float32) * factor * gain[None]
+                    out[j, kind] = part.astype(jnp.bfloat16)
+                out[j, 2] = v_ref[:, :, pl.ds(at, HD)]
 
 
 def prepare(place, query, key, value, qk_gain):
@@ -89,11 +92,9 @@
             num_scalar_prefetch=1,
             grid=(frames // step,),
             in_specs=[tall, tall, tall, pl.BlockSpec((2, inner), lambda n, _: (0, 0))],
-            out_specs=[out] * SIDE
-            + [pl.BlockSpec((SIDE * SIDE, 3, step, rows, HD), lambda n, _: (0, 0, n, 0, 0))],
-        ),
-        out_shape=[shape] * SIDE
-        + [jax.ShapeDtypeStruct((SIDE * SIDE, 3, frames, rows, HD), jnp.bfloat16)],
+            out_specs=[out] * (2 * SIDE),
+        ),
+        out_shape=[shape] * (2 * SIDE),
         compiler_params=pltpu.CompilerParams(vmem_limit_bytes=60 * MIB),
         cost_estimate=pl.CostEstimate(
             flops=10 * query.size, bytes_accessed=12 * query.size, transcendentals=0
@@ -105,7 +106,7 @@
 def attend_kernel(count, place, gate_ref, _, *refs):
     sent = refs[:count]
     out, q_all, k_all, v_all, s_even, s_odd, m_even, m_odd, gates, result = refs[count:]
-    frames, rows = sent[0].shape[2:4]
+    frames, rows = sent[0].shape[-3:-1]
     tokens = frames * rows
     length = SIDE * SIDE * tokens
     block, chunk = 256, 512
@@ -113,16 +114,16 @@
     scale = LOG2E / math.sqrt(HD)
 
     def part_of(n):
+        i, j = divmod(n, SIDE)
         if count == 1:
-            return sent[0], n, n
-        i, j = divmod(n, SIDE)
-        source = index_of(place, AXES, SIDE - i, SIDE - j)
-        return (sent[i], 0, source) if j == 0 else (sent[SIDE + j - 1], i, source)
+            return sent[0], (i, j), lax.rem(place[0] + SIDE - j, SIDE) * SIDE + i
+        source = index_of(place, ("z", "x"), SIDE - i, SIDE - j)
+        return (sent[i], (0,), source) if j == 0 else (sent[SIDE + j - 1], (i,), source)
 
     for n in range(SIDE * SIDE):
         ref, index, _ = part_of(n)
         for kind, whole in enumerate((q_all, k_all, v_all)):
-            whole[n * tokens : (n + 1) * tokens, :HD] = ref[index, kind].reshape(tokens, HD)
+            whole[n * tokens : (n + 1) * tokens, :HD] = ref[(*index, kind)].reshape(tokens, HD)
     v_all[:, HD:] = jnp.ones((length, HD), jnp.bfloat16)
     for at in range(SIDE * frames):
         gates[at * rows : (at + 1) * rows, :] = jnp.broadcast_to(
@@ -185,12 +186,12 @@
 
 
 def attend(place, gate, before, *sent):
-    frames, rows = sent[0].shape[2:4]
+    frames, rows = sent[0].shape[-3:-1]
     length = SIDE * SIDE * frames * rows
     block = 256
     one = pl.BlockSpec((1, 3, frames, rows, HD), lambda n, _: (0, 0, 0, 0, 0))
     whole = pl.BlockSpec((SIDE, 3, frames, rows, HD), lambda n, _: (0, 0, 0, 0, 0))
-    every = pl.BlockSpec((SIDE * SIDE, 3, frames, rows, HD), lambda n, _: (0, 0, 0, 0, 0))
+    every = pl.BlockSpec((SIDE, SIDE, 3, frames, rows, HD), lambda n, _: (0, 0, 0, 0, 0, 0))
     return pl.pallas_call(
         functools.partial(attend_kernel, len(sent)),
         grid_spec=pltpu.PrefetchScalarGridSpec(
@@ -212,9 +213,9 @@
             ],
         ),
         out_shape=jax.ShapeDtypeStruct((SIDE * SIDE, frames, rows, HD), jnp.bfloat16),
-        compiler_params=pltpu.CompilerParams(vmem_limit_bytes=60 * MIB),
+        compiler_params=pltpu.CompilerParams(vmem_limit_bytes=ATTEND_MIB * MIB),
         cost_estimate=pl.CostEstimate(
-            flops=28 * length * length * HD, bytes_accessed=8 * length * HD, transcendentals=length * length
+            flops=int(17 * length * length * HD) if len(sent) > 1 else 28 * length * length * HD, bytes_accessed=length if len(sent) > 1 else 8 * length * HD, transcendentals=0
         ),
         name="attend",
     )(place, gate, before, *sent)
@@ -249,22 +250,22 @@
     )(*parts)
 
 
-def hand_kernel(place, *refs):
+def hand_kernel(ends, *refs):
     *behind, fresh, _, out = refs
 
-    @pl.when(place[3] != 0)
+    @pl.when(ends[1] != 0)
     def _():
         for head, part in enumerate(behind):
             for group in range(part.shape[0]):
                 at = (group * len(behind) + head) * HD
                 out[0, :, at : at + HD] = part[group]
 
-    @pl.when(place[3] == 0)
+    @pl.when(ends[1] == 0)
     def _():
         out[0] = fresh[...]
 
 
-def hand_over(place, behind, fresh, gated):
+def hand_over(ends, behind, fresh, gated):
     rows, inner = fresh.shape
     part = pl.BlockSpec(behind[0].shape, lambda n, _: (0, 0, 0))
     return pl.pallas_call(
@@ -274,13 +275,13 @@
             grid=(1,),
             in_specs=[part] * len(behind)
             + [pl.BlockSpec((rows, inner), lambda n, _: (0, 0)), pl.BlockSpec(memory_space=pl.ANY)],
-            out_specs=pl.BlockSpec((1, rows, inner), lambda n, place: (place[2], 0, 0)),
+            out_specs=pl.BlockSpec((1, rows, inner), lambda n, ends: (ends[0], 0, 0)),
         ),
         out_shape=jax.ShapeDtypeStruct(gated.shape, gated.dtype),
         input_output_aliases={len(behind) + 2: 0},
         compiler_params=pltpu.CompilerParams(vmem_limit_bytes=60 * MIB),
         name="hand_over",
-    )(place, *behind, fresh, gated)
+    )(ends, *behind, fresh, gated)
 
 
 def level_gate(steps, gate_weight):
@@ -294,24 +295,28 @@
 def shards(query, key, value, qk_gain, timesteps, gate_weight, slot, fresh):
     index = lax.axis_index("seq")
     section = lax.axis_index("section")
-    place = jnp.stack([index // SIDE, index % SIDE, slot[0], section]).astype(jnp.int32)
+    place = jnp.stack([index // SIDE, index % SIDE]).astype(jnp.int32)
+    ends = jnp.stack([slot[0], section]).astype(jnp.int32)
     columns = lax.dynamic_slice_in_dim(gate_weight, index * (2 * HD), 2 * HD, 1)
     gate = level_gate(timesteps, columns)
     prepared = prepare(place, query, key, value, qk_gain)
-    *ahead, direct = prepared
-    held = [ahead[0], moved(ahead[1], AXES[0], 1), None, moved(ahead[3], AXES[0], 3)]
-    held[2] = moved(ahead[2], AXES[0], 2)
-    sent = [*held, *second_stage(stacked(held), AXES[1])]
-    direct = [exchange(after(direct, held[1], held[3]))]
+    ahead, back = list(prepared[:SIDE]), list(prepared[SIDE:])
+    back = first_stage(back, "x")
+    ahead[2] = after(ahead[2], back[2])
+    ahead = first_stage(ahead, "z")
+    columns_of_z = [[x * SIDE + z for z in range(SIDE)] for x in range(SIDE)]
+    back[3] = after(back[3], ahead[1], ahead[3])
+    direct = exchange(jnp.stack(back, axis=1), axis_index_groups=columns_of_z)
+    sent = [*ahead, *second_stage(stacked(ahead), "x")]
     sections = lax.axis_size("section")
     parts, behind, before = [], [], qk_gain
-    for head, operands in enumerate((sent, direct)):
+    for head, operands in enumerate((sent, [direct])):
         before = attend(place, gate[:, head * HD : (head + 1) * HD], before, *operands)
         returned = exchange(before)
         leaving = leaving_frame(slot, returned)
         behind.append(lax.ppermute(leaving, "section", [(n, n + 1) for n in range(sections - 1)]))
         parts.append(returned)
-    return hand_over(place, behind, fresh, assemble(parts))
+    return hand_over(ends, behind, fresh, assemble(parts))
 
 
 def solution(mesh):

time: 205 us -> 192 us (0.937)
  waiting for transfers between devices: 93.1 us -> 69.2 us
  starting transfers between devices: 55.7 us -> 63.4 us
  other arithmetic: 2.65 us -> 7.21 us
    ppermute x6 -> x9, waiting for transfers between devices: 80.7 us -> 46.4 us  [moved(): return lax.ppermute(value, 'seq', pairs)]
    all_to_all x3, starting transfers between devices: 19.4 us -> 31.7 us  [exchange(): lax.all_to_all(pieces, 'seq', split_axis=0, concat_axis=0, tiled=True, **...]
    all_to_all x3, waiting for transfers between devices: 12.3 us -> 22.8 us  [exchange(): lax.all_to_all(pieces, 'seq', split_axis=0, concat_axis=0, tiled=True, **...]
    ppermute x2, starting transfers between devices: 22 us -> 11.8 us  [shards(): lax.ppermute(leaving, 'section', [(n, n + 1) for n in range(sections - 1)])]
    ppermute x6 -> x9, starting transfers between devices: 14.2 us -> 19.9 us  [moved(): return lax.ppermute(value, 'seq', pairs)]
    another operation x2 -> x4, other arithmetic: 0.78 us -> 4.37 us  [the longest x1 3.01 us: shards(): direct = exchange(jnp.stack(back, axis=1), axis_index_groups=columns_of_z)]
  transfers between devices with their start and end apart: 11 -> 14, of which waited for: 6 -> 8; matrix products, arithmetic and copies ran while one was open for 3% -> 6% of each run, Pallas kernels for 17% -> 18%
where the time goes in v5:
time: 192 us
  waiting for transfers between devices  69.2 us (36%)
  starting transfers between devices  63.4 us (33%)
  Pallas kernels  44.4 us (23%)
  other arithmetic  7.21 us (4%)
  local copies, waits for them, and re-layouts  6.36 us (3%)
    ppermute x9, waiting for transfers between devices, moved(): return lax.ppermute(value, 'seq', pairs)  46.4 us
    all_to_all x3, starting transfers between devices, exchange(): lax.all_to_all(pieces, 'seq', split_axis=0, concat_axis=0, tiled=True, **...  31.7 us
    pallas_call x2, Pallas kernels, attend(): pl.pallas_call(functools.partial(attend_kernel, len(sent)), grid_spec=plt...  31.3 us
    all_to_all x3, waiting for transfers between devices, exchange(): lax.all_to_all(pieces, 'seq', split_axis=0, concat_axis=0, tiled=True, **...  22.8 us
    ppermute x9, starting transfers between devices, moved(): return lax.ppermute(value, 'seq', pairs)  19.9 us
    ppermute x2, starting transfers between devices, shards(): lax.ppermute(leaving, 'section', [(n, n + 1) for n in range(sections - 1)])  11.8 us
    pallas_call x1, Pallas kernels, prepare(): pl.pallas_call(prepare_kernel, grid_spec=pltpu.PrefetchScalarGridSpec(num...  6.97 us
  transfers between devices with their start and end apart: 14, of which 8 were waited for; matrix products, arithmetic and copies ran while one was open for 6% of the time, Pallas kernels for 18%

profile of v5, /device:TPU:17, one launch (start us, length us, event | category | flops | bytes accessed | tf_op | source)
XLA Modules:
  0.0 191.5 jit_solution(6727490232673454090)
XLA Ops:
  0.0 0.0 copy-start
  0.0 0.6 pad_add_fusion.1.place
  0.6 7.0 %prepare.1 = (bf16[4,3,8,24,128]{4,3,2,1,0:T(8,128)(2,1)}, bf16[4,3,8,24,128]{4,3,2,1,0:T(8,128)(2,1)}, bf16[4,3,8,24,128]{4,3,2,1,0:T(8,128)(2,1)}, bf16[4,3,8,...) custom-call(s32[2]{0:T(128)} %pad_add_fusion.1.place, ...), custom_call_target="tpu_custom_call" | custom-call | flops 7864320 | bytes 9437184 | tf_op jit(solution)/shard_map/prepare/pallas_call | solution.py:89
  7.6 2.8 %collective-permute-start.1 = (bf16[4,3,8,24,128]{4,3,2,1,0:T(8,128)(2,1)}, bf16[4,3,8,24,128]{4,3,2,1,0:T(8,128)(2,1)S(1)}, u32[]{:S(2)}, u32[]{:S(2)}) collective-permute-start(bf16[4,3,8,24,128]{4,3,2,1,0:T(8,128)(2,1)} %get-tuple-element.18), channel_id=1, source_target_pairs={{0,8},{1,9},{2,10},{3,11},{4,12},{5,13},{6,14},{7,15},{8,0},{9,1},... | collective-permute-start | bytes 1769480 | tf_op jit(solution)/shard_map/ppermute | solution.py:27
  10.4 3.0 %collective-permute-start = (bf16[4,3,8,24,128]{4,3,2,1,0:T(8,128)(2,1)}, bf16[4,3,8,24,128]{4,3,2,1,0:T(8,128)(2,1)S(1)}, u32[]{:S(2)}, u32[]{:S(2)}) collective-permute-start(bf16[4,3,8,24,128]{4,3,2,1,0:T(8,128)(2,1)} %get-tuple-element.16), channel_id=1, source_target_pairs={{0,1},{1,2},{2,3},{3,0},{4,5},{5,6},{6,7},{7,4},{8,9},{9,10},{10,1... | collective-permute-start | bytes 1769480 | tf_op jit(solution)/shard_map/ppermute | solution.py:27
  13.4 3.0 %collective-permute-start.3 = (bf16[4,3,8,24,128]{4,3,2,1,0:T(8,128)(2,1)}, bf16[4,3,8,24,128]{4,3,2,1,0:T(8,128)(2,1)S(1)}, u32[]{:S(2)}, u32[]{:S(2)}) collective-permute-start(bf16[4,3,8,24,128]{4,3,2,1,0:T(8,128)(2,1)} %get-tuple-element.20), channel_id=1, source_target_pairs={{0,3},{1,0},{2,1},{3,2},{4,7},{5,4},{6,5},{7,6},{8,11},{9,8},{10,9... | collective-permute-start | bytes 1769480 | tf_op jit(solution)/shard_map/ppermute | solution.py:27
  16.5 0.9 collective-permute-start.9
  17.3 0.6 collective-permute-start.8
  17.9 1.8 fusion.9
  19.8 3.9 %collective-permute-done.1 = bf16[4,3,8,24,128]{4,3,2,1,0:T(8,128)(2,1)S(1)} collective-permute-done((bf16[4,3,8,24,128]{4,3,2,1,0:T(8,128)(2,1)}, bf16[4,3,8,24,128]{4,3,2,1,0:T(8,128)(2,1)S(1)}, u32[]{:S(2)}, u32[]{:S(2)}) %collective-permute-start.1) | collective-permute-done | bytes 589856 | tf_op jit(solution)/shard_map/ppermute | solution.py:27
  23.6 6.9 %collective-permute-start.2 = (bf16[4,3,8,24,128]{4,3,2,1,0:T(8,128)(2,1)}, bf16[4,3,8,24,128]{4,3,2,1,0:T(8,128)(2,1)}, u32[]{:S(2)}, u32[]{:S(2)}) collective-permute-start(bf16[4,3,8,24,128]{4,3,2,1,0:T(8,128)(2,1)} %get-tuple-element.19), channel_id=1, source_target_pairs={{0,2},{1,3},{2,0},{3,1},{4,6},{5,7},{6,4},{7,5},{8,10},{9,11},{10,... | collective-permute-start | bytes 1769480 | tf_op jit(solution)/shard_map/ppermute | solution.py:27
  30.5 3.3 %collective-permute-done.refs_1_ = bf16[4,3,8,24,128]{4,3,2,1,0:T(8,128)(2,1)S(1)} collective-permute-done((bf16[4,3,8,24,128]{4,3,2,1,0:T(8,128)(2,1)}, bf16[4,3,8,24,128]{4,3,2,1,0:T(8,128)(2,1)S(1)}, u32[]{:S(2)}, u32[]{:S(2)}) %collective-permute-start) | collective-permute-done | bytes 589856 | tf_op jit(solution)/shard_map/ppermute | solution.py:27
  33.9 23.9 %collective-permute-done.3.refs_3_ = bf16[4,3,8,24,128]{4,3,2,1,0:T(8,128)(2,1)S(1)} collective-permute-done((bf16[4,3,8,24,128]{4,3,2,1,0:T(8,128)(2,1)}, bf16[4,3,8,24,128]{4,3,2,1,0:T(8,128)(2,1)S(1)}, u32[]{:S(2)}, u32[]{:S(2)}) %collective-permute-start.3) | collective-permute-done | bytes 589856 | tf_op jit(solution)/shard_map/ppermute | solution.py:27
  57.8 0.0 copy-start.2
  57.8 0.0 collective-permute-done.9
  57.8 0.0 collective-permute-done.8
  57.8 3.0 %pad_maximum_fusion = bf16[4,4,3,8,24,128]{5,4,3,2,1,0:T(8,128)(2,1)} fusion(bf16[4,1,3,8,24,128]{5,4,3,2,1,0:T(8,128)(2,1)S(1)} %bitcast.17, bf16[4,1,3,8,24,128]{5,4,3,2,1,0:T(8,128)(2,1)S(1)} %bitcast.16, bf16[4,1,3,8,24,128]{5,4,3,2,1,0:T(8,128)(2,1)S(1)} %bitcast.18, bf16[4,1,3,8,24,128]{5,4,3,2,1,0:T(8,128)(2,1)} %bitcast.15), kind=kLoop, calls=%fused_computation | loop fusion | flops 3538944 | bytes 4718592 | tf_op jit(solution)/shard_map/stack | solution.py:309
  60.8 4.6 %all-to-all-start.1 = ((bf16[4,4,3,8,24,128]{5,4,3,2,1,0:T(8,128)(2,1)}), bf16[4,4,3,8,24,128]{5,4,3,2,1,0:T(8,128)(2,1)}, u32[]{:S(2)}, u32[]{:S(2)}) async-start(bf16[4,4,3,8,24,128]{5,4,3,2,1,0:T(8,128)(2,1)} %pad_maximum_fusion), calls=%async_computation.1 | async-start | bytes 4718592 | tf_op jit(solution)/shard_map/all_to_all | solution.py:31
  65.4 0.0 copy-start.8
  65.5 0.0 copy-done.2
  65.5 0.0 copy-start.11
  65.6 0.0 copy-start.1
  65.6 0.0 copy-start.4
  65.6 0.0 copy-start.5
  65.6 0.0 collective-permute-done.2.refs_2_
  65.6 1.2 fusion.11
  66.8 0.0 copy-done.8
  66.8 1.0 pad_maximum_fusion.1
  67.7 0.3 collective-permute-start.4
  68.0 0.0 copy-done.7
  68.0 1.0 pad_maximum_fusion.2
  69.0 1.8 collective-permute-start.5
  70.8 0.9 pad_maximum_fusion.3
  71.7 0.6 collective-permute-start.6
  72.3 0.0 copy-done.11
  72.3 0.1 fusion.2
  72.4 0.0 copy-done
  72.5 0.2 fusion
  72.6 8.4 %collective-permute-done.4.refs_4_ = bf16[4,3,8,24,128]{4,3,2,1,0:T(8,128)(2,1)} collective-permute-done((bf16[4,3,8,24,128]{4,3,2,1,0:T(8,128)(2,1)}, bf16[4,3,8,24,128]{4,3,2,1,0:T(8,128)(2,1)}, u32[]{:S(2)}, u32[]{:S(2)}) %collective-permute-start.4) | collective-permute-done | bytes 589856 | tf_op jit(solution)/shard_map/ppermute | solution.py:27
  81.1 6.8 %collective-permute-done.5.refs_5_ = bf16[4,3,8,24,128]{4,3,2,1,0:T(8,128)(2,1)} collective-permute-done((bf16[4,3,8,24,128]{4,3,2,1,0:T(8,128)(2,1)}, bf16[4,3,8,24,128]{4,3,2,1,0:T(8,128)(2,1)}, u32[]{:S(2)}, u32[]{:S(2)}) %collective-permute-start.5) | collective-permute-done | bytes 589856 | tf_op jit(solution)/shard_map/ppermute | solution.py:27
  87.9 0.0 collective-permute-done.6.refs_6_
  87.9 0.0 copy-done.1
  87.9 0.0 copy-done.4
  87.9 0.0 copy-done.5
  87.9 0.0 copy-start.3
  87.9 1.1 copy-done.3
  88.9 15.6 %attend.2._ = bf16[16,8,24,128]{3,2,1,0:T(8,128)(2,1)} custom-call(s32[2]{0:T(128)S(1)} %copy-done.5, f32[8,128]{1,0:T(8,128)S(1)} %get-tuple-element.38.gate_ref, f32[2,4096]{1,0:T(2,128)S(1)} %copy-done.4, bf16[4,3,8,24,128]{4,3,2,1,0:T(8,128)(2,1)S(1)} %copy-done.1, bf16[4,3,8,24,128]{4,3,2,1,0:T(8,128)(2,1)S(1)} %collective-permute-done.refs_1_, ...), custom_call_target="tpu_custom_call" | custom-call | flops 20535312384 | bytes 3072 | tf_op jit(solution)/shard_map/attend/pallas_call | solution.py:195
  104.5 6.3 %all-to-all-done.1.refs_0_ = bf16[4,4,3,8,24,128]{5,4,3,2,1,0:T(8,128)(2,1)} async-done(((bf16[4,4,3,8,24,128]{5,4,3,2,1,0:T(8,128)(2,1)}), bf16[4,4,3,8,24,128]{5,4,3,2,1,0:T(8,128)(2,1)}, u32[]{:S(2)}, u32[]{:S(2)}) %all-to-all-start.1) | async-done | bytes 2359328 | tf_op jit(solution)/shard_map/all_to_all | solution.py:31
  110.8 22.1 %all-to-all-start = ((bf16[16,8,24,128]{3,2,1,0:T(8,128)(2,1)}), bf16[16,8,24,128]{3,2,1,0:T(8,128)(2,1)}, u32[]{:S(2)}, u32[]{:S(2)}) async-start(bf16[16,8,24,128]{3,2,1,0:T(8,128)(2,1)} %attend.2._), calls=%async_computation | async-start | bytes 1572864 | tf_op jit(solution)/shard_map/all_to_all | solution.py:31
  132.9 15.7 %attend.3 = bf16[16,8,24,128]{3,2,1,0:T(8,128)(2,1)} custom-call(s32[2]{0:T(128)S(1)} %copy-done.5, f32[8,128]{1,0:T(8,128)S(1)} %get-tuple-element.37.gate_ref, bf16[16,8,24,128]{3,2,1,0:T(8,128)(2,1)} %attend.2._, bf16[4,4,3,8,24,128]{5,4,3,2,1,0:T(8,128)(2,1)} %all-to-all-done.1.refs_0_), custom_call_target="tpu_custom_call" | custom-call | flops 33822867456 | bytes 3145728 | tf_op jit(solution)/shard_map/attend/pallas_call | solution.py:195
  148.7 4.1 %all-to-all-done.refs_0_ = bf16[16,8,24,128]{3,2,1,0:T(8,128)(2,1)} async-done(((bf16[16,8,24,128]{3,2,1,0:T(8,128)(2,1)}), bf16[16,8,24,128]{3,2,1,0:T(8,128)(2,1)}, u32[]{:S(2)}, u32[]{:S(2)}) %all-to-all-start) | async-done | bytes 786464 | tf_op jit(solution)/shard_map/all_to_all | solution.py:31
  152.8 5.0 %all-to-all-start.2 = ((bf16[16,8,24,128]{3,2,1,0:T(8,128)(2,1)}), bf16[16,8,24,128]{3,2,1,0:T(8,128)(2,1)S(1)}, u32[]{:S(2)}, u32[]{:S(2)}) async-start(bf16[16,8,24,128]{3,2,1,0:T(8,128)(2,1)} %attend.3), calls=%async_computation.2 | async-start | bytes 1572864 | tf_op jit(solution)/shard_map/all_to_all | solution.py:31
  158.4 0.9 dynamic-slice_bitcast_fusion.1
  159.3 5.3 %collective-permute-start.7 = (bf16[16,24,128]{2,1,0:T(8,128)(2,1)S(1)}, bf16[16,24,128]{2,1,0:T(8,128)(2,1)S(1)}, u32[]{:S(2)}, u32[]{:S(2)}) collective-permute-start(bf16[16,24,128]{2,1,0:T(8,128)(2,1)S(1)} %dynamic-slice_bitcast_fusion.1), channel_id=1, source_target_pairs={{0,16},{16,32},{32,48},{48,64},{64,80},{80,96},{96,112},{112,128},... | collective-permute-start | bytes 294920 | tf_op jit(solution)/shard_map/ppermute | solution.py:317
  164.6 12.4 %all-to-all-done.2.refs_1_ = bf16[16,8,24,128]{3,2,1,0:T(8,128)(2,1)S(1)} async-done(((bf16[16,8,24,128]{3,2,1,0:T(8,128)(2,1)}), bf16[16,8,24,128]{3,2,1,0:T(8,128)(2,1)S(1)}, u32[]{:S(2)}, u32[]{:S(2)}) %all-to-all-start.2) | async-done | bytes 786464 | tf_op jit(solution)/shard_map/all_to_all | solution.py:31
  177.0 6.5 %collective-permute-start.10 = (bf16[16,24,128]{2,1,0:T(8,128)(2,1)S(1)}, bf16[16,24,128]{2,1,0:T(8,128)(2,1)S(1)}, u32[]{:S(2)}, u32[]{:S(2)}) collective-permute-start(bf16[16,24,128]{2,1,0:T(8,128)(2,1)S(1)} %dynamic-slice_bitcast_fusion), channel_id=1, source_target_pairs={{0,16},{16,32},{32,48},{48,64},{64,80},{80,96},{96,112},{112,128},... | collective-permute-start | bytes 294920 | tf_op jit(solution)/shard_map/ppermute | solution.py:317
  183.5 0.6 pad_add_fusion.ends
  184.1 0.0 copy-done.6
  184.1 3.7 %assemble.1.refs_3_ = bf16[8,24,4096]{2,1,0:T(8,128)(2,1)} custom-call(bf16[16,8,24,128]{3,2,1,0:T(8,128)(2,1)} %all-to-all-done.refs_0_, bf16[16,8,24,128]{3,2,1,0:T(8,128)(2,1)} %copy-done.6), custom_call_target="tpu_custom_call" | custom-call | bytes 3145728 | tf_op jit(solution)/shard_map/assemble/pallas_call | solution.py:241
  187.8 0.0 collective-permute-done.7.refs_0_
  187.8 0.0 collective-permute-done.10.refs_1_
  187.8 0.6 copy-done.9
  188.5 0.6 copy-done.10
  189.1 2.4 %hand_over.1 = bf16[8,24,4096]{2,1,0:T(8,128)(2,1)} custom-call(s32[2]{0:T(128)} %pad_add_fusion.ends, bf16[16,24,128]{2,1,0:T(8,128)(2,1)} %copy-done.9, bf16[16,24,128]{2,1,0:T(8,128)(2,1)} %copy-done.10, bf16[24,4096]{1,0:T(8,128)(2,1)} %refs_2_.1, bf16[8,24,4096]{2,1,0:T(8,128)(2,1)} %assemble.1.refs_3_), custom_call_target="tpu_custom_call", output_to_operand_aliasing={{}: (4, {})} | custom-call | tf_op jit(solution)/shard_map/hand_over/pallas_call | solution.py:271
  (10 shorter events, 0.1 us)
Async XLA Ops:
  0.0 72.4 %copy-start = (bf16[256,4096]{1,0:T(8,128)(2,1)S(1)}, bf16[256,4096]{1,0:T(8,128)(2,1)}, u32[]{:S(2)}) copy-start(bf16[256,4096]{1,0:T(8,128)(2,1)} %param.13) | copy-start | bytes 6291460
  7.6 16.0 %collective-permute-start.1 = (bf16[4,3,8,24,128]{4,3,2,1,0:T(8,128)(2,1)}, bf16[4,3,8,24,128]{4,3,2,1,0:T(8,128)(2,1)S(1)}, u32[]{:S(2)}, u32[]{:S(2)}) collective-permute-start(bf16[4,3,8,24,128]{4,3,2,1,0:T(8,128)(2,1)} %get-tuple-element.18), channel_id=1, source_target_pairs={{0,8},{1,9},{2,10},{3,11},{4,12},{5,13},{6,14},{7,15},{8,0},{9,1},... | collective-permute-start | bytes 1769480 | tf_op jit(solution)/shard_map/ppermute | solution.py:27
  10.4 23.4 %collective-permute-start = (bf16[4,3,8,24,128]{4,3,2,1,0:T(8,128)(2,1)}, bf16[4,3,8,24,128]{4,3,2,1,0:T(8,128)(2,1)S(1)}, u32[]{:S(2)}, u32[]{:S(2)}) collective-permute-start(bf16[4,3,8,24,128]{4,3,2,1,0:T(8,128)(2,1)} %get-tuple-element.16), channel_id=1, source_target_pairs={{0,1},{1,2},{2,3},{3,0},{4,5},{5,6},{6,7},{7,4},{8,9},{9,10},{10,1... | collective-permute-start | bytes 1769480 | tf_op jit(solution)/shard_map/ppermute | solution.py:27
  13.4 44.4 %collective-permute-start.3 = (bf16[4,3,8,24,128]{4,3,2,1,0:T(8,128)(2,1)}, bf16[4,3,8,24,128]{4,3,2,1,0:T(8,128)(2,1)S(1)}, u32[]{:S(2)}, u32[]{:S(2)}) collective-permute-start(bf16[4,3,8,24,128]{4,3,2,1,0:T(8,128)(2,1)} %get-tuple-element.20), channel_id=1, source_target_pairs={{0,3},{1,0},{2,1},{3,2},{4,7},{5,4},{6,5},{7,6},{8,11},{9,8},{10,9... | collective-permute-start | bytes 1769480 | tf_op jit(solution)/shard_map/ppermute | solution.py:27
  16.5 41.3 %collective-permute-start.9 = (bf16[4,3,8,24,128]{4,3,2,1,0:T(8,128)(2,1)}, bf16[4,3,8,24,128]{4,3,2,1,0:T(8,128)(2,1)S(1)}, u32[]{:S(2)}, u32[]{:S(2)}) collective-permute-start(bf16[4,3,8,24,128]{4,3,2,1,0:T(8,128)(2,1)} %get-tuple-element.23), channel_id=1, source_target_pairs={{0,12},{1,13},{2,14},{3,15},{4,0},{5,1},{6,2},{7,3},{8,4},{9,5},{1... | collective-permute-start | bytes 1769480 | tf_op jit(solution)/shard_map/ppermute | solution.py:27
  17.3 40.5 %collective-permute-start.8 = (bf16[4,3,8,24,128]{4,3,2,1,0:T(8,128)(2,1)}, bf16[4,3,8,24,128]{4,3,2,1,0:T(8,128)(2,1)S(1)}, u32[]{:S(2)}, u32[]{:S(2)}) collective-permute-start(bf16[4,3,8,24,128]{4,3,2,1,0:T(8,128)(2,1)} %get-tuple-element.22), channel_id=1, source_target_pairs={{0,4},{1,5},{2,6},{3,7},{4,8},{5,9},{6,10},{7,11},{8,12},{9,13},{1... | collective-permute-start | bytes 1769480 | tf_op jit(solution)/shard_map/ppermute | solution.py:27
  23.6 41.9 %collective-permute-start.2 = (bf16[4,3,8,24,128]{4,3,2,1,0:T(8,128)(2,1)}, bf16[4,3,8,24,128]{4,3,2,1,0:T(8,128)(2,1)}, u32[]{:S(2)}, u32[]{:S(2)}) collective-permute-start(bf16[4,3,8,24,128]{4,3,2,1,0:T(8,128)(2,1)} %get-tuple-element.19), channel_id=1, source_target_pairs={{0,2},{1,3},{2,0},{3,1},{4,6},{5,7},{6,4},{7,5},{8,10},{9,11},{10,... | collective-permute-start | bytes 1769480 | tf_op jit(solution)/shard_map/ppermute | solution.py:27
  57.8 7.7 %copy-start.2 = (bf16[4,3,8,24,128]{4,3,2,1,0:T(8,128)(2,1)}, bf16[4,3,8,24,128]{4,3,2,1,0:T(8,128)(2,1)S(1)}, u32[]{:S(2)}) copy-start(bf16[4,3,8,24,128]{4,3,2,1,0:T(8,128)(2,1)S(1)} %collective-permute-done.3.refs_3_) | copy-start | bytes 1769476
  60.8 50.0 %all-to-all-start.1 = ((bf16[4,4,3,8,24,128]{5,4,3,2,1,0:T(8,128)(2,1)}), bf16[4,4,3,8,24,128]{5,4,3,2,1,0:T(8,128)(2,1)}, u32[]{:S(2)}, u32[]{:S(2)}) async-start(bf16[4,4,3,8,24,128]{5,4,3,2,1,0:T(8,128)(2,1)} %pad_maximum_fusion), calls=%async_computation.1 | async-start | bytes 4718592 | tf_op jit(solution)/shard_map/all_to_all | solution.py:31
  65.4 1.3 copy-start.8
  65.4 2.6 %copy-start.7 = (bf16[1,3,8,24,128]{4,3,2,1,0:T(8,128)(2,1)S(1)}, bf16[1,3,8,24,128]{4,3,2,1,0:T(8,128)(2,1)}, u32[]{:S(2)}) copy-start(bf16[1,3,8,24,128]{4,3,2,1,0:T(8,128)(2,1)} %get-tuple-element.26) | copy-start | bytes 442372
  65.5 6.8 %copy-start.11 = (s32[8]{0:T(128)S(1)}, s32[8]{0:T(128)}, u32[]{:S(2)}) copy-start(s32[8]{0:T(128)} %param.12) | copy-start | bytes 100
  65.6 22.3 %copy-start.1 = (bf16[4,3,8,24,128]{4,3,2,1,0:T(8,128)(2,1)S(1)}, bf16[4,3,8,24,128]{4,3,2,1,0:T(8,128)(2,1)}, u32[]{:S(2)}) copy-start(bf16[4,3,8,24,128]{4,3,2,1,0:T(8,128)(2,1)} %get-tuple-element.15.refs_0_) | copy-start | bytes 1769476
  65.6 22.3 %copy-start.4 = (f32[2,4096]{1,0:T(2,128)S(1)}, f32[2,4096]{1,0:T(2,128)}, u32[]{:S(2)}) copy-start(f32[2,4096]{1,0:T(2,128)} %_.1) | copy-start | bytes 98308
  65.6 22.3 %copy-start.5 = (s32[2]{0:T(128)S(1)}, s32[2]{0:T(128)}, u32[]{:S(2)}) copy-start(s32[2]{0:T(128)} %pad_add_fusion.1.place) | copy-start | bytes 28
  67.7 13.3 %collective-permute-start.4 = (bf16[4,3,8,24,128]{4,3,2,1,0:T(8,128)(2,1)}, bf16[4,3,8,24,128]{4,3,2,1,0:T(8,128)(2,1)}, u32[]{:S(2)}, u32[]{:S(2)}) collective-permute-start(bf16[4,3,8,24,128]{4,3,2,1,0:T(8,128)(2,1)} %pad_maximum_fusion.1), channel_id=1, source_target_pairs={{0,4},{1,5},{2,6},{3,7},{4,8},{5,9},{6,10},{7,11},{8,12},{9,13},{1... | collective-permute-start | bytes 1769480 | tf_op jit(solution)/shard_map/ppermute | solution.py:27
  69.0 18.8 %collective-permute-start.5 = (bf16[4,3,8,24,128]{4,3,2,1,0:T(8,128)(2,1)}, bf16[4,3,8,24,128]{4,3,2,1,0:T(8,128)(2,1)}, u32[]{:S(2)}, u32[]{:S(2)}) collective-permute-start(bf16[4,3,8,24,128]{4,3,2,1,0:T(8,128)(2,1)} %pad_maximum_fusion.2), channel_id=1, source_target_pairs={{0,8},{1,9},{2,10},{3,11},{4,12},{5,13},{6,14},{7,15},{8,0},{9,1},... | collective-permute-start | bytes 1769480 | tf_op jit(solution)/shard_map/ppermute | solution.py:27
  71.7 16.2 %collective-permute-start.6 = (bf16[4,3,8,24,128]{4,3,2,1,0:T(8,128)(2,1)}, bf16[4,3,8,24,128]{4,3,2,1,0:T(8,128)(2,1)}, u32[]{:S(2)}, u32[]{:S(2)}) collective-permute-start(bf16[4,3,8,24,128]{4,3,2,1,0:T(8,128)(2,1)} %pad_maximum_fusion.3), channel_id=1, source_target_pairs={{0,12},{1,13},{2,14},{3,15},{4,0},{5,1},{6,2},{7,3},{8,4},{9,5},{1... | collective-permute-start | bytes 1769480 | tf_op jit(solution)/shard_map/ppermute | solution.py:27
  87.9 1.1 copy-start.3
  110.8 42.0 %all-to-all-start = ((bf16[16,8,24,128]{3,2,1,0:T(8,128)(2,1)}), bf16[16,8,24,128]{3,2,1,0:T(8,128)(2,1)}, u32[]{:S(2)}, u32[]{:S(2)}) async-start(bf16[16,8,24,128]{3,2,1,0:T(8,128)(2,1)} %attend.2._), calls=%async_computation | async-start | bytes 1572864 | tf_op jit(solution)/shard_map/all_to_all | solution.py:31
  152.8 24.2 %all-to-all-start.2 = ((bf16[16,8,24,128]{3,2,1,0:T(8,128)(2,1)}), bf16[16,8,24,128]{3,2,1,0:T(8,128)(2,1)S(1)}, u32[]{:S(2)}, u32[]{:S(2)}) async-start(bf16[16,8,24,128]{3,2,1,0:T(8,128)(2,1)} %attend.3), calls=%async_computation.2 | async-start | bytes 1572864 | tf_op jit(solution)/shard_map/all_to_all | solution.py:31
  159.3 28.5 %collective-permute-start.7 = (bf16[16,24,128]{2,1,0:T(8,128)(2,1)S(1)}, bf16[16,24,128]{2,1,0:T(8,128)(2,1)S(1)}, u32[]{:S(2)}, u32[]{:S(2)}) collective-permute-start(bf16[16,24,128]{2,1,0:T(8,128)(2,1)S(1)} %dynamic-slice_bitcast_fusion.1), channel_id=1, source_target_pairs={{0,16},{16,32},{32,48},{48,64},{64,80},{80,96},{96,112},{112,128},... | collective-permute-start | bytes 294920 | tf_op jit(solution)/shard_map/ppermute | solution.py:317
  177.0 7.1 %copy-start.6 = (bf16[16,8,24,128]{3,2,1,0:T(8,128)(2,1)}, bf16[16,8,24,128]{3,2,1,0:T(8,128)(2,1)S(1)}, u32[]{:S(2)}) copy-start(bf16[16,8,24,128]{3,2,1,0:T(8,128)(2,1)S(1)} %all-to-all-done.2.refs_1_) | copy-start | bytes 2359300
  177.0 10.8 %collective-permute-start.10 = (bf16[16,24,128]{2,1,0:T(8,128)(2,1)S(1)}, bf16[16,24,128]{2,1,0:T(8,128)(2,1)S(1)}, u32[]{:S(2)}, u32[]{:S(2)}) collective-permute-start(bf16[16,24,128]{2,1,0:T(8,128)(2,1)S(1)} %dynamic-slice_bitcast_fusion), channel_id=1, source_target_pairs={{0,16},{16,32},{32,48},{48,64},{64,80},{80,96},{96,112},{112,128},... | collective-permute-start | bytes 294920 | tf_op jit(solution)/shard_map/ppermute | solution.py:317
  187.8 0.6 copy-start.9
  188.5 0.6 copy-start.10

commit v6 on v4

--- a/solution.py
+++ b/solution.py
@@ -13,6 +13,7 @@
 LOG2E = 1.4426950408889634
 AXES = (("z", "x"), ("x", "z"))
 MIB = 1024 * 1024
+BLOCK = 512
 
 
 def moved(value, axis, steps):
@@ -102,7 +103,7 @@
     frames, rows = held[0].shape[2:4]
     tokens = frames * rows
     length = SIDE * SIDE * tokens
-    block, chunk = 256, 512
+    block, chunk = BLOCK, 512
     blocks = length // block
     scale = LOG2E / math.sqrt(HD)
 
@@ -113,7 +114,7 @@
                 part = held[i][0, kind] if j == 0 else arrived[j - 1][i, kind]
                 whole[at : at + tokens, :HD] = part.reshape(tokens, HD)
     v_all[:, HD:] = jnp.ones((length, HD), jnp.bfloat16)
-    for at in range(SIDE * frames):
+    for at in range(gates.shape[0] // rows):
         gates[at * rows : (at + 1) * rows, :] = jnp.broadcast_to(
             gate_ref[at % frames : at % frames + 1, :], (rows, HD)
         )
@@ -156,7 +157,7 @@
             m_next[...] = jnp.broadcast_to(jnp.max(peak, axis=1, keepdims=True), (block, HD))
         if current is not None:
             attended = (total[:, :HD] / total[:, HD:]).astype(jnp.bfloat16).astype(jnp.float32)
-            gate = gates[rows_of(current % (SIDE * tokens // block)), :]
+            gate = gates[rows_of(current % (gates.shape[0] // block)), :]
             result[rows_of(current), :] = (gate * attended).astype(jnp.bfloat16)
 
     even, odd = (s_even, m_even), (s_odd, m_odd)
@@ -179,7 +180,7 @@
 def attend(axes, place, gate, before, held, arrived):
     frames, rows = held[0].shape[2:4]
     length = SIDE * SIDE * frames * rows
-    block = 256
+    block = BLOCK
     one = pl.BlockSpec((1, 3, frames, rows, HD), lambda n, _: (0, 0, 0, 0, 0))
     whole = pl.BlockSpec((SIDE, 3, frames, rows, HD), lambda n, _: (0, 0, 0, 0, 0))
     return pl.pallas_call(
@@ -199,14 +200,14 @@
                 pltpu.VMEM((block, length), jnp.float32),
                 pltpu.VMEM((block, HD), jnp.float32),
                 pltpu.VMEM((block, HD), jnp.float32),
-                pltpu.VMEM((SIDE * frames * rows, HD), jnp.float32),
+                pltpu.VMEM((math.lcm(frames * rows, block), HD), jnp.float32),
                 pltpu.VMEM((length, HD), jnp.bfloat16),
             ],
         ),
         out_shape=jax.ShapeDtypeStruct((SIDE * SIDE, frames, rows, HD), jnp.bfloat16),
         compiler_params=pltpu.CompilerParams(vmem_limit_bytes=60 * MIB),
         cost_estimate=pl.CostEstimate(
-            flops=int(0.1 * length * length * HD) if axes[0] == "z" else 28 * length * length * HD, bytes_accessed=length if axes[0] == "z" else 8 * length * HD, transcendentals=0
+            flops=int(0.5 * length * length * HD) if axes[0] == "z" else 28 * length * length * HD, bytes_accessed=length if axes[0] == "z" else 8 * length * HD, transcendentals=0
         ),
         name="attend",
     )(place, gate, before, *held, *arrived)
@@ -241,38 +242,38 @@
     )(*parts)
 
 
-def hand_kernel(place, *refs):
+def hand_kernel(slot, place, *refs):
     *behind, fresh, _, out = refs
 
-    @pl.when(place[3] != 0)
+    @pl.when(place[2] != 0)
     def _():
         for head, part in enumerate(behind):
             for group in range(part.shape[0]):
                 at = (group * len(behind) + head) * HD
                 out[0, :, at : at + HD] = part[group]
 
-    @pl.when(place[3] == 0)
+    @pl.when(place[2] == 0)
     def _():
         out[0] = fresh[...]
 
 
-def hand_over(place, behind, fresh, gated):
+def hand_over(slot, place, behind, fresh, gated):
     rows, inner = fresh.shape
-    part = pl.BlockSpec(behind[0].shape, lambda n, _: (0, 0, 0))
+    part = pl.BlockSpec(behind[0].shape, lambda n, *_: (0, 0, 0))
     return pl.pallas_call(
         hand_kernel,
         grid_spec=pltpu.PrefetchScalarGridSpec(
-            num_scalar_prefetch=1,
+            num_scalar_prefetch=2,
             grid=(1,),
             in_specs=[part] * len(behind)
-            + [pl.BlockSpec((rows, inner), lambda n, _: (0, 0)), pl.BlockSpec(memory_space=pl.ANY)],
-            out_specs=pl.BlockSpec((1, rows, inner), lambda n, place: (place[2], 0, 0)),
+            + [pl.BlockSpec((rows, inner), lambda n, *_: (0, 0)), pl.BlockSpec(memory_space=pl.ANY)],
+            out_specs=pl.BlockSpec((1, rows, inner), lambda n, slot, _: (slot[0], 0, 0)),
         ),
         out_shape=jax.ShapeDtypeStruct(gated.shape, gated.dtype),
-        input_output_aliases={len(behind) + 2: 0},
+        input_output_aliases={len(behind) + 3: 0},
         compiler_params=pltpu.CompilerParams(vmem_limit_bytes=60 * MIB),
         name="hand_over",
-    )(place, *behind, fresh, gated)
+    )(slot, place, *behind, fresh, gated)
 
 
 def level_gate(steps, gate_weight):
@@ -286,7 +287,7 @@
 def shards(query, key, value, qk_gain, timesteps, gate_weight, slot, fresh):
     index = lax.axis_index("seq")
     section = lax.axis_index("section")
-    place = jnp.stack([index // SIDE, index % SIDE, slot[0], section]).astype(jnp.int32)
+    place = jnp.stack([index // SIDE, index % SIDE, section]).astype(jnp.int32)
     columns = lax.dynamic_slice_in_dim(gate_weight, index * (2 * HD), 2 * HD, 1)
     gate = level_gate(timesteps, columns)
     prepared = prepare(place, query, key, value, qk_gain)
@@ -303,11 +304,13 @@
         arrived = second_stage(stacks[head], AXES[head][1])
         result = attend(AXES[head], place, gate[:, head * HD : (head + 1) * HD], before, held[head], arrived)
         before = result
+        if parts:
+            result = after(result, parts[0])
         returned = lax.all_to_all(result, "seq", split_axis=0, concat_axis=0, tiled=True)
         leaving = leaving_frame(slot, returned)
         behind.append(lax.ppermute(leaving, "section", [(n, n + 1) for n in range(sections - 1)]))
         parts.append(returned)
-    return hand_over(place, behind, fresh, assemble(parts))
+    return hand_over(slot, place, behind, fresh, assemble(parts))
 
 
 def solution(mesh):

time: 194 us -> 197 us (1.015)
  starting transfers between devices: 66.1 us -> 68.8 us
  waiting for transfers between devices: 70.1 us -> 72.3 us
    all_to_all x2, waiting for transfers between devices: 18 us -> 32.8 us  [shards(): lax.all_to_all(result, 'seq', split_axis=0, concat_axis=0, tiled=True)]
    ppermute x12, waiting for transfers between devices: 52 us -> 39.5 us  [moved(): return lax.ppermute(value, 'seq', pairs)]
    all_to_all x2, starting transfers between devices: 15.7 us -> 19.2 us  [shards(): lax.all_to_all(result, 'seq', split_axis=0, concat_axis=0, tiled=True)]
    ppermute x2, starting transfers between devices: 15 us -> 12.5 us  [shards(): lax.ppermute(leaving, 'section', [(n, n + 1) for n in range(sections - 1)])]
  transfers between devices with their start and end apart: 16 -> 16, of which waited for: 7 -> 6; matrix products, arithmetic and copies ran while one was open for 4% -> 4% of each run, Pallas kernels for 18% -> 17%
where the time goes in v6:
time: 197 us
  waiting for transfers between devices  72.3 us (37%)
  starting transfers between devices  68.8 us (35%)
  Pallas kernels  43.4 us (22%)
  other arithmetic  6.54 us (3%)
  local copies, waits for them, and re-layouts  4.53 us (2%)
    ppermute x12, waiting for transfers between devices, moved(): return lax.ppermute(value, 'seq', pairs)  39.5 us
    ppermute x12, starting transfers between devices, moved(): return lax.ppermute(value, 'seq', pairs)  37.1 us
    all_to_all x2, waiting for transfers between devices, shards(): lax.all_to_all(result, 'seq', split_axis=0, concat_axis=0, tiled=True)  32.8 us
    pallas_call x2, Pallas kernels, attend(): pl.pallas_call(functools.partial(attend_kernel, axes), grid_spec=pltpu.Pr...  30.3 us
    all_to_all x2, starting transfers between devices, shards(): lax.all_to_all(result, 'seq', split_axis=0, concat_axis=0, tiled=True)  19.2 us
    ppermute x2, starting transfers between devices, shards(): lax.ppermute(leaving, 'section', [(n, n + 1) for n in range(sections - 1)])  12.5 us
    pallas_call x1, Pallas kernels, prepare(): pl.pallas_call(prepare_kernel, grid_spec=pltpu.PrefetchScalarGridSpec(num...  7.05 us
    another operation x6, other arithmetic, stacked(): return [jnp.stack([piece[j] for piece in held]) for j in range(1, SIDE)]  5.8 us
  transfers between devices with their start and end apart: 16, of which 6 were waited for; matrix products, arithmetic and copies ran while one was open for 4% of the time, Pallas kernels for 17%

profile of v6, /device:TPU:17, one launch (start us, length us, event | category | flops | bytes accessed | tf_op | source)
XLA Modules:
  0.0 196.6 jit_solution(4265609101022854723)
XLA Ops:
  0.0 0.0 copy-start
  0.0 0.6 pad_add_fusion.place
  0.6 7.1 %prepare.1 = (bf16[4,3,8,24,128]{4,3,2,1,0:T(8,128)(2,1)}, bf16[4,3,8,24,128]{4,3,2,1,0:T(8,128)(2,1)}, bf16[4,3,8,24,128]{4,3,2,1,0:T(8,128)(2,1)}, bf16[4,3,8,...) custom-call(s32[3]{0:T(128)} %pad_add_fusion.place, ...), custom_call_target="tpu_custom_call" | custom-call | flops 7864320 | bytes 9437184 | tf_op jit(solution)/shard_map/prepare/pallas_call | solution.py:83
  7.7 2.8 %collective-permute-start.1 = (bf16[4,3,8,24,128]{4,3,2,1,0:T(8,128)(2,1)}, bf16[4,3,8,24,128]{4,3,2,1,0:T(8,128)(2,1)S(1)}, u32[]{:S(2)}, u32[]{:S(2)}) collective-permute-start(bf16[4,3,8,24,128]{4,3,2,1,0:T(8,128)(2,1)} %get-tuple-element.19), channel_id=1, source_target_pairs={{0,8},{1,9},{2,10},{3,11},{4,12},{5,13},{6,14},{7,15},{8,0},{9,1},... | collective-permute-start | bytes 1769480 | tf_op jit(solution)/shard_map/ppermute | solution.py:28
  10.5 0.3 collective-permute-start.3
  10.8 2.4 %collective-permute-start.4 = (bf16[4,3,8,24,128]{4,3,2,1,0:T(8,128)(2,1)}, bf16[4,3,8,24,128]{4,3,2,1,0:T(8,128)(2,1)S(1)}, u32[]{:S(2)}, u32[]{:S(2)}) collective-permute-start(bf16[4,3,8,24,128]{4,3,2,1,0:T(8,128)(2,1)} %get-tuple-element.23), channel_id=1, source_target_pairs={{0,12},{1,13},{2,14},{3,15},{4,0},{5,1},{6,2},{7,3},{8,4},{9,5},{1... | collective-permute-start | bytes 1769480 | tf_op jit(solution)/shard_map/ppermute | solution.py:28
  13.2 3.0 %collective-permute-start = (bf16[4,3,8,24,128]{4,3,2,1,0:T(8,128)(2,1)}, bf16[4,3,8,24,128]{4,3,2,1,0:T(8,128)(2,1)S(1)}, u32[]{:S(2)}, u32[]{:S(2)}) collective-permute-start(bf16[4,3,8,24,128]{4,3,2,1,0:T(8,128)(2,1)} %get-tuple-element.17), channel_id=1, source_target_pairs={{0,1},{1,2},{2,3},{3,0},{4,5},{5,6},{6,7},{7,4},{8,9},{9,10},{10,1... | collective-permute-start | bytes 1769480 | tf_op jit(solution)/shard_map/ppermute | solution.py:28
  16.2 3.0 %collective-permute-start.5 = (bf16[4,3,8,24,128]{4,3,2,1,0:T(8,128)(2,1)}, bf16[4,3,8,24,128]{4,3,2,1,0:T(8,128)(2,1)S(1)}, u32[]{:S(2)}, u32[]{:S(2)}) collective-permute-start(bf16[4,3,8,24,128]{4,3,2,1,0:T(8,128)(2,1)} %get-tuple-element.25), channel_id=1, source_target_pairs={{0,3},{1,0},{2,1},{3,2},{4,7},{5,4},{6,5},{7,6},{8,11},{9,8},{10,9... | collective-permute-start | bytes 1769480 | tf_op jit(solution)/shard_map/ppermute | solution.py:28
  19.2 1.4 fusion.9
  20.6 3.1 %collective-permute-done.1.refs_2_ = bf16[4,3,8,24,128]{4,3,2,1,0:T(8,128)(2,1)S(1)} collective-permute-done((bf16[4,3,8,24,128]{4,3,2,1,0:T(8,128)(2,1)}, bf16[4,3,8,24,128]{4,3,2,1,0:T(8,128)(2,1)S(1)}, u32[]{:S(2)}, u32[]{:S(2)}) %collective-permute-start.1) | collective-permute-done | bytes 589856 | tf_op jit(solution)/shard_map/ppermute | solution.py:28
  23.7 0.0 copy-done.12
  23.7 6.9 %collective-permute-start.2 = (bf16[4,3,8,24,128]{4,3,2,1,0:T(8,128)(2,1)S(1)}, bf16[4,3,8,24,128]{4,3,2,1,0:T(8,128)(2,1)S(1)}, u32[]{:S(2)}, u32[]{:S(2)}) collective-permute-start(bf16[4,3,8,24,128]{4,3,2,1,0:T(8,128)(2,1)S(1)} %copy-done.12), channel_id=1, source_target_pairs={{0,2},{1,3},{2,0},{3,1},{4,6},{5,7},{6,4},{7,5},{8,10},{9,11},{10,... | collective-permute-start | bytes 1769480 | tf_op jit(solution)/shard_map/ppermute | solution.py:28
  30.7 0.0 copy-done.7
  30.7 6.7 %collective-permute-done.3.refs_1_ = bf16[4,3,8,24,128]{4,3,2,1,0:T(8,128)(2,1)S(1)} collective-permute-done((bf16[4,3,8,24,128]{4,3,2,1,0:T(8,128)(2,1)}, bf16[4,3,8,24,128]{4,3,2,1,0:T(8,128)(2,1)S(1)}, u32[]{:S(2)}, u32[]{:S(2)}) %collective-permute-start.3) | collective-permute-done | bytes 589856 | tf_op jit(solution)/shard_map/ppermute | solution.py:28
  37.4 0.0 collective-permute-done.4.refs_3_
  37.4 0.0 copy-start.9
  37.5 1.1 pad_maximum_fusion.2
  38.6 0.9 pad_maximum_fusion.1
  39.5 0.0 copy-done.8
  39.5 0.0 copy-done.9
  39.5 0.9 pad_maximum_fusion
  40.4 0.0 collective-permute-done.refs_1_
  40.4 20.5 %collective-permute-done.5.refs_3_ = bf16[4,3,8,24,128]{4,3,2,1,0:T(8,128)(2,1)S(1)} collective-permute-done((bf16[4,3,8,24,128]{4,3,2,1,0:T(8,128)(2,1)}, bf16[4,3,8,24,128]{4,3,2,1,0:T(8,128)(2,1)S(1)}, u32[]{:S(2)}, u32[]{:S(2)}) %collective-permute-start.5) | collective-permute-done | bytes 589856 | tf_op jit(solution)/shard_map/ppermute | solution.py:28
  61.0 0.0 collective-permute-done.2.refs_2_
  61.0 0.0 copy-start.4
  61.1 0.0 copy-start.13
  61.1 1.1 pad_maximum_fusion.5
  62.2 0.0 copy-done.2
  62.2 0.0 collective-permute-start.8
  62.2 0.9 pad_maximum_fusion.4
  63.1 0.0 copy-done.3
  63.1 0.0 copy-done.4
  63.1 0.9 collective-permute-start.7
  64.0 0.9 pad_maximum_fusion.3
  64.9 0.6 collective-permute-start.6
  65.5 0.0 copy-done.13
  65.5 13.0 %collective-permute-start.12 = (bf16[4,3,8,24,128]{4,3,2,1,0:T(8,128)(2,1)}, bf16[4,3,8,24,128]{4,3,2,1,0:T(8,128)(2,1)}, u32[]{:S(2)}, u32[]{:S(2)}) collective-permute-start(bf16[4,3,8,24,128]{4,3,2,1,0:T(8,128)(2,1)} %pad_maximum_fusion.2), channel_id=1, source_target_pairs={{0,3},{1,0},{2,1},{3,2},{4,7},{5,4},{6,5},{7,6},{8,11},{9,8},{10,9... | collective-permute-start | bytes 1769480 | tf_op jit(solution)/shard_map/ppermute | solution.py:28
  78.5 0.8 collective-permute-start.11
  79.4 0.0 collective-permute-done.8.refs_6_
  79.4 3.4 %collective-permute-start.10 = (bf16[4,3,8,24,128]{4,3,2,1,0:T(8,128)(2,1)}, bf16[4,3,8,24,128]{4,3,2,1,0:T(8,128)(2,1)}, u32[]{:S(2)}, u32[]{:S(2)}) collective-permute-start(bf16[4,3,8,24,128]{4,3,2,1,0:T(8,128)(2,1)} %pad_maximum_fusion), channel_id=1, source_target_pairs={{0,1},{1,2},{2,3},{3,0},{4,5},{5,6},{6,7},{7,4},{8,9},{9,10},{10,1... | collective-permute-start | bytes 1769480 | tf_op jit(solution)/shard_map/ppermute | solution.py:28
  82.8 0.1 fusion.2
  82.9 0.0 copy-done
  82.9 0.2 fusion
  83.0 0.6 fusion.17
  83.7 0.0 collective-permute-done.7.refs_5_
  83.7 9.2 %collective-permute-done.6.refs_4_ = bf16[4,3,8,24,128]{4,3,2,1,0:T(8,128)(2,1)} collective-permute-done((bf16[4,3,8,24,128]{4,3,2,1,0:T(8,128)(2,1)}, bf16[4,3,8,24,128]{4,3,2,1,0:T(8,128)(2,1)}, u32[]{:S(2)}, u32[]{:S(2)}) %collective-permute-start.6) | collective-permute-done | bytes 589856 | tf_op jit(solution)/shard_map/ppermute | solution.py:28
  92.9 15.1 %attend.2._ = bf16[16,8,24,128]{3,2,1,0:T(8,128)(2,1)} custom-call(s32[3]{0:T(128)} %pad_add_fusion.place, f32[8,128]{1,0:T(8,128)} %get-tuple-element.52.gate_ref, f32[2,4096]{1,0:T(2,128)} %_.1, bf16[4,3,8,24,128]{4,3,2,1,0:T(8,128)(2,1)} %get-tuple-element.16.refs_0_, bf16[4,3,8,24,128]{4,3,2,1,0:T(8,128)(2,1)} %copy-done.2, ...), custom_call_target="tpu_custom_call" | custom-call | flops 603979776 | bytes 3072 | tf_op jit(solution)/shard_map/attend/pallas_call | solution.py:186
  108.0 14.9 %all-to-all-start = ((bf16[16,8,24,128]{3,2,1,0:T(8,128)(2,1)}), bf16[16,8,24,128]{3,2,1,0:T(8,128)(2,1)S(1)}, u32[]{:S(2)}, u32[]{:S(2)}) async-start(bf16[16,8,24,128]{3,2,1,0:T(8,128)(2,1)} %attend.2._), calls=%async_computation | async-start | bytes 1572864 | tf_op jit(solution)/shard_map/all_to_all | solution.py:309
  122.9 0.0 collective-permute-done.12.refs_6_
  122.9 0.0 collective-permute-done.11.refs_5_
  122.9 0.0 collective-permute-done.10.refs_4_
  123.0 15.1 %attend.3 = bf16[16,8,24,128]{3,2,1,0:T(8,128)(2,1)} custom-call(s32[3]{0:T(128)} %pad_add_fusion.place, f32[8,128]{1,0:T(8,128)} %get-tuple-element.51.gate_ref, bf16[16,8,24,128]{3,2,1,0:T(8,128)(2,1)} %attend.2._, bf16[4,3,8,24,128]{4,3,2,1,0:T(8,128)(2,1)} %get-tuple-element.21.refs_0_, bf16[4,3,8,24,128]{4,3,2,1,0:T(8,128)(2,1)} %copy-done.8, ...), custom_call_target="tpu_custom_call" | custom-call | flops 33822867456 | bytes 3145728 | tf_op jit(solution)/shard_map/attend/pallas_call | solution.py:186
  138.1 16.3 %all-to-all-done.refs_0_ = bf16[16,8,24,128]{3,2,1,0:T(8,128)(2,1)S(1)} async-done(((bf16[16,8,24,128]{3,2,1,0:T(8,128)(2,1)}), bf16[16,8,24,128]{3,2,1,0:T(8,128)(2,1)S(1)}, u32[]{:S(2)}, u32[]{:S(2)}) %all-to-all-start) | async-done | bytes 786464 | tf_op jit(solution)/shard_map/all_to_all | solution.py:309
  154.4 4.3 %all-to-all-start.1 = ((bf16[16,8,24,128]{3,2,1,0:T(8,128)(2,1)}), bf16[16,8,24,128]{3,2,1,0:T(8,128)(2,1)}, u32[]{:S(2)}, u32[]{:S(2)}) async-start(bf16[16,8,24,128]{3,2,1,0:T(8,128)(2,1)} %attend.3), calls=%async_computation.1 | async-start | bytes 1572864 | tf_op jit(solution)/shard_map/all_to_all | solution.py:309
  159.3 3.6 %collective-permute-start.9 = (bf16[16,24,128]{2,1,0:T(8,128)(2,1)S(1)}, bf16[16,24,128]{2,1,0:T(8,128)(2,1)S(1)}, u32[]{:S(2)}, u32[]{:S(2)}) collective-permute-start(bf16[16,24,128]{2,1,0:T(8,128)(2,1)S(1)} %dynamic-slice_bitcast_fusion.1), channel_id=1, source_target_pairs={{0,16},{16,32},{32,48},{48,64},{64,80},{80,96},{96,112},{112,128},... | collective-permute-start | bytes 294920 | tf_op jit(solution)/shard_map/ppermute | solution.py:311
  162.9 16.5 %all-to-all-done.1.refs_1_ = bf16[16,8,24,128]{3,2,1,0:T(8,128)(2,1)} async-done(((bf16[16,8,24,128]{3,2,1,0:T(8,128)(2,1)}), bf16[16,8,24,128]{3,2,1,0:T(8,128)(2,1)}, u32[]{:S(2)}, u32[]{:S(2)}) %all-to-all-start.1) | async-done | bytes 786464 | tf_op jit(solution)/shard_map/all_to_all | solution.py:309
  179.4 0.9 dynamic-slice_bitcast_fusion
  180.3 8.9 %collective-permute-start.13 = (bf16[16,24,128]{2,1,0:T(8,128)(2,1)S(1)}, bf16[16,24,128]{2,1,0:T(8,128)(2,1)S(1)}, u32[]{:S(2)}, u32[]{:S(2)}) collective-permute-start(bf16[16,24,128]{2,1,0:T(8,128)(2,1)S(1)} %dynamic-slice_bitcast_fusion), channel_id=1, source_target_pairs={{0,16},{16,32},{32,48},{48,64},{64,80},{80,96},{96,112},{112,128},... | collective-permute-start | bytes 294920 | tf_op jit(solution)/shard_map/ppermute | solution.py:311
  189.2 3.7 %assemble.1.refs_3_ = bf16[8,24,4096]{2,1,0:T(8,128)(2,1)} custom-call(bf16[16,8,24,128]{3,2,1,0:T(8,128)(2,1)} %copy-done.1, bf16[16,8,24,128]{3,2,1,0:T(8,128)(2,1)} %all-to-all-done.1.refs_1_), custom_call_target="tpu_custom_call" | custom-call | bytes 3145728 | tf_op jit(solution)/shard_map/assemble/pallas_call | solution.py:233
  193.0 0.0 collective-permute-done.9.refs_0_
  193.0 0.0 collective-permute-done.13.refs_1_
  193.0 0.6 copy-done.10
  193.6 0.6 copy-done.11
  194.2 2.4 %hand_over.1 = bf16[8,24,4096]{2,1,0:T(8,128)(2,1)} custom-call(s32[1]{0:T(128)} %copy.11.slot, s32[3]{0:T(128)} %pad_add_fusion.place, bf16[16,24,128]{2,1,0:T(8,128)(2,1)} %copy-done.10, bf16[16,24,128]{2,1,0:T(8,128)(2,1)} %copy-done.11, bf16[24,4096]{1,0:T(8,128)(2,1)} %refs_2_.1, ...), custom_call_target="tpu_custom_call", output_to_operand_aliasing={{}: (5, {})} | custom-call | tf_op jit(solution)/shard_map/hand_over/pallas_call | solution.py:263
  (22 shorter events, 0.3 us)
Async XLA Ops:
  0.0 82.9 %copy-start = (bf16[256,4096]{1,0:T(8,128)(2,1)S(1)}, bf16[256,4096]{1,0:T(8,128)(2,1)}, u32[]{:S(2)}) copy-start(bf16[256,4096]{1,0:T(8,128)(2,1)} %param.13) | copy-start | bytes 6291460
  7.7 16.1 %copy-start.12 = (bf16[4,3,8,24,128]{4,3,2,1,0:T(8,128)(2,1)S(1)}, bf16[4,3,8,24,128]{4,3,2,1,0:T(8,128)(2,1)}, u32[]{:S(2)}) copy-start(bf16[4,3,8,24,128]{4,3,2,1,0:T(8,128)(2,1)} %get-tuple-element.20) | copy-start | bytes 1769476
  7.7 16.0 %collective-permute-start.1 = (bf16[4,3,8,24,128]{4,3,2,1,0:T(8,128)(2,1)}, bf16[4,3,8,24,128]{4,3,2,1,0:T(8,128)(2,1)S(1)}, u32[]{:S(2)}, u32[]{:S(2)}) collective-permute-start(bf16[4,3,8,24,128]{4,3,2,1,0:T(8,128)(2,1)} %get-tuple-element.19), channel_id=1, source_target_pairs={{0,8},{1,9},{2,10},{3,11},{4,12},{5,13},{6,14},{7,15},{8,0},{9,1},... | collective-permute-start | bytes 1769480 | tf_op jit(solution)/shard_map/ppermute | solution.py:28
  10.5 26.9 %collective-permute-start.3 = (bf16[4,3,8,24,128]{4,3,2,1,0:T(8,128)(2,1)}, bf16[4,3,8,24,128]{4,3,2,1,0:T(8,128)(2,1)S(1)}, u32[]{:S(2)}, u32[]{:S(2)}) collective-permute-start(bf16[4,3,8,24,128]{4,3,2,1,0:T(8,128)(2,1)} %get-tuple-element.22), channel_id=1, source_target_pairs={{0,4},{1,5},{2,6},{3,7},{4,8},{5,9},{6,10},{7,11},{8,12},{9,13},{1... | collective-permute-start | bytes 1769480 | tf_op jit(solution)/shard_map/ppermute | solution.py:28
  10.8 26.6 %collective-permute-start.4 = (bf16[4,3,8,24,128]{4,3,2,1,0:T(8,128)(2,1)}, bf16[4,3,8,24,128]{4,3,2,1,0:T(8,128)(2,1)S(1)}, u32[]{:S(2)}, u32[]{:S(2)}) collective-permute-start(bf16[4,3,8,24,128]{4,3,2,1,0:T(8,128)(2,1)} %get-tuple-element.23), channel_id=1, source_target_pairs={{0,12},{1,13},{2,14},{3,15},{4,0},{5,1},{6,2},{7,3},{8,4},{9,5},{1... | collective-permute-start | bytes 1769480 | tf_op jit(solution)/shard_map/ppermute | solution.py:28
  13.2 27.2 %collective-permute-start = (bf16[4,3,8,24,128]{4,3,2,1,0:T(8,128)(2,1)}, bf16[4,3,8,24,128]{4,3,2,1,0:T(8,128)(2,1)S(1)}, u32[]{:S(2)}, u32[]{:S(2)}) collective-permute-start(bf16[4,3,8,24,128]{4,3,2,1,0:T(8,128)(2,1)} %get-tuple-element.17), channel_id=1, source_target_pairs={{0,1},{1,2},{2,3},{3,0},{4,5},{5,6},{6,7},{7,4},{8,9},{9,10},{10,1... | collective-permute-start | bytes 1769480 | tf_op jit(solution)/shard_map/ppermute | solution.py:28
  16.2 44.8 %collective-permute-start.5 = (bf16[4,3,8,24,128]{4,3,2,1,0:T(8,128)(2,1)}, bf16[4,3,8,24,128]{4,3,2,1,0:T(8,128)(2,1)S(1)}, u32[]{:S(2)}, u32[]{:S(2)}) collective-permute-start(bf16[4,3,8,24,128]{4,3,2,1,0:T(8,128)(2,1)} %get-tuple-element.25), channel_id=1, source_target_pairs={{0,3},{1,0},{2,1},{3,2},{4,7},{5,4},{6,5},{7,6},{8,11},{9,8},{10,9... | collective-permute-start | bytes 1769480 | tf_op jit(solution)/shard_map/ppermute | solution.py:28
  23.7 7.0 %copy-start.7 = (bf16[4,3,8,24,128]{4,3,2,1,0:T(8,128)(2,1)}, bf16[4,3,8,24,128]{4,3,2,1,0:T(8,128)(2,1)S(1)}, u32[]{:S(2)}) copy-start(bf16[4,3,8,24,128]{4,3,2,1,0:T(8,128)(2,1)S(1)} %collective-permute-done.1.refs_2_) | copy-start | bytes 1769476
  23.7 37.3 %collective-permute-start.2 = (bf16[4,3,8,24,128]{4,3,2,1,0:T(8,128)(2,1)S(1)}, bf16[4,3,8,24,128]{4,3,2,1,0:T(8,128)(2,1)S(1)}, u32[]{:S(2)}, u32[]{:S(2)}) collective-permute-start(bf16[4,3,8,24,128]{4,3,2,1,0:T(8,128)(2,1)S(1)} %copy-done.12), channel_id=1, source_target_pairs={{0,2},{1,3},{2,0},{3,1},{4,6},{5,7},{6,4},{7,5},{8,10},{9,11},{10,... | collective-permute-start | bytes 1769480 | tf_op jit(solution)/shard_map/ppermute | solution.py:28
  37.4 2.1 %copy-start.8 = (bf16[4,3,8,24,128]{4,3,2,1,0:T(8,128)(2,1)}, bf16[4,3,8,24,128]{4,3,2,1,0:T(8,128)(2,1)S(1)}, u32[]{:S(2)}) copy-start(bf16[4,3,8,24,128]{4,3,2,1,0:T(8,128)(2,1)S(1)} %collective-permute-done.3.refs_1_) | copy-start | bytes 1769476
  37.4 2.0 %copy-start.9 = (bf16[4,3,8,24,128]{4,3,2,1,0:T(8,128)(2,1)}, bf16[4,3,8,24,128]{4,3,2,1,0:T(8,128)(2,1)S(1)}, u32[]{:S(2)}) copy-start(bf16[4,3,8,24,128]{4,3,2,1,0:T(8,128)(2,1)S(1)} %collective-permute-done.4.refs_3_) | copy-start | bytes 1769476
  40.4 21.8 %copy-start.2 = (bf16[4,3,8,24,128]{4,3,2,1,0:T(8,128)(2,1)}, bf16[4,3,8,24,128]{4,3,2,1,0:T(8,128)(2,1)S(1)}, u32[]{:S(2)}) copy-start(bf16[4,3,8,24,128]{4,3,2,1,0:T(8,128)(2,1)S(1)} %collective-permute-done.refs_1_) | copy-start | bytes 1769476
  60.9 2.2 %copy-start.3 = (bf16[4,3,8,24,128]{4,3,2,1,0:T(8,128)(2,1)}, bf16[4,3,8,24,128]{4,3,2,1,0:T(8,128)(2,1)S(1)}, u32[]{:S(2)}) copy-start(bf16[4,3,8,24,128]{4,3,2,1,0:T(8,128)(2,1)S(1)} %collective-permute-done.5.refs_3_) | copy-start | bytes 1769476
  61.0 2.1 %copy-start.4 = (bf16[4,3,8,24,128]{4,3,2,1,0:T(8,128)(2,1)}, bf16[4,3,8,24,128]{4,3,2,1,0:T(8,128)(2,1)S(1)}, u32[]{:S(2)}) copy-start(bf16[4,3,8,24,128]{4,3,2,1,0:T(8,128)(2,1)S(1)} %collective-permute-done.2.refs_2_) | copy-start | bytes 1769476
  61.1 4.4 %copy-start.13 = (s32[8]{0:T(128)S(1)}, s32[8]{0:T(128)}, u32[]{:S(2)}) copy-start(s32[8]{0:T(128)} %param.12) | copy-start | bytes 100
  62.2 17.2 %collective-permute-start.8 = (bf16[4,3,8,24,128]{4,3,2,1,0:T(8,128)(2,1)}, bf16[4,3,8,24,128]{4,3,2,1,0:T(8,128)(2,1)S(1)}, u32[]{:S(2)}, u32[]{:S(2)}) collective-permute-start(bf16[4,3,8,24,128]{4,3,2,1,0:T(8,128)(2,1)} %pad_maximum_fusion.5), channel_id=1, source_target_pairs={{0,12},{1,13},{2,14},{3,15},{4,0},{5,1},{6,2},{7,3},{8,4},{9,5},{1... | collective-permute-start | bytes 1769480 | tf_op jit(solution)/shard_map/ppermute | solution.py:28
  63.1 20.5 %collective-permute-start.7 = (bf16[4,3,8,24,128]{4,3,2,1,0:T(8,128)(2,1)}, bf16[4,3,8,24,128]{4,3,2,1,0:T(8,128)(2,1)S(1)}, u32[]{:S(2)}, u32[]{:S(2)}) collective-permute-start(bf16[4,3,8,24,128]{4,3,2,1,0:T(8,128)(2,1)} %pad_maximum_fusion.4), channel_id=1, source_target_pairs={{0,8},{1,9},{2,10},{3,11},{4,12},{5,13},{6,14},{7,15},{8,0},{9,1},... | collective-permute-start | bytes 1769480 | tf_op jit(solution)/shard_map/ppermute | solution.py:28
  64.9 27.9 %collective-permute-start.6 = (bf16[4,3,8,24,128]{4,3,2,1,0:T(8,128)(2,1)}, bf16[4,3,8,24,128]{4,3,2,1,0:T(8,128)(2,1)}, u32[]{:S(2)}, u32[]{:S(2)}) collective-permute-start(bf16[4,3,8,24,128]{4,3,2,1,0:T(8,128)(2,1)} %pad_maximum_fusion.3), channel_id=1, source_target_pairs={{0,4},{1,5},{2,6},{3,7},{4,8},{5,9},{6,10},{7,11},{8,12},{9,13},{1... | collective-permute-start | bytes 1769480 | tf_op jit(solution)/shard_map/ppermute | solution.py:28
  65.5 57.4 %collective-permute-start.12 = (bf16[4,3,8,24,128]{4,3,2,1,0:T(8,128)(2,1)}, bf16[4,3,8,24,128]{4,3,2,1,0:T(8,128)(2,1)}, u32[]{:S(2)}, u32[]{:S(2)}) collective-permute-start(bf16[4,3,8,24,128]{4,3,2,1,0:T(8,128)(2,1)} %pad_maximum_fusion.2), channel_id=1, source_target_pairs={{0,3},{1,0},{2,1},{3,2},{4,7},{5,4},{6,5},{7,6},{8,11},{9,8},{10,9... | collective-permute-start | bytes 1769480 | tf_op jit(solution)/shard_map/ppermute | solution.py:28
  78.5 44.4 %collective-permute-start.11 = (bf16[4,3,8,24,128]{4,3,2,1,0:T(8,128)(2,1)}, bf16[4,3,8,24,128]{4,3,2,1,0:T(8,128)(2,1)}, u32[]{:S(2)}, u32[]{:S(2)}) collective-permute-start(bf16[4,3,8,24,128]{4,3,2,1,0:T(8,128)(2,1)} %pad_maximum_fusion.1), channel_id=1, source_target_pairs={{0,2},{1,3},{2,0},{3,1},{4,6},{5,7},{6,4},{7,5},{8,10},{9,11},{10,... | collective-permute-start | bytes 1769480 | tf_op jit(solution)/shard_map/ppermute | solution.py:28
  79.4 13.5 %copy-start.5 = (bf16[4,3,8,24,128]{4,3,2,1,0:T(8,128)(2,1)}, bf16[4,3,8,24,128]{4,3,2,1,0:T(8,128)(2,1)S(1)}, u32[]{:S(2)}) copy-start(bf16[4,3,8,24,128]{4,3,2,1,0:T(8,128)(2,1)S(1)} %collective-permute-done.8.refs_6_) | copy-start | bytes 1769476
  79.4 43.6 %collective-permute-start.10 = (bf16[4,3,8,24,128]{4,3,2,1,0:T(8,128)(2,1)}, bf16[4,3,8,24,128]{4,3,2,1,0:T(8,128)(2,1)}, u32[]{:S(2)}, u32[]{:S(2)}) collective-permute-start(bf16[4,3,8,24,128]{4,3,2,1,0:T(8,128)(2,1)} %pad_maximum_fusion), channel_id=1, source_target_pairs={{0,1},{1,2},{2,3},{3,0},{4,5},{5,6},{6,7},{7,4},{8,9},{9,10},{10,1... | collective-permute-start | bytes 1769480 | tf_op jit(solution)/shard_map/ppermute | solution.py:28
  83.7 9.2 %copy-start.6 = (bf16[4,3,8,24,128]{4,3,2,1,0:T(8,128)(2,1)}, bf16[4,3,8,24,128]{4,3,2,1,0:T(8,128)(2,1)S(1)}, u32[]{:S(2)}) copy-start(bf16[4,3,8,24,128]{4,3,2,1,0:T(8,128)(2,1)S(1)} %collective-permute-done.7.refs_5_) | copy-start | bytes 1769476
  108.0 46.4 %all-to-all-start = ((bf16[16,8,24,128]{3,2,1,0:T(8,128)(2,1)}), bf16[16,8,24,128]{3,2,1,0:T(8,128)(2,1)S(1)}, u32[]{:S(2)}, u32[]{:S(2)}) async-start(bf16[16,8,24,128]{3,2,1,0:T(8,128)(2,1)} %attend.2._), calls=%async_computation | async-start | bytes 1572864 | tf_op jit(solution)/shard_map/all_to_all | solution.py:309
  154.3 34.9 %copy-start.1 = (bf16[16,8,24,128]{3,2,1,0:T(8,128)(2,1)}, bf16[16,8,24,128]{3,2,1,0:T(8,128)(2,1)S(1)}, u32[]{:S(2)}) copy-start(bf16[16,8,24,128]{3,2,1,0:T(8,128)(2,1)S(1)} %all-to-all-done.refs_0_) | copy-start | bytes 2359300
  154.4 25.1 %all-to-all-start.1 = ((bf16[16,8,24,128]{3,2,1,0:T(8,128)(2,1)}), bf16[16,8,24,128]{3,2,1,0:T(8,128)(2,1)}, u32[]{:S(2)}, u32[]{:S(2)}) async-start(bf16[16,8,24,128]{3,2,1,0:T(8,128)(2,1)} %attend.3), calls=%async_computation.1 | async-start | bytes 1572864 | tf_op jit(solution)/shard_map/all_to_all | solution.py:309
  159.3 33.6 %collective-permute-start.9 = (bf16[16,24,128]{2,1,0:T(8,128)(2,1)S(1)}, bf16[16,24,128]{2,1,0:T(8,128)(2,1)S(1)}, u32[]{:S(2)}, u32[]{:S(2)}) collective-permute-start(bf16[16,24,128]{2,1,0:T(8,128)(2,1)S(1)} %dynamic-slice_bitcast_fusion.1), channel_id=1, source_target_pairs={{0,16},{16,32},{32,48},{48,64},{64,80},{80,96},{96,112},{112,128},... | collective-permute-start | bytes 294920 | tf_op jit(solution)/shard_map/ppermute | solution.py:311
  180.3 12.6 %collective-permute-start.13 = (bf16[16,24,128]{2,1,0:T(8,128)(2,1)S(1)}, bf16[16,24,128]{2,1,0:T(8,128)(2,1)S(1)}, u32[]{:S(2)}, u32[]{:S(2)}) collective-permute-start(bf16[16,24,128]{2,1,0:T(8,128)(2,1)S(1)} %dynamic-slice_bitcast_fusion), channel_id=1, source_target_pairs={{0,16},{16,32},{32,48},{48,64},{64,80},{80,96},{96,112},{112,128},... | collective-permute-start | bytes 294920 | tf_op jit(solution)/shard_map/ppermute | solution.py:311
  193.0 0.6 copy-start.10
  193.6 0.6 copy-start.11

commit v7 on v5

--- a/solution.py
+++ b/solution.py
@@ -12,7 +12,8 @@
 SIDE = 4
 LOG2E = 1.4426950408889634
 MIB = 1024 * 1024
-ATTEND_MIB = 30
+ATTEND_MIB = 60
+BLOCK = 512
 
 
 def moved(value, axis, steps):
@@ -52,7 +53,7 @@
     return lax.rem(place[0] + steps["x"], SIDE) * SIDE + lax.rem(place[1] + steps["z"], SIDE)
 
 
-def prepare_kernel(place, q_ref, k_ref, v_ref, gain_ref, *outs):
+def prepare_kernel(head, place, q_ref, k_ref, v_ref, gain_ref, *outs):
     inner = q_ref.shape[2]
 
     def factor_of(ref):
@@ -65,36 +66,34 @@
         return lax.rsqrt(mean + 1e-06)
 
     q_factor, k_factor = factor_of(q_ref), factor_of(k_ref)
-    for head in range(2):
-        for i in range(SIDE):
-            for j in range(SIDE):
-                group = index_of(place, ("z", "x"), i, j)
-                if head:
-                    group = lax.rem(place[0] + i, SIDE) * SIDE + j
-                at = pl.multiple_of((group * 2 + head) * HD, HD)
-                out = outs[head * SIDE + i]
-                for kind, (ref, factor) in enumerate(((q_ref, q_factor), (k_ref, k_factor))):
-                    gain = gain_ref[kind : kind + 1, pl.ds(at, HD)]
-                    part = ref[:, :, pl.ds(at, HD)].astype(jnp.float32) * factor * gain[None]
-                    out[j, kind] = part.astype(jnp.bfloat16)
-                out[j, 2] = v_ref[:, :, pl.ds(at, HD)]
-
-
-def prepare(place, query, key, value, qk_gain):
+    for i in range(SIDE):
+        for j in range(SIDE):
+            group = index_of(place, ("z", "x"), i, j)
+            if head:
+                group = lax.rem(place[0] + i, SIDE) * SIDE + j
+            at = pl.multiple_of((group * 2 + head) * HD, HD)
+            for kind, (ref, factor) in enumerate(((q_ref, q_factor), (k_ref, k_factor))):
+                gain = gain_ref[kind : kind + 1, pl.ds(at, HD)]
+                part = ref[:, :, pl.ds(at, HD)].astype(jnp.float32) * factor * gain[None]
+                outs[i][j, kind] = part.astype(jnp.bfloat16)
+            outs[i][j, 2] = v_ref[:, :, pl.ds(at, HD)]
+
+
+def prepare(head, place, query, key, value, qk_gain):
     frames, rows, inner = query.shape
     step = 2
     tall = pl.BlockSpec((step, rows, inner), lambda n, _: (n, 0, 0))
     out = pl.BlockSpec((SIDE, 3, step, rows, HD), lambda n, _: (0, 0, n, 0, 0))
     shape = jax.ShapeDtypeStruct((SIDE, 3, frames, rows, HD), jnp.bfloat16)
     return pl.pallas_call(
-        prepare_kernel,
+        functools.partial(prepare_kernel, head),
         grid_spec=pltpu.PrefetchScalarGridSpec(
             num_scalar_prefetch=1,
             grid=(frames // step,),
             in_specs=[tall, tall, tall, pl.BlockSpec((2, inner), lambda n, _: (0, 0))],
-            out_specs=[out] * (2 * SIDE),
-        ),
-        out_shape=[shape] * (2 * SIDE),
+            out_specs=[out] * SIDE,
+        ),
+        out_shape=[shape] * SIDE,
         compiler_params=pltpu.CompilerParams(vmem_limit_bytes=60 * MIB),
         cost_estimate=pl.CostEstimate(
             flops=10 * query.size, bytes_accessed=12 * query.size, transcendentals=0
@@ -109,7 +108,7 @@
     frames, rows = sent[0].shape[-3:-1]
     tokens = frames * rows
     length = SIDE * SIDE * tokens
-    block, chunk = 256, 512
+    block, chunk = BLOCK, 512
     blocks = length // block
     scale = LOG2E / math.sqrt(HD)
 
@@ -125,7 +124,7 @@
         for kind, whole in enumerate((q_all, k_all, v_all)):
             whole[n * tokens : (n + 1) * tokens, :HD] = ref[(*index, kind)].reshape(tokens, HD)
     v_all[:, HD:] = jnp.ones((length, HD), jnp.bfloat16)
-    for at in range(SIDE * frames):
+    for at in range(gates.shape[0] // rows):
         gates[at * rows : (at + 1) * rows, :] = jnp.broadcast_to(
             gate_ref[at % frames : at % frames + 1, :], (rows, HD)
         )
@@ -168,7 +167,7 @@
             m_next[...] = jnp.broadcast_to(jnp.max(peak, axis=1, keepdims=True), (block, HD))
         if current is not None:
             attended = (total[:, :HD] / total[:, HD:]).astype(jnp.bfloat16).astype(jnp.float32)
-            gate = gates[rows_of(current % (SIDE * tokens // block)), :]
+            gate = gates[rows_of(current % (gates.shape[0] // block)), :]
             result[rows_of(current), :] = (gate * attended).astype(jnp.bfloat16)
 
     even, odd = (s_even, m_even), (s_odd, m_odd)
@@ -188,7 +187,7 @@
 def attend(place, gate, before, *sent):
     frames, rows = sent[0].shape[-3:-1]
     length = SIDE * SIDE * frames * rows
-    block = 256
+    block = BLOCK
     one = pl.BlockSpec((1, 3, frames, rows, HD), lambda n, _: (0, 0, 0, 0, 0))
     whole = pl.BlockSpec((SIDE, 3, frames, rows, HD), lambda n, _: (0, 0, 0, 0, 0))
     every = pl.BlockSpec((SIDE, SIDE, 3, frames, rows, HD), lambda n, _: (0, 0, 0, 0, 0, 0))
@@ -208,7 +207,7 @@
                 pltpu.VMEM((block, length), jnp.float32),
                 pltpu.VMEM((block, HD), jnp.float32),
                 pltpu.VMEM((block, HD), jnp.float32),
-                pltpu.VMEM((SIDE * frames * rows, HD), jnp.float32),
+                pltpu.VMEM((math.lcm(frames * rows, block), HD), jnp.float32),
                 pltpu.VMEM((length, HD), jnp.bfloat16),
             ],
         ),
@@ -250,38 +249,38 @@
     )(*parts)
 
 
-def hand_kernel(ends, *refs):
+def hand_kernel(slot, place, *refs):
     *behind, fresh, _, out = refs
 
-    @pl.when(ends[1] != 0)
+    @pl.when(place[2] != 0)
     def _():
         for head, part in enumerate(behind):
             for group in range(part.shape[0]):
                 at = (group * len(behind) + head) * HD
                 out[0, :, at : at + HD] = part[group]
 
-    @pl.when(ends[1] == 0)
+    @pl.when(place[2] == 0)
     def _():
         out[0] = fresh[...]
 
 
-def hand_over(ends, behind, fresh, gated):
+def hand_over(slot, place, behind, fresh, gated):
     rows, inner = fresh.shape
-    part = pl.BlockSpec(behind[0].shape, lambda n, _: (0, 0, 0))
+    part = pl.BlockSpec(behind[0].shape, lambda n, *_: (0, 0, 0))
     return pl.pallas_call(
         hand_kernel,
         grid_spec=pltpu.PrefetchScalarGridSpec(
-            num_scalar_prefetch=1,
+            num_scalar_prefetch=2,
             grid=(1,),
             in_specs=[part] * len(behind)
-            + [pl.BlockSpec((rows, inner), lambda n, _: (0, 0)), pl.BlockSpec(memory_space=pl.ANY)],
-            out_specs=pl.BlockSpec((1, rows, inner), lambda n, ends: (ends[0], 0, 0)),
+            + [pl.BlockSpec((rows, inner), lambda n, *_: (0, 0)), pl.BlockSpec(memory_space=pl.ANY)],
+            out_specs=pl.BlockSpec((1, rows, inner), lambda n, slot, _: (slot[0], 0, 0)),
         ),
         out_shape=jax.ShapeDtypeStruct(gated.shape, gated.dtype),
-        input_output_aliases={len(behind) + 2: 0},
+        input_output_aliases={len(behind) + 3: 0},
         compiler_params=pltpu.CompilerParams(vmem_limit_bytes=60 * MIB),
         name="hand_over",
-    )(ends, *behind, fresh, gated)
+    )(slot, place, *behind, fresh, gated)
 
 
 def level_gate(steps, gate_weight):
@@ -295,14 +294,12 @@
 def shards(query, key, value, qk_gain, timesteps, gate_weight, slot, fresh):
     index = lax.axis_index("seq")
     section = lax.axis_index("section")
-    place = jnp.stack([index // SIDE, index % SIDE]).astype(jnp.int32)
-    ends = jnp.stack([slot[0], section]).astype(jnp.int32)
+    place = jnp.stack([index // SIDE, index % SIDE, section]).astype(jnp.int32)
     columns = lax.dynamic_slice_in_dim(gate_weight, index * (2 * HD), 2 * HD, 1)
     gate = level_gate(timesteps, columns)
-    prepared = prepare(place, query, key, value, qk_gain)
-    ahead, back = list(prepared[:SIDE]), list(prepared[SIDE:])
+    ahead = list(prepare(0, place, query, key, value, qk_gain))
+    back = list(prepare(1, after(place, ahead[0]), query, key, value, qk_gain))
     back = first_stage(back, "x")
-    ahead[2] = after(ahead[2], back[2])
     ahead = first_stage(ahead, "z")
     columns_of_z = [[x * SIDE + z for z in range(SIDE)] for x in range(SIDE)]
     back[3] = after(back[3], ahead[1], ahead[3])
@@ -312,11 +309,11 @@
     parts, behind, before = [], [], qk_gain
     for head, operands in enumerate((sent, [direct])):
         before = attend(place, gate[:, head * HD : (head + 1) * HD], before, *operands)
-        returned = exchange(before)
+        returned = exchange(after(before, *parts))
         leaving = leaving_frame(slot, returned)
         behind.append(lax.ppermute(leaving, "section", [(n, n + 1) for n in range(sections - 1)]))
         parts.append(returned)
-    return hand_over(ends, behind, fresh, assemble(parts))
+    return hand_over(slot, place, behind, fresh, assemble(parts))
 
 
 def solution(mesh):

time: 192 us -> 190 us (0.990)
  Pallas kernels: 44.4 us -> 47.9 us
  starting transfers between devices: 63.4 us -> 60.5 us
    all_to_all x3, starting transfers between devices: 31.7 us -> 18.1 us  [exchange(): lax.all_to_all(pieces, 'seq', split_axis=0, concat_axis=0, tiled=True, **...]
    ppermute x9, starting transfers between devices: 19.9 us -> 28.6 us  [moved(): return lax.ppermute(value, 'seq', pairs)]
    pallas_call x1 -> x2, Pallas kernels: 6.97 us -> 11.6 us  [prepare(): pl.pallas_call(functools.partial(prepare_kernel, head), grid_spec=pltpu.P...]
    ppermute x2, starting transfers between devices: 11.8 us -> 13.8 us  [shards(): lax.ppermute(leaving, 'section', [(n, n + 1) for n in range(sections - 1)])]
  transfers between devices with their start and end apart: 14 -> 14, of which waited for: 8 -> 9; matrix products, arithmetic and copies ran while one was open for 6% -> 5% of each run, Pallas kernels for 18% -> 21%
where the time goes in v7:
time: 190 us; the launch traced here: 189 us
  waiting for transfers between devices  68.5 us (36%)
  starting transfers between devices  60.5 us (32%)
  Pallas kernels  47.9 us (25%)
  local copies, waits for them, and re-layouts  5.86 us (3%)
  other arithmetic  5.45 us (3%)
    ppermute x9, waiting for transfers between devices, moved(): return lax.ppermute(value, 'seq', pairs)  45.6 us
    pallas_call x2, Pallas kernels, attend(): pl.pallas_call(functools.partial(attend_kernel, len(sent)), grid_spec=plt...  30.2 us
    ppermute x9, starting transfers between devices, moved(): return lax.ppermute(value, 'seq', pairs)  28.6 us
    all_to_all x3, waiting for transfers between devices, exchange(): lax.all_to_all(pieces, 'seq', split_axis=0, concat_axis=0, tiled=True, **...  22.9 us
    all_to_all x3, starting transfers between devices, exchange(): lax.all_to_all(pieces, 'seq', split_axis=0, concat_axis=0, tiled=True, **...  18.1 us
    ppermute x2, starting transfers between devices, shards(): lax.ppermute(leaving, 'section', [(n, n + 1) for n in range(sections - 1)])  13.8 us
    pallas_call x2, Pallas kernels, prepare(): pl.pallas_call(functools.partial(prepare_kernel, head), grid_spec=pltpu.P...  11.6 us
  transfers between devices with their start and end apart: 14, of which 9 were waited for; matrix products, arithmetic and copies ran while one was open for 5% of the time, Pallas kernels for 21%

profile of v7, /device:TPU:17, one launch (start us, length us, event | category | flops | bytes accessed | tf_op | source)
XLA Modules:
  0.0 189.2 jit_solution(13700472267566537616)
XLA Ops:
  0.0 0.0 copy-start
  0.0 0.7 pad_add_fusion.place
  0.7 5.7 %prepare.2 = (bf16[4,3,8,24,128]{4,3,2,1,0:T(8,128)(2,1)}, bf16[4,3,8,24,128]{4,3,2,1,0:T(8,128)(2,1)}, bf16[4,3,8,24,128]{4,3,2,1,0:T(8,128)(2,1)}, bf16[4,3,8,24,128]{4,3,2,1,0:T(8,128)(2,1)}) custom-call(s32[3]{0:T(128)} %pad_add_fusion.place, bf16[8,24,4096]{2,1,0:T(8,128)(2,1)} %q_ref.3, bf16[8,24,4096]{2,1,0:T(8,128)(2,1)} %k_ref.3, ...), custom_call_target="tpu_custom_call" | custom-call | flops 7864320 | bytes 9437184 | tf_op jit(solution)/shard_map/prepare/pallas_call | solution.py:88
  6.3 3.0 %collective-permute-start = (bf16[4,3,8,24,128]{4,3,2,1,0:T(8,128)(2,1)}, bf16[4,3,8,24,128]{4,3,2,1,0:T(8,128)(2,1)}, u32[]{:S(2)}, u32[]{:S(2)}) collective-permute-start(bf16[4,3,8,24,128]{4,3,2,1,0:T(8,128)(2,1)} %get-tuple-element.17), channel_id=1, source_target_pairs={{0,1},{1,2},{2,3},{3,0},{4,5},{5,6},{6,7},{7,4},{8,9},{9,10},{10,1... | collective-permute-start | bytes 1769480 | tf_op jit(solution)/shard_map/ppermute | solution.py:28
  9.3 3.1 %collective-permute-start.2 = (bf16[4,3,8,24,128]{4,3,2,1,0:T(8,128)(2,1)}, bf16[4,3,8,24,128]{4,3,2,1,0:T(8,128)(2,1)}, u32[]{:S(2)}, u32[]{:S(2)}) collective-permute-start(bf16[4,3,8,24,128]{4,3,2,1,0:T(8,128)(2,1)} %get-tuple-element.19), channel_id=1, source_target_pairs={{0,3},{1,0},{2,1},{3,2},{4,7},{5,4},{6,5},{7,6},{8,11},{9,8},{10,9... | collective-permute-start | bytes 1769480 | tf_op jit(solution)/shard_map/ppermute | solution.py:28
  12.4 0.0 copy-start.2
  12.4 5.9 %prepare.3 = (bf16[4,3,8,24,128]{4,3,2,1,0:T(8,128)(2,1)}, bf16[4,3,8,24,128]{4,3,2,1,0:T(8,128)(2,1)}, bf16[4,3,8,24,128]{4,3,2,1,0:T(8,128)(2,1)}, bf16[4,3,8,24,128]{4,3,2,1,0:T(8,128)(2,1)}) custom-call(s32[3]{0:T(128)} %pad_add_fusion.place, bf16[8,24,4096]{2,1,0:T(8,128)(2,1)} %q_ref.3, bf16[8,24,4096]{2,1,0:T(8,128)(2,1)} %k_ref.3, ...), custom_call_target="tpu_custom_call" | custom-call | flops 7864320 | bytes 9437184 | tf_op jit(solution)/shard_map/prepare/pallas_call | solution.py:88
  18.3 2.5 %collective-permute-start.9 = (bf16[4,3,8,24,128]{4,3,2,1,0:T(8,128)(2,1)}, bf16[4,3,8,24,128]{4,3,2,1,0:T(8,128)(2,1)S(1)}, u32[]{:S(2)}, u32[]{:S(2)}) collective-permute-start(bf16[4,3,8,24,128]{4,3,2,1,0:T(8,128)(2,1)} %get-tuple-element.24), channel_id=1, source_target_pairs={{0,12},{1,13},{2,14},{3,15},{4,0},{5,1},{6,2},{7,3},{8,4},{9,5},{1... | collective-permute-start | bytes 1769480 | tf_op jit(solution)/shard_map/ppermute | solution.py:28
  20.8 0.0 collective-permute-start.7
  20.8 1.7 collective-permute-start.8
  22.6 0.0 copy-done.2
  22.6 7.5 %collective-permute-done.refs_1_ = bf16[4,3,8,24,128]{4,3,2,1,0:T(8,128)(2,1)} collective-permute-done((bf16[4,3,8,24,128]{4,3,2,1,0:T(8,128)(2,1)}, bf16[4,3,8,24,128]{4,3,2,1,0:T(8,128)(2,1)}, u32[]{:S(2)}, u32[]{:S(2)}) %collective-permute-start) | collective-permute-done | bytes 589856 | tf_op jit(solution)/shard_map/ppermute | solution.py:28
  30.1 12.9 %collective-permute-start.1 = (bf16[4,3,8,24,128]{4,3,2,1,0:T(8,128)(2,1)}, bf16[4,3,8,24,128]{4,3,2,1,0:T(8,128)(2,1)S(1)}, u32[]{:S(2)}, u32[]{:S(2)}) collective-permute-start(bf16[4,3,8,24,128]{4,3,2,1,0:T(8,128)(2,1)} %get-tuple-element.18), channel_id=1, source_target_pairs={{0,2},{1,3},{2,0},{3,1},{4,6},{5,7},{6,4},{7,5},{8,10},{9,11},{10,... | collective-permute-start | bytes 1769480 | tf_op jit(solution)/shard_map/ppermute | solution.py:28
  43.0 0.0 collective-permute-done.2.refs_3_
  43.0 0.0 collective-permute-done.9
  43.0 0.0 collective-permute-done.7
  43.0 4.6 %collective-permute-done.8 = bf16[4,3,8,24,128]{4,3,2,1,0:T(8,128)(2,1)S(1)} collective-permute-done((bf16[4,3,8,24,128]{4,3,2,1,0:T(8,128)(2,1)}, bf16[4,3,8,24,128]{4,3,2,1,0:T(8,128)(2,1)S(1)}, u32[]{:S(2)}, u32[]{:S(2)}) %collective-permute-start.8) | collective-permute-done | bytes 589856 | tf_op jit(solution)/shard_map/ppermute | solution.py:28
  47.6 2.8 %pad_maximum_fusion = bf16[4,4,3,8,24,128]{5,4,3,2,1,0:T(8,128)(2,1)} fusion(bf16[4,1,3,8,24,128]{5,4,3,2,1,0:T(8,128)(2,1)S(1)} %bitcast.16, bf16[4,1,3,8,24,128]{5,4,3,2,1,0:T(8,128)(2,1)S(1)} %bitcast.18, bf16[4,1,3,8,24,128]{5,4,3,2,1,0:T(8,128)(2,1)S(1)} %bitcast.17, bf16[4,1,3,8,24,128]{5,4,3,2,1,0:T(8,128)(2,1)} %bitcast.15), kind=kLoop, calls=%fused_computation | loop fusion | flops 3538944 | bytes 4718592 | tf_op jit(solution)/shard_map/stack | solution.py:306
  50.4 5.4 %all-to-all-start.1 = ((bf16[4,4,3,8,24,128]{5,4,3,2,1,0:T(8,128)(2,1)}), bf16[4,4,3,8,24,128]{5,4,3,2,1,0:T(8,128)(2,1)}, u32[]{:S(2)}, u32[]{:S(2)}) async-start(bf16[4,4,3,8,24,128]{5,4,3,2,1,0:T(8,128)(2,1)} %pad_maximum_fusion), calls=%async_computation.1 | async-start | bytes 4718592 | tf_op jit(solution)/shard_map/all_to_all | solution.py:32
  55.7 1.1 fusion.10
  56.8 1.1 fusion.12
  58.0 0.0 copy-start.6
  58.0 10.8 %collective-permute-done.1.refs_2_ = bf16[4,3,8,24,128]{4,3,2,1,0:T(8,128)(2,1)S(1)} collective-permute-done((bf16[4,3,8,24,128]{4,3,2,1,0:T(8,128)(2,1)}, bf16[4,3,8,24,128]{4,3,2,1,0:T(8,128)(2,1)S(1)}, u32[]{:S(2)}, u32[]{:S(2)}) %collective-permute-start.1) | collective-permute-done | bytes 589856 | tf_op jit(solution)/shard_map/ppermute | solution.py:28
  68.8 0.0 copy-start.3
  68.8 0.8 copy-done.3
  69.6 0.1 pad_maximum_fusion.1
  69.7 2.4 %collective-permute-start.3 = (bf16[4,3,8,24,128]{4,3,2,1,0:T(8,128)(2,1)S(1)}, bf16[4,3,8,24,128]{4,3,2,1,0:T(8,128)(2,1)}, u32[]{:S(2)}, u32[]{:S(2)}) collective-permute-start(bf16[4,3,8,24,128]{4,3,2,1,0:T(8,128)(2,1)S(1)} %pad_maximum_fusion.1), channel_id=1, source_target_pairs={{0,4},{1,5},{2,6},{3,7},{4,8},{5,9},{6,10},{7,11},{8,12},{9,13},{1... | collective-permute-start | bytes 1769480 | tf_op jit(solution)/shard_map/ppermute | solution.py:28
  72.1 0.9 pad_maximum_fusion.2
  73.0 2.4 %collective-permute-start.4 = (bf16[4,3,8,24,128]{4,3,2,1,0:T(8,128)(2,1)}, bf16[4,3,8,24,128]{4,3,2,1,0:T(8,128)(2,1)}, u32[]{:S(2)}, u32[]{:S(2)}) collective-permute-start(bf16[4,3,8,24,128]{4,3,2,1,0:T(8,128)(2,1)} %pad_maximum_fusion.2), channel_id=1, source_target_pairs={{0,8},{1,9},{2,10},{3,11},{4,12},{5,13},{6,14},{7,15},{8,0},{9,1},... | collective-permute-start | bytes 1769480 | tf_op jit(solution)/shard_map/ppermute | solution.py:28
  75.4 0.9 pad_maximum_fusion.3
  76.3 0.6 collective-permute-start.5
  76.9 0.0 copy-done.6
  76.9 0.1 fusion.2
  77.0 0.0 copy-done
  77.0 0.2 fusion
  77.2 0.6 fusion.13
  77.8 8.7 %collective-permute-done.3.refs_4_ = bf16[4,3,8,24,128]{4,3,2,1,0:T(8,128)(2,1)} collective-permute-done((bf16[4,3,8,24,128]{4,3,2,1,0:T(8,128)(2,1)S(1)}, bf16[4,3,8,24,128]{4,3,2,1,0:T(8,128)(2,1)}, u32[]{:S(2)}, u32[]{:S(2)}) %collective-permute-start.3) | collective-permute-done | bytes 589856 | tf_op jit(solution)/shard_map/ppermute | solution.py:28
  86.5 13.5 %collective-permute-done.4.refs_5_ = bf16[4,3,8,24,128]{4,3,2,1,0:T(8,128)(2,1)} collective-permute-done((bf16[4,3,8,24,128]{4,3,2,1,0:T(8,128)(2,1)}, bf16[4,3,8,24,128]{4,3,2,1,0:T(8,128)(2,1)}, u32[]{:S(2)}, u32[]{:S(2)}) %collective-permute-start.4) | collective-permute-done | bytes 589856 | tf_op jit(solution)/shard_map/ppermute | solution.py:28
  100.0 0.6 collective-permute-done.5.refs_6_
  100.5 15.1 %attend.2._ = bf16[16,8,24,128]{3,2,1,0:T(8,128)(2,1)} custom-call(s32[3]{0:T(128)} %pad_add_fusion.place, f32[8,128]{1,0:T(8,128)} %get-tuple-element.40.gate_ref, f32[2,4096]{1,0:T(2,128)} %gain_ref.3, bf16[4,3,8,24,128]{4,3,2,1,0:T(8,128)(2,1)} %get-tuple-element.16.refs_0_, bf16[4,3,8,24,128]{4,3,2,1,0:T(8,128)(2,1)} %collective-permute-done.refs_1_, ...), custom_call_target="tpu_custom_call" | custom-call | flops 20535312384 | bytes 3072 | tf_op jit(solution)/shard_map/attend/pallas_call | solution.py:194
  115.7 4.9 %all-to-all-done.1.refs_0_ = bf16[4,4,3,8,24,128]{5,4,3,2,1,0:T(8,128)(2,1)} async-done(((bf16[4,4,3,8,24,128]{5,4,3,2,1,0:T(8,128)(2,1)}), bf16[4,4,3,8,24,128]{5,4,3,2,1,0:T(8,128)(2,1)}, u32[]{:S(2)}, u32[]{:S(2)}) %all-to-all-start.1) | async-done | bytes 2359328 | tf_op jit(solution)/shard_map/all_to_all | solution.py:32
  120.5 8.0 %all-to-all-start = ((bf16[16,8,24,128]{3,2,1,0:T(8,128)(2,1)}), bf16[16,8,24,128]{3,2,1,0:T(8,128)(2,1)S(1)}, u32[]{:S(2)}, u32[]{:S(2)}) async-start(bf16[16,8,24,128]{3,2,1,0:T(8,128)(2,1)} %attend.2._), calls=%async_computation | async-start | bytes 1572864 | tf_op jit(solution)/shard_map/all_to_all | solution.py:32
  128.6 15.1 %attend.3 = bf16[16,8,24,128]{3,2,1,0:T(8,128)(2,1)} custom-call(s32[3]{0:T(128)} %pad_add_fusion.place, f32[8,128]{1,0:T(8,128)} %get-tuple-element.39.gate_ref, bf16[16,8,24,128]{3,2,1,0:T(8,128)(2,1)} %attend.2._, bf16[4,4,3,8,24,128]{5,4,3,2,1,0:T(8,128)(2,1)} %all-to-all-done.1.refs_0_), custom_call_target="tpu_custom_call" | custom-call | flops 33822867456 | bytes 3145728 | tf_op jit(solution)/shard_map/attend/pallas_call | solution.py:194
  143.7 4.8 %all-to-all-done.refs_0_ = bf16[16,8,24,128]{3,2,1,0:T(8,128)(2,1)S(1)} async-done(((bf16[16,8,24,128]{3,2,1,0:T(8,128)(2,1)}), bf16[16,8,24,128]{3,2,1,0:T(8,128)(2,1)S(1)}, u32[]{:S(2)}, u32[]{:S(2)}) %all-to-all-start) | async-done | bytes 786464 | tf_op jit(solution)/shard_map/all_to_all | solution.py:32
  148.4 0.0 copy-start.1
  148.4 4.7 %all-to-all-start.2 = ((bf16[16,8,24,128]{3,2,1,0:T(8,128)(2,1)}), bf16[16,8,24,128]{3,2,1,0:T(8,128)(2,1)}, u32[]{:S(2)}, u32[]{:S(2)}) async-start(bf16[16,8,24,128]{3,2,1,0:T(8,128)(2,1)} %attend.3), calls=%async_computation.2 | async-start | bytes 1572864 | tf_op jit(solution)/shard_map/all_to_all | solution.py:32
  153.8 5.1 %collective-permute-start.6 = (bf16[16,24,128]{2,1,0:T(8,128)(2,1)S(1)}, bf16[16,24,128]{2,1,0:T(8,128)(2,1)S(1)}, u32[]{:S(2)}, u32[]{:S(2)}) collective-permute-start(bf16[16,24,128]{2,1,0:T(8,128)(2,1)S(1)} %dynamic-slice_bitcast_fusion.1), channel_id=1, source_target_pairs={{0,16},{16,32},{32,48},{48,64},{64,80},{80,96},{96,112},{112,128},... | collective-permute-start | bytes 294920 | tf_op jit(solution)/shard_map/ppermute | solution.py:314
  158.9 13.3 %all-to-all-done.2.refs_1_ = bf16[16,8,24,128]{3,2,1,0:T(8,128)(2,1)} async-done(((bf16[16,8,24,128]{3,2,1,0:T(8,128)(2,1)}), bf16[16,8,24,128]{3,2,1,0:T(8,128)(2,1)}, u32[]{:S(2)}, u32[]{:S(2)}) %all-to-all-start.2) | async-done | bytes 786464 | tf_op jit(solution)/shard_map/all_to_all | solution.py:32
  172.2 0.9 dynamic-slice_bitcast_fusion
  173.1 8.7 %collective-permute-start.10 = (bf16[16,24,128]{2,1,0:T(8,128)(2,1)S(1)}, bf16[16,24,128]{2,1,0:T(8,128)(2,1)S(1)}, u32[]{:S(2)}, u32[]{:S(2)}) collective-permute-start(bf16[16,24,128]{2,1,0:T(8,128)(2,1)S(1)} %dynamic-slice_bitcast_fusion), channel_id=1, source_target_pairs={{0,16},{16,32},{32,48},{48,64},{64,80},{80,96},{96,112},{112,128},... | collective-permute-start | bytes 294920 | tf_op jit(solution)/shard_map/ppermute | solution.py:314
  181.8 0.0 copy-done.1
  181.8 3.7 %assemble.1.refs_3_ = bf16[8,24,4096]{2,1,0:T(8,128)(2,1)} custom-call(bf16[16,8,24,128]{3,2,1,0:T(8,128)(2,1)} %copy-done.1, bf16[16,8,24,128]{3,2,1,0:T(8,128)(2,1)} %all-to-all-done.2.refs_1_), custom_call_target="tpu_custom_call" | custom-call | bytes 3145728 | tf_op jit(solution)/shard_map/assemble/pallas_call | solution.py:240
  185.5 0.0 collective-permute-done.6.refs_0_
  185.5 0.0 copy-start.4
  185.5 0.0 collective-permute-done.10.refs_1_
  185.5 0.6 copy-done.4
  186.2 0.0 copy-start.5
  186.2 0.6 copy-done.5
  186.8 2.4 %hand_over.1 = bf16[8,24,4096]{2,1,0:T(8,128)(2,1)} custom-call(s32[1]{0:T(128)} %copy.11.slot, s32[3]{0:T(128)} %pad_add_fusion.place, bf16[16,24,128]{2,1,0:T(8,128)(2,1)} %copy-done.4, bf16[16,24,128]{2,1,0:T(8,128)(2,1)} %copy-done.5, bf16[24,4096]{1,0:T(8,128)(2,1)} %refs_2_.1, bf16[8,24,4096]{2,1,0:T(8,128)(2,1)} %assemble.1.refs_3_), custom_call_target="tpu_custom_call", output_to_operand_aliasing={{}: (5, {})} | custom-call | tf_op jit(solution)/shard_map/hand_over/pallas_call | solution.py:270
  (5 shorter events, 0.1 us)
Async XLA Ops:
  0.0 77.0 %copy-start = (bf16[256,4096]{1,0:T(8,128)(2,1)S(1)}, bf16[256,4096]{1,0:T(8,128)(2,1)}, u32[]{:S(2)}) copy-start(bf16[256,4096]{1,0:T(8,128)(2,1)} %param.13) | copy-start | bytes 6291460
  6.3 23.8 %collective-permute-start = (bf16[4,3,8,24,128]{4,3,2,1,0:T(8,128)(2,1)}, bf16[4,3,8,24,128]{4,3,2,1,0:T(8,128)(2,1)}, u32[]{:S(2)}, u32[]{:S(2)}) collective-permute-start(bf16[4,3,8,24,128]{4,3,2,1,0:T(8,128)(2,1)} %get-tuple-element.17), channel_id=1, source_target_pairs={{0,1},{1,2},{2,3},{3,0},{4,5},{5,6},{6,7},{7,4},{8,9},{9,10},{10,1... | collective-permute-start | bytes 1769480 | tf_op jit(solution)/shard_map/ppermute | solution.py:28
  9.3 33.7 %collective-permute-start.2 = (bf16[4,3,8,24,128]{4,3,2,1,0:T(8,128)(2,1)}, bf16[4,3,8,24,128]{4,3,2,1,0:T(8,128)(2,1)}, u32[]{:S(2)}, u32[]{:S(2)}) collective-permute-start(bf16[4,3,8,24,128]{4,3,2,1,0:T(8,128)(2,1)} %get-tuple-element.19), channel_id=1, source_target_pairs={{0,3},{1,0},{2,1},{3,2},{4,7},{5,4},{6,5},{7,6},{8,11},{9,8},{10,9... | collective-permute-start | bytes 1769480 | tf_op jit(solution)/shard_map/ppermute | solution.py:28
  12.4 10.1 %copy-start.2 = (bf16[4,3,8,24,128]{4,3,2,1,0:T(8,128)(2,1)S(1)}, bf16[4,3,8,24,128]{4,3,2,1,0:T(8,128)(2,1)}, u32[]{:S(2)}) copy-start(bf16[4,3,8,24,128]{4,3,2,1,0:T(8,128)(2,1)} %get-tuple-element.16.refs_0_) | copy-start | bytes 1769476
  18.3 24.7 %collective-permute-start.9 = (bf16[4,3,8,24,128]{4,3,2,1,0:T(8,128)(2,1)}, bf16[4,3,8,24,128]{4,3,2,1,0:T(8,128)(2,1)S(1)}, u32[]{:S(2)}, u32[]{:S(2)}) collective-permute-start(bf16[4,3,8,24,128]{4,3,2,1,0:T(8,128)(2,1)} %get-tuple-element.24), channel_id=1, source_target_pairs={{0,12},{1,13},{2,14},{3,15},{4,0},{5,1},{6,2},{7,3},{8,4},{9,5},{1... | collective-permute-start | bytes 1769480 | tf_op jit(solution)/shard_map/ppermute | solution.py:28
  20.8 22.2 %collective-permute-start.7 = (bf16[4,3,8,24,128]{4,3,2,1,0:T(8,128)(2,1)}, bf16[4,3,8,24,128]{4,3,2,1,0:T(8,128)(2,1)S(1)}, u32[]{:S(2)}, u32[]{:S(2)}) collective-permute-start(bf16[4,3,8,24,128]{4,3,2,1,0:T(8,128)(2,1)} %get-tuple-element.22), channel_id=1, source_target_pairs={{0,4},{1,5},{2,6},{3,7},{4,8},{5,9},{6,10},{7,11},{8,12},{9,13},{1... | collective-permute-start | bytes 1769480 | tf_op jit(solution)/shard_map/ppermute | solution.py:28
  20.8 26.7 %collective-permute-start.8 = (bf16[4,3,8,24,128]{4,3,2,1,0:T(8,128)(2,1)}, bf16[4,3,8,24,128]{4,3,2,1,0:T(8,128)(2,1)S(1)}, u32[]{:S(2)}, u32[]{:S(2)}) collective-permute-start(bf16[4,3,8,24,128]{4,3,2,1,0:T(8,128)(2,1)} %get-tuple-element.23), channel_id=1, source_target_pairs={{0,8},{1,9},{2,10},{3,11},{4,12},{5,13},{6,14},{7,15},{8,0},{9,1},... | collective-permute-start | bytes 1769480 | tf_op jit(solution)/shard_map/ppermute | solution.py:28
  30.1 38.7 %collective-permute-start.1 = (bf16[4,3,8,24,128]{4,3,2,1,0:T(8,128)(2,1)}, bf16[4,3,8,24,128]{4,3,2,1,0:T(8,128)(2,1)S(1)}, u32[]{:S(2)}, u32[]{:S(2)}) collective-permute-start(bf16[4,3,8,24,128]{4,3,2,1,0:T(8,128)(2,1)} %get-tuple-element.18), channel_id=1, source_target_pairs={{0,2},{1,3},{2,0},{3,1},{4,6},{5,7},{6,4},{7,5},{8,10},{9,11},{10,... | collective-permute-start | bytes 1769480 | tf_op jit(solution)/shard_map/ppermute | solution.py:28
  50.4 70.2 %all-to-all-start.1 = ((bf16[4,4,3,8,24,128]{5,4,3,2,1,0:T(8,128)(2,1)}), bf16[4,4,3,8,24,128]{5,4,3,2,1,0:T(8,128)(2,1)}, u32[]{:S(2)}, u32[]{:S(2)}) async-start(bf16[4,4,3,8,24,128]{5,4,3,2,1,0:T(8,128)(2,1)} %pad_maximum_fusion), calls=%async_computation.1 | async-start | bytes 4718592 | tf_op jit(solution)/shard_map/all_to_all | solution.py:32
  58.0 18.9 %copy-start.6 = (s32[8]{0:T(128)S(1)}, s32[8]{0:T(128)}, u32[]{:S(2)}) copy-start(s32[8]{0:T(128)} %param.12) | copy-start | bytes 100
  68.8 0.8 copy-start.3
  69.7 16.8 %collective-permute-start.3 = (bf16[4,3,8,24,128]{4,3,2,1,0:T(8,128)(2,1)S(1)}, bf16[4,3,8,24,128]{4,3,2,1,0:T(8,128)(2,1)}, u32[]{:S(2)}, u32[]{:S(2)}) collective-permute-start(bf16[4,3,8,24,128]{4,3,2,1,0:T(8,128)(2,1)S(1)} %pad_maximum_fusion.1), channel_id=1, source_target_pairs={{0,4},{1,5},{2,6},{3,7},{4,8},{5,9},{6,10},{7,11},{8,12},{9,13},{1... | collective-permute-start | bytes 1769480 | tf_op jit(solution)/shard_map/ppermute | solution.py:28
  73.0 27.0 %collective-permute-start.4 = (bf16[4,3,8,24,128]{4,3,2,1,0:T(8,128)(2,1)}, bf16[4,3,8,24,128]{4,3,2,1,0:T(8,128)(2,1)}, u32[]{:S(2)}, u32[]{:S(2)}) collective-permute-start(bf16[4,3,8,24,128]{4,3,2,1,0:T(8,128)(2,1)} %pad_maximum_fusion.2), channel_id=1, source_target_pairs={{0,8},{1,9},{2,10},{3,11},{4,12},{5,13},{6,14},{7,15},{8,0},{9,1},... | collective-permute-start | bytes 1769480 | tf_op jit(solution)/shard_map/ppermute | solution.py:28
  76.3 24.3 %collective-permute-start.5 = (bf16[4,3,8,24,128]{4,3,2,1,0:T(8,128)(2,1)}, bf16[4,3,8,24,128]{4,3,2,1,0:T(8,128)(2,1)}, u32[]{:S(2)}, u32[]{:S(2)}) collective-permute-start(bf16[4,3,8,24,128]{4,3,2,1,0:T(8,128)(2,1)} %pad_maximum_fusion.3), channel_id=1, source_target_pairs={{0,12},{1,13},{2,14},{3,15},{4,0},{5,1},{6,2},{7,3},{8,4},{9,5},{1... | collective-permute-start | bytes 1769480 | tf_op jit(solution)/shard_map/ppermute | solution.py:28
  120.5 27.9 %all-to-all-start = ((bf16[16,8,24,128]{3,2,1,0:T(8,128)(2,1)}), bf16[16,8,24,128]{3,2,1,0:T(8,128)(2,1)S(1)}, u32[]{:S(2)}, u32[]{:S(2)}) async-start(bf16[16,8,24,128]{3,2,1,0:T(8,128)(2,1)} %attend.2._), calls=%async_computation | async-start | bytes 1572864 | tf_op jit(solution)/shard_map/all_to_all | solution.py:32
  148.4 33.4 %copy-start.1 = (bf16[16,8,24,128]{3,2,1,0:T(8,128)(2,1)}, bf16[16,8,24,128]{3,2,1,0:T(8,128)(2,1)S(1)}, u32[]{:S(2)}) copy-start(bf16[16,8,24,128]{3,2,1,0:T(8,128)(2,1)S(1)} %all-to-all-done.refs_0_) | copy-start | bytes 2359300
  148.4 23.8 %all-to-all-start.2 = ((bf16[16,8,24,128]{3,2,1,0:T(8,128)(2,1)}), bf16[16,8,24,128]{3,2,1,0:T(8,128)(2,1)}, u32[]{:S(2)}, u32[]{:S(2)}) async-start(bf16[16,8,24,128]{3,2,1,0:T(8,128)(2,1)} %attend.3), calls=%async_computation.2 | async-start | bytes 1572864 | tf_op jit(solution)/shard_map/all_to_all | solution.py:32
  153.8 31.7 %collective-permute-start.6 = (bf16[16,24,128]{2,1,0:T(8,128)(2,1)S(1)}, bf16[16,24,128]{2,1,0:T(8,128)(2,1)S(1)}, u32[]{:S(2)}, u32[]{:S(2)}) collective-permute-start(bf16[16,24,128]{2,1,0:T(8,128)(2,1)S(1)} %dynamic-slice_bitcast_fusion.1), channel_id=1, source_target_pairs={{0,16},{16,32},{32,48},{48,64},{64,80},{80,96},{96,112},{112,128},... | collective-permute-start | bytes 294920 | tf_op jit(solution)/shard_map/ppermute | solution.py:314
  173.1 12.4 %collective-permute-start.10 = (bf16[16,24,128]{2,1,0:T(8,128)(2,1)S(1)}, bf16[16,24,128]{2,1,0:T(8,128)(2,1)S(1)}, u32[]{:S(2)}, u32[]{:S(2)}) collective-permute-start(bf16[16,24,128]{2,1,0:T(8,128)(2,1)S(1)} %dynamic-slice_bitcast_fusion), channel_id=1, source_target_pairs={{0,16},{16,32},{32,48},{48,64},{64,80},{80,96},{96,112},{112,128},... | collective-permute-start | bytes 294920 | tf_op jit(solution)/shard_map/ppermute | solution.py:314
  185.5 0.6 copy-start.4
  186.2 0.6 copy-start.5

commit v8 on v7

--- a/solution.py
+++ b/solution.py
@@ -102,9 +102,9 @@
     )(place, query, key, value, qk_gain)
 
 
-def attend_kernel(count, place, gate_ref, _, *refs):
+def attend_kernel(count, slot, place, gate_ref, _, *refs):
     sent = refs[:count]
-    out, q_all, k_all, v_all, s_even, s_odd, m_even, m_odd, gates, result = refs[count:]
+    out, leaving, q_all, k_all, v_all, s_even, s_odd, m_even, m_odd, gates, result = refs[count:]
     frames, rows = sent[0].shape[-3:-1]
     tokens = frames * rows
     length = SIDE * SIDE * tokens
@@ -181,24 +181,29 @@
     step(blocks - 1, *odd, blocks - 2, *even)
     step(None, None, None, blocks - 1, *odd)
     for n in range(SIDE * SIDE):
-        out[part_of(n)[2]] = result[n * tokens : (n + 1) * tokens, :].reshape(frames, rows, HD)
-
-
-def attend(place, gate, before, *sent):
+        source = part_of(n)[2]
+        out[source] = result[n * tokens : (n + 1) * tokens, :].reshape(frames, rows, HD)
+        leaving[source] = out[source, slot[0]]
+
+
+def attend(slot, place, gate, before, *sent):
     frames, rows = sent[0].shape[-3:-1]
     length = SIDE * SIDE * frames * rows
     block = BLOCK
-    one = pl.BlockSpec((1, 3, frames, rows, HD), lambda n, _: (0, 0, 0, 0, 0))
-    whole = pl.BlockSpec((SIDE, 3, frames, rows, HD), lambda n, _: (0, 0, 0, 0, 0))
-    every = pl.BlockSpec((SIDE, SIDE, 3, frames, rows, HD), lambda n, _: (0, 0, 0, 0, 0, 0))
+    one = pl.BlockSpec((1, 3, frames, rows, HD), lambda n, *_: (0, 0, 0, 0, 0))
+    whole = pl.BlockSpec((SIDE, 3, frames, rows, HD), lambda n, *_: (0, 0, 0, 0, 0))
+    every = pl.BlockSpec((SIDE, SIDE, 3, frames, rows, HD), lambda n, *_: (0, 0, 0, 0, 0, 0))
     return pl.pallas_call(
         functools.partial(attend_kernel, len(sent)),
         grid_spec=pltpu.PrefetchScalarGridSpec(
-            num_scalar_prefetch=1,
+            num_scalar_prefetch=2,
             grid=(1,),
-            in_specs=[pl.BlockSpec((frames, HD), lambda n, _: (0, 0)), pl.BlockSpec(memory_space=pl.ANY)]
+            in_specs=[pl.BlockSpec((frames, HD), lambda n, *_: (0, 0)), pl.BlockSpec(memory_space=pl.ANY)]
             + ([every] if len(sent) == 1 else [one] * SIDE + [whole] * (SIDE - 1)),
-            out_specs=pl.BlockSpec((SIDE * SIDE, frames, rows, HD), lambda n, _: (0, 0, 0, 0)),
+            out_specs=[
+                pl.BlockSpec((SIDE * SIDE, frames, rows, HD), lambda n, *_: (0, 0, 0, 0)),
+                pl.BlockSpec((SIDE * SIDE, rows, HD), lambda n, *_: (0, 0, 0)),
+            ],
             scratch_shapes=[
                 pltpu.VMEM((length, HD), jnp.bfloat16),
                 pltpu.VMEM((length, HD), jnp.bfloat16),
@@ -211,76 +216,78 @@
                 pltpu.VMEM((length, HD), jnp.bfloat16),
             ],
         ),
-        out_shape=jax.ShapeDtypeStruct((SIDE * SIDE, frames, rows, HD), jnp.bfloat16),
+        out_shape=[
+            jax.ShapeDtypeStruct((SIDE * SIDE, frames, rows, HD), jnp.bfloat16),
+            jax.ShapeDtypeStruct((SIDE * SIDE, rows, HD), jnp.bfloat16),
+        ],
         compiler_params=pltpu.CompilerParams(vmem_limit_bytes=ATTEND_MIB * MIB),
         cost_estimate=pl.CostEstimate(
             flops=int(17 * length * length * HD) if len(sent) > 1 else 28 * length * length * HD, bytes_accessed=length if len(sent) > 1 else 8 * length * HD, transcendentals=0
         ),
         name="attend",
-    )(place, gate, before, *sent)
-
-
-def leaving_frame(slot, returned):
-    return lax.dynamic_index_in_dim(returned, slot[0], 1, keepdims=False)
-
-
-def assemble_kernel(*refs):
-    *parts, out = refs
-    for head, own in enumerate(parts):
-        for group in range(own.shape[0]):
-            at = (group * len(parts) + head) * HD
-            out[:, :, at : at + HD] = own[group]
-
-
-def assemble(parts):
+    )(slot, place, gate, before, *sent)
+
+
+def hand_kernel(slot, behind, _, out):
+    out[:, 0] = behind[...]
+
+
+def hand_over(slot, behind, result):
+    sources, rows, _ = behind.shape
+    return pl.pallas_call(
+        hand_kernel,
+        grid_spec=pltpu.PrefetchScalarGridSpec(
+            num_scalar_prefetch=1,
+            grid=(1,),
+            in_specs=[
+                pl.BlockSpec(behind.shape, lambda n, _: (0, 0, 0)),
+                pl.BlockSpec(memory_space=pl.ANY),
+            ],
+            out_specs=pl.BlockSpec((sources, 1, rows, HD), lambda n, slot: (0, slot[0], 0, 0)),
+        ),
+        out_shape=jax.ShapeDtypeStruct(result.shape, result.dtype),
+        input_output_aliases={2: 0},
+        compiler_params=pltpu.CompilerParams(vmem_limit_bytes=60 * MIB),
+        name="hand_over",
+    )(slot, behind, result)
+
+
+def assemble_kernel(slot, place, *refs):
+    *parts, fresh, out = refs
+    step = out.shape[0]
+    for n in range(step):
+        new = jnp.logical_and(pl.program_id(0) * step + n == slot[0], place[2] == 0)
+
+        @pl.when(jnp.logical_not(new))
+        def _(n=n):
+            for head, own in enumerate(parts):
+                for group in range(own.shape[0]):
+                    at = (group * len(parts) + head) * HD
+                    out[n, :, at : at + HD] = own[group, n]
+
+        @pl.when(new)
+        def _(n=n):
+            out[n] = fresh[...]
+
+
+def assemble(slot, place, parts, fresh):
     groups, frames, rows, _ = parts[0].shape
-    inner = groups * len(parts) * HD
+    inner = fresh.shape[1]
     step = 2
-    own = pl.BlockSpec((groups, step, rows, HD), lambda n: (0, n, 0, 0))
+    own = pl.BlockSpec((groups, step, rows, HD), lambda n, *_: (0, n, 0, 0))
     return pl.pallas_call(
         assemble_kernel,
-        grid=(frames // step,),
-        in_specs=[own] * len(parts),
-        out_specs=pl.BlockSpec((step, rows, inner), lambda n: (n, 0, 0)),
+        grid_spec=pltpu.PrefetchScalarGridSpec(
+            num_scalar_prefetch=2,
+            grid=(frames // step,),
+            in_specs=[own] * len(parts) + [pl.BlockSpec((rows, inner), lambda n, *_: (0, 0))],
+            out_specs=pl.BlockSpec((step, rows, inner), lambda n, *_: (n, 0, 0)),
+        ),
         out_shape=jax.ShapeDtypeStruct((frames, rows, inner), jnp.bfloat16),
         compiler_params=pltpu.CompilerParams(vmem_limit_bytes=60 * MIB),
         cost_estimate=pl.CostEstimate(flops=0, bytes_accessed=4 * frames * rows * inner, transcendentals=0),
         name="assemble",
-    )(*parts)
-
-
-def hand_kernel(slot, place, *refs):
-    *behind, fresh, _, out = refs
-
-    @pl.when(place[2] != 0)
-    def _():
-        for head, part in enumerate(behind):
-            for group in range(part.shape[0]):
-                at = (group * len(behind) + head) * HD
-                out[0, :, at : at + HD] = part[group]
-
-    @pl.when(place[2] == 0)
-    def _():
-        out[0] = fresh[...]
-
-
-def hand_over(slot, place, behind, fresh, gated):
-    rows, inner = fresh.shape
-    part = pl.BlockSpec(behind[0].shape, lambda n, *_: (0, 0, 0))
-    return pl.pallas_call(
-        hand_kernel,
-        grid_spec=pltpu.PrefetchScalarGridSpec(
-            num_scalar_prefetch=2,
-            grid=(1,),
-            in_specs=[part] * len(behind)
-            + [pl.BlockSpec((rows, inner), lambda n, *_: (0, 0)), pl.BlockSpec(memory_space=pl.ANY)],
-            out_specs=pl.BlockSpec((1, rows, inner), lambda n, slot, _: (slot[0], 0, 0)),
-        ),
-        out_shape=jax.ShapeDtypeStruct(gated.shape, gated.dtype),
-        input_output_aliases={len(behind) + 3: 0},
-        compiler_params=pltpu.CompilerParams(vmem_limit_bytes=60 * MIB),
-        name="hand_over",
-    )(slot, place, *behind, fresh, gated)
+    )(slot, place, *parts, fresh)
 
 
 def level_gate(steps, gate_weight):
@@ -306,14 +313,12 @@
     direct = exchange(jnp.stack(back, axis=1), axis_index_groups=columns_of_z)
     sent = [*ahead, *second_stage(stacked(ahead), "x")]
     sections = lax.axis_size("section")
-    parts, behind, before = [], [], qk_gain
+    parts, before = [], qk_gain
     for head, operands in enumerate((sent, [direct])):
-        before = attend(place, gate[:, head * HD : (head + 1) * HD], before, *operands)
-        returned = exchange(after(before, *parts))
-        leaving = leaving_frame(slot, returned)
-        behind.append(lax.ppermute(leaving, "section", [(n, n + 1) for n in range(sections - 1)]))
-        parts.append(returned)
-    return hand_over(slot, place, behind, fresh, assemble(parts))
+        result, before = attend(slot, place, gate[:, head * HD : (head + 1) * HD], before, *operands)
+        behind = lax.ppermute(before, "section", [(n, n + 1) for n in range(sections - 1)])
+        parts.append(exchange(after(hand_over(slot, behind, result), *parts)))
+    return assemble(slot, place, parts, fresh)
 
 
 def solution(mesh):

time: 190 us -> 194 us (1.021)
  blocking collectives: 0 us -> 30.4 us
  waiting for transfers between devices: 68.5 us -> 48.8 us
  starting transfers between devices: 60.5 us -> 51.6 us
    all_to_all x0 -> x1, blocking collectives: none -> 30.4 us  [exchange(): lax.all_to_all(pieces, 'seq', split_axis=0, concat_axis=0, tiled=True, **...]
    all_to_all x3 -> x2, waiting for transfers between devices: 22.9 us -> 0.01 us  [exchange(): lax.all_to_all(pieces, 'seq', split_axis=0, concat_axis=0, tiled=True, **...]
    ppermute x2, starting transfers between devices: 13.8 us -> 8.78 us  [shards(): lax.ppermute(before, 'section', [(n, n + 1) for n in range(sections - 1)])]
    all_to_all x3 -> x2, starting transfers between devices: 18.1 us -> 14.2 us  [exchange(): lax.all_to_all(pieces, 'seq', split_axis=0, concat_axis=0, tiled=True, **...]
    ppermute x2, waiting for transfers between devices: 0.01 us -> 3.87 us  [shards(): lax.ppermute(before, 'section', [(n, n + 1) for n in range(sections - 1)])]
  transfers between devices with their start and end apart: 14 -> 13, of which waited for: 9 -> 8; matrix products, arithmetic and copies ran while one was open for 5% -> 4% of each run, Pallas kernels for 21% -> 21%
where the time goes in v8:
time: 194 us; the launch traced here: 192 us
  starting transfers between devices  51.6 us (27%)
  Pallas kernels  49.5 us (26%)
  waiting for transfers between devices  48.8 us (25%)
  blocking collectives  30.4 us (16%)
  other arithmetic  5.45 us (3%)
  local copies, waits for them, and re-layouts  4.95 us (3%)
    ppermute x9, waiting for transfers between devices, moved(): return lax.ppermute(value, 'seq', pairs)  45 us
    all_to_all x1, blocking collectives, exchange(): lax.all_to_all(pieces, 'seq', split_axis=0, concat_axis=0, tiled=True, **...  30.4 us
    pallas_call x2, Pallas kernels, attend(): pl.pallas_call(functools.partial(attend_kernel, len(sent)), grid_spec=plt...  30.3 us
    ppermute x9, starting transfers between devices, moved(): return lax.ppermute(value, 'seq', pairs)  28.6 us
    all_to_all x2, starting transfers between devices, exchange(): lax.all_to_all(pieces, 'seq', split_axis=0, concat_axis=0, tiled=True, **...  14.2 us
    pallas_call x2, Pallas kernels, prepare(): pl.pallas_call(functools.partial(prepare_kernel, head), grid_spec=pltpu.P...  11.6 us
    ppermute x2, starting transfers between devices, shards(): lax.ppermute(before, 'section', [(n, n + 1) for n in range(sections - 1)])  8.78 us
    pallas_call x1, Pallas kernels, assemble(): pl.pallas_call(assemble_kernel, grid_spec=pltpu.PrefetchScalarGridSpec(nu...  4.5 us
  transfers between devices with their start and end apart: 13, of which 8 were waited for; matrix products, arithmetic and copies ran while one was open for 4% of the time, Pallas kernels for 21%

profile of v8, /device:TPU:17, one launch (start us, length us, event | category | flops | bytes accessed | tf_op | source)
XLA Modules:
  0.0 191.7 jit_solution(8444220421709195523)
XLA Ops:
  0.0 0.0 copy-start
  0.0 0.7 pad_add_fusion.place
  0.7 5.7 %prepare.2 = (bf16[4,3,8,24,128]{4,3,2,1,0:T(8,128)(2,1)}, bf16[4,3,8,24,128]{4,3,2,1,0:T(8,128)(2,1)}, bf16[4,3,8,24,128]{4,3,2,1,0:T(8,128)(2,1)}, bf16[4,3,8,24,128]{4,3,2,1,0:T(8,128)(2,1)}) custom-call(s32[3]{0:T(128)} %pad_add_fusion.place, bf16[8,24,4096]{2,1,0:T(8,128)(2,1)} %q_ref.3, bf16[8,24,4096]{2,1,0:T(8,128)(2,1)} %k_ref.3, ...), custom_call_target="tpu_custom_call" | custom-call | flops 7864320 | bytes 9437184 | tf_op jit(solution)/shard_map/prepare/pallas_call | solution.py:88
  6.3 3.0 %collective-permute-start = (bf16[4,3,8,24,128]{4,3,2,1,0:T(8,128)(2,1)}, bf16[4,3,8,24,128]{4,3,2,1,0:T(8,128)(2,1)}, u32[]{:S(2)}, u32[]{:S(2)}) collective-permute-start(bf16[4,3,8,24,128]{4,3,2,1,0:T(8,128)(2,1)} %get-tuple-element.21), channel_id=1, source_target_pairs={{0,1},{1,2},{2,3},{3,0},{4,5},{5,6},{6,7},{7,4},{8,9},{9,10},{10,1... | collective-permute-start | bytes 1769480 | tf_op jit(solution)/shard_map/ppermute | solution.py:28
  9.3 3.1 %collective-permute-start.2 = (bf16[4,3,8,24,128]{4,3,2,1,0:T(8,128)(2,1)}, bf16[4,3,8,24,128]{4,3,2,1,0:T(8,128)(2,1)}, u32[]{:S(2)}, u32[]{:S(2)}) collective-permute-start(bf16[4,3,8,24,128]{4,3,2,1,0:T(8,128)(2,1)} %get-tuple-element.23), channel_id=1, source_target_pairs={{0,3},{1,0},{2,1},{3,2},{4,7},{5,4},{6,5},{7,6},{8,11},{9,8},{10,9... | collective-permute-start | bytes 1769480 | tf_op jit(solution)/shard_map/ppermute | solution.py:28
  12.4 0.0 copy-start.2
  12.4 5.9 %prepare.3 = (bf16[4,3,8,24,128]{4,3,2,1,0:T(8,128)(2,1)}, bf16[4,3,8,24,128]{4,3,2,1,0:T(8,128)(2,1)}, bf16[4,3,8,24,128]{4,3,2,1,0:T(8,128)(2,1)}, bf16[4,3,8,24,128]{4,3,2,1,0:T(8,128)(2,1)}) custom-call(s32[3]{0:T(128)} %pad_add_fusion.place, bf16[8,24,4096]{2,1,0:T(8,128)(2,1)} %q_ref.3, bf16[8,24,4096]{2,1,0:T(8,128)(2,1)} %k_ref.3, ...), custom_call_target="tpu_custom_call" | custom-call | flops 7864320 | bytes 9437184 | tf_op jit(solution)/shard_map/prepare/pallas_call | solution.py:88
  18.3 2.5 %collective-permute-start.9 = (bf16[4,3,8,24,128]{4,3,2,1,0:T(8,128)(2,1)}, bf16[4,3,8,24,128]{4,3,2,1,0:T(8,128)(2,1)S(1)}, u32[]{:S(2)}, u32[]{:S(2)}) collective-permute-start(bf16[4,3,8,24,128]{4,3,2,1,0:T(8,128)(2,1)} %get-tuple-element.30), channel_id=1, source_target_pairs={{0,12},{1,13},{2,14},{3,15},{4,0},{5,1},{6,2},{7,3},{8,4},{9,5},{1... | collective-permute-start | bytes 1769480 | tf_op jit(solution)/shard_map/ppermute | solution.py:28
  20.8 0.0 collective-permute-start.7
  20.8 1.7 collective-permute-start.8
  22.6 0.0 copy-done.2
  22.6 7.5 %collective-permute-done.refs_1_ = bf16[4,3,8,24,128]{4,3,2,1,0:T(8,128)(2,1)} collective-permute-done((bf16[4,3,8,24,128]{4,3,2,1,0:T(8,128)(2,1)}, bf16[4,3,8,24,128]{4,3,2,1,0:T(8,128)(2,1)}, u32[]{:S(2)}, u32[]{:S(2)}) %collective-permute-start) | collective-permute-done | bytes 589856 | tf_op jit(solution)/shard_map/ppermute | solution.py:28
  30.1 12.9 %collective-permute-start.1 = (bf16[4,3,8,24,128]{4,3,2,1,0:T(8,128)(2,1)}, bf16[4,3,8,24,128]{4,3,2,1,0:T(8,128)(2,1)S(1)}, u32[]{:S(2)}, u32[]{:S(2)}) collective-permute-start(bf16[4,3,8,24,128]{4,3,2,1,0:T(8,128)(2,1)} %get-tuple-element.22), channel_id=1, source_target_pairs={{0,2},{1,3},{2,0},{3,1},{4,6},{5,7},{6,4},{7,5},{8,10},{9,11},{10,... | collective-permute-start | bytes 1769480 | tf_op jit(solution)/shard_map/ppermute | solution.py:28
  43.0 0.0 collective-permute-done.2.refs_3_
  43.0 0.0 collective-permute-done.9
  43.0 0.0 collective-permute-done.7
  43.0 4.6 %collective-permute-done.8 = bf16[4,3,8,24,128]{4,3,2,1,0:T(8,128)(2,1)S(1)} collective-permute-done((bf16[4,3,8,24,128]{4,3,2,1,0:T(8,128)(2,1)}, bf16[4,3,8,24,128]{4,3,2,1,0:T(8,128)(2,1)S(1)}, u32[]{:S(2)}, u32[]{:S(2)}) %collective-permute-start.8) | collective-permute-done | bytes 589856 | tf_op jit(solution)/shard_map/ppermute | solution.py:28
  47.6 2.8 %pad_maximum_fusion = bf16[4,4,3,8,24,128]{5,4,3,2,1,0:T(8,128)(2,1)} fusion(bf16[4,1,3,8,24,128]{5,4,3,2,1,0:T(8,128)(2,1)S(1)} %bitcast.8, bf16[4,1,3,8,24,128]{5,4,3,2,1,0:T(8,128)(2,1)S(1)} %bitcast.10, bf16[4,1,3,8,24,128]{5,4,3,2,1,0:T(8,128)(2,1)S(1)} %bitcast.9, bf16[4,1,3,8,24,128]{5,4,3,2,1,0:T(8,128)(2,1)} %bitcast.7), kind=kLoop, calls=%fused_computation | loop fusion | flops 3538944 | bytes 4718592 | tf_op jit(solution)/shard_map/stack | solution.py:313
  50.4 5.4 %all-to-all-start.1 = ((bf16[4,4,3,8,24,128]{5,4,3,2,1,0:T(8,128)(2,1)}), bf16[4,4,3,8,24,128]{5,4,3,2,1,0:T(8,128)(2,1)}, u32[]{:S(2)}, u32[]{:S(2)}) async-start(bf16[4,4,3,8,24,128]{5,4,3,2,1,0:T(8,128)(2,1)} %pad_maximum_fusion), calls=%async_computation.1 | async-start | bytes 4718592 | tf_op jit(solution)/shard_map/all_to_all | solution.py:32
  55.7 1.1 fusion.10
  56.8 1.1 fusion.12
  58.0 0.0 copy-start.6
  58.0 10.8 %collective-permute-done.1.refs_2_ = bf16[4,3,8,24,128]{4,3,2,1,0:T(8,128)(2,1)S(1)} collective-permute-done((bf16[4,3,8,24,128]{4,3,2,1,0:T(8,128)(2,1)}, bf16[4,3,8,24,128]{4,3,2,1,0:T(8,128)(2,1)S(1)}, u32[]{:S(2)}, u32[]{:S(2)}) %collective-permute-start.1) | collective-permute-done | bytes 589856 | tf_op jit(solution)/shard_map/ppermute | solution.py:28
  68.8 0.0 copy-start.3
  68.8 0.8 copy-done.3
  69.6 0.1 pad_maximum_fusion.1
  69.7 2.4 %collective-permute-start.3 = (bf16[4,3,8,24,128]{4,3,2,1,0:T(8,128)(2,1)S(1)}, bf16[4,3,8,24,128]{4,3,2,1,0:T(8,128)(2,1)}, u32[]{:S(2)}, u32[]{:S(2)}) collective-permute-start(bf16[4,3,8,24,128]{4,3,2,1,0:T(8,128)(2,1)S(1)} %pad_maximum_fusion.1), channel_id=1, source_target_pairs={{0,4},{1,5},{2,6},{3,7},{4,8},{5,9},{6,10},{7,11},{8,12},{9,13},{1... | collective-permute-start | bytes 1769480 | tf_op jit(solution)/shard_map/ppermute | solution.py:28
  72.1 0.9 pad_maximum_fusion.2
  73.0 2.4 %collective-permute-start.4 = (bf16[4,3,8,24,128]{4,3,2,1,0:T(8,128)(2,1)}, bf16[4,3,8,24,128]{4,3,2,1,0:T(8,128)(2,1)}, u32[]{:S(2)}, u32[]{:S(2)}) collective-permute-start(bf16[4,3,8,24,128]{4,3,2,1,0:T(8,128)(2,1)} %pad_maximum_fusion.2), channel_id=1, source_target_pairs={{0,8},{1,9},{2,10},{3,11},{4,12},{5,13},{6,14},{7,15},{8,0},{9,1},... | collective-permute-start | bytes 1769480 | tf_op jit(solution)/shard_map/ppermute | solution.py:28
  75.4 0.9 pad_maximum_fusion.3
  76.3 0.6 collective-permute-start.5
  77.5 0.0 copy-done.6
  77.6 0.1 fusion.2
  77.7 0.0 copy-done
  77.7 0.2 fusion
  77.8 0.6 fusion.13
  78.4 8.1 %collective-permute-done.3.refs_4_ = bf16[4,3,8,24,128]{4,3,2,1,0:T(8,128)(2,1)} collective-permute-done((bf16[4,3,8,24,128]{4,3,2,1,0:T(8,128)(2,1)S(1)}, bf16[4,3,8,24,128]{4,3,2,1,0:T(8,128)(2,1)}, u32[]{:S(2)}, u32[]{:S(2)}) %collective-permute-start.3) | collective-permute-done | bytes 589856 | tf_op jit(solution)/shard_map/ppermute | solution.py:28
  86.5 13.5 %collective-permute-done.4.refs_5_ = bf16[4,3,8,24,128]{4,3,2,1,0:T(8,128)(2,1)} collective-permute-done((bf16[4,3,8,24,128]{4,3,2,1,0:T(8,128)(2,1)}, bf16[4,3,8,24,128]{4,3,2,1,0:T(8,128)(2,1)}, u32[]{:S(2)}, u32[]{:S(2)}) %collective-permute-start.4) | collective-permute-done | bytes 589856 | tf_op jit(solution)/shard_map/ppermute | solution.py:28
  100.0 0.6 collective-permute-done.5.refs_6_
  100.5 15.1 %attend.2 = (bf16[16,8,24,128]{3,2,1,0:T(8,128)(2,1)}, bf16[16,24,128]{2,1,0:T(8,128)(2,1)}) custom-call(s32[1]{0:T(128)S(6)} %copy.13.slot, s32[3]{0:T(128)} %pad_add_fusion.place, f32[8,128]{1,0:T(8,128)} %get-tuple-element.48.gate_ref, f32[2,4096]{1,0:T(2,128)} %gain_ref.3, bf16[4,3,8,24,128]{4,3,2,1,0:T(8,128)(2,1)} %get-tuple-element.20.refs_0_, ...), custom_call_target="tpu_custom_call" | custom-call | flops 20535312384 | bytes 3072 | tf_op jit(solution)/shard_map/attend/pallas_call | solution.py:196
  115.7 4.3 %collective-permute-start.6 = (bf16[16,24,128]{2,1,0:T(8,128)(2,1)}, bf16[16,24,128]{2,1,0:T(8,128)(2,1)S(1)}, u32[]{:S(2)}, u32[]{:S(2)}) collective-permute-start(bf16[16,24,128]{2,1,0:T(8,128)(2,1)} %get-tuple-element.24._), channel_id=1, source_target_pairs={{0,16},{16,32},{32,48},{48,64},{64,80},{80,96},{96,112},{112,128},... | collective-permute-start | bytes 294920 | tf_op jit(solution)/shard_map/ppermute | solution.py:319
  120.0 1.9 %collective-permute-done.6.behind = bf16[16,24,128]{2,1,0:T(8,128)(2,1)S(1)} collective-permute-done((bf16[16,24,128]{2,1,0:T(8,128)(2,1)}, bf16[16,24,128]{2,1,0:T(8,128)(2,1)S(1)}, u32[]{:S(2)}, u32[]{:S(2)}) %collective-permute-start.6) | collective-permute-done | bytes 98336 | tf_op jit(solution)/shard_map/ppermute | solution.py:319
  121.9 0.0 copy-start.5
  121.9 0.6 copy-done.5
  122.6 1.5 hand_over.2
  124.1 0.0 all-to-all-done.1.refs_0_
  124.1 8.9 %all-to-all-start = ((bf16[16,8,24,128]{3,2,1,0:T(8,128)(2,1)}), bf16[16,8,24,128]{3,2,1,0:T(8,128)(2,1)S(1)}, u32[]{:S(2)}, u32[]{:S(2)}) async-start(bf16[16,8,24,128]{3,2,1,0:T(8,128)(2,1)} %hand_over.2), calls=%async_computation | async-start | bytes 1572864 | tf_op jit(solution)/shard_map/all_to_all | solution.py:32
  133.0 15.2 %attend.3 = (bf16[16,8,24,128]{3,2,1,0:T(8,128)(2,1)}, bf16[16,24,128]{2,1,0:T(8,128)(2,1)}) custom-call(s32[1]{0:T(128)S(6)} %copy.13.slot, s32[3]{0:T(128)} %pad_add_fusion.place, f32[8,128]{1,0:T(8,128)} %get-tuple-element.47.gate_ref, bf16[16,24,128]{2,1,0:T(8,128)(2,1)} %get-tuple-element.24._, bf16[4,4,3,8,24,128]{5,4,3,2,1,0:T(8,128)(2,1)} %all-to-all-done.1.refs_0_), custom_call_target="tpu_custom_call" | custom-call | flops 33822867456 | bytes 3145728 | tf_op jit(solution)/shard_map/attend/pallas_call | solution.py:196
  148.2 4.5 %collective-permute-start.10 = (bf16[16,24,128]{2,1,0:T(8,128)(2,1)}, bf16[16,24,128]{2,1,0:T(8,128)(2,1)S(1)}, u32[]{:S(2)}, u32[]{:S(2)}) collective-permute-start(bf16[16,24,128]{2,1,0:T(8,128)(2,1)} %get-tuple-element.32), channel_id=1, source_target_pairs={{0,16},{16,32},{32,48},{48,64},{64,80},{80,96},{96,112},{112,128},... | collective-permute-start | bytes 294920 | tf_op jit(solution)/shard_map/ppermute | solution.py:319
  152.6 1.9 %collective-permute-done.10.behind = bf16[16,24,128]{2,1,0:T(8,128)(2,1)S(1)} collective-permute-done((bf16[16,24,128]{2,1,0:T(8,128)(2,1)}, bf16[16,24,128]{2,1,0:T(8,128)(2,1)S(1)}, u32[]{:S(2)}, u32[]{:S(2)}) %collective-permute-start.10) | collective-permute-done | bytes 98336 | tf_op jit(solution)/shard_map/ppermute | solution.py:319
  154.6 0.0 copy-start.4
  154.6 0.6 copy-done.4
  155.2 1.6 hand_over.3
  156.8 0.0 all-to-all-done.refs_0_
  156.8 0.0 copy-start.1
  156.8 30.4 %all_to_all.15.refs_1_ = bf16[16,8,24,128]{3,2,1,0:T(8,128)(2,1)} all-to-all(bf16[16,8,24,128]{3,2,1,0:T(8,128)(2,1)} %hand_over.3), channel_id=1, replica_groups=mesh['section'=16,'seq'=16] {'seq'}, dimensions={0} | all-to-all | bytes 1572864 | tf_op jit(solution)/shard_map/all_to_all | solution.py:32
  187.1 0.0 copy-done.1
  187.2 4.5 %assemble.1 = bf16[8,24,4096]{2,1,0:T(8,128)(2,1)} custom-call(s32[1]{0:T(128)S(6)} %copy.13.slot, s32[3]{0:T(128)} %pad_add_fusion.place, bf16[16,8,24,128]{3,2,1,0:T(8,128)(2,1)} %copy-done.1, bf16[16,8,24,128]{3,2,1,0:T(8,128)(2,1)} %all_to_all.15.refs_1_, bf16[24,4096]{1,0:T(8,128)(2,1)} %refs_2_.1), custom_call_target="tpu_custom_call" | custom-call | bytes 3145728 | tf_op jit(solution)/shard_map/assemble/pallas_call | solution.py:278
  (4 shorter events, 0.1 us)
Async XLA Ops:
  0.0 77.7 %copy-start = (bf16[256,4096]{1,0:T(8,128)(2,1)S(1)}, bf16[256,4096]{1,0:T(8,128)(2,1)}, u32[]{:S(2)}) copy-start(bf16[256,4096]{1,0:T(8,128)(2,1)} %param.13) | copy-start | bytes 6291460
  6.3 23.8 %collective-permute-start = (bf16[4,3,8,24,128]{4,3,2,1,0:T(8,128)(2,1)}, bf16[4,3,8,24,128]{4,3,2,1,0:T(8,128)(2,1)}, u32[]{:S(2)}, u32[]{:S(2)}) collective-permute-start(bf16[4,3,8,24,128]{4,3,2,1,0:T(8,128)(2,1)} %get-tuple-element.21), channel_id=1, source_target_pairs={{0,1},{1,2},{2,3},{3,0},{4,5},{5,6},{6,7},{7,4},{8,9},{9,10},{10,1... | collective-permute-start | bytes 1769480 | tf_op jit(solution)/shard_map/ppermute | solution.py:28
  9.3 33.7 %collective-permute-start.2 = (bf16[4,3,8,24,128]{4,3,2,1,0:T(8,128)(2,1)}, bf16[4,3,8,24,128]{4,3,2,1,0:T(8,128)(2,1)}, u32[]{:S(2)}, u32[]{:S(2)}) collective-permute-start(bf16[4,3,8,24,128]{4,3,2,1,0:T(8,128)(2,1)} %get-tuple-element.23), channel_id=1, source_target_pairs={{0,3},{1,0},{2,1},{3,2},{4,7},{5,4},{6,5},{7,6},{8,11},{9,8},{10,9... | collective-permute-start | bytes 1769480 | tf_op jit(solution)/shard_map/ppermute | solution.py:28
  12.4 10.1 %copy-start.2 = (bf16[4,3,8,24,128]{4,3,2,1,0:T(8,128)(2,1)S(1)}, bf16[4,3,8,24,128]{4,3,2,1,0:T(8,128)(2,1)}, u32[]{:S(2)}) copy-start(bf16[4,3,8,24,128]{4,3,2,1,0:T(8,128)(2,1)} %get-tuple-element.20.refs_0_) | copy-start | bytes 1769476
  18.3 24.7 %collective-permute-start.9 = (bf16[4,3,8,24,128]{4,3,2,1,0:T(8,128)(2,1)}, bf16[4,3,8,24,128]{4,3,2,1,0:T(8,128)(2,1)S(1)}, u32[]{:S(2)}, u32[]{:S(2)}) collective-permute-start(bf16[4,3,8,24,128]{4,3,2,1,0:T(8,128)(2,1)} %get-tuple-element.30), channel_id=1, source_target_pairs={{0,12},{1,13},{2,14},{3,15},{4,0},{5,1},{6,2},{7,3},{8,4},{9,5},{1... | collective-permute-start | bytes 1769480 | tf_op jit(solution)/shard_map/ppermute | solution.py:28
  20.8 22.2 %collective-permute-start.7 = (bf16[4,3,8,24,128]{4,3,2,1,0:T(8,128)(2,1)}, bf16[4,3,8,24,128]{4,3,2,1,0:T(8,128)(2,1)S(1)}, u32[]{:S(2)}, u32[]{:S(2)}) collective-permute-start(bf16[4,3,8,24,128]{4,3,2,1,0:T(8,128)(2,1)} %get-tuple-element.28), channel_id=1, source_target_pairs={{0,4},{1,5},{2,6},{3,7},{4,8},{5,9},{6,10},{7,11},{8,12},{9,13},{1... | collective-permute-start | bytes 1769480 | tf_op jit(solution)/shard_map/ppermute | solution.py:28
  20.8 26.7 %collective-permute-start.8 = (bf16[4,3,8,24,128]{4,3,2,1,0:T(8,128)(2,1)}, bf16[4,3,8,24,128]{4,3,2,1,0:T(8,128)(2,1)S(1)}, u32[]{:S(2)}, u32[]{:S(2)}) collective-permute-start(bf16[4,3,8,24,128]{4,3,2,1,0:T(8,128)(2,1)} %get-tuple-element.29), channel_id=1, source_target_pairs={{0,8},{1,9},{2,10},{3,11},{4,12},{5,13},{6,14},{7,15},{8,0},{9,1},... | collective-permute-start | bytes 1769480 | tf_op jit(solution)/shard_map/ppermute | solution.py:28
  30.1 38.7 %collective-permute-start.1 = (bf16[4,3,8,24,128]{4,3,2,1,0:T(8,128)(2,1)}, bf16[4,3,8,24,128]{4,3,2,1,0:T(8,128)(2,1)S(1)}, u32[]{:S(2)}, u32[]{:S(2)}) collective-permute-start(bf16[4,3,8,24,128]{4,3,2,1,0:T(8,128)(2,1)} %get-tuple-element.22), channel_id=1, source_target_pairs={{0,2},{1,3},{2,0},{3,1},{4,6},{5,7},{6,4},{7,5},{8,10},{9,11},{10,... | collective-permute-start | bytes 1769480 | tf_op jit(solution)/shard_map/ppermute | solution.py:28
  50.4 73.7 %all-to-all-start.1 = ((bf16[4,4,3,8,24,128]{5,4,3,2,1,0:T(8,128)(2,1)}), bf16[4,4,3,8,24,128]{5,4,3,2,1,0:T(8,128)(2,1)}, u32[]{:S(2)}, u32[]{:S(2)}) async-start(bf16[4,4,3,8,24,128]{5,4,3,2,1,0:T(8,128)(2,1)} %pad_maximum_fusion), calls=%async_computation.1 | async-start | bytes 4718592 | tf_op jit(solution)/shard_map/all_to_all | solution.py:32
  58.0 19.6 %copy-start.6 = (s32[8]{0:T(128)S(1)}, s32[8]{0:T(128)}, u32[]{:S(2)}) copy-start(s32[8]{0:T(128)} %param.12) | copy-start | bytes 100
  68.8 0.8 copy-start.3
  69.7 16.8 %collective-permute-start.3 = (bf16[4,3,8,24,128]{4,3,2,1,0:T(8,128)(2,1)S(1)}, bf16[4,3,8,24,128]{4,3,2,1,0:T(8,128)(2,1)}, u32[]{:S(2)}, u32[]{:S(2)}) collective-permute-start(bf16[4,3,8,24,128]{4,3,2,1,0:T(8,128)(2,1)S(1)} %pad_maximum_fusion.1), channel_id=1, source_target_pairs={{0,4},{1,5},{2,6},{3,7},{4,8},{5,9},{6,10},{7,11},{8,12},{9,13},{1... | collective-permute-start | bytes 1769480 | tf_op jit(solution)/shard_map/ppermute | solution.py:28
  73.0 27.0 %collective-permute-start.4 = (bf16[4,3,8,24,128]{4,3,2,1,0:T(8,128)(2,1)}, bf16[4,3,8,24,128]{4,3,2,1,0:T(8,128)(2,1)}, u32[]{:S(2)}, u32[]{:S(2)}) collective-permute-start(bf16[4,3,8,24,128]{4,3,2,1,0:T(8,128)(2,1)} %pad_maximum_fusion.2), channel_id=1, source_target_pairs={{0,8},{1,9},{2,10},{3,11},{4,12},{5,13},{6,14},{7,15},{8,0},{9,1},... | collective-permute-start | bytes 1769480 | tf_op jit(solution)/shard_map/ppermute | solution.py:28
  76.3 24.3 %collective-permute-start.5 = (bf16[4,3,8,24,128]{4,3,2,1,0:T(8,128)(2,1)}, bf16[4,3,8,24,128]{4,3,2,1,0:T(8,128)(2,1)}, u32[]{:S(2)}, u32[]{:S(2)}) collective-permute-start(bf16[4,3,8,24,128]{4,3,2,1,0:T(8,128)(2,1)} %pad_maximum_fusion.3), channel_id=1, source_target_pairs={{0,12},{1,13},{2,14},{3,15},{4,0},{5,1},{6,2},{7,3},{8,4},{9,5},{1... | collective-permute-start | bytes 1769480 | tf_op jit(solution)/shard_map/ppermute | solution.py:28
  115.7 6.2 %collective-permute-start.6 = (bf16[16,24,128]{2,1,0:T(8,128)(2,1)}, bf16[16,24,128]{2,1,0:T(8,128)(2,1)S(1)}, u32[]{:S(2)}, u32[]{:S(2)}) collective-permute-start(bf16[16,24,128]{2,1,0:T(8,128)(2,1)} %get-tuple-element.24._), channel_id=1, source_target_pairs={{0,16},{16,32},{32,48},{48,64},{64,80},{80,96},{96,112},{112,128},... | collective-permute-start | bytes 294920 | tf_op jit(solution)/shard_map/ppermute | solution.py:319
  121.9 0.6 copy-start.5
  124.1 32.7 %all-to-all-start = ((bf16[16,8,24,128]{3,2,1,0:T(8,128)(2,1)}), bf16[16,8,24,128]{3,2,1,0:T(8,128)(2,1)S(1)}, u32[]{:S(2)}, u32[]{:S(2)}) async-start(bf16[16,8,24,128]{3,2,1,0:T(8,128)(2,1)} %hand_over.2), calls=%async_computation | async-start | bytes 1572864 | tf_op jit(solution)/shard_map/all_to_all | solution.py:32
  148.2 6.4 %collective-permute-start.10 = (bf16[16,24,128]{2,1,0:T(8,128)(2,1)}, bf16[16,24,128]{2,1,0:T(8,128)(2,1)S(1)}, u32[]{:S(2)}, u32[]{:S(2)}) collective-permute-start(bf16[16,24,128]{2,1,0:T(8,128)(2,1)} %get-tuple-element.32), channel_id=1, source_target_pairs={{0,16},{16,32},{32,48},{48,64},{64,80},{80,96},{96,112},{112,128},... | collective-permute-start | bytes 294920 | tf_op jit(solution)/shard_map/ppermute | solution.py:319
  154.6 0.6 copy-start.4
  156.8 30.4 %copy-start.1 = (bf16[16,8,24,128]{3,2,1,0:T(8,128)(2,1)}, bf16[16,8,24,128]{3,2,1,0:T(8,128)(2,1)S(1)}, u32[]{:S(2)}) copy-start(bf16[16,8,24,128]{3,2,1,0:T(8,128)(2,1)S(1)} %all-to-all-done.refs_0_) | copy-start | bytes 2359300

commit v9 on v7

--- a/solution.py
+++ b/solution.py
@@ -224,63 +224,52 @@
     return lax.dynamic_index_in_dim(returned, slot[0], 1, keepdims=False)
 
 
-def assemble_kernel(*refs):
-    *parts, out = refs
-    for head, own in enumerate(parts):
-        for group in range(own.shape[0]):
-            at = (group * len(parts) + head) * HD
-            out[:, :, at : at + HD] = own[group]
-
-
-def assemble(parts):
+def assemble_kernel(slot, place, *refs):
+    fresh, out = refs[-2:]
+    heads = (len(refs) - 2) // 2
+    step = out.shape[0]
+    for n in range(step):
+        here = pl.program_id(0) * step + n == slot[0]
+
+        def fill(pieces, n=n):
+            for head, (own, index) in enumerate(pieces):
+                for group in range(own.shape[0]):
+                    at = (group * heads + head) * HD
+                    out[n, :, at : at + HD] = own[(group, *index)]
+
+        @pl.when(jnp.logical_not(here))
+        def _(n=n, fill=fill):
+            fill([(own, (n,)) for own in refs[:heads]])
+
+        @pl.when(jnp.logical_and(here, place[2] != 0))
+        def _(fill=fill):
+            fill([(behind, ()) for behind in refs[heads : 2 * heads]])
+
+        @pl.when(jnp.logical_and(here, place[2] == 0))
+        def _(n=n):
+            out[n] = fresh[...]
+
+
+def assemble(slot, place, parts, behind, fresh):
     groups, frames, rows, _ = parts[0].shape
-    inner = groups * len(parts) * HD
-    step = 2
-    own = pl.BlockSpec((groups, step, rows, HD), lambda n: (0, n, 0, 0))
+    inner = fresh.shape[1]
+    step = 4
+    own = pl.BlockSpec((groups, step, rows, HD), lambda n, *_: (0, n, 0, 0))
+    frame = pl.BlockSpec((groups, rows, HD), lambda n, *_: (0, 0, 0))
     return pl.pallas_call(
         assemble_kernel,
-        grid=(frames // step,),
-        in_specs=[own] * len(parts),
-        out_specs=pl.BlockSpec((step, rows, inner), lambda n: (n, 0, 0)),
+        grid_spec=pltpu.PrefetchScalarGridSpec(
+            num_scalar_prefetch=2,
+            grid=(frames // step,),
+            in_specs=[own] * len(parts)
+            + [frame] * len(parts)
+            + [pl.BlockSpec((rows, inner), lambda n, *_: (0, 0))],
+            out_specs=pl.BlockSpec((step, rows, inner), lambda n, *_: (n, 0, 0)),
+        ),
         out_shape=jax.ShapeDtypeStruct((frames, rows, inner), jnp.bfloat16),
         compiler_params=pltpu.CompilerParams(vmem_limit_bytes=60 * MIB),
-        cost_estimate=pl.CostEstimate(flops=0, bytes_accessed=4 * frames * rows * inner, transcendentals=0),
         name="assemble",
-    )(*parts)
-
-
-def hand_kernel(slot, place, *refs):
-    *behind, fresh, _, out = refs
-
-    @pl.when(place[2] != 0)
-    def _():
-        for head, part in enumerate(behind):
-            for group in range(part.shape[0]):
-                at = (group * len(behind) + head) * HD
-                out[0, :, at : at + HD] = part[group]
-
-    @pl.when(place[2] == 0)
-    def _():
-        out[0] = fresh[...]
-
-
-def hand_over(slot, place, behind, fresh, gated):
-    rows, inner = fresh.shape
-    part = pl.BlockSpec(behind[0].shape, lambda n, *_: (0, 0, 0))
-    return pl.pallas_call(
-        hand_kernel,
-        grid_spec=pltpu.PrefetchScalarGridSpec(
-            num_scalar_prefetch=2,
-            grid=(1,),
-            in_specs=[part] * len(behind)
-            + [pl.BlockSpec((rows, inner), lambda n, *_: (0, 0)), pl.BlockSpec(memory_space=pl.ANY)],
-            out_specs=pl.BlockSpec((1, rows, inner), lambda n, slot, _: (slot[0], 0, 0)),
-        ),
-        out_shape=jax.ShapeDtypeStruct(gated.shape, gated.dtype),
-        input_output_aliases={len(behind) + 3: 0},
-        compiler_params=pltpu.CompilerParams(vmem_limit_bytes=60 * MIB),
-        name="hand_over",
-    )(slot, place, *behind, fresh, gated)
+    )(slot, place, *parts, *behind, fresh)
 
 
 def level_gate(steps, gate_weight):
@@ -313,7 +302,7 @@
         leaving = leaving_frame(slot, returned)
         behind.append(lax.ppermute(leaving, "section", [(n, n + 1) for n in range(sections - 1)]))
         parts.append(returned)
-    return hand_over(slot, place, behind, fresh, assemble(parts))
+    return assemble(slot, place, parts, behind, fresh)
 
 
 def solution(mesh):

time: 190 us -> 190 us (level)
  waiting for transfers between devices: 68.5 us -> 71.7 us
  Pallas kernels: 47.9 us -> 45 us
    pallas_call x2 -> x1, Pallas kernels: 6.13 us -> 3.26 us  [assemble(): pl.pallas_call(assemble_kernel, grid_spec=pltpu.PrefetchScalarGridSpec(nu...]
    all_to_all x3, starting transfers between devices: 18.1 us -> 20.1 us  [exchange(): lax.all_to_all(pieces, 'seq', split_axis=0, concat_axis=0, tiled=True, **...]
  transfers between devices with their start and end apart: 14 -> 14, of which waited for: 9 -> 10; matrix products, arithmetic and copies ran while one was open for 5% -> 5% of each run, Pallas kernels for 21% -> 19%
where the time goes in v9:
time: 190 us; the launch traced here: 188 us
  waiting for transfers between devices  71.7 us (38%)
  starting transfers between devices  59.8 us (31%)
  Pallas kernels  45 us (24%)
  other arithmetic  5.45 us (3%)
  local copies, waits for them, and re-layouts  5.24 us (3%)
    ppermute x9, waiting for transfers between devices, moved(): return lax.ppermute(value, 'seq', pairs)  45.5 us
    pallas_call x2, Pallas kernels, attend(): pl.pallas_call(functools.partial(attend_kernel, len(sent)), grid_spec=plt...  30.2 us
    ppermute x9, starting transfers between devices, moved(): return lax.ppermute(value, 'seq', pairs)  27.5 us
    all_to_all x3, waiting for transfers between devices, exchange(): lax.all_to_all(pieces, 'seq', split_axis=0, concat_axis=0, tiled=True, **...  24.6 us
    all_to_all x3, starting transfers between devices, exchange(): lax.all_to_all(pieces, 'seq', split_axis=0, concat_axis=0, tiled=True, **...  20.1 us
    ppermute x2, starting transfers between devices, shards(): lax.ppermute(leaving, 'section', [(n, n + 1) for n in range(sections - 1)])  12.1 us
    pallas_call x2, Pallas kernels, prepare(): pl.pallas_call(functools.partial(prepare_kernel, head), grid_spec=pltpu.P...  11.6 us
  transfers between devices with their start and end apart: 14, of which 10 were waited for; matrix products, arithmetic and copies ran while one was open for 5% of the time, Pallas kernels for 19%

profile of v9, /device:TPU:17, one launch (start us, length us, event | category | flops | bytes accessed | tf_op | source)
XLA Modules:
  0.0 188.2 jit_solution(11284799460752586470)
XLA Ops:
  0.0 0.0 copy-start
  0.0 0.7 pad_add_fusion.place
  0.7 5.7 %prepare.2 = (bf16[4,3,8,24,128]{4,3,2,1,0:T(8,128)(2,1)}, bf16[4,3,8,24,128]{4,3,2,1,0:T(8,128)(2,1)}, bf16[4,3,8,24,128]{4,3,2,1,0:T(8,128)(2,1)}, bf16[4,3,8,24,128]{4,3,2,1,0:T(8,128)(2,1)}) custom-call(s32[3]{0:T(128)} %pad_add_fusion.place, bf16[8,24,4096]{2,1,0:T(8,128)(2,1)} %q_ref.3, bf16[8,24,4096]{2,1,0:T(8,128)(2,1)} %k_ref.3, ...), custom_call_target="tpu_custom_call" | custom-call | flops 7864320 | bytes 9437184 | tf_op jit(solution)/shard_map/prepare/pallas_call | solution.py:88
  6.3 3.0 %collective-permute-start = (bf16[4,3,8,24,128]{4,3,2,1,0:T(8,128)(2,1)}, bf16[4,3,8,24,128]{4,3,2,1,0:T(8,128)(2,1)}, u32[]{:S(2)}, u32[]{:S(2)}) collective-permute-start(bf16[4,3,8,24,128]{4,3,2,1,0:T(8,128)(2,1)} %get-tuple-element.17), channel_id=1, source_target_pairs={{0,1},{1,2},{2,3},{3,0},{4,5},{5,6},{6,7},{7,4},{8,9},{9,10},{10,1... | collective-permute-start | bytes 1769480 | tf_op jit(solution)/shard_map/ppermute | solution.py:28
  9.3 3.1 %collective-permute-start.2 = (bf16[4,3,8,24,128]{4,3,2,1,0:T(8,128)(2,1)}, bf16[4,3,8,24,128]{4,3,2,1,0:T(8,128)(2,1)}, u32[]{:S(2)}, u32[]{:S(2)}) collective-permute-start(bf16[4,3,8,24,128]{4,3,2,1,0:T(8,128)(2,1)} %get-tuple-element.19), channel_id=1, source_target_pairs={{0,3},{1,0},{2,1},{3,2},{4,7},{5,4},{6,5},{7,6},{8,11},{9,8},{10,9... | collective-permute-start | bytes 1769480 | tf_op jit(solution)/shard_map/ppermute | solution.py:28
  12.4 0.0 copy-start.2
  12.4 5.9 %prepare.3 = (bf16[4,3,8,24,128]{4,3,2,1,0:T(8,128)(2,1)}, bf16[4,3,8,24,128]{4,3,2,1,0:T(8,128)(2,1)}, bf16[4,3,8,24,128]{4,3,2,1,0:T(8,128)(2,1)}, bf16[4,3,8,24,128]{4,3,2,1,0:T(8,128)(2,1)}) custom-call(s32[3]{0:T(128)} %pad_add_fusion.place, bf16[8,24,4096]{2,1,0:T(8,128)(2,1)} %q_ref.3, bf16[8,24,4096]{2,1,0:T(8,128)(2,1)} %k_ref.3, ...), custom_call_target="tpu_custom_call" | custom-call | flops 7864320 | bytes 9437184 | tf_op jit(solution)/shard_map/prepare/pallas_call | solution.py:88
  18.3 2.5 %collective-permute-start.8 = (bf16[4,3,8,24,128]{4,3,2,1,0:T(8,128)(2,1)}, bf16[4,3,8,24,128]{4,3,2,1,0:T(8,128)(2,1)S(1)}, u32[]{:S(2)}, u32[]{:S(2)}) collective-permute-start(bf16[4,3,8,24,128]{4,3,2,1,0:T(8,128)(2,1)} %get-tuple-element.24), channel_id=1, source_target_pairs={{0,12},{1,13},{2,14},{3,15},{4,0},{5,1},{6,2},{7,3},{8,4},{9,5},{1... | collective-permute-start | bytes 1769480 | tf_op jit(solution)/shard_map/ppermute | solution.py:28
  20.8 0.5 collective-permute-start.7
  21.3 0.6 collective-permute-start.6
  21.9 0.0 copy-done.2
  22.0 8.1 %collective-permute-done.refs_1_ = bf16[4,3,8,24,128]{4,3,2,1,0:T(8,128)(2,1)} collective-permute-done((bf16[4,3,8,24,128]{4,3,2,1,0:T(8,128)(2,1)}, bf16[4,3,8,24,128]{4,3,2,1,0:T(8,128)(2,1)}, u32[]{:S(2)}, u32[]{:S(2)}) %collective-permute-start) | collective-permute-done | bytes 589856 | tf_op jit(solution)/shard_map/ppermute | solution.py:28
  30.1 12.9 %collective-permute-start.1 = (bf16[4,3,8,24,128]{4,3,2,1,0:T(8,128)(2,1)}, bf16[4,3,8,24,128]{4,3,2,1,0:T(8,128)(2,1)S(1)}, u32[]{:S(2)}, u32[]{:S(2)}) collective-permute-start(bf16[4,3,8,24,128]{4,3,2,1,0:T(8,128)(2,1)} %get-tuple-element.18), channel_id=1, source_target_pairs={{0,2},{1,3},{2,0},{3,1},{4,6},{5,7},{6,4},{7,5},{8,10},{9,11},{10,... | collective-permute-start | bytes 1769480 | tf_op jit(solution)/shard_map/ppermute | solution.py:28
  43.0 0.0 collective-permute-done.2.refs_3_
  43.0 0.0 collective-permute-done.8
  43.0 0.0 collective-permute-done.7
  43.0 7.4 %collective-permute-done.6 = bf16[4,3,8,24,128]{4,3,2,1,0:T(8,128)(2,1)S(1)} collective-permute-done((bf16[4,3,8,24,128]{4,3,2,1,0:T(8,128)(2,1)}, bf16[4,3,8,24,128]{4,3,2,1,0:T(8,128)(2,1)S(1)}, u32[]{:S(2)}, u32[]{:S(2)}) %collective-permute-start.6) | collective-permute-done | bytes 589856 | tf_op jit(solution)/shard_map/ppermute | solution.py:28
  50.4 2.8 %pad_maximum_fusion = bf16[4,4,3,8,24,128]{5,4,3,2,1,0:T(8,128)(2,1)} fusion(bf16[4,1,3,8,24,128]{5,4,3,2,1,0:T(8,128)(2,1)S(1)} %bitcast.16, bf16[4,1,3,8,24,128]{5,4,3,2,1,0:T(8,128)(2,1)S(1)} %bitcast.17, bf16[4,1,3,8,24,128]{5,4,3,2,1,0:T(8,128)(2,1)S(1)} %bitcast.18, bf16[4,1,3,8,24,128]{5,4,3,2,1,0:T(8,128)(2,1)} %bitcast.15), kind=kLoop, calls=%fused_computation | loop fusion | flops 3538944 | bytes 4718592 | tf_op jit(solution)/shard_map/stack | solution.py:295
  53.2 5.7 %all-to-all-start.1 = ((bf16[4,4,3,8,24,128]{5,4,3,2,1,0:T(8,128)(2,1)}), bf16[4,4,3,8,24,128]{5,4,3,2,1,0:T(8,128)(2,1)}, u32[]{:S(2)}, u32[]{:S(2)}) async-start(bf16[4,4,3,8,24,128]{5,4,3,2,1,0:T(8,128)(2,1)} %pad_maximum_fusion), calls=%async_computation.1 | async-start | bytes 4718592 | tf_op jit(solution)/shard_map/all_to_all | solution.py:32
  58.9 1.1 fusion.12
  60.0 1.1 fusion.10
  61.1 0.0 copy-start.6
  61.1 7.6 %collective-permute-done.1.refs_2_ = bf16[4,3,8,24,128]{4,3,2,1,0:T(8,128)(2,1)S(1)} collective-permute-done((bf16[4,3,8,24,128]{4,3,2,1,0:T(8,128)(2,1)}, bf16[4,3,8,24,128]{4,3,2,1,0:T(8,128)(2,1)S(1)}, u32[]{:S(2)}, u32[]{:S(2)}) %collective-permute-start.1) | collective-permute-done | bytes 589856 | tf_op jit(solution)/shard_map/ppermute | solution.py:28
  68.7 0.0 copy-start.3
  68.8 0.8 copy-done.3
  69.6 0.1 pad_maximum_fusion.1
  69.6 1.3 collective-permute-start.3
  71.0 0.9 pad_maximum_fusion.2
  71.9 2.5 %collective-permute-start.4 = (bf16[4,3,8,24,128]{4,3,2,1,0:T(8,128)(2,1)}, bf16[4,3,8,24,128]{4,3,2,1,0:T(8,128)(2,1)}, u32[]{:S(2)}, u32[]{:S(2)}) collective-permute-start(bf16[4,3,8,24,128]{4,3,2,1,0:T(8,128)(2,1)} %pad_maximum_fusion.2), channel_id=1, source_target_pairs={{0,8},{1,9},{2,10},{3,11},{4,12},{5,13},{6,14},{7,15},{8,0},{9,1},... | collective-permute-start | bytes 1769480 | tf_op jit(solution)/shard_map/ppermute | solution.py:28
  74.3 0.9 pad_maximum_fusion.3
  75.2 1.2 collective-permute-start.5
  76.4 0.0 copy-done.6
  76.4 0.1 fusion.2
  76.5 0.0 copy-done
  76.5 0.2 fusion
  76.6 0.6 fusion.13
  77.2 8.0 %collective-permute-done.3.refs_4_ = bf16[4,3,8,24,128]{4,3,2,1,0:T(8,128)(2,1)} collective-permute-done((bf16[4,3,8,24,128]{4,3,2,1,0:T(8,128)(2,1)S(1)}, bf16[4,3,8,24,128]{4,3,2,1,0:T(8,128)(2,1)}, u32[]{:S(2)}, u32[]{:S(2)}) %collective-permute-start.3) | collective-permute-done | bytes 589856 | tf_op jit(solution)/shard_map/ppermute | solution.py:28
  85.3 13.7 %collective-permute-done.4.refs_5_ = bf16[4,3,8,24,128]{4,3,2,1,0:T(8,128)(2,1)} collective-permute-done((bf16[4,3,8,24,128]{4,3,2,1,0:T(8,128)(2,1)}, bf16[4,3,8,24,128]{4,3,2,1,0:T(8,128)(2,1)}, u32[]{:S(2)}, u32[]{:S(2)}) %collective-permute-start.4) | collective-permute-done | bytes 589856 | tf_op jit(solution)/shard_map/ppermute | solution.py:28
  99.0 0.6 collective-permute-done.5.refs_6_
  99.6 15.1 %attend.2._ = bf16[16,8,24,128]{3,2,1,0:T(8,128)(2,1)} custom-call(s32[3]{0:T(128)} %pad_add_fusion.place, f32[8,128]{1,0:T(8,128)} %get-tuple-element.40.gate_ref, f32[2,4096]{1,0:T(2,128)} %gain_ref.3, bf16[4,3,8,24,128]{4,3,2,1,0:T(8,128)(2,1)} %get-tuple-element.16.refs_0_, bf16[4,3,8,24,128]{4,3,2,1,0:T(8,128)(2,1)} %collective-permute-done.refs_1_, ...), custom_call_target="tpu_custom_call" | custom-call | flops 20535312384 | bytes 3072 | tf_op jit(solution)/shard_map/attend/pallas_call | solution.py:194
  114.7 5.5 %all-to-all-done.1.refs_0_ = bf16[4,4,3,8,24,128]{5,4,3,2,1,0:T(8,128)(2,1)} async-done(((bf16[4,4,3,8,24,128]{5,4,3,2,1,0:T(8,128)(2,1)}), bf16[4,4,3,8,24,128]{5,4,3,2,1,0:T(8,128)(2,1)}, u32[]{:S(2)}, u32[]{:S(2)}) %all-to-all-start.1) | async-done | bytes 2359328 | tf_op jit(solution)/shard_map/all_to_all | solution.py:32
  120.2 8.2 %all-to-all-start = ((bf16[16,8,24,128]{3,2,1,0:T(8,128)(2,1)}), bf16[16,8,24,128]{3,2,1,0:T(8,128)(2,1)S(1)}, u32[]{:S(2)}, u32[]{:S(2)}) async-start(bf16[16,8,24,128]{3,2,1,0:T(8,128)(2,1)} %attend.2._), calls=%async_computation | async-start | bytes 1572864 | tf_op jit(solution)/shard_map/all_to_all | solution.py:32
  128.3 15.1 %attend.3 = bf16[16,8,24,128]{3,2,1,0:T(8,128)(2,1)} custom-call(s32[3]{0:T(128)} %pad_add_fusion.place, f32[8,128]{1,0:T(8,128)} %get-tuple-element.39.gate_ref, bf16[16,8,24,128]{3,2,1,0:T(8,128)(2,1)} %attend.2._, bf16[4,4,3,8,24,128]{5,4,3,2,1,0:T(8,128)(2,1)} %all-to-all-done.1.refs_0_), custom_call_target="tpu_custom_call" | custom-call | flops 33822867456 | bytes 3145728 | tf_op jit(solution)/shard_map/attend/pallas_call | solution.py:194
  143.4 4.1 %all-to-all-done.refs_0_ = bf16[16,8,24,128]{3,2,1,0:T(8,128)(2,1)S(1)} async-done(((bf16[16,8,24,128]{3,2,1,0:T(8,128)(2,1)}), bf16[16,8,24,128]{3,2,1,0:T(8,128)(2,1)S(1)}, u32[]{:S(2)}, u32[]{:S(2)}) %all-to-all-start) | async-done | bytes 786464 | tf_op jit(solution)/shard_map/all_to_all | solution.py:32
  147.5 0.0 copy-start.1
  147.5 6.3 %all-to-all-start.2 = ((bf16[16,8,24,128]{3,2,1,0:T(8,128)(2,1)}), bf16[16,8,24,128]{3,2,1,0:T(8,128)(2,1)}, u32[]{:S(2)}, u32[]{:S(2)}) async-start(bf16[16,8,24,128]{3,2,1,0:T(8,128)(2,1)} %attend.3), calls=%async_computation.2 | async-start | bytes 1572864 | tf_op jit(solution)/shard_map/all_to_all | solution.py:32
  154.5 3.6 %collective-permute-start.9 = (bf16[16,24,128]{2,1,0:T(8,128)(2,1)S(1)}, bf16[16,24,128]{2,1,0:T(8,128)(2,1)S(1)}, u32[]{:S(2)}, u32[]{:S(2)}) collective-permute-start(bf16[16,24,128]{2,1,0:T(8,128)(2,1)S(1)} %dynamic-slice_bitcast_fusion.1), channel_id=1, source_target_pairs={{0,16},{16,32},{32,48},{48,64},{64,80},{80,96},{96,112},{112,128},... | collective-permute-start | bytes 294920 | tf_op jit(solution)/shard_map/ppermute | solution.py:303
  158.1 15.1 %all-to-all-done.2.refs_1_ = bf16[16,8,24,128]{3,2,1,0:T(8,128)(2,1)} async-done(((bf16[16,8,24,128]{3,2,1,0:T(8,128)(2,1)}), bf16[16,8,24,128]{3,2,1,0:T(8,128)(2,1)}, u32[]{:S(2)}, u32[]{:S(2)}) %all-to-all-start.2) | async-done | bytes 786464 | tf_op jit(solution)/shard_map/all_to_all | solution.py:32
  173.2 0.9 dynamic-slice_bitcast_fusion
  174.1 8.6 %collective-permute-start.10 = (bf16[16,24,128]{2,1,0:T(8,128)(2,1)S(1)}, bf16[16,24,128]{2,1,0:T(8,128)(2,1)S(1)}, u32[]{:S(2)}, u32[]{:S(2)}) collective-permute-start(bf16[16,24,128]{2,1,0:T(8,128)(2,1)S(1)} %dynamic-slice_bitcast_fusion), channel_id=1, source_target_pairs={{0,16},{16,32},{32,48},{48,64},{64,80},{80,96},{96,112},{112,128},... | collective-permute-start | bytes 294920 | tf_op jit(solution)/shard_map/ppermute | solution.py:303
  182.6 0.0 collective-permute-done.9.refs_2_
  182.6 0.0 copy-start.4
  182.7 1.6 collective-permute-done.10.refs_3_
  184.3 0.0 copy-done.1
  184.3 0.0 copy-done.4
  184.3 0.0 copy-start.5
  184.3 0.6 copy-done.5
  184.9 3.3 %assemble.1 = bf16[8,24,4096]{2,1,0:T(8,128)(2,1)} custom-call(s32[1]{0:T(128)} %copy.9.slot, s32[3]{0:T(128)} %pad_add_fusion.place, bf16[16,8,24,128]{3,2,1,0:T(8,128)(2,1)} %copy-done.1, bf16[16,8,24,128]{3,2,1,0:T(8,128)(2,1)} %all-to-all-done.2.refs_1_, bf16[16,24,128]{2,1,0:T(8,128)(2,1)} %copy-done.4, bf16[16,24,128]{2,1,0:T(8,128)(2,1)} %copy-done.5, ...), custom_call_target="tpu_custom_call" | custom-call | tf_op jit(solution)/shard_map/assemble/pallas_call | solution.py:259
  (5 shorter events, 0.1 us)
Async XLA Ops:
  0.0 76.5 %copy-start = (bf16[256,4096]{1,0:T(8,128)(2,1)S(1)}, bf16[256,4096]{1,0:T(8,128)(2,1)}, u32[]{:S(2)}) copy-start(bf16[256,4096]{1,0:T(8,128)(2,1)} %param.13) | copy-start | bytes 6291460
  6.3 23.8 %collective-permute-start = (bf16[4,3,8,24,128]{4,3,2,1,0:T(8,128)(2,1)}, bf16[4,3,8,24,128]{4,3,2,1,0:T(8,128)(2,1)}, u32[]{:S(2)}, u32[]{:S(2)}) collective-permute-start(bf16[4,3,8,24,128]{4,3,2,1,0:T(8,128)(2,1)} %get-tuple-element.17), channel_id=1, source_target_pairs={{0,1},{1,2},{2,3},{3,0},{4,5},{5,6},{6,7},{7,4},{8,9},{9,10},{10,1... | collective-permute-start | bytes 1769480 | tf_op jit(solution)/shard_map/ppermute | solution.py:28
  9.3 33.7 %collective-permute-start.2 = (bf16[4,3,8,24,128]{4,3,2,1,0:T(8,128)(2,1)}, bf16[4,3,8,24,128]{4,3,2,1,0:T(8,128)(2,1)}, u32[]{:S(2)}, u32[]{:S(2)}) collective-permute-start(bf16[4,3,8,24,128]{4,3,2,1,0:T(8,128)(2,1)} %get-tuple-element.19), channel_id=1, source_target_pairs={{0,3},{1,0},{2,1},{3,2},{4,7},{5,4},{6,5},{7,6},{8,11},{9,8},{10,9... | collective-permute-start | bytes 1769480 | tf_op jit(solution)/shard_map/ppermute | solution.py:28
  12.4 9.5 %copy-start.2 = (bf16[4,3,8,24,128]{4,3,2,1,0:T(8,128)(2,1)S(1)}, bf16[4,3,8,24,128]{4,3,2,1,0:T(8,128)(2,1)}, u32[]{:S(2)}) copy-start(bf16[4,3,8,24,128]{4,3,2,1,0:T(8,128)(2,1)} %get-tuple-element.16.refs_0_) | copy-start | bytes 1769476
  18.3 24.7 %collective-permute-start.8 = (bf16[4,3,8,24,128]{4,3,2,1,0:T(8,128)(2,1)}, bf16[4,3,8,24,128]{4,3,2,1,0:T(8,128)(2,1)S(1)}, u32[]{:S(2)}, u32[]{:S(2)}) collective-permute-start(bf16[4,3,8,24,128]{4,3,2,1,0:T(8,128)(2,1)} %get-tuple-element.24), channel_id=1, source_target_pairs={{0,12},{1,13},{2,14},{3,15},{4,0},{5,1},{6,2},{7,3},{8,4},{9,5},{1... | collective-permute-start | bytes 1769480 | tf_op jit(solution)/shard_map/ppermute | solution.py:28
  20.8 22.2 %collective-permute-start.7 = (bf16[4,3,8,24,128]{4,3,2,1,0:T(8,128)(2,1)}, bf16[4,3,8,24,128]{4,3,2,1,0:T(8,128)(2,1)S(1)}, u32[]{:S(2)}, u32[]{:S(2)}) collective-permute-start(bf16[4,3,8,24,128]{4,3,2,1,0:T(8,128)(2,1)} %get-tuple-element.23), channel_id=1, source_target_pairs={{0,8},{1,9},{2,10},{3,11},{4,12},{5,13},{6,14},{7,15},{8,0},{9,1},... | collective-permute-start | bytes 1769480 | tf_op jit(solution)/shard_map/ppermute | solution.py:28
  21.3 29.1 %collective-permute-start.6 = (bf16[4,3,8,24,128]{4,3,2,1,0:T(8,128)(2,1)}, bf16[4,3,8,24,128]{4,3,2,1,0:T(8,128)(2,1)S(1)}, u32[]{:S(2)}, u32[]{:S(2)}) collective-permute-start(bf16[4,3,8,24,128]{4,3,2,1,0:T(8,128)(2,1)} %get-tuple-element.22), channel_id=1, source_target_pairs={{0,4},{1,5},{2,6},{3,7},{4,8},{5,9},{6,10},{7,11},{8,12},{9,13},{1... | collective-permute-start | bytes 1769480 | tf_op jit(solution)/shard_map/ppermute | solution.py:28
  30.1 38.7 %collective-permute-start.1 = (bf16[4,3,8,24,128]{4,3,2,1,0:T(8,128)(2,1)}, bf16[4,3,8,24,128]{4,3,2,1,0:T(8,128)(2,1)S(1)}, u32[]{:S(2)}, u32[]{:S(2)}) collective-permute-start(bf16[4,3,8,24,128]{4,3,2,1,0:T(8,128)(2,1)} %get-tuple-element.18), channel_id=1, source_target_pairs={{0,2},{1,3},{2,0},{3,1},{4,6},{5,7},{6,4},{7,5},{8,10},{9,11},{10,... | collective-permute-start | bytes 1769480 | tf_op jit(solution)/shard_map/ppermute | solution.py:28
  53.2 66.9 %all-to-all-start.1 = ((bf16[4,4,3,8,24,128]{5,4,3,2,1,0:T(8,128)(2,1)}), bf16[4,4,3,8,24,128]{5,4,3,2,1,0:T(8,128)(2,1)}, u32[]{:S(2)}, u32[]{:S(2)}) async-start(bf16[4,4,3,8,24,128]{5,4,3,2,1,0:T(8,128)(2,1)} %pad_maximum_fusion), calls=%async_computation.1 | async-start | bytes 4718592 | tf_op jit(solution)/shard_map/all_to_all | solution.py:32
  61.1 15.3 %copy-start.6 = (s32[8]{0:T(128)S(1)}, s32[8]{0:T(128)}, u32[]{:S(2)}) copy-start(s32[8]{0:T(128)} %param.12) | copy-start | bytes 100
  68.7 0.8 copy-start.3
  69.6 15.6 %collective-permute-start.3 = (bf16[4,3,8,24,128]{4,3,2,1,0:T(8,128)(2,1)S(1)}, bf16[4,3,8,24,128]{4,3,2,1,0:T(8,128)(2,1)}, u32[]{:S(2)}, u32[]{:S(2)}) collective-permute-start(bf16[4,3,8,24,128]{4,3,2,1,0:T(8,128)(2,1)S(1)} %pad_maximum_fusion.1), channel_id=1, source_target_pairs={{0,4},{1,5},{2,6},{3,7},{4,8},{5,9},{6,10},{7,11},{8,12},{9,13},{1... | collective-permute-start | bytes 1769480 | tf_op jit(solution)/shard_map/ppermute | solution.py:28
  71.9 27.1 %collective-permute-start.4 = (bf16[4,3,8,24,128]{4,3,2,1,0:T(8,128)(2,1)}, bf16[4,3,8,24,128]{4,3,2,1,0:T(8,128)(2,1)}, u32[]{:S(2)}, u32[]{:S(2)}) collective-permute-start(bf16[4,3,8,24,128]{4,3,2,1,0:T(8,128)(2,1)} %pad_maximum_fusion.2), channel_id=1, source_target_pairs={{0,8},{1,9},{2,10},{3,11},{4,12},{5,13},{6,14},{7,15},{8,0},{9,1},... | collective-permute-start | bytes 1769480 | tf_op jit(solution)/shard_map/ppermute | solution.py:28
  75.2 24.4 %collective-permute-start.5 = (bf16[4,3,8,24,128]{4,3,2,1,0:T(8,128)(2,1)}, bf16[4,3,8,24,128]{4,3,2,1,0:T(8,128)(2,1)}, u32[]{:S(2)}, u32[]{:S(2)}) collective-permute-start(bf16[4,3,8,24,128]{4,3,2,1,0:T(8,128)(2,1)} %pad_maximum_fusion.3), channel_id=1, source_target_pairs={{0,12},{1,13},{2,14},{3,15},{4,0},{5,1},{6,2},{7,3},{8,4},{9,5},{1... | collective-permute-start | bytes 1769480 | tf_op jit(solution)/shard_map/ppermute | solution.py:28
  120.2 27.3 %all-to-all-start = ((bf16[16,8,24,128]{3,2,1,0:T(8,128)(2,1)}), bf16[16,8,24,128]{3,2,1,0:T(8,128)(2,1)S(1)}, u32[]{:S(2)}, u32[]{:S(2)}) async-start(bf16[16,8,24,128]{3,2,1,0:T(8,128)(2,1)} %attend.2._), calls=%async_computation | async-start | bytes 1572864 | tf_op jit(solution)/shard_map/all_to_all | solution.py:32
  147.5 36.7 %copy-start.1 = (bf16[16,8,24,128]{3,2,1,0:T(8,128)(2,1)}, bf16[16,8,24,128]{3,2,1,0:T(8,128)(2,1)S(1)}, u32[]{:S(2)}) copy-start(bf16[16,8,24,128]{3,2,1,0:T(8,128)(2,1)S(1)} %all-to-all-done.refs_0_) | copy-start | bytes 2359300
  147.5 25.6 %all-to-all-start.2 = ((bf16[16,8,24,128]{3,2,1,0:T(8,128)(2,1)}), bf16[16,8,24,128]{3,2,1,0:T(8,128)(2,1)}, u32[]{:S(2)}, u32[]{:S(2)}) async-start(bf16[16,8,24,128]{3,2,1,0:T(8,128)(2,1)} %attend.3), calls=%async_computation.2 | async-start | bytes 1572864 | tf_op jit(solution)/shard_map/all_to_all | solution.py:32
  154.5 28.1 %collective-permute-start.9 = (bf16[16,24,128]{2,1,0:T(8,128)(2,1)S(1)}, bf16[16,24,128]{2,1,0:T(8,128)(2,1)S(1)}, u32[]{:S(2)}, u32[]{:S(2)}) collective-permute-start(bf16[16,24,128]{2,1,0:T(8,128)(2,1)S(1)} %dynamic-slice_bitcast_fusion.1), channel_id=1, source_target_pairs={{0,16},{16,32},{32,48},{48,64},{64,80},{80,96},{96,112},{112,128},... | collective-permute-start | bytes 294920 | tf_op jit(solution)/shard_map/ppermute | solution.py:303
  174.1 10.2 %collective-permute-start.10 = (bf16[16,24,128]{2,1,0:T(8,128)(2,1)S(1)}, bf16[16,24,128]{2,1,0:T(8,128)(2,1)S(1)}, u32[]{:S(2)}, u32[]{:S(2)}) collective-permute-start(bf16[16,24,128]{2,1,0:T(8,128)(2,1)S(1)} %dynamic-slice_bitcast_fusion), channel_id=1, source_target_pairs={{0,16},{16,32},{32,48},{48,64},{64,80},{80,96},{96,112},{112,128},... | collective-permute-start | bytes 294920 | tf_op jit(solution)/shard_map/ppermute | solution.py:303
  182.6 1.6 copy-start.4
  184.3 0.6 copy-start.5

commit v10 on v9

--- a/solution.py
+++ b/solution.py
@@ -81,7 +81,7 @@
 
 def prepare(head, place, query, key, value, qk_gain):
     frames, rows, inner = query.shape
-    step = 2
+    step = 4
     tall = pl.BlockSpec((step, rows, inner), lambda n, _: (n, 0, 0))
     out = pl.BlockSpec((SIDE, 3, step, rows, HD), lambda n, _: (0, 0, n, 0, 0))
     shape = jax.ShapeDtypeStruct((SIDE, 3, frames, rows, HD), jnp.bfloat16)

time: 190 us -> 189 us (level)
  no operation moved by 1% of the time
where the time goes in v10:
time: 189 us; the launch traced here: 187 us
  waiting for transfers between devices  72.8 us (39%)
  starting transfers between devices  59.4 us (31%)
  Pallas kernels  43.6 us (23%)
  other arithmetic  5.45 us (3%)
  local copies, waits for them, and re-layouts  5.24 us (3%)
    ppermute x9, waiting for transfers between devices, moved(): return lax.ppermute(value, 'seq', pairs)  46.2 us
    pallas_call x2, Pallas kernels, attend(): pl.pallas_call(functools.partial(attend_kernel, len(sent)), grid_spec=plt...  30.2 us
    ppermute x9, starting transfers between devices, moved(): return lax.ppermute(value, 'seq', pairs)  27.5 us
    all_to_all x3, waiting for transfers between devices, exchange(): lax.all_to_all(pieces, 'seq', split_axis=0, concat_axis=0, tiled=True, **...  25 us
    all_to_all x3, starting transfers between devices, exchange(): lax.all_to_all(pieces, 'seq', split_axis=0, concat_axis=0, tiled=True, **...  19.7 us
    ppermute x2, starting transfers between devices, shards(): lax.ppermute(leaving, 'section', [(n, n + 1) for n in range(sections - 1)])  12.2 us
    pallas_call x2, Pallas kernels, prepare(): pl.pallas_call(functools.partial(prepare_kernel, head), grid_spec=pltpu.P...  10.2 us
  transfers between devices with their start and end apart: 14, of which 10 were waited for; matrix products, arithmetic and copies ran while one was open for 5% of the time, Pallas kernels for 19%

profile of v10, /device:TPU:17, one launch (start us, length us, event | category | flops | bytes accessed | tf_op | source)
XLA Modules:
  0.0 187.5 jit_solution(3998480344018028210)
XLA Ops:
  0.0 0.0 copy-start
  0.0 0.7 pad_add_fusion.place
  0.7 5.0 %prepare.2 = (bf16[4,3,8,24,128]{4,3,2,1,0:T(8,128)(2,1)}, bf16[4,3,8,24,128]{4,3,2,1,0:T(8,128)(2,1)}, bf16[4,3,8,24,128]{4,3,2,1,0:T(8,128)(2,1)}, bf16[4,3,8,24,128]{4,3,2,1,0:T(8,128)(2,1)}) custom-call(s32[3]{0:T(128)} %pad_add_fusion.place, bf16[8,24,4096]{2,1,0:T(8,128)(2,1)} %q_ref.3, bf16[8,24,4096]{2,1,0:T(8,128)(2,1)} %k_ref.3, ...), custom_call_target="tpu_custom_call" | custom-call | flops 7864320 | bytes 9437184 | tf_op jit(solution)/shard_map/prepare/pallas_call | solution.py:88
  5.7 3.0 %collective-permute-start = (bf16[4,3,8,24,128]{4,3,2,1,0:T(8,128)(2,1)}, bf16[4,3,8,24,128]{4,3,2,1,0:T(8,128)(2,1)}, u32[]{:S(2)}, u32[]{:S(2)}) collective-permute-start(bf16[4,3,8,24,128]{4,3,2,1,0:T(8,128)(2,1)} %get-tuple-element.17), channel_id=1, source_target_pairs={{0,1},{1,2},{2,3},{3,0},{4,5},{5,6},{6,7},{7,4},{8,9},{9,10},{10,1... | collective-permute-start | bytes 1769480 | tf_op jit(solution)/shard_map/ppermute | solution.py:28
  8.6 3.1 %collective-permute-start.2 = (bf16[4,3,8,24,128]{4,3,2,1,0:T(8,128)(2,1)}, bf16[4,3,8,24,128]{4,3,2,1,0:T(8,128)(2,1)}, u32[]{:S(2)}, u32[]{:S(2)}) collective-permute-start(bf16[4,3,8,24,128]{4,3,2,1,0:T(8,128)(2,1)} %get-tuple-element.19), channel_id=1, source_target_pairs={{0,3},{1,0},{2,1},{3,2},{4,7},{5,4},{6,5},{7,6},{8,11},{9,8},{10,9... | collective-permute-start | bytes 1769480 | tf_op jit(solution)/shard_map/ppermute | solution.py:28
  11.8 0.0 copy-start.2
  11.8 5.2 %prepare.3 = (bf16[4,3,8,24,128]{4,3,2,1,0:T(8,128)(2,1)}, bf16[4,3,8,24,128]{4,3,2,1,0:T(8,128)(2,1)}, bf16[4,3,8,24,128]{4,3,2,1,0:T(8,128)(2,1)}, bf16[4,3,8,24,128]{4,3,2,1,0:T(8,128)(2,1)}) custom-call(s32[3]{0:T(128)} %pad_add_fusion.place, bf16[8,24,4096]{2,1,0:T(8,128)(2,1)} %q_ref.3, bf16[8,24,4096]{2,1,0:T(8,128)(2,1)} %k_ref.3, ...), custom_call_target="tpu_custom_call" | custom-call | flops 7864320 | bytes 9437184 | tf_op jit(solution)/shard_map/prepare/pallas_call | solution.py:88
  16.9 2.5 %collective-permute-start.8 = (bf16[4,3,8,24,128]{4,3,2,1,0:T(8,128)(2,1)}, bf16[4,3,8,24,128]{4,3,2,1,0:T(8,128)(2,1)S(1)}, u32[]{:S(2)}, u32[]{:S(2)}) collective-permute-start(bf16[4,3,8,24,128]{4,3,2,1,0:T(8,128)(2,1)} %get-tuple-element.24), channel_id=1, source_target_pairs={{0,12},{1,13},{2,14},{3,15},{4,0},{5,1},{6,2},{7,3},{8,4},{9,5},{1... | collective-permute-start | bytes 1769480 | tf_op jit(solution)/shard_map/ppermute | solution.py:28
  19.4 0.5 collective-permute-start.7
  19.9 0.6 collective-permute-start.6
  20.5 0.0 copy-done.2
  20.6 8.8 %collective-permute-done.refs_1_ = bf16[4,3,8,24,128]{4,3,2,1,0:T(8,128)(2,1)} collective-permute-done((bf16[4,3,8,24,128]{4,3,2,1,0:T(8,128)(2,1)}, bf16[4,3,8,24,128]{4,3,2,1,0:T(8,128)(2,1)}, u32[]{:S(2)}, u32[]{:S(2)}) %collective-permute-start) | collective-permute-done | bytes 589856 | tf_op jit(solution)/shard_map/ppermute | solution.py:28
  29.4 12.9 %collective-permute-start.1 = (bf16[4,3,8,24,128]{4,3,2,1,0:T(8,128)(2,1)}, bf16[4,3,8,24,128]{4,3,2,1,0:T(8,128)(2,1)S(1)}, u32[]{:S(2)}, u32[]{:S(2)}) collective-permute-start(bf16[4,3,8,24,128]{4,3,2,1,0:T(8,128)(2,1)} %get-tuple-element.18), channel_id=1, source_target_pairs={{0,2},{1,3},{2,0},{3,1},{4,6},{5,7},{6,4},{7,5},{8,10},{9,11},{10,... | collective-permute-start | bytes 1769480 | tf_op jit(solution)/shard_map/ppermute | solution.py:28
  42.3 0.0 collective-permute-done.2.refs_3_
  42.3 0.0 collective-permute-done.8
  42.3 0.0 collective-permute-done.7
  42.3 6.7 %collective-permute-done.6 = bf16[4,3,8,24,128]{4,3,2,1,0:T(8,128)(2,1)S(1)} collective-permute-done((bf16[4,3,8,24,128]{4,3,2,1,0:T(8,128)(2,1)}, bf16[4,3,8,24,128]{4,3,2,1,0:T(8,128)(2,1)S(1)}, u32[]{:S(2)}, u32[]{:S(2)}) %collective-permute-start.6) | collective-permute-done | bytes 589856 | tf_op jit(solution)/shard_map/ppermute | solution.py:28
  49.0 2.8 %pad_maximum_fusion = bf16[4,4,3,8,24,128]{5,4,3,2,1,0:T(8,128)(2,1)} fusion(bf16[4,1,3,8,24,128]{5,4,3,2,1,0:T(8,128)(2,1)S(1)} %bitcast.16, bf16[4,1,3,8,24,128]{5,4,3,2,1,0:T(8,128)(2,1)S(1)} %bitcast.17, bf16[4,1,3,8,24,128]{5,4,3,2,1,0:T(8,128)(2,1)S(1)} %bitcast.18, bf16[4,1,3,8,24,128]{5,4,3,2,1,0:T(8,128)(2,1)} %bitcast.15), kind=kLoop, calls=%fused_computation | loop fusion | flops 3538944 | bytes 4718592 | tf_op jit(solution)/shard_map/stack | solution.py:295
  51.8 5.7 %all-to-all-start.1 = ((bf16[4,4,3,8,24,128]{5,4,3,2,1,0:T(8,128)(2,1)}), bf16[4,4,3,8,24,128]{5,4,3,2,1,0:T(8,128)(2,1)}, u32[]{:S(2)}, u32[]{:S(2)}) async-start(bf16[4,4,3,8,24,128]{5,4,3,2,1,0:T(8,128)(2,1)} %pad_maximum_fusion), calls=%async_computation.1 | async-start | bytes 4718592 | tf_op jit(solution)/shard_map/all_to_all | solution.py:32
  57.5 1.1 fusion.12
  58.6 1.1 fusion.10
  59.7 0.0 copy-start.6
  59.7 8.4 %collective-permute-done.1.refs_2_ = bf16[4,3,8,24,128]{4,3,2,1,0:T(8,128)(2,1)S(1)} collective-permute-done((bf16[4,3,8,24,128]{4,3,2,1,0:T(8,128)(2,1)}, bf16[4,3,8,24,128]{4,3,2,1,0:T(8,128)(2,1)S(1)}, u32[]{:S(2)}, u32[]{:S(2)}) %collective-permute-start.1) | collective-permute-done | bytes 589856 | tf_op jit(solution)/shard_map/ppermute | solution.py:28
  68.1 0.0 copy-start.3
  68.1 0.8 copy-done.3
  68.9 0.1 pad_maximum_fusion.1
  69.0 1.3 collective-permute-start.3
  70.3 0.9 pad_maximum_fusion.2
  71.2 2.5 %collective-permute-start.4 = (bf16[4,3,8,24,128]{4,3,2,1,0:T(8,128)(2,1)}, bf16[4,3,8,24,128]{4,3,2,1,0:T(8,128)(2,1)}, u32[]{:S(2)}, u32[]{:S(2)}) collective-permute-start(bf16[4,3,8,24,128]{4,3,2,1,0:T(8,128)(2,1)} %pad_maximum_fusion.2), channel_id=1, source_target_pairs={{0,8},{1,9},{2,10},{3,11},{4,12},{5,13},{6,14},{7,15},{8,0},{9,1},... | collective-permute-start | bytes 1769480 | tf_op jit(solution)/shard_map/ppermute | solution.py:28
  73.6 0.9 pad_maximum_fusion.3
  74.5 1.2 collective-permute-start.5
  75.7 0.0 copy-done.6
  75.7 0.1 fusion.2
  75.8 0.0 copy-done
  75.8 0.2 fusion
  76.0 0.6 fusion.13
  76.6 8.0 %collective-permute-done.3.refs_4_ = bf16[4,3,8,24,128]{4,3,2,1,0:T(8,128)(2,1)} collective-permute-done((bf16[4,3,8,24,128]{4,3,2,1,0:T(8,128)(2,1)S(1)}, bf16[4,3,8,24,128]{4,3,2,1,0:T(8,128)(2,1)}, u32[]{:S(2)}, u32[]{:S(2)}) %collective-permute-start.3) | collective-permute-done | bytes 589856 | tf_op jit(solution)/shard_map/ppermute | solution.py:28
  84.6 13.7 %collective-permute-done.4.refs_5_ = bf16[4,3,8,24,128]{4,3,2,1,0:T(8,128)(2,1)} collective-permute-done((bf16[4,3,8,24,128]{4,3,2,1,0:T(8,128)(2,1)}, bf16[4,3,8,24,128]{4,3,2,1,0:T(8,128)(2,1)}, u32[]{:S(2)}, u32[]{:S(2)}) %collective-permute-start.4) | collective-permute-done | bytes 589856 | tf_op jit(solution)/shard_map/ppermute | solution.py:28
  98.3 0.6 collective-permute-done.5.refs_6_
  98.9 15.1 %attend.2._ = bf16[16,8,24,128]{3,2,1,0:T(8,128)(2,1)} custom-call(s32[3]{0:T(128)} %pad_add_fusion.place, f32[8,128]{1,0:T(8,128)} %get-tuple-element.40.gate_ref, f32[2,4096]{1,0:T(2,128)} %gain_ref.3, bf16[4,3,8,24,128]{4,3,2,1,0:T(8,128)(2,1)} %get-tuple-element.16.refs_0_, bf16[4,3,8,24,128]{4,3,2,1,0:T(8,128)(2,1)} %collective-permute-done.refs_1_, ...), custom_call_target="tpu_custom_call" | custom-call | flops 20535312384 | bytes 3072 | tf_op jit(solution)/shard_map/attend/pallas_call | solution.py:194
  114.0 5.9 %all-to-all-done.1.refs_0_ = bf16[4,4,3,8,24,128]{5,4,3,2,1,0:T(8,128)(2,1)} async-done(((bf16[4,4,3,8,24,128]{5,4,3,2,1,0:T(8,128)(2,1)}), bf16[4,4,3,8,24,128]{5,4,3,2,1,0:T(8,128)(2,1)}, u32[]{:S(2)}, u32[]{:S(2)}) %all-to-all-start.1) | async-done | bytes 2359328 | tf_op jit(solution)/shard_map/all_to_all | solution.py:32
  119.9 7.8 %all-to-all-start = ((bf16[16,8,24,128]{3,2,1,0:T(8,128)(2,1)}), bf16[16,8,24,128]{3,2,1,0:T(8,128)(2,1)S(1)}, u32[]{:S(2)}, u32[]{:S(2)}) async-start(bf16[16,8,24,128]{3,2,1,0:T(8,128)(2,1)} %attend.2._), calls=%async_computation | async-start | bytes 1572864 | tf_op jit(solution)/shard_map/all_to_all | solution.py:32
  127.7 15.1 %attend.3 = bf16[16,8,24,128]{3,2,1,0:T(8,128)(2,1)} custom-call(s32[3]{0:T(128)} %pad_add_fusion.place, f32[8,128]{1,0:T(8,128)} %get-tuple-element.39.gate_ref, bf16[16,8,24,128]{3,2,1,0:T(8,128)(2,1)} %attend.2._, bf16[4,4,3,8,24,128]{5,4,3,2,1,0:T(8,128)(2,1)} %all-to-all-done.1.refs_0_), custom_call_target="tpu_custom_call" | custom-call | flops 33822867456 | bytes 3145728 | tf_op jit(solution)/shard_map/attend/pallas_call | solution.py:194
  142.8 4.1 %all-to-all-done.refs_0_ = bf16[16,8,24,128]{3,2,1,0:T(8,128)(2,1)S(1)} async-done(((bf16[16,8,24,128]{3,2,1,0:T(8,128)(2,1)}), bf16[16,8,24,128]{3,2,1,0:T(8,128)(2,1)S(1)}, u32[]{:S(2)}, u32[]{:S(2)}) %all-to-all-start) | async-done | bytes 786464 | tf_op jit(solution)/shard_map/all_to_all | solution.py:32
  146.9 0.0 copy-start.1
  146.9 6.3 %all-to-all-start.2 = ((bf16[16,8,24,128]{3,2,1,0:T(8,128)(2,1)}), bf16[16,8,24,128]{3,2,1,0:T(8,128)(2,1)}, u32[]{:S(2)}, u32[]{:S(2)}) async-start(bf16[16,8,24,128]{3,2,1,0:T(8,128)(2,1)} %attend.3), calls=%async_computation.2 | async-start | bytes 1572864 | tf_op jit(solution)/shard_map/all_to_all | solution.py:32
  153.8 3.6 %collective-permute-start.9 = (bf16[16,24,128]{2,1,0:T(8,128)(2,1)S(1)}, bf16[16,24,128]{2,1,0:T(8,128)(2,1)S(1)}, u32[]{:S(2)}, u32[]{:S(2)}) collective-permute-start(bf16[16,24,128]{2,1,0:T(8,128)(2,1)S(1)} %dynamic-slice_bitcast_fusion.1), channel_id=1, source_target_pairs={{0,16},{16,32},{32,48},{48,64},{64,80},{80,96},{96,112},{112,128},... | collective-permute-start | bytes 294920 | tf_op jit(solution)/shard_map/ppermute | solution.py:303
  157.4 15.0 %all-to-all-done.2.refs_1_ = bf16[16,8,24,128]{3,2,1,0:T(8,128)(2,1)} async-done(((bf16[16,8,24,128]{3,2,1,0:T(8,128)(2,1)}), bf16[16,8,24,128]{3,2,1,0:T(8,128)(2,1)}, u32[]{:S(2)}, u32[]{:S(2)}) %all-to-all-start.2) | async-done | bytes 786464 | tf_op jit(solution)/shard_map/all_to_all | solution.py:32
  172.5 0.9 dynamic-slice_bitcast_fusion
  173.4 8.6 %collective-permute-start.10 = (bf16[16,24,128]{2,1,0:T(8,128)(2,1)S(1)}, bf16[16,24,128]{2,1,0:T(8,128)(2,1)S(1)}, u32[]{:S(2)}, u32[]{:S(2)}) collective-permute-start(bf16[16,24,128]{2,1,0:T(8,128)(2,1)S(1)} %dynamic-slice_bitcast_fusion), channel_id=1, source_target_pairs={{0,16},{16,32},{32,48},{48,64},{64,80},{80,96},{96,112},{112,128},... | collective-permute-start | bytes 294920 | tf_op jit(solution)/shard_map/ppermute | solution.py:303
  182.0 0.0 collective-permute-done.9.refs_2_
  182.0 0.0 copy-start.4
  182.0 1.6 collective-permute-done.10.refs_3_
  183.6 0.0 copy-done.1
  183.6 0.0 copy-done.4
  183.6 0.0 copy-start.5
  183.6 0.6 copy-done.5
  184.2 3.3 %assemble.1 = bf16[8,24,4096]{2,1,0:T(8,128)(2,1)} custom-call(s32[1]{0:T(128)} %copy.9.slot, s32[3]{0:T(128)} %pad_add_fusion.place, bf16[16,8,24,128]{3,2,1,0:T(8,128)(2,1)} %copy-done.1, bf16[16,8,24,128]{3,2,1,0:T(8,128)(2,1)} %all-to-all-done.2.refs_1_, bf16[16,24,128]{2,1,0:T(8,128)(2,1)} %copy-done.4, bf16[16,24,128]{2,1,0:T(8,128)(2,1)} %copy-done.5, ...), custom_call_target="tpu_custom_call" | custom-call | tf_op jit(solution)/shard_map/assemble/pallas_call | solution.py:259
  (5 shorter events, 0.1 us)
Async XLA Ops:
  0.0 75.8 %copy-start = (bf16[256,4096]{1,0:T(8,128)(2,1)S(1)}, bf16[256,4096]{1,0:T(8,128)(2,1)}, u32[]{:S(2)}) copy-start(bf16[256,4096]{1,0:T(8,128)(2,1)} %param.13) | copy-start | bytes 6291460
  5.7 23.8 %collective-permute-start = (bf16[4,3,8,24,128]{4,3,2,1,0:T(8,128)(2,1)}, bf16[4,3,8,24,128]{4,3,2,1,0:T(8,128)(2,1)}, u32[]{:S(2)}, u32[]{:S(2)}) collective-permute-start(bf16[4,3,8,24,128]{4,3,2,1,0:T(8,128)(2,1)} %get-tuple-element.17), channel_id=1, source_target_pairs={{0,1},{1,2},{2,3},{3,0},{4,5},{5,6},{6,7},{7,4},{8,9},{9,10},{10,1... | collective-permute-start | bytes 1769480 | tf_op jit(solution)/shard_map/ppermute | solution.py:28
  8.6 33.7 %collective-permute-start.2 = (bf16[4,3,8,24,128]{4,3,2,1,0:T(8,128)(2,1)}, bf16[4,3,8,24,128]{4,3,2,1,0:T(8,128)(2,1)}, u32[]{:S(2)}, u32[]{:S(2)}) collective-permute-start(bf16[4,3,8,24,128]{4,3,2,1,0:T(8,128)(2,1)} %get-tuple-element.19), channel_id=1, source_target_pairs={{0,3},{1,0},{2,1},{3,2},{4,7},{5,4},{6,5},{7,6},{8,11},{9,8},{10,9... | collective-permute-start | bytes 1769480 | tf_op jit(solution)/shard_map/ppermute | solution.py:28
  11.8 8.8 %copy-start.2 = (bf16[4,3,8,24,128]{4,3,2,1,0:T(8,128)(2,1)S(1)}, bf16[4,3,8,24,128]{4,3,2,1,0:T(8,128)(2,1)}, u32[]{:S(2)}) copy-start(bf16[4,3,8,24,128]{4,3,2,1,0:T(8,128)(2,1)} %get-tuple-element.16.refs_0_) | copy-start | bytes 1769476
  16.9 25.4 %collective-permute-start.8 = (bf16[4,3,8,24,128]{4,3,2,1,0:T(8,128)(2,1)}, bf16[4,3,8,24,128]{4,3,2,1,0:T(8,128)(2,1)S(1)}, u32[]{:S(2)}, u32[]{:S(2)}) collective-permute-start(bf16[4,3,8,24,128]{4,3,2,1,0:T(8,128)(2,1)} %get-tuple-element.24), channel_id=1, source_target_pairs={{0,12},{1,13},{2,14},{3,15},{4,0},{5,1},{6,2},{7,3},{8,4},{9,5},{1... | collective-permute-start | bytes 1769480 | tf_op jit(solution)/shard_map/ppermute | solution.py:28
  19.4 22.9 %collective-permute-start.7 = (bf16[4,3,8,24,128]{4,3,2,1,0:T(8,128)(2,1)}, bf16[4,3,8,24,128]{4,3,2,1,0:T(8,128)(2,1)S(1)}, u32[]{:S(2)}, u32[]{:S(2)}) collective-permute-start(bf16[4,3,8,24,128]{4,3,2,1,0:T(8,128)(2,1)} %get-tuple-element.23), channel_id=1, source_target_pairs={{0,8},{1,9},{2,10},{3,11},{4,12},{5,13},{6,14},{7,15},{8,0},{9,1},... | collective-permute-start | bytes 1769480 | tf_op jit(solution)/shard_map/ppermute | solution.py:28
  19.9 29.1 %collective-permute-start.6 = (bf16[4,3,8,24,128]{4,3,2,1,0:T(8,128)(2,1)}, bf16[4,3,8,24,128]{4,3,2,1,0:T(8,128)(2,1)S(1)}, u32[]{:S(2)}, u32[]{:S(2)}) collective-permute-start(bf16[4,3,8,24,128]{4,3,2,1,0:T(8,128)(2,1)} %get-tuple-element.22), channel_id=1, source_target_pairs={{0,4},{1,5},{2,6},{3,7},{4,8},{5,9},{6,10},{7,11},{8,12},{9,13},{1... | collective-permute-start | bytes 1769480 | tf_op jit(solution)/shard_map/ppermute | solution.py:28
  29.4 38.7 %collective-permute-start.1 = (bf16[4,3,8,24,128]{4,3,2,1,0:T(8,128)(2,1)}, bf16[4,3,8,24,128]{4,3,2,1,0:T(8,128)(2,1)S(1)}, u32[]{:S(2)}, u32[]{:S(2)}) collective-permute-start(bf16[4,3,8,24,128]{4,3,2,1,0:T(8,128)(2,1)} %get-tuple-element.18), channel_id=1, source_target_pairs={{0,2},{1,3},{2,0},{3,1},{4,6},{5,7},{6,4},{7,5},{8,10},{9,11},{10,... | collective-permute-start | bytes 1769480 | tf_op jit(solution)/shard_map/ppermute | solution.py:28
  51.8 68.1 %all-to-all-start.1 = ((bf16[4,4,3,8,24,128]{5,4,3,2,1,0:T(8,128)(2,1)}), bf16[4,4,3,8,24,128]{5,4,3,2,1,0:T(8,128)(2,1)}, u32[]{:S(2)}, u32[]{:S(2)}) async-start(bf16[4,4,3,8,24,128]{5,4,3,2,1,0:T(8,128)(2,1)} %pad_maximum_fusion), calls=%async_computation.1 | async-start | bytes 4718592 | tf_op jit(solution)/shard_map/all_to_all | solution.py:32
  59.7 16.0 %copy-start.6 = (s32[8]{0:T(128)S(1)}, s32[8]{0:T(128)}, u32[]{:S(2)}) copy-start(s32[8]{0:T(128)} %param.12) | copy-start | bytes 100
  68.1 0.8 copy-start.3
  69.0 15.6 %collective-permute-start.3 = (bf16[4,3,8,24,128]{4,3,2,1,0:T(8,128)(2,1)S(1)}, bf16[4,3,8,24,128]{4,3,2,1,0:T(8,128)(2,1)}, u32[]{:S(2)}, u32[]{:S(2)}) collective-permute-start(bf16[4,3,8,24,128]{4,3,2,1,0:T(8,128)(2,1)S(1)} %pad_maximum_fusion.1), channel_id=1, source_target_pairs={{0,4},{1,5},{2,6},{3,7},{4,8},{5,9},{6,10},{7,11},{8,12},{9,13},{1... | collective-permute-start | bytes 1769480 | tf_op jit(solution)/shard_map/ppermute | solution.py:28
  71.2 27.1 %collective-permute-start.4 = (bf16[4,3,8,24,128]{4,3,2,1,0:T(8,128)(2,1)}, bf16[4,3,8,24,128]{4,3,2,1,0:T(8,128)(2,1)}, u32[]{:S(2)}, u32[]{:S(2)}) collective-permute-start(bf16[4,3,8,24,128]{4,3,2,1,0:T(8,128)(2,1)} %pad_maximum_fusion.2), channel_id=1, source_target_pairs={{0,8},{1,9},{2,10},{3,11},{4,12},{5,13},{6,14},{7,15},{8,0},{9,1},... | collective-permute-start | bytes 1769480 | tf_op jit(solution)/shard_map/ppermute | solution.py:28
  74.5 24.4 %collective-permute-start.5 = (bf16[4,3,8,24,128]{4,3,2,1,0:T(8,128)(2,1)}, bf16[4,3,8,24,128]{4,3,2,1,0:T(8,128)(2,1)}, u32[]{:S(2)}, u32[]{:S(2)}) collective-permute-start(bf16[4,3,8,24,128]{4,3,2,1,0:T(8,128)(2,1)} %pad_maximum_fusion.3), channel_id=1, source_target_pairs={{0,12},{1,13},{2,14},{3,15},{4,0},{5,1},{6,2},{7,3},{8,4},{9,5},{1... | collective-permute-start | bytes 1769480 | tf_op jit(solution)/shard_map/ppermute | solution.py:28
  119.9 27.0 %all-to-all-start = ((bf16[16,8,24,128]{3,2,1,0:T(8,128)(2,1)}), bf16[16,8,24,128]{3,2,1,0:T(8,128)(2,1)S(1)}, u32[]{:S(2)}, u32[]{:S(2)}) async-start(bf16[16,8,24,128]{3,2,1,0:T(8,128)(2,1)} %attend.2._), calls=%async_computation | async-start | bytes 1572864 | tf_op jit(solution)/shard_map/all_to_all | solution.py:32
  146.9 36.7 %copy-start.1 = (bf16[16,8,24,128]{3,2,1,0:T(8,128)(2,1)}, bf16[16,8,24,128]{3,2,1,0:T(8,128)(2,1)S(1)}, u32[]{:S(2)}) copy-start(bf16[16,8,24,128]{3,2,1,0:T(8,128)(2,1)S(1)} %all-to-all-done.refs_0_) | copy-start | bytes 2359300
  146.9 25.6 %all-to-all-start.2 = ((bf16[16,8,24,128]{3,2,1,0:T(8,128)(2,1)}), bf16[16,8,24,128]{3,2,1,0:T(8,128)(2,1)}, u32[]{:S(2)}, u32[]{:S(2)}) async-start(bf16[16,8,24,128]{3,2,1,0:T(8,128)(2,1)} %attend.3), calls=%async_computation.2 | async-start | bytes 1572864 | tf_op jit(solution)/shard_map/all_to_all | solution.py:32
  153.8 28.1 %collective-permute-start.9 = (bf16[16,24,128]{2,1,0:T(8,128)(2,1)S(1)}, bf16[16,24,128]{2,1,0:T(8,128)(2,1)S(1)}, u32[]{:S(2)}, u32[]{:S(2)}) collective-permute-start(bf16[16,24,128]{2,1,0:T(8,128)(2,1)S(1)} %dynamic-slice_bitcast_fusion.1), channel_id=1, source_target_pairs={{0,16},{16,32},{32,48},{48,64},{64,80},{80,96},{96,112},{112,128},... | collective-permute-start | bytes 294920 | tf_op jit(solution)/shard_map/ppermute | solution.py:303
  173.4 10.2 %collective-permute-start.10 = (bf16[16,24,128]{2,1,0:T(8,128)(2,1)S(1)}, bf16[16,24,128]{2,1,0:T(8,128)(2,1)S(1)}, u32[]{:S(2)}, u32[]{:S(2)}) collective-permute-start(bf16[16,24,128]{2,1,0:T(8,128)(2,1)S(1)} %dynamic-slice_bitcast_fusion), channel_id=1, source_target_pairs={{0,16},{16,32},{32,48},{48,64},{64,80},{80,96},{96,112},{112,128},... | collective-permute-start | bytes 294920 | tf_op jit(solution)/shard_map/ppermute | solution.py:303
  182.0 1.6 copy-start.4
  183.6 0.6 copy-start.5
